TPU v7x, 32 devices: a whole 2x2x4 slice. The times are simulated.
32 devices in a mesh: mesh: 16 (over z, y, core), harm: 2 (over x).
Axes of the slice: x: 2, y: 2, z: 4, core: 2. Of those that a mesh axis runs over, the one named last changes fastest.
Arguments:
- bias_source: float32 [3, 128, 16, 256], P(None, 'mesh', 'harm'), may hold values from -6 to 6
- bias_start: float32 [3, 128, 16, 256], P(None, 'mesh', 'harm'), may hold values from -6 to 6
- region: int32 [128, 16, 256], P('mesh', 'harm'), may hold values from 0 to 3
- table_index: int32 [4], replicated, may hold values from 0 to 3
- bh_base: float32 [4], replicated, may hold values from 0.5 to 2
- bh_slope: float32 [4, 8], replicated, may hold values from 0.02 to 0.2
- conductivity: float32 [4], replicated, may hold values from 0.05 to 1
- harmonic_numbers: int32 [8], replicated, may hold values from 1 to 32
- ripple_source: float32 [8, 2, 3, 128, 16, 256], P('harm', None, None, 'mesh'), may hold values from -6 to 6
- ripple_start: float32 [8, 2, 3, 128, 16, 256], P('harm', None, None, 'mesh'), may hold values from -2 to 2
Outputs:
- bias_field: float32 [3, 128, 16, 256], P(None, 'mesh', 'harm')
- ripple_field: float32 [8, 2, 3, 128, 16, 256], P('harm', None, None, 'mesh')
- loss_density: float32 [128, 16, 256], P('mesh', 'harm')
All inputs are finite; a program needn't handle non-finite values.
Results may differ from a plain program's by a relative error of at most 0.0001.
Values sent between devices are 32-bit elements; how exact they have to be, the bound alone decides.
No kernel may reach another device: no remote copies, remote signals or barrier semaphores. Data moves between devices by JAX's collectives and lax.ppermute only.
A program may use at most 128 MiB of HBM per device.

v0:
```python
import jax
import jax.numpy as jnp
from jax import lax
from jax.sharding import PartitionSpec as P

ITERS_B = 2
ITERS_R = 2
KNOTS = 8
MATS = 4
TABLES = 4


kappa = 0.05
knot_step = 1.5
soft_width = 0.5
omega_step = 0.25


def with_halo(block, sides, width):
    for axis, dim in sides:
        count = lax.axis_size(axis)
        forward = [(i, i + 1) for i in range(count - 1)]
        backward = [(target, source) for source, target in forward]
        low = lax.ppermute(
            lax.slice_in_dim(block, block.shape[dim] - width, None, axis=dim), axis, forward
        )
        high = lax.ppermute(lax.slice_in_dim(block, 0, width, axis=dim), axis, backward)
        block = jnp.concatenate([low, block, high], axis=dim)
    return block


def beside(padded):
    return [
        padded[..., 2:, 1:-1, 1:-1],
        padded[..., :-2, 1:-1, 1:-1],
        padded[..., 1:-1, 2:, 1:-1],
        padded[..., 1:-1, :-2, 1:-1],
        padded[..., 1:-1, 1:-1, 2:],
        padded[..., 1:-1, 1:-1, :-2],
    ]


def flux_squared(padded):
    center = padded[:, 1:-1, 1:-1, 1:-1]
    along_first = padded[:, 2:, 1:-1, 1:-1] - center
    along_second = padded[:, 1:-1, 2:, 1:-1] - center
    along_third = padded[:, 1:-1, 1:-1, 2:] - center
    flux_one = along_second[2] - along_third[1]
    flux_two = along_third[0] - along_first[2]
    flux_three = along_first[1] - along_second[0]
    return flux_one * flux_one + flux_two * flux_two + flux_three * flux_three


def material(region, table_index, bh_base, bh_slope, conductivity):
    choose = (table_index[:, None] == jnp.arange(TABLES)[None, :]).astype(jnp.float32)
    region_base = jnp.sum(choose * bh_base[None, :], axis=1)
    region_slope = jnp.sum(choose[:, :, None] * bh_slope[None, :, :], axis=1)
    cell_base = jnp.zeros(region.shape, jnp.float32)
    cell_sigma = jnp.zeros(region.shape, jnp.float32)
    cell_slope = [jnp.zeros(region.shape, jnp.float32) for knot in range(KNOTS)]
    for member_id in range(MATS):
        member = (region == member_id).astype(jnp.float32)
        cell_base = cell_base + member * region_base[member_id]
        cell_sigma = cell_sigma + member * conductivity[member_id]
        for knot in range(KNOTS):
            cell_slope[knot] = cell_slope[knot] + member * region_slope[member_id, knot]
    return (cell_base, cell_slope, cell_sigma)


def reluctivity(flux_sq, cell_base, cell_slope):
    value = cell_base
    slope_sum = jnp.zeros_like(flux_sq)
    for knot in range(KNOTS):
        scaled = (flux_sq - knot_step * knot) / soft_width
        value = value + cell_slope[knot] * soft_width * jax.nn.softplus(scaled)
        slope_sum = slope_sum + cell_slope[knot] * jax.nn.sigmoid(scaled)
    return (value, value + 2.0 * flux_sq * slope_sum)


def couplings(padded_cells):
    center = padded_cells[1:-1, 1:-1, 1:-1]
    weights = [0.5 * (center + other) for other in beside(padded_cells)]
    total = weights[0]
    for weight in weights[1:]:
        total = total + weight
    return (weights, total + kappa)


def relax(padded_field, padded_cells, source):
    weights, total = couplings(padded_cells)
    pull = jnp.zeros_like(source)
    for weight, other in zip(weights, beside(padded_field)):
        pull = pull + weight * other
    return (source + pull) / total


def complex_relax(padded_field, source, weights, total, damping):
    pull = jnp.zeros_like(source)
    for weight, other in zip(weights, beside(padded_field)):
        pull = pull + weight * other
    rhs = source + pull
    real_part = rhs[..., 0, :, :, :, :]
    imag_part = rhs[..., 1, :, :, :, :]
    damp = damping[..., None, :, :, :]
    denom = total * total + damp * damp
    new_real = (real_part * total + imag_part * damp) / denom
    new_imag = (imag_part * total - real_part * damp) / denom
    return jnp.stack([new_real, new_imag], axis=-5)


def bias_halo(potential):
    extended = with_halo(potential, (("mesh", 1), ("harm", 2)), 1)
    return jnp.pad(extended, ((0, 0), (0, 0), (0, 0), (1, 1)))


def cell_halo(values):
    extended = with_halo(values, (("mesh", 0), ("harm", 1)), 1)
    return jnp.pad(extended, ((0, 0), (0, 0), (1, 1)))


def harmonic_loss(ripple, omegas, cell_sigma):
    power = jnp.sum(ripple * ripple, axis=(1, 2))
    factor = 0.5 * omegas * omegas
    return jnp.sum(factor[:, None, None, None] * cell_sigma * power, axis=0)


def body(
    bias_source,
    bias_start,
    region,
    table_index,
    bh_base,
    bh_slope,
    conductivity,
    harmonic_numbers,
    ripple_source,
    ripple_start,
):
    cell_base, cell_slope, cell_sigma = material(
        region, table_index, bh_base, bh_slope, conductivity
    )
    field = bias_start
    for sweep_index in range(ITERS_B):
        padded = bias_halo(field)
        reluct, unused = reluctivity(flux_squared(padded), cell_base, cell_slope)
        field = relax(padded, cell_halo(reluct), bias_source)
    padded = bias_halo(field)
    unused, incremental = reluctivity(flux_squared(padded), cell_base, cell_slope)
    omegas_all = omega_step * harmonic_numbers.astype(jnp.float32)
    count = ripple_source.shape[0]
    omegas = lax.dynamic_slice_in_dim(omegas_all, lax.axis_index("harm") * count, count)
    moved_nu, moved_sigma = (
        lax.all_gather(incremental, "harm", axis=1, tiled=True),
        lax.all_gather(cell_sigma, "harm", axis=1, tiled=True),
    )
    extended = with_halo(moved_nu, (("mesh", 0),), 1)
    weights, total = couplings(jnp.pad(extended, ((0, 0), (1, 1), (1, 1))))
    damping = omegas[:, None, None, None] * moved_sigma
    ripple = ripple_start
    for sweep_index in range(ITERS_R):
        wider = with_halo(ripple, (("mesh", 3),), 1)
        wider = jnp.pad(wider, ((0, 0), (0, 0), (0, 0), (0, 0), (1, 1), (1, 1)))
        ripple = complex_relax(wider, ripple_source, weights, total, damping)
    local_loss = harmonic_loss(ripple, omegas, moved_sigma)
    loss = lax.psum_scatter(local_loss, "harm", scatter_dimension=1, tiled=True)
    return (field, ripple, loss)


def solution(mesh):
    return jax.shard_map(
        body,
        mesh=mesh,
        in_specs=(
            P(None, "mesh", "harm", None),
            P(None, "mesh", "harm", None),
            P("mesh", "harm", None),
            P(),
            P(),
            P(),
            P(),
            P(),
            P("harm", None, None, "mesh", None, None),
            P("harm", None, None, "mesh", None, None),
        ),
        out_specs=(
            P(None, "mesh", "harm", None),
            P("harm", None, None, "mesh", None, None),
            P("mesh", "harm", None),
        ),
        check_vma=False,
    )
```

profile of v0, /device:TPU:12, one launch (start us, length us, event | category | flops | bytes accessed | tf_op | source)
XLA Modules:
  0.0 246.5 jit_solution(113440704642583734)
XLA Ops:
  8.1 1.9 collective-permute-start.1
  10.0 2.4 collective-permute-start
  14.0 1.5 fusion.317
  16.9 4.1 %select_add_fusion = (f32[8,8,256]{2,1,0:T(8,128)}, pred[8,8,256]{2,1,0:T(8,128)(4,1)S(1)}, pred[8,8,256]{2,1,0:T(8,128)(4,1)S(1)}, pred[8,8,256]{2,1,0:T(8,128)(4,1)S(1)}, pred[8,8,256]{2,1,0:T(8,128)(4,1)S(1)}) fusion(f32[]{:T(128)} %bitcast.63, f32[]{:T(128)} %bitcast.62, f32[]{:T(128)} %bitcast.61, f32[]{:T(128)} %bitcast.60, s32[8,8,256]{2,1,0:T(8,128)} %param.12), kind=kLoop, calls=%fused_computation.487 | loop fusion | flops 180224 | bytes 196624 | tf_op jit(solution)/shard_map/add | solution.py:64
  22.7 3.4 %collective-permute-start.3 = (f32[3,10,1,256]{3,2,1,0:T(1,128)S(1)}, f32[3,10,1,256]{3,2,1,0:T(1,128)S(1)}, u32[]{:S(2)}, u32[]{:S(2)}) collective-permute-start(f32[3,10,1,256]{3,2,1,0:T(1,128)S(1)} %get-tuple-element.48), channel_id=1, source_target_pairs={{0,1},{2,3},{4,5},{6,7},{8,9},{10,11},{12,13},{14,15},{16,17},{18,... | collective-permute-start | bytes 92168 | tf_op jit(solution)/shard_map/ppermute | solution.py:24
  26.1 1.3 collective-permute-start.2
  28.1 3.8 %collective-permute-done.2 = f32[3,10,1,256]{3,2,1,0:T(1,128)S(1)} collective-permute-done((f32[3,10,1,256]{3,2,1,0:T(1,128)S(1)}, f32[3,10,1,256]{3,2,1,0:T(1,128)S(1)}, u32[]{:S(2)}, u32[]{:S(2)}) %collective-permute-start.2) | collective-permute-done | bytes 30752 | tf_op jit(solution)/shard_map/ppermute | solution.py:27
  33.6 22.8 %fusion.74 = f32[8,8,256]{2,1,0:T(8,128)S(1)} fusion(f32[3,8,8,256]{3,2,1,0:T(8,128)S(1)} %get-tuple-element.59, f32[3,8,8,256]{3,2,1,0:T(8,128)S(1)} %get-tuple-element.60, f32[3,8,8,256]{3,2,1,0:T(8,128)S(1)} %get-tuple-element.58, pred[8,8,256]{2,1,0:T(8,128)(4,1)S(1)} %get-tuple-element.11, f32[]{:T(128)} %bitcast.3, ...), kind=kLoop, calls=%fused_computation.190 | loop fusion | flops 2588672 | bytes 524432 | tf_op jit(solution)/shard_map/add | solution.py:75
  56.4 2.2 collective-permute-start.4
  58.6 2.4 collective-permute-start.5
  61.1 2.5 %collective-permute-done.5 = f32[1,8,256]{2,1,0:T(8,128)S(1)} collective-permute-done((f32[1,8,256]{2,1,0:T(8,128)S(1)}, f32[1,8,256]{2,1,0:T(8,128)S(1)}, u32[]{:S(2)}, u32[]{:S(2)}) %collective-permute-start.5) | collective-permute-done | bytes 8224 | tf_op jit(solution)/shard_map/ppermute | solution.py:24
  63.6 1.7 collective-permute-start.7
  65.3 1.3 collective-permute-start.6
  66.7 4.2 %collective-permute-done.6 = f32[10,1,256]{2,1,0:T(1,128)S(1)} collective-permute-done((f32[10,1,256]{2,1,0:T(1,128)S(1)}, f32[10,1,256]{2,1,0:T(1,128)S(1)}, u32[]{:S(2)}, u32[]{:S(2)}) %collective-permute-start.6) | collective-permute-done | bytes 10272 | tf_op jit(solution)/shard_map/ppermute | solution.py:27
  71.5 1.9 collective-permute-start.8
  73.4 3.6 %collective-permute-start.9 = (f32[3,1,8,256]{3,2,1,0:T(8,128)S(1)}, f32[3,1,8,256]{3,2,1,0:T(8,128)S(1)}, u32[]{:S(2)}, u32[]{:S(2)}) collective-permute-start(f32[3,1,8,256]{3,2,1,0:T(8,128)S(1)} %get-tuple-element.57), channel_id=1, source_target_pairs={{2,0},{4,2},{6,4},{8,6},{10,8},{12,10},{14,12},{16,14},{18,16},{20... | collective-permute-start | bytes 73736 | tf_op jit(solution)/shard_map/ppermute | solution.py:27
  77.1 3.2 %collective-permute-done.9 = f32[3,1,8,256]{3,2,1,0:T(8,128)S(1)} collective-permute-done((f32[3,1,8,256]{3,2,1,0:T(8,128)S(1)}, f32[3,1,8,256]{3,2,1,0:T(8,128)S(1)}, u32[]{:S(2)}, u32[]{:S(2)}) %collective-permute-start.9) | collective-permute-done | bytes 24608 | tf_op jit(solution)/shard_map/ppermute | solution.py:27
  80.3 1.6 collective-permute-start.11
  81.9 1.3 collective-permute-start.10
  83.5 4.2 %collective-permute-done.10 = f32[3,10,1,256]{3,2,1,0:T(1,128)S(1)} collective-permute-done((f32[3,10,1,256]{3,2,1,0:T(1,128)S(1)}, f32[3,10,1,256]{3,2,1,0:T(1,128)S(1)}, u32[]{:S(2)}, u32[]{:S(2)}) %collective-permute-start.10) | collective-permute-done | bytes 30752 | tf_op jit(solution)/shard_map/ppermute | solution.py:27
  88.4 22.8 %fusion.90 = f32[8,8,256]{2,1,0:T(8,128)S(1)} fusion(f32[3,8,8,256]{3,2,1,0:T(8,128)S(1)} %get-tuple-element.52, f32[3,8,8,256]{3,2,1,0:T(8,128)S(1)} %get-tuple-element.51, f32[3,8,8,256]{3,2,1,0:T(8,128)S(1)} %get-tuple-element.55, pred[8,8,256]{2,1,0:T(8,128)(4,1)S(1)} %get-tuple-element.11, f32[]{:T(128)} %bitcast.3, ...), kind=kLoop, calls=%fused_computation.206 | loop fusion | flops 2588672 | bytes 524432 | tf_op jit(solution)/shard_map/add | solution.py:75
  111.2 1.9 collective-permute-start.12
  113.2 3.9 %collective-permute-start.13 = (f32[1,8,256]{2,1,0:T(8,128)S(1)}, f32[1,8,256]{2,1,0:T(8,128)S(1)}, u32[]{:S(2)}, u32[]{:S(2)}) collective-permute-start(f32[1,8,256]{2,1,0:T(8,128)S(1)} %get-tuple-element.72), channel_id=1, source_target_pairs={{0,2},{2,4},{4,6},{6,8},{8,10},{10,12},{12,14},{14,16},{16,18},{18... | collective-permute-start | bytes 24584 | tf_op jit(solution)/shard_map/ppermute | solution.py:24
  118.1 4.5 %collective-permute-start.23 = (f32[4,2,3,1,16,256]{5,4,3,2,1,0:T(8,128)}, f32[4,2,3,1,16,256]{5,4,3,2,1,0:T(8,128)}, u32[]{:S(2)}, u32[]{:S(2)}) collective-permute-start(f32[4,2,3,1,16,256]{5,4,3,2,1,0:T(8,128)} %get-tuple-element.40), channel_id=1, source_target_pairs={{0,2},{2,4},{4,6},{6,8},{8,10},{10,12},{12,14},{14,16},{16,18},{18... | collective-permute-start | bytes 1179656 | tf_op jit(solution)/shard_map/ppermute | solution.py:24
  122.6 1.9 collective-permute-start.21
  124.6 1.9 collective-permute-start.15
  126.5 1.3 collective-permute-start.14
  128.4 3.7 %collective-permute-done.14 = f32[10,1,256]{2,1,0:T(1,128)S(1)} collective-permute-done((f32[10,1,256]{2,1,0:T(1,128)S(1)}, f32[10,1,256]{2,1,0:T(1,128)S(1)}, u32[]{:S(2)}, u32[]{:S(2)}) %collective-permute-start.14) | collective-permute-done | bytes 10272 | tf_op jit(solution)/shard_map/ppermute | solution.py:27
  133.3 1.9 collective-permute-start.16
  135.2 3.6 %collective-permute-start.17 = (f32[3,1,8,256]{3,2,1,0:T(8,128)}, f32[3,1,8,256]{3,2,1,0:T(8,128)}, u32[]{:S(2)}, u32[]{:S(2)}) collective-permute-start(f32[3,1,8,256]{3,2,1,0:T(8,128)} %get-tuple-element.54), channel_id=1, source_target_pairs={{2,0},{4,2},{6,4},{8,6},{10,8},{12,10},{14,12},{16,14},{18,16},{20... | collective-permute-start | bytes 73736 | tf_op jit(solution)/shard_map/ppermute | solution.py:27
  141.6 1.6 collective-permute-start.19
  143.2 1.3 collective-permute-start.18
  145.3 3.7 %collective-permute-done.18 = f32[3,10,1,256]{3,2,1,0:T(1,128)S(1)} collective-permute-done((f32[3,10,1,256]{3,2,1,0:T(1,128)S(1)}, f32[3,10,1,256]{3,2,1,0:T(1,128)S(1)}, u32[]{:S(2)}, u32[]{:S(2)}) %collective-permute-start.18) | collective-permute-done | bytes 30752 | tf_op jit(solution)/shard_map/ppermute | solution.py:27
  150.3 23.7 %fusion.107 = f32[8,8,256]{2,1,0:T(8,128)S(1)} fusion(f32[3,8,8,256]{3,2,1,0:T(8,128)S(1)} %get-tuple-element.43, f32[3,8,8,256]{3,2,1,0:T(8,128)S(1)} %get-tuple-element.50, f32[3,8,8,256]{3,2,1,0:T(8,128)S(1)} %get-tuple-element.42, pred[8,8,256]{2,1,0:T(8,128)(4,1)} %copy-done.21, f32[]{:T(128)} %bitcast.3, pred[8,8,256]{2,1,0:T(8,128)(4,1)} %copy-done.20, ...), kind=kLoop, calls=%fused_computation.223 | loop fusion | flops 3260416 | bytes 524432 | tf_op jit(solution)/shard_map/add | solution.py:77
  174.0 4.9 %all_gather.6 = f32[8,16,256]{2,1,0:T(8,128)S(1)} all-gather(f32[8,8,256]{2,1,0:T(8,128)S(1)} %fusion.107), channel_id=1, replica_groups=mesh['mesh'=16,'harm'=2] {'harm'}, dimensions={1}, use_global_device_ids=true | all-gather | bytes 196608 | tf_op jit(solution)/shard_map/all_gather | solution.py:153
  178.9 2.7 %collective-permute-start.22 = (f32[1,16,256]{2,1,0:T(8,128)S(1)}, f32[1,16,256]{2,1,0:T(8,128)S(1)}, u32[]{:S(2)}, u32[]{:S(2)}) collective-permute-start(f32[1,16,256]{2,1,0:T(8,128)S(1)} %get-tuple-element.65), channel_id=1, source_target_pairs={{0,2},{2,4},{4,6},{6,8},{8,10},{10,12},{12,14},{14,16},{16,18},{18... | collective-permute-start | bytes 49160 | tf_op jit(solution)/shard_map/ppermute | solution.py:24
  181.7 2.8 %collective-permute-start.20 = (f32[1,16,256]{2,1,0:T(8,128)S(1)}, f32[1,16,256]{2,1,0:T(8,128)S(1)}, u32[]{:S(2)}, u32[]{:S(2)}) collective-permute-start(f32[1,16,256]{2,1,0:T(8,128)S(1)} %get-tuple-element.66), channel_id=1, source_target_pairs={{2,0},{4,2},{6,4},{8,6},{10,8},{12,10},{14,12},{16,14},{18,16},{20... | collective-permute-start | bytes 49160 | tf_op jit(solution)/shard_map/ppermute | solution.py:27
  184.5 5.3 %all_gather.7 = f32[8,16,256]{2,1,0:T(8,128)S(1)} all-gather(f32[8,8,256]{2,1,0:T(8,128)} %get-tuple-element.7), channel_id=1, replica_groups=mesh['mesh'=16,'harm'=2] {'harm'}, dimensions={1}, use_global_device_ids=true | all-gather | bytes 196608 | tf_op jit(solution)/shard_map/all_gather | solution.py:154
  190.5 5.2 %select_maximum_fusion.3 = f32[4,2,3,10,18,258]{5,4,3,2,1,0:T(8,128)S(1)} fusion(f32[4,2,3,1,16,256]{5,4,3,2,1,0:T(8,128)} %collective-permute-done.21, f32[4,2,3,8,16,256]{5,4,3,2,1,0:T(8,128)S(1)} %copy-done, f32[4,2,3,1,16,256]{5,4,3,2,1,0:T(8,128)} %collective-permute-done.23), kind=kLoop, calls=%fused_computation.7 | loop fusion | flops 16718400 | bytes 8390400 | tf_op jit(solution)/shard_map/concatenate | solution.py:28
  195.8 4.6 %fusion.12 = f32[4,2,3,8,16,256]{5,4,3,2,1,0:T(8,128)S(1)} fusion(f32[4,2,3,8,16,256]{5,4,3,2,1,0:T(8,128)} %param.18, f32[4,2,3,10,18,258]{5,4,3,2,1,0:T(8,128)S(1)} %select_maximum_fusion.3, f32[4,2,3,8,16,256]{5,4,3,2,1,0:T(8,128)S(1)} %copy-done, f32[4,2,3,1,16,256]{5,4,3,2,1,0:T(8,128)} %collective-permute-done.23, ...), kind=kLoop, calls=%fused_computation.30 | loop fusion | flops 11010048 | bytes 23592960 | tf_op jit(solution)/shard_map/add | solution.py:101
  201.2 2.3 collective-permute-start.25
  203.5 3.6 %collective-permute-start.24 = (f32[4,2,3,1,16,256]{5,4,3,2,1,0:T(8,128)S(1)}, f32[4,2,3,1,16,256]{5,4,3,2,1,0:T(8,128)S(1)}, u32[]{:S(2)}, u32[]{:S(2)}) collective-permute-start(f32[4,2,3,1,16,256]{5,4,3,2,1,0:T(8,128)S(1)} %get-tuple-element.39), channel_id=1, source_target_pairs={{2,0},{4,2},{6,4},{8,6},{10,8},{12,10},{14,12},{16,14},{18,16},{20... | collective-permute-start | bytes 1179656 | tf_op jit(solution)/shard_map/ppermute | solution.py:27
  207.1 3.2 %collective-permute-done.25 = f32[4,2,3,1,16,256]{5,4,3,2,1,0:T(8,128)S(1)} collective-permute-done((f32[4,2,3,1,16,256]{5,4,3,2,1,0:T(8,128)S(1)}, f32[4,2,3,1,16,256]{5,4,3,2,1,0:T(8,128)S(1)}, u32[]{:S(2)}, u32[]{:S(2)}) %collective-permute-start.25) | collective-permute-done | bytes 393248 | tf_op jit(solution)/shard_map/ppermute | solution.py:24
  210.2 5.6 %collective-permute-done.24 = f32[4,2,3,1,16,256]{5,4,3,2,1,0:T(8,128)S(1)} collective-permute-done((f32[4,2,3,1,16,256]{5,4,3,2,1,0:T(8,128)S(1)}, f32[4,2,3,1,16,256]{5,4,3,2,1,0:T(8,128)S(1)}, u32[]{:S(2)}, u32[]{:S(2)}) %collective-permute-start.24) | collective-permute-done | bytes 393248 | tf_op jit(solution)/shard_map/ppermute | solution.py:27
  215.9 4.6 %select_maximum_fusion = f32[4,2,3,10,18,258]{5,4,3,2,1,0:T(8,128)S(1)} fusion(f32[4,2,3,1,16,256]{5,4,3,2,1,0:T(8,128)S(1)} %collective-permute-done.24, f32[4,2,3,1,16,256]{5,4,3,2,1,0:T(8,128)S(1)} %collective-permute-done.25, f32[4,1,3,8,16,256]{5,4,3,2,1,0:T(8,128)S(1)} %get-tuple-element.37, f32[4,1,3,8,16,256]{5,4,3,2,1,0:T(8,128)S(1)} %get-tuple-element.36), kind=kLoop, calls=%fused_computation.4 | loop fusion | flops 20062080 | bytes 8390400 | tf_op jit(solution)/shard_map/concatenate | solution.py:28
  220.5 4.7 %fusion.4 = f32[4,2,3,8,16,256]{5,4,3,2,1,0:T(8,128)S(1)} fusion(f32[4,2,3,8,16,256]{5,4,3,2,1,0:T(8,128)} %param.18, f32[4,2,3,10,18,258]{5,4,3,2,1,0:T(8,128)S(1)} %select_maximum_fusion, f32[4,2,3,1,16,256]{5,4,3,2,1,0:T(8,128)S(1)} %collective-permute-done.25, f32[4,1,3,8,16,256]{5,4,3,2,1,0:T(8,128)S(1)} %get-tuple-element.37, ...), kind=kLoop, calls=%fused_computation.14 | loop fusion | flops 12582912 | bytes 23592960 | tf_op jit(solution)/shard_map/add | solution.py:101
  225.9 2.3 multiply_reduce_fusion
  228.9 10.7 %reduce-scatter.2.cloned.1.call-done = f32[8,8,256]{2,1,0:T(8,128)} async-done(((f32[8,16,256]{2,1,0:T(8,128)}), f32[8,8,256]{2,1,0:T(8,128)}) %reduce-scatter.2.cloned.1.call-update) | async-done | bytes 65552 | tf_op jit(solution)/shard_map/reduce_scatter | solution.py:165
  (107 shorter events, 19.7 us)
Async XLA Ops:
  7.2 64.0 %copy-start.5 = (f32[3,8,8,256]{3,2,1,0:T(8,128)S(1)}, f32[3,8,8,256]{3,2,1,0:T(8,128)}, u32[]{:S(2)}) copy-start(f32[3,8,8,256]{3,2,1,0:T(8,128)} %param.11) | copy-start | bytes 589828
  7.2 64.0 %copy-start.18 = (f32[3,8,8,256]{3,2,1,0:T(8,128)S(1)}, f32[3,8,8,256]{3,2,1,0:T(8,128)}, u32[]{:S(2)}) copy-start(f32[3,8,8,256]{3,2,1,0:T(8,128)} %param.10) | copy-start | bytes 589828
  7.2 232.4 %reduce-scatter.2.cloned.1.call-start = ((), (), s32[]{:S(2)}) async-start(), calls=%async_computation.1 | async-start | bytes 196608 | tf_op jit(solution)/shard_map/reduce_scatter | solution.py:165
  8.1 14.6 %collective-permute-start.1 = (f32[3,1,8,256]{3,2,1,0:T(8,128)S(1)}, f32[3,1,8,256]{3,2,1,0:T(8,128)S(1)}, u32[]{:S(2)}, u32[]{:S(2)}) collective-permute-start(f32[3,1,8,256]{3,2,1,0:T(8,128)S(1)} %get-tuple-element.61), channel_id=1, source_target_pairs={{2,0},{4,2},{6,4},{8,6},{10,8},{12,10},{14,12},{16,14},{18,16},{20... | collective-permute-start | bytes 73736 | tf_op jit(solution)/shard_map/ppermute | solution.py:27
  10.0 11.7 %collective-permute-start = (f32[3,1,8,256]{3,2,1,0:T(8,128)S(1)}, f32[3,1,8,256]{3,2,1,0:T(8,128)S(1)}, u32[]{:S(2)}, u32[]{:S(2)}) collective-permute-start(f32[3,1,8,256]{3,2,1,0:T(8,128)S(1)} %get-tuple-element.62), channel_id=1, source_target_pairs={{0,2},{2,4},{4,6},{6,8},{8,10},{10,12},{12,14},{14,16},{16,18},{18... | collective-permute-start | bytes 73736 | tf_op jit(solution)/shard_map/ppermute | solution.py:24
  21.0 67.3 %copy-start.19 = (pred[8,8,256]{2,1,0:T(8,128)(4,1)}, pred[8,8,256]{2,1,0:T(8,128)(4,1)S(1)}, u32[]{:S(2)}) copy-start(pred[8,8,256]{2,1,0:T(8,128)(4,1)S(1)} %get-tuple-element.9) | copy-start | bytes 49156
  21.0 67.3 %copy-start.20 = (pred[8,8,256]{2,1,0:T(8,128)(4,1)}, pred[8,8,256]{2,1,0:T(8,128)(4,1)S(1)}, u32[]{:S(2)}) copy-start(pred[8,8,256]{2,1,0:T(8,128)(4,1)S(1)} %get-tuple-element.10) | copy-start | bytes 49156
  21.0 67.3 %copy-start.21 = (pred[8,8,256]{2,1,0:T(8,128)(4,1)}, pred[8,8,256]{2,1,0:T(8,128)(4,1)S(1)}, u32[]{:S(2)}) copy-start(pred[8,8,256]{2,1,0:T(8,128)(4,1)S(1)} %get-tuple-element.11) | copy-start | bytes 49156
  22.7 5.4 %collective-permute-start.3 = (f32[3,10,1,256]{3,2,1,0:T(1,128)S(1)}, f32[3,10,1,256]{3,2,1,0:T(1,128)S(1)}, u32[]{:S(2)}, u32[]{:S(2)}) collective-permute-start(f32[3,10,1,256]{3,2,1,0:T(1,128)S(1)} %get-tuple-element.48), channel_id=1, source_target_pairs={{0,1},{2,3},{4,5},{6,7},{8,9},{10,11},{12,13},{14,15},{16,17},{18,... | collective-permute-start | bytes 92168 | tf_op jit(solution)/shard_map/ppermute | solution.py:24
  26.1 5.8 %collective-permute-start.2 = (f32[3,10,1,256]{3,2,1,0:T(1,128)S(1)}, f32[3,10,1,256]{3,2,1,0:T(1,128)S(1)}, u32[]{:S(2)}, u32[]{:S(2)}) collective-permute-start(f32[3,10,1,256]{3,2,1,0:T(1,128)S(1)} %get-tuple-element.49), channel_id=1, source_target_pairs={{1,0},{3,2},{5,4},{7,6},{9,8},{11,10},{13,12},{15,14},{17,16},{19,... | collective-permute-start | bytes 92168 | tf_op jit(solution)/shard_map/ppermute | solution.py:27
  56.4 60.7 %copy-start = (f32[4,2,3,8,16,256]{5,4,3,2,1,0:T(8,128)S(1)}, f32[4,2,3,8,16,256]{5,4,3,2,1,0:T(8,128)}, u32[]{:S(2)}) copy-start(f32[4,2,3,8,16,256]{5,4,3,2,1,0:T(8,128)} %param.19) | copy-start | bytes 9437188
  56.4 4.7 %collective-permute-start.4 = (f32[1,8,256]{2,1,0:T(8,128)S(1)}, f32[1,8,256]{2,1,0:T(8,128)S(1)}, u32[]{:S(2)}, u32[]{:S(2)}) collective-permute-start(f32[1,8,256]{2,1,0:T(8,128)S(1)} %get-tuple-element.73), channel_id=1, source_target_pairs={{2,0},{4,2},{6,4},{8,6},{10,8},{12,10},{14,12},{16,14},{18,16},{20... | collective-permute-start | bytes 24584 | tf_op jit(solution)/shard_map/ppermute | solution.py:27
  58.6 5.0 %collective-permute-start.5 = (f32[1,8,256]{2,1,0:T(8,128)S(1)}, f32[1,8,256]{2,1,0:T(8,128)S(1)}, u32[]{:S(2)}, u32[]{:S(2)}) collective-permute-start(f32[1,8,256]{2,1,0:T(8,128)S(1)} %get-tuple-element.74), channel_id=1, source_target_pairs={{0,2},{2,4},{4,6},{6,8},{8,10},{10,12},{12,14},{14,16},{16,18},{18... | collective-permute-start | bytes 24584 | tf_op jit(solution)/shard_map/ppermute | solution.py:24
  63.6 3.1 %collective-permute-start.7 = (f32[10,1,256]{2,1,0:T(1,128)S(1)}, f32[10,1,256]{2,1,0:T(1,128)S(1)}, u32[]{:S(2)}, u32[]{:S(2)}) collective-permute-start(f32[10,1,256]{2,1,0:T(1,128)S(1)} %get-tuple-element.69), channel_id=1, source_target_pairs={{0,1},{2,3},{4,5},{6,7},{8,9},{10,11},{12,13},{14,15},{16,17},{18,... | collective-permute-start | bytes 30728 | tf_op jit(solution)/shard_map/ppermute | solution.py:24
  65.3 5.6 %collective-permute-start.6 = (f32[10,1,256]{2,1,0:T(1,128)S(1)}, f32[10,1,256]{2,1,0:T(1,128)S(1)}, u32[]{:S(2)}, u32[]{:S(2)}) collective-permute-start(f32[10,1,256]{2,1,0:T(1,128)S(1)} %get-tuple-element.70), channel_id=1, source_target_pairs={{1,0},{3,2},{5,4},{7,6},{9,8},{11,10},{13,12},{15,14},{17,16},{19,... | collective-permute-start | bytes 30728 | tf_op jit(solution)/shard_map/ppermute | solution.py:27
  71.2 56.6 %copy-start.22 = (s32[8]{0:T(128)S(1)}, s32[8]{0:T(128)}, u32[]{:S(2)}) copy-start(s32[8]{0:T(128)} %param.17) | copy-start | bytes 100
  71.5 5.6 %collective-permute-start.8 = (f32[3,1,8,256]{3,2,1,0:T(8,128)S(1)}, f32[3,1,8,256]{3,2,1,0:T(8,128)S(1)}, u32[]{:S(2)}, u32[]{:S(2)}) collective-permute-start(f32[3,1,8,256]{3,2,1,0:T(8,128)S(1)} %get-tuple-element.56), channel_id=1, source_target_pairs={{0,2},{2,4},{4,6},{6,8},{8,10},{10,12},{12,14},{14,16},{16,18},{18... | collective-permute-start | bytes 73736 | tf_op jit(solution)/shard_map/ppermute | solution.py:24
  73.4 6.8 %collective-permute-start.9 = (f32[3,1,8,256]{3,2,1,0:T(8,128)S(1)}, f32[3,1,8,256]{3,2,1,0:T(8,128)S(1)}, u32[]{:S(2)}, u32[]{:S(2)}) collective-permute-start(f32[3,1,8,256]{3,2,1,0:T(8,128)S(1)} %get-tuple-element.57), channel_id=1, source_target_pairs={{2,0},{4,2},{6,4},{8,6},{10,8},{12,10},{14,12},{16,14},{18,16},{20... | collective-permute-start | bytes 73736 | tf_op jit(solution)/shard_map/ppermute | solution.py:27
  80.3 3.2 %collective-permute-start.11 = (f32[3,10,1,256]{3,2,1,0:T(1,128)S(1)}, f32[3,10,1,256]{3,2,1,0:T(1,128)S(1)}, u32[]{:S(2)}, u32[]{:S(2)}) collective-permute-start(f32[3,10,1,256]{3,2,1,0:T(1,128)S(1)} %get-tuple-element.46), channel_id=1, source_target_pairs={{0,1},{2,3},{4,5},{6,7},{8,9},{10,11},{12,13},{14,15},{16,17},{18,... | collective-permute-start | bytes 92168 | tf_op jit(solution)/shard_map/ppermute | solution.py:24
  81.9 5.8 %collective-permute-start.10 = (f32[3,10,1,256]{3,2,1,0:T(1,128)S(1)}, f32[3,10,1,256]{3,2,1,0:T(1,128)S(1)}, u32[]{:S(2)}, u32[]{:S(2)}) collective-permute-start(f32[3,10,1,256]{3,2,1,0:T(1,128)S(1)} %get-tuple-element.47), channel_id=1, source_target_pairs={{1,0},{3,2},{5,4},{7,6},{9,8},{11,10},{13,12},{15,14},{17,16},{19,... | collective-permute-start | bytes 92168 | tf_op jit(solution)/shard_map/ppermute | solution.py:27
  111.2 13.3 %collective-permute-start.12 = (f32[1,8,256]{2,1,0:T(8,128)S(1)}, f32[1,8,256]{2,1,0:T(8,128)S(1)}, u32[]{:S(2)}, u32[]{:S(2)}) collective-permute-start(f32[1,8,256]{2,1,0:T(8,128)S(1)} %get-tuple-element.71), channel_id=1, source_target_pairs={{2,0},{4,2},{6,4},{8,6},{10,8},{12,10},{14,12},{16,14},{18,16},{20... | collective-permute-start | bytes 24584 | tf_op jit(solution)/shard_map/ppermute | solution.py:27
  113.2 11.4 %collective-permute-start.13 = (f32[1,8,256]{2,1,0:T(8,128)S(1)}, f32[1,8,256]{2,1,0:T(8,128)S(1)}, u32[]{:S(2)}, u32[]{:S(2)}) collective-permute-start(f32[1,8,256]{2,1,0:T(8,128)S(1)} %get-tuple-element.72), channel_id=1, source_target_pairs={{0,2},{2,4},{4,6},{6,8},{8,10},{10,12},{12,14},{14,16},{16,18},{18... | collective-permute-start | bytes 24584 | tf_op jit(solution)/shard_map/ppermute | solution.py:24
  118.1 72.4 %collective-permute-start.23 = (f32[4,2,3,1,16,256]{5,4,3,2,1,0:T(8,128)}, f32[4,2,3,1,16,256]{5,4,3,2,1,0:T(8,128)}, u32[]{:S(2)}, u32[]{:S(2)}) collective-permute-start(f32[4,2,3,1,16,256]{5,4,3,2,1,0:T(8,128)} %get-tuple-element.40), channel_id=1, source_target_pairs={{0,2},{2,4},{4,6},{6,8},{8,10},{10,12},{12,14},{14,16},{16,18},{18... | collective-permute-start | bytes 1179656 | tf_op jit(solution)/shard_map/ppermute | solution.py:24
  122.6 67.9 %collective-permute-start.21 = (f32[4,2,3,1,16,256]{5,4,3,2,1,0:T(8,128)}, f32[4,2,3,1,16,256]{5,4,3,2,1,0:T(8,128)}, u32[]{:S(2)}, u32[]{:S(2)}) collective-permute-start(f32[4,2,3,1,16,256]{5,4,3,2,1,0:T(8,128)} %get-tuple-element.41), channel_id=1, source_target_pairs={{2,0},{4,2},{6,4},{8,6},{10,8},{12,10},{14,12},{16,14},{18,16},{20... | collective-permute-start | bytes 1179656 | tf_op jit(solution)/shard_map/ppermute | solution.py:27
  124.6 3.8 %collective-permute-start.15 = (f32[10,1,256]{2,1,0:T(1,128)S(1)}, f32[10,1,256]{2,1,0:T(1,128)S(1)}, u32[]{:S(2)}, u32[]{:S(2)}) collective-permute-start(f32[10,1,256]{2,1,0:T(1,128)S(1)} %get-tuple-element.67), channel_id=1, source_target_pairs={{0,1},{2,3},{4,5},{6,7},{8,9},{10,11},{12,13},{14,15},{16,17},{18,... | collective-permute-start | bytes 30728 | tf_op jit(solution)/shard_map/ppermute | solution.py:24
  126.5 5.6 %collective-permute-start.14 = (f32[10,1,256]{2,1,0:T(1,128)S(1)}, f32[10,1,256]{2,1,0:T(1,128)S(1)}, u32[]{:S(2)}, u32[]{:S(2)}) collective-permute-start(f32[10,1,256]{2,1,0:T(1,128)S(1)} %get-tuple-element.68), channel_id=1, source_target_pairs={{1,0},{3,2},{5,4},{7,6},{9,8},{11,10},{13,12},{15,14},{17,16},{19,... | collective-permute-start | bytes 30728 | tf_op jit(solution)/shard_map/ppermute | solution.py:27
  132.6 57.8 %copy-start.6 = (f32[3,8,8,256]{3,2,1,0:T(8,128)}, f32[3,8,8,256]{3,2,1,0:T(8,128)S(1)}, u32[]{:S(2)}) copy-start(f32[3,8,8,256]{3,2,1,0:T(8,128)S(1)} %fusion.34) | copy-start | bytes 589828
  133.3 6.3 %collective-permute-start.16 = (f32[3,1,8,256]{3,2,1,0:T(8,128)}, f32[3,1,8,256]{3,2,1,0:T(8,128)}, u32[]{:S(2)}, u32[]{:S(2)}) collective-permute-start(f32[3,1,8,256]{3,2,1,0:T(8,128)} %get-tuple-element.53), channel_id=1, source_target_pairs={{0,2},{2,4},{4,6},{6,8},{8,10},{10,12},{12,14},{14,16},{16,18},{18... | collective-permute-start | bytes 73736 | tf_op jit(solution)/shard_map/ppermute | solution.py:24
  135.2 5.6 %collective-permute-start.17 = (f32[3,1,8,256]{3,2,1,0:T(8,128)}, f32[3,1,8,256]{3,2,1,0:T(8,128)}, u32[]{:S(2)}, u32[]{:S(2)}) collective-permute-start(f32[3,1,8,256]{3,2,1,0:T(8,128)} %get-tuple-element.54), channel_id=1, source_target_pairs={{2,0},{4,2},{6,4},{8,6},{10,8},{12,10},{14,12},{16,14},{18,16},{20... | collective-permute-start | bytes 73736 | tf_op jit(solution)/shard_map/ppermute | solution.py:27
  141.6 3.7 %collective-permute-start.19 = (f32[3,10,1,256]{3,2,1,0:T(1,128)S(1)}, f32[3,10,1,256]{3,2,1,0:T(1,128)S(1)}, u32[]{:S(2)}, u32[]{:S(2)}) collective-permute-start(f32[3,10,1,256]{3,2,1,0:T(1,128)S(1)} %get-tuple-element.44), channel_id=1, source_target_pairs={{0,1},{2,3},{4,5},{6,7},{8,9},{10,11},{12,13},{14,15},{16,17},{18,... | collective-permute-start | bytes 92168 | tf_op jit(solution)/shard_map/ppermute | solution.py:24
  143.2 5.8 %collective-permute-start.18 = (f32[3,10,1,256]{3,2,1,0:T(1,128)S(1)}, f32[3,10,1,256]{3,2,1,0:T(1,128)S(1)}, u32[]{:S(2)}, u32[]{:S(2)}) collective-permute-start(f32[3,10,1,256]{3,2,1,0:T(1,128)S(1)} %get-tuple-element.45), channel_id=1, source_target_pairs={{1,0},{3,2},{5,4},{7,6},{9,8},{11,10},{13,12},{15,14},{17,16},{19,... | collective-permute-start | bytes 92168 | tf_op jit(solution)/shard_map/ppermute | solution.py:27
  178.9 10.8 %collective-permute-start.22 = (f32[1,16,256]{2,1,0:T(8,128)S(1)}, f32[1,16,256]{2,1,0:T(8,128)S(1)}, u32[]{:S(2)}, u32[]{:S(2)}) collective-permute-start(f32[1,16,256]{2,1,0:T(8,128)S(1)} %get-tuple-element.65), channel_id=1, source_target_pairs={{0,2},{2,4},{4,6},{6,8},{8,10},{10,12},{12,14},{14,16},{16,18},{18... | collective-permute-start | bytes 49160 | tf_op jit(solution)/shard_map/ppermute | solution.py:24
  181.7 8.1 %collective-permute-start.20 = (f32[1,16,256]{2,1,0:T(8,128)S(1)}, f32[1,16,256]{2,1,0:T(8,128)S(1)}, u32[]{:S(2)}, u32[]{:S(2)}) collective-permute-start(f32[1,16,256]{2,1,0:T(8,128)S(1)} %get-tuple-element.66), channel_id=1, source_target_pairs={{2,0},{4,2},{6,4},{8,6},{10,8},{12,10},{14,12},{16,14},{18,16},{20... | collective-permute-start | bytes 49160 | tf_op jit(solution)/shard_map/ppermute | solution.py:27
  189.8 5.9 %copy-start.16 = (f32[8,16,256]{2,1,0:T(8,128)}, f32[8,16,256]{2,1,0:T(8,128)S(1)}, u32[]{:S(2)}) copy-start(f32[8,16,256]{2,1,0:T(8,128)S(1)} %all_gather.7) | copy-start | bytes 393220
  190.2 5.6 %copy-start.7 = (f32[8,16,256]{2,1,0:T(8,128)}, f32[8,16,256]{2,1,0:T(8,128)S(1)}, u32[]{:S(2)}) copy-start(f32[8,16,256]{2,1,0:T(8,128)S(1)} %get-tuple-element.14) | copy-start | bytes 393220
  190.2 5.6 %copy-start.9 = (f32[8,16,256]{2,1,0:T(8,128)}, f32[8,16,256]{2,1,0:T(8,128)S(1)}, u32[]{:S(2)}) copy-start(f32[8,16,256]{2,1,0:T(8,128)S(1)} %get-tuple-element.15) | copy-start | bytes 393220
  190.2 5.6 %copy-start.11 = (f32[8,16,256]{2,1,0:T(8,128)}, f32[8,16,256]{2,1,0:T(8,128)S(1)}, u32[]{:S(2)}) copy-start(f32[8,16,256]{2,1,0:T(8,128)S(1)} %get-tuple-element.16) | copy-start | bytes 393220
  190.2 5.6 %copy-start.13 = (f32[8,16,256]{2,1,0:T(8,128)}, f32[8,16,256]{2,1,0:T(8,128)S(1)}, u32[]{:S(2)}) copy-start(f32[8,16,256]{2,1,0:T(8,128)S(1)} %get-tuple-element.17) | copy-start | bytes 393220
  190.2 5.6 %copy-start.15 = (f32[8,16,256]{2,1,0:T(8,128)}, f32[8,16,256]{2,1,0:T(8,128)S(1)}, u32[]{:S(2)}) copy-start(f32[8,16,256]{2,1,0:T(8,128)S(1)} %get-tuple-element.19) | copy-start | bytes 393220
  190.4 10.0 %copy-start.1 = (f32[4,8,16,256]{3,2,1,0:T(8,128)}, f32[4,8,16,256]{3,2,1,0:T(8,128)S(1)}, u32[]{:S(2)}) copy-start(f32[4,8,16,256]{3,2,1,0:T(8,128)S(1)} %get-tuple-element.63) | copy-start | bytes 1572868
  190.5 10.0 %copy-start.3 = (f32[4,8,16,256]{3,2,1,0:T(8,128)}, f32[4,8,16,256]{3,2,1,0:T(8,128)S(1)}, u32[]{:S(2)}) copy-start(f32[4,8,16,256]{3,2,1,0:T(8,128)S(1)} %get-tuple-element.64) | copy-start | bytes 1572868
  201.2 9.1 %collective-permute-start.25 = (f32[4,2,3,1,16,256]{5,4,3,2,1,0:T(8,128)S(1)}, f32[4,2,3,1,16,256]{5,4,3,2,1,0:T(8,128)S(1)}, u32[]{:S(2)}, u32[]{:S(2)}) collective-permute-start(f32[4,2,3,1,16,256]{5,4,3,2,1,0:T(8,128)S(1)} %get-tuple-element.38), channel_id=1, source_target_pairs={{0,2},{2,4},{4,6},{6,8},{8,10},{10,12},{12,14},{14,16},{16,18},{18... | collective-permute-start | bytes 1179656 | tf_op jit(solution)/shard_map/ppermute | solution.py:24
  203.5 17.0 %copy-start.8 = (f32[8,16,256]{2,1,0:T(8,128)S(1)}, f32[8,16,256]{2,1,0:T(8,128)}, u32[]{:S(2)}) copy-start(f32[8,16,256]{2,1,0:T(8,128)} %copy-done.7) | copy-start | bytes 393220
  203.5 17.0 %copy-start.10 = (f32[8,16,256]{2,1,0:T(8,128)S(1)}, f32[8,16,256]{2,1,0:T(8,128)}, u32[]{:S(2)}) copy-start(f32[8,16,256]{2,1,0:T(8,128)} %copy-done.9) | copy-start | bytes 393220
  203.5 17.0 %copy-start.12 = (f32[8,16,256]{2,1,0:T(8,128)S(1)}, f32[8,16,256]{2,1,0:T(8,128)}, u32[]{:S(2)}) copy-start(f32[8,16,256]{2,1,0:T(8,128)} %copy-done.11) | copy-start | bytes 393220
  203.5 17.0 %copy-start.14 = (f32[8,16,256]{2,1,0:T(8,128)S(1)}, f32[8,16,256]{2,1,0:T(8,128)}, u32[]{:S(2)}) copy-start(f32[8,16,256]{2,1,0:T(8,128)} %copy-done.13) | copy-start | bytes 393220
  203.5 12.4 %collective-permute-start.24 = (f32[4,2,3,1,16,256]{5,4,3,2,1,0:T(8,128)S(1)}, f32[4,2,3,1,16,256]{5,4,3,2,1,0:T(8,128)S(1)}, u32[]{:S(2)}, u32[]{:S(2)}) collective-permute-start(f32[4,2,3,1,16,256]{5,4,3,2,1,0:T(8,128)S(1)} %get-tuple-element.39), channel_id=1, source_target_pairs={{2,0},{4,2},{6,4},{8,6},{10,8},{12,10},{14,12},{16,14},{18,16},{20... | collective-permute-start | bytes 1179656 | tf_op jit(solution)/shard_map/ppermute | solution.py:27
  220.5 4.7 %copy-start.2 = (f32[4,8,16,256]{3,2,1,0:T(8,128)S(1)}, f32[4,8,16,256]{3,2,1,0:T(8,128)}, u32[]{:S(2)}) copy-start(f32[4,8,16,256]{3,2,1,0:T(8,128)} %copy-done.1) | copy-start | bytes 1572868
  (2 other events, 6.9 us)
Sparse Core Ops, SparseCore 0:
  229.0 10.5 reduce-scatter.1
where the time goes:
time: 250 us; the launch traced here: 246 us
  other arithmetic  107 us (43%)
  starting transfers between devices  60.6 us (24%)
  waiting for transfers between devices  46.4 us (19%)
  between operations  14.9 us (6%)
  blocking collectives  10.2 us (4%)
  local copies, waits for them, and re-layouts  7.11 us (3%)
    add x2, other arithmetic, reluctivity(): value = value + cell_slope[knot] * soft_width * jax.nn.softplus(scaled)  45.7 us
    ppermute x13, starting transfers between devices, with_halo(): lax.ppermute(lax.slice_in_dim(block, block.shape[dim] - width, None, axis...  32.5 us
    ppermute x13, waiting for transfers between devices, with_halo(): lax.ppermute(lax.slice_in_dim(block, 0, width, axis=dim), axis, backward)  29.6 us
    ppermute x13, starting transfers between devices, with_halo(): lax.ppermute(lax.slice_in_dim(block, 0, width, axis=dim), axis, backward)  28.1 us
    add x1, other arithmetic, reluctivity(): return (value, value + 2.0 * flux_sq * slope_sum)  23.7 us
    concatenate x11, other arithmetic, with_halo(): block = jnp.concatenate([low, block, high], axis=dim)  12.3 us
    reduce_scatter x1, waiting for transfers between devices, body(): loss = lax.psum_scatter(local_loss, 'harm', scatter_dimension=1, tiled=True)  10.7 us
    add x2, other arithmetic, complex_relax(): rhs = source + pull  9.25 us
  transfers between devices with their start and end apart: 27, of which 13 were waited for; matrix products, arithmetic and copies ran while one was open for 17% of the time, Pallas kernels for 0%

commit v1 on v0

v1 whole, which is shorter than its diff:
```python
import functools
import math

import jax
import jax.numpy as jnp
from jax import lax
from jax.experimental import pallas as pl
from jax.experimental.pallas import tpu as pltpu
from jax.sharding import PartitionSpec as P

ITERS_B = 2
ITERS_R = 2
KNOTS = 8
MATS = 4

kappa = 0.05
knot_step = 1.5
soft_width = 0.5
omega_step = 0.25

NUD_LOW, NUD_HIGH = ITERS_R, ITERS_R
A_LOW = [NUD_LOW + ITERS_B - step for step in range(ITERS_B + 1)]
A_HIGH = [NUD_HIGH + 1 + 2 * (ITERS_B - step) for step in range(ITERS_B + 1)]
S_LOW, S_HIGH = A_LOW[1], A_HIGH[1]
G_LOW, G_HIGH = A_LOW[0], A_HIGH[0] - 1

VMEM = pl.BlockSpec(memory_space=pltpu.VMEM)
SMEM = pl.BlockSpec(memory_space=pltpu.SMEM)
ANY = pl.BlockSpec(memory_space=pl.ANY)


def up(value, axis):
    return pltpu.roll(value, value.shape[axis] - 1, axis)


def down(value, axis):
    return pltpu.roll(value, 1, axis)


def index(shape, axis):
    return lax.broadcasted_iota(jnp.int32, shape, axis)


class Edges:
    def __init__(self, shape):
        rows, lanes = index(shape, 0), index(shape, 1)
        self.last_row, self.first_row = rows == shape[0] - 1, rows == 0
        self.last_lane, self.first_lane = lanes == shape[1] - 1, lanes == 0

    def sides(self):
        return ((up, 0, self.last_row), (down, 0, self.first_row), (up, 1, self.last_lane), (down, 1, self.first_lane))


def couplings(center, above, below, edges):
    weights = [0.5 * (center + above), 0.5 * (center + below)]
    total = weights[0] + weights[1]
    for move, axis, edge in edges.sides():
        weight = 0.5 * (center + jnp.where(edge, 0.0, move(center, axis)))
        total = total + weight
        weights.append(jnp.where(edge, 0.0, weight))
    return weights, total + kappa


def pull(weights, center, above, below):
    return (
        weights[0] * above
        + weights[1] * below
        + weights[2] * up(center, 0)
        + weights[3] * down(center, 0)
        + weights[4] * up(center, 1)
        + weights[5] * down(center, 1)
    )


def flux_squared(field, plane, edges):
    ax, ay, az = (field[part, plane] for part in range(3))
    ay_first, az_first = field[1, plane + 1], field[2, plane + 1]
    second = [jnp.where(edges.last_row, 0.0, up(value, 0)) for value in (ax, az)]
    third = [jnp.where(edges.last_lane, 0.0, up(value, 1)) for value in (ax, ay)]
    flux_one = (second[1] - az) - (third[1] - ay)
    flux_two = (third[0] - ax) - (az_first - az)
    flux_three = (ay_first - ay) - (second[0] - ax)
    return flux_one * flux_one + flux_two * flux_two + flux_three * flux_three


def reluctivity(flux_sq, base, slope_of, incremental):
    doubled = flux_sq / soft_width
    rising, falling = jnp.exp(doubled), jnp.exp(-doubled)
    value, slope_sum = 0.0, 0.0
    for knot in range(KNOTS):
        slope = slope_of(knot)
        offset = knot_step * knot / soft_width
        shift = math.exp(offset)
        small = jnp.minimum(rising * (1.0 / shift), falling * shift)
        grown = 1.0 + small
        value = value + slope * (jnp.maximum(doubled - offset, 0.0) + jnp.log(grown))
        if incremental:
            part = 1.0 / grown
            slope_sum = slope_sum + slope * jnp.where(doubled >= offset, part, small * part)
    nu = base + soft_width * value
    if incremental:
        nu = nu + 2.0 * flux_sq * slope_sum
    return nu


def pack_kernel(start, source, region, whole, forward, backward):
    planes = region.shape[0]
    marks = region[...].astype(jnp.float32)
    for part in range(3):
        whole[part * planes:(part + 1) * planes] = start[part]
        whole[(3 + part) * planes:(4 + part) * planes] = source[part]
        forward[part * A_LOW[0]:(part + 1) * A_LOW[0]] = start[part, planes - A_LOW[0]:]
        at = 3 * A_LOW[0] + part * S_LOW
        forward[at:at + S_LOW] = source[part, planes - S_LOW:]
        backward[part * A_HIGH[0]:(part + 1) * A_HIGH[0]] = start[part, :A_HIGH[0]]
        at = 3 * A_HIGH[0] + part * S_HIGH
        backward[at:at + S_HIGH] = source[part, :S_HIGH]
    whole[6 * planes:] = marks
    forward[3 * (A_LOW[0] + S_LOW):] = marks[planes - G_LOW:]
    backward[3 * (A_HIGH[0] + S_HIGH):] = marks[:G_HIGH]


LOW_SIZE = 3 * (A_LOW[0] + S_LOW) + G_LOW
HIGH_SIZE = 3 * (A_HIGH[0] + S_HIGH) + G_HIGH


def bias_kernel(others, meshes, *refs):
    wholes, lows, highs = refs[:others + 1], refs[others + 1:2 * others + 2], refs[2 * others + 2:3 * others + 3]
    table_index, bh_base, bh_slope, conductivity = refs[3 * others + 3:3 * others + 7]
    field_out, nud_out, sigma_out = refs[3 * others + 7:3 * others + 10]
    a0, a1, src, marks, nu, slopes, bases = refs[3 * others + 10:]
    planes = wholes[0].shape[0] // 7
    rows_each, lanes = wholes[0].shape[1:]
    rows = rows_each * (others + 1)
    mine = lax.axis_index("harm")
    here = lax.axis_index("mesh")
    for turn in range(others + 1):
        owner = lax.rem(mine + others + 1 - turn, others + 1)
        at = pl.ds(pl.multiple_of(owner * rows_each, rows_each), rows_each)
        whole, low, high = wholes[turn], lows[turn], highs[turn]

        def place(target, part, below, own, above, first_low, first_own, first_high):
            for count, origin, first, onto in (
                (below, low, first_low, 0), (own, whole, first_own, below), (above, high, first_high, below + own)
            ):
                target[part + (slice(onto, onto + count), at, slice(None))] = origin[first:first + count]

        for part in range(3):
            place(a0, (part,), A_LOW[0], planes, A_HIGH[0], part * A_LOW[0], part * planes, part * A_HIGH[0])
            place(
                src, (part,), S_LOW, planes, S_HIGH,
                3 * A_LOW[0] + part * S_LOW, (3 + part) * planes, 3 * A_HIGH[0] + part * S_HIGH,
            )
        place(
            marks, (), G_LOW, planes, G_HIGH, 3 * (A_LOW[0] + S_LOW), 6 * planes, 3 * (A_HIGH[0] + S_HIGH)
        )

    edges = Edges((rows, lanes))
    tables = [table_index[member] for member in range(MATS)]
    base_of = [bh_base[table] for table in tables]
    slope_of = [[bh_slope[table, knot] for table in tables] for knot in range(KNOTS)]
    sigma_of = [conductivity[member] for member in range(MATS)]

    def inside(plane):
        low_ok = jnp.logical_or(plane >= 0, here > 0)
        high_ok = jnp.logical_or(plane < planes, here < meshes - 1)
        return jnp.where(jnp.logical_and(low_ok, high_ok), 1.0, 0.0)

    def choose(mark, values):
        chosen = jnp.where(mark == 1.0, values[1], values[0])
        for member in range(2, MATS):
            chosen = jnp.where(mark == float(member), values[member], chosen)
        return chosen

    def relax_into(target, step, old):
        def body(at, carry):
            plane = at - A_LOW[step]
            near = plane + A_LOW[step] + 1
            weights, total = couplings(nu[near], nu[near + 1], nu[near - 1], edges)
            scale = inside(plane) / total
            from_old = plane + A_LOW[step - 1]
            for part in range(3):
                moved = pull(weights, old[part, from_old], old[part, from_old + 1], old[part, from_old - 1])
                target[part, at] = (src[part, plane + S_LOW] + moved) * scale
            return carry

        lax.fori_loop(0, planes + A_LOW[step] + A_HIGH[step], body, 0)

    def first_nu(at, carry):
        mark = marks[at]
        bases[at] = choose(mark, base_of)
        for knot in range(KNOTS):
            slopes[knot, at] = choose(mark, slope_of[knot])
        value = reluctivity(flux_squared(a0, at, edges), bases[at], lambda knot: slopes[knot, at], False)
        nu[at] = value * inside(at - G_LOW)
        return carry

    lax.fori_loop(0, planes + G_LOW + G_HIGH, first_nu, 0)
    fields = (a0, a1)
    for step in range(1, ITERS_B + 1):
        old, new = fields[(step - 1) % 2], fields[step % 2]
        relax_into(new, step, old)
        last = step == ITERS_B
        lower = NUD_LOW if last else A_LOW[step + 1] + 1
        upper = NUD_HIGH if last else A_HIGH[step + 1] + 1

        def next_nu(at, carry):
            plane = at - lower
            known = plane + G_LOW
            value = reluctivity(
                flux_squared(new, plane + A_LOW[step], edges), bases[known], lambda knot: slopes[knot, known], last
            )
            value = value * inside(plane)
            if last:
                nud_out[at] = value
            else:
                nu[at] = value
            return carry

        lax.fori_loop(0, planes + lower + upper, next_nu, 0)

    def sigma_at(at, carry):
        sigma_out[at] = choose(marks[at - (ITERS_R - 1) + G_LOW], sigma_of)
        return carry

    lax.fori_loop(0, planes + 2 * (ITERS_R - 1), sigma_at, 0)
    own_rows = pl.ds(pl.multiple_of(mine * rows_each, rows_each), rows_each)
    final = fields[ITERS_B % 2]
    for part in range(3):
        field_out[part] = final[part, A_LOW[ITERS_B]:A_LOW[ITERS_B] + planes, own_rows, :]


def ripple_kernel(
    shares, meshes, harmonic_numbers, nud, sigma, start, source, low, high, ripple_out, loss_out, r0, r1, src, loss, sems
):
    count, planes = start.shape[0], start.shape[3]
    rows, lanes = start.shape[4:]
    mine = lax.axis_index("harm")
    here = lax.axis_index("mesh")
    copies = [
        pltpu.make_async_copy(low.at[:, :, :, 0:2], r0.at[:, :, :, 0:2], sems.at[0]),
        pltpu.make_async_copy(low.at[:, :, :, 2:3], src.at[:, :, :, 0:1], sems.at[1]),
        pltpu.make_async_copy(start, r0.at[:, :, :, 2:planes + 2], sems.at[2]),
        pltpu.make_async_copy(source, src.at[:, :, :, 1:planes + 1], sems.at[3]),
        pltpu.make_async_copy(high.at[:, :, :, 0:2], r0.at[:, :, :, planes + 2:planes + 4], sems.at[4]),
        pltpu.make_async_copy(high.at[:, :, :, 2:3], src.at[:, :, :, planes + 1:planes + 2], sems.at[5]),
    ]
    for copy in copies:
        copy.start()
    for copy in copies:
        copy.wait()
    edges = Edges((rows, lanes))
    omegas = [omega_step * harmonic_numbers[mine * count + harmonic].astype(jnp.float32) for harmonic in range(count)]

    def sweep(old, offset, plane, store):
        near = plane + NUD_LOW
        weights, total = couplings(nud[near], nud[near + 1], nud[near - 1], edges)
        conduct = sigma[plane + 1]
        for harmonic in range(count):
            damp = omegas[harmonic] * conduct
            inverse = 1.0 / (total * total + damp * damp)
            straight, turned = total * inverse, damp * inverse
            power = 0.0
            for part in range(3):
                sides = []
                for piece in range(2):
                    field = old.at[harmonic, piece, part]
                    moved = pull(weights, field[plane + offset], field[plane + offset + 1], field[plane + offset - 1])
                    sides.append(src[harmonic, piece, part, plane + 1] + moved)
                real = sides[0] * straight + sides[1] * turned
                imag = sides[1] * straight - sides[0] * turned
                power = power + (real * real + imag * imag)
                store(harmonic, part, real, imag)
            yield harmonic, conduct, power

    def first(at, carry):
        plane = at - 1
        low_ok = jnp.logical_or(plane >= 0, here > 0)
        high_ok = jnp.logical_or(plane < planes, here < meshes - 1)
        keep = jnp.where(jnp.logical_and(low_ok, high_ok), 1.0, 0.0)

        def store(harmonic, part, real, imag):
            r1[harmonic, 0, part, at] = real * keep
            r1[harmonic, 1, part, at] = imag * keep

        for unused in sweep(r0, 2, plane, store):
            pass
        return carry

    lax.fori_loop(0, planes + 2, first, 0)

    def second(plane, carry):
        def store(harmonic, part, real, imag):
            ripple_out[harmonic, 0, part, plane] = real
            ripple_out[harmonic, 1, part, plane] = imag

        summed = 0.0
        for harmonic, conduct, power in sweep(r1, 1, plane, store):
            summed = summed + (0.5 * omegas[harmonic] * omegas[harmonic]) * conduct * power
        loss[plane] = summed
        return carry

    lax.fori_loop(0, planes, second, 0)
    rows_each = rows // shares
    for turn in range(shares):
        owner = lax.rem(mine + turn, shares)
        loss_out[turn] = loss[:, pl.ds(pl.multiple_of(owner * rows_each, rows_each), rows_each), :]


def body(
    meshes, shares, bias_source, bias_start, region, table_index, bh_base, bh_slope, conductivity, harmonic_numbers,
    ripple_source, ripple_start,
):
    f32 = jnp.float32
    unused, planes, rows_each, lanes = bias_start.shape
    rows = rows_each * shares
    count = ripple_start.shape[0]
    upward = [(i, i + 1) for i in range(meshes - 1)]
    downward = [(i + 1, i) for i in range(meshes - 1)]
    turned = [[(i, (i + turn) % shares) for i in range(shares)] for turn in range(1, shares)]

    whole, forward, backward = pl.pallas_call(
        pack_kernel,
        out_shape=[jax.ShapeDtypeStruct((size, rows_each, lanes), f32) for size in (7 * planes, LOW_SIZE, HIGH_SIZE)],
        in_specs=[VMEM] * 3,
        out_specs=[VMEM] * 3,
        name="pack",
    )(bias_start, bias_source, region)
    wholes = [whole] + [lax.ppermute(whole, "harm", pairs) for pairs in turned]
    low = lax.ppermute(forward, "mesh", upward)
    high = lax.ppermute(backward, "mesh", downward)
    lows = [low] + [lax.ppermute(low, "harm", pairs) for pairs in turned]
    highs = [high] + [lax.ppermute(high, "harm", pairs) for pairs in turned]

    ripple_up = jnp.concatenate([ripple_start[:, :, :, planes - 2:], ripple_source[:, :, :, planes - 1:]], axis=3)
    ripple_down = jnp.concatenate([ripple_start[:, :, :, :2], ripple_source[:, :, :, :1]], axis=3)
    ripple_low = lax.ppermute(ripple_up, "mesh", upward)
    ripple_high = lax.ppermute(ripple_down, "mesh", downward)

    def scratch(*shape):
        return pltpu.VMEM(shape, f32)

    field, nud, sigma = pl.pallas_call(
        functools.partial(bias_kernel, shares - 1, meshes),
        out_shape=[
            jax.ShapeDtypeStruct(bias_start.shape, f32),
            jax.ShapeDtypeStruct((planes + NUD_LOW + NUD_HIGH, rows, lanes), f32),
            jax.ShapeDtypeStruct((planes + 2 * (ITERS_R - 1), rows, lanes), f32),
        ],
        in_specs=[VMEM] * (3 * shares) + [SMEM] * 4,
        out_specs=[VMEM] * 3,
        scratch_shapes=[
            scratch(3, planes + A_LOW[0] + A_HIGH[0], rows, lanes),
            scratch(3, planes + A_LOW[1] + A_HIGH[1], rows, lanes),
            scratch(3, planes + S_LOW + S_HIGH, rows, lanes),
            scratch(planes + G_LOW + G_HIGH, rows, lanes),
            scratch(planes + G_LOW + G_HIGH, rows, lanes),
            scratch(KNOTS, planes + G_LOW + G_HIGH, rows, lanes),
            scratch(planes + G_LOW + G_HIGH, rows, lanes),
        ],
        compiler_params=pltpu.CompilerParams(vmem_limit_bytes=56 * 2**20),
        name="bias",
    )(*wholes, *lows, *highs, table_index, bh_base, bh_slope, conductivity)

    ripple, losses = pl.pallas_call(
        functools.partial(ripple_kernel, shares, meshes),
        out_shape=[
            jax.ShapeDtypeStruct(ripple_start.shape, f32),
            jax.ShapeDtypeStruct((shares, planes, rows_each, lanes), f32),
        ],
        in_specs=[SMEM, VMEM, VMEM] + [ANY] * 4,
        out_specs=[VMEM] * 2,
        scratch_shapes=[
            scratch(count, 2, 3, planes + 4, rows, lanes),
            scratch(count, 2, 3, planes + 2, rows, lanes),
            scratch(count, 2, 3, planes + 2, rows, lanes),
            scratch(planes, rows, lanes),
            pltpu.SemaphoreType.DMA((6,)),
        ],
        compiler_params=pltpu.CompilerParams(vmem_limit_bytes=56 * 2**20),
        name="ripple",
    )(harmonic_numbers, nud, sigma, ripple_start, ripple_source, ripple_low, ripple_high)
    loss = losses[0]
    for turn, pairs in enumerate(turned):
        loss = loss + lax.ppermute(losses[turn + 1], "harm", pairs)
    return field, ripple, loss


def solution(mesh):
    return jax.shard_map(
        functools.partial(body, mesh.shape["mesh"], mesh.shape["harm"]),
        mesh=mesh,
        in_specs=(
            P(None, "mesh", "harm", None),
            P(None, "mesh", "harm", None),
            P("mesh", "harm", None),
            P(),
            P(),
            P(),
            P(),
            P(),
            P("harm", None, None, "mesh", None, None),
            P("harm", None, None, "mesh", None, None),
        ),
        out_specs=(
            P(None, "mesh", "harm", None),
            P("harm", None, None, "mesh", None, None),
            P("mesh", "harm", None),
        ),
        check_vma=False,
    )
```

time: 250 us -> 83.7 us (0.33); the launches traced: 246 us -> 83.3 us
  other arithmetic: 107 us -> 2.72 us
  starting transfers between devices: 60.6 us -> 15.1 us
  Pallas kernels: 0 us -> 27.7 us
  waiting for transfers between devices: 46.4 us -> 30.5 us
  between operations: 14.9 us -> 0.74 us
  blocking collectives: 10.2 us -> 0 us
    add x8 -> x1, other arithmetic: 82.9 us -> 1.48 us  [body(): loss = loss + lax.ppermute(losses[turn + 1], 'harm', pairs)]
    ppermute x26 -> x8, starting transfers between devices: 60.6 us -> 15.1 us  [the longest x1 3.63 us: body(): ripple_high = lax.ppermute(ripple_down, 'mesh', downward)]
    pallas_call x0 -> x3, Pallas kernels: none -> 27.7 us  [the longest x1 13.2 us: body(): pl.pallas_call(functools.partial(ripple_kernel, shares, meshes), out_shap...]
    concatenate x11 -> x2, other arithmetic: 12.3 us -> 1.25 us  [the longest x1 1.13 us: body(): jnp.concatenate([ripple_start[:, :, :, :2], ripple_source[:, :, :, :1]],...]
    reduce_scatter x1 -> x0, waiting for transfers between devices: 10.7 us -> none  [body(): loss = lax.psum_scatter(local_loss, 'harm', scatter_dimension=1, tiled=True)]
    all_gather x2 -> x0, blocking collectives: 10.2 us -> none  [the longest x1 5.27 us: body(): lax.all_gather(cell_sigma, 'harm', axis=1, tiled=True)]
    ppermute x26 -> x8, waiting for transfers between devices: 35.7 us -> 30.5 us  [the longest x1 20.8 us: body(): high = lax.ppermute(backward, 'mesh', downward)]
    reduce_sum x4 -> x0, other arithmetic: 4.64 us -> none  [the longest x1 2.25 us: harmonic_loss(): power = jnp.sum(ripple * ripple, axis=(1, 2))]
  transfers between devices with their start and end apart: 27 -> 8, of which waited for: 13 -> 3; matrix products, arithmetic and copies ran while one was open for 17% -> 1% of each run, Pallas kernels for 0% -> 17%
where the time goes in v1:
time: 83.7 us; the launch traced here: 83.3 us
  waiting for transfers between devices  30.5 us (36%)
  Pallas kernels  27.7 us (33%)
  starting transfers between devices  15.1 us (18%)
  local copies, waits for them, and re-layouts  6.52 us (8%)
  other arithmetic  2.72 us (3%)
    ppermute x1, waiting for transfers between devices, body(): high = lax.ppermute(backward, 'mesh', downward)  20.8 us
    pallas_call x1, Pallas kernels, body(): pl.pallas_call(functools.partial(ripple_kernel, shares, meshes), out_shap...  13.2 us
    pallas_call x1, Pallas kernels, body(): pl.pallas_call(functools.partial(bias_kernel, shares - 1, meshes), out_sh...  12.4 us
    ppermute x1, waiting for transfers between devices, body(): lows = [low] + [lax.ppermute(low, 'harm', pairs) for pairs in turned]  6.98 us
    ppermute x1, starting transfers between devices, body(): ripple_high = lax.ppermute(ripple_down, 'mesh', downward)  3.63 us
    unnamed x14, local copies, waits for them, and re-layouts  2.94 us
    ppermute x1, waiting for transfers between devices, body(): loss = loss + lax.ppermute(losses[turn + 1], 'harm', pairs)  2.77 us
    ppermute x1, starting transfers between devices, body(): low = lax.ppermute(forward, 'mesh', upward)  2.11 us
  transfers between devices with their start and end apart: 8, of which 3 were waited for; matrix products, arithmetic and copies ran while one was open for 1% of the time, Pallas kernels for 17%

profile of v1, /device:TPU:12, one launch (start us, length us, event | category | flops | bytes accessed | tf_op | source)
XLA Modules:
  0.0 83.3 jit_solution(15857648462475723060)
XLA Ops:
  0.6 1.2 %fusion.1 = (f32[4,2,3,1,16,256]{5,4,3,2,1,0:T(8,128)S(1)}, f32[4,2,3,1,16,256]{5,4,3,2,1,0:T(8,128)S(1)}) fusion(f32[4,2,3,8,16,256]{5,4,3,2,1,0:T(8,128)} %source.3), kind=kLoop, calls=%fused_computation.5 | loop fusion | bytes 1572864 | tf_op jit(solution)/shard_map/slice | solution.py:336
  1.8 1.5 %fusion = (f32[4,2,3,2,16,256]{5,4,3,2,1,0:T(8,128)S(1)}, f32[4,2,3,2,16,256]{5,4,3,2,1,0:T(8,128)S(1)}) fusion(f32[4,2,3,8,16,256]{5,4,3,2,1,0:T(8,128)} %start.3), kind=kLoop, calls=%fused_computation.4 | loop fusion | bytes 3145728 | tf_op jit(solution)/shard_map/slice | solution.py:336
  3.4 0.1 pad_maximum_fusion
  3.5 1.9 %collective-permute-start.5 = (f32[4,2,3,3,16,256]{5,4,3,2,1,0:T(8,128)S(1)}, f32[4,2,3,3,16,256]{5,4,3,2,1,0:T(8,128)S(1)}, u32[]{:S(2)}, u32[]{:S(2)}) collective-permute-start(f32[4,2,3,3,16,256]{5,4,3,2,1,0:T(8,128)S(1)} %pad_maximum_fusion), channel_id=1, source_target_pairs={{0,2},{2,4},{4,6},{6,8},{8,10},{10,12},{12,14},{14,16},{16,18},{18... | collective-permute-start | bytes 3538952 | tf_op jit(solution)/shard_map/ppermute | solution.py:337
  5.4 1.1 %pad_maximum_fusion.1 = f32[4,2,3,3,16,256]{5,4,3,2,1,0:T(8,128)} fusion(f32[4,2,3,1,16,256]{5,4,3,2,1,0:T(8,128)S(1)} %get-tuple-element.21, f32[4,2,3,2,16,256]{5,4,3,2,1,0:T(8,128)S(1)} %get-tuple-element.19), kind=kLoop, calls=%fused_computation.1 | loop fusion | flops 294912 | bytes 2359296 | tf_op jit(solution)/shard_map/concatenate | solution.py:336
  6.6 3.6 %collective-permute-start.6 = (f32[4,2,3,3,16,256]{5,4,3,2,1,0:T(8,128)}, f32[4,2,3,3,16,256]{5,4,3,2,1,0:T(8,128)S(1)}, u32[]{:S(2)}, u32[]{:S(2)}) collective-permute-start(f32[4,2,3,3,16,256]{5,4,3,2,1,0:T(8,128)} %pad_maximum_fusion.1), channel_id=1, source_target_pairs={{2,0},{4,2},{6,4},{8,6},{10,8},{12,10},{14,12},{16,14},{18,16},{20... | collective-permute-start | bytes 3538952 | tf_op jit(solution)/shard_map/ppermute | solution.py:338
  10.2 2.0 %pack.1 = (f32[56,8,256]{2,1,0:T(8,128)}, f32[25,8,256]{2,1,0:T(8,128)}, f32[42,8,256]{2,1,0:T(8,128)}) custom-call(f32[3,8,8,256]{3,2,1,0:T(8,128)} %start.2, f32[3,8,8,256]{3,2,1,0:T(8,128)} %source.2, s32[8,8,256]{2,1,0:T(8,128)} %region.1), custom_call_target="tpu_custom_call" | custom-call | tf_op jit(solution)/shard_map/pack/pallas_call | solution.py:322
  12.2 1.9 %collective-permute-start.3 = (f32[42,8,256]{2,1,0:T(8,128)}, f32[42,8,256]{2,1,0:T(8,128)S(1)}, u32[]{:S(2)}, u32[]{:S(2)}) collective-permute-start(f32[42,8,256]{2,1,0:T(8,128)} %get-tuple-element.13), channel_id=1, source_target_pairs={{2,0},{4,2},{6,4},{8,6},{10,8},{12,10},{14,12},{16,14},{18,16},{20... | collective-permute-start | bytes 1032200 | tf_op jit(solution)/shard_map/ppermute | solution.py:331
  14.1 1.6 %collective-permute-start = (f32[56,8,256]{2,1,0:T(8,128)}, f32[56,8,256]{2,1,0:T(8,128)S(1)}, u32[]{:S(2)}, u32[]{:S(2)}) collective-permute-start(f32[56,8,256]{2,1,0:T(8,128)} %get-tuple-element.11.refs_0_), channel_id=1, source_target_pairs={{0,1},{1,0},{2,3},{3,2},{4,5},{5,4},{6,7},{7,6},{8,9},{9,8},{10,11... | collective-permute-start | bytes 1376264 | tf_op jit(solution)/shard_map/ppermute | solution.py:329
  15.7 2.1 %collective-permute-start.1 = (f32[25,8,256]{2,1,0:T(8,128)}, f32[25,8,256]{2,1,0:T(8,128)S(1)}, u32[]{:S(2)}, u32[]{:S(2)}) collective-permute-start(f32[25,8,256]{2,1,0:T(8,128)} %get-tuple-element.12), channel_id=1, source_target_pairs={{0,2},{2,4},{4,6},{6,8},{8,10},{10,12},{12,14},{14,16},{16,18},{18... | collective-permute-start | bytes 614408 | tf_op jit(solution)/shard_map/ppermute | solution.py:330
  17.8 20.8 %collective-permute-done.3.refs_4_ = f32[42,8,256]{2,1,0:T(8,128)S(1)} collective-permute-done((f32[42,8,256]{2,1,0:T(8,128)}, f32[42,8,256]{2,1,0:T(8,128)S(1)}, u32[]{:S(2)}, u32[]{:S(2)}) %collective-permute-start.3) | collective-permute-done | bytes 344096 | tf_op jit(solution)/shard_map/ppermute | solution.py:331
  38.6 0.0 copy-start.3
  38.6 1.5 %collective-permute-start.4 = (f32[42,8,256]{2,1,0:T(8,128)S(1)}, f32[42,8,256]{2,1,0:T(8,128)S(1)}, u32[]{:S(2)}, u32[]{:S(2)}) collective-permute-start(f32[42,8,256]{2,1,0:T(8,128)S(1)} %collective-permute-done.3.refs_4_), channel_id=1, source_target_pairs={{0,1},{1,0},{2,3},{3,2},{4,5},{5,4},{6,7},{7,6},{8,9},{9,8},{10,11... | collective-permute-start | bytes 1032200 | tf_op jit(solution)/shard_map/ppermute | solution.py:333
  40.1 0.0 collective-permute-done.1.refs_2_
  40.1 0.0 copy-start.5
  40.1 1.0 %collective-permute-start.2 = (f32[25,8,256]{2,1,0:T(8,128)S(1)}, f32[25,8,256]{2,1,0:T(8,128)S(1)}, u32[]{:S(2)}, u32[]{:S(2)}) collective-permute-start(f32[25,8,256]{2,1,0:T(8,128)S(1)} %collective-permute-done.1.refs_2_), channel_id=1, source_target_pairs={{0,1},{1,0},{2,3},{3,2},{4,5},{5,4},{6,7},{7,6},{8,9},{9,8},{10,11... | collective-permute-start | bytes 614408 | tf_op jit(solution)/shard_map/ppermute | solution.py:332
  41.0 7.0 %collective-permute-done.2.refs_3_ = f32[25,8,256]{2,1,0:T(8,128)S(1)} collective-permute-done((f32[25,8,256]{2,1,0:T(8,128)S(1)}, f32[25,8,256]{2,1,0:T(8,128)S(1)}, u32[]{:S(2)}, u32[]{:S(2)}) %collective-permute-start.2) | collective-permute-done | bytes 204832 | tf_op jit(solution)/shard_map/ppermute | solution.py:332
  48.0 0.0 copy-start.6
  48.0 0.0 collective-permute-done.refs_1_
  48.0 0.0 copy-start.2
  48.0 0.0 collective-permute-done.4.refs_5_
  48.0 0.0 copy-done.3
  48.0 0.0 copy-done.5
  48.1 0.7 copy-done.6
  48.7 0.2 copy-done.2
  48.9 0.0 copy-start.4
  48.9 0.7 copy-done.4
  49.6 12.4 %bias.1 = (f32[3,8,8,256]{3,2,1,0:T(8,128)}, f32[12,16,256]{2,1,0:T(8,128)}, f32[10,16,256]{2,1,0:T(8,128)}) custom-call(f32[56,8,256]{2,1,0:T(8,128)} %get-tuple-element.11.refs_0_, f32[56,8,256]{2,1,0:T(8,128)} %copy-done.2, f32[25,8,256]{2,1,0:T(8,128)} %copy-done.5, f32[25,8,256]{2,1,0:T(8,128)} %copy-done.6, f32[42,8,256]{2,1,0:T(8,128)} %copy-done.3, ...), custom_call_target="tpu_custom_call" | custom-call | tf_op jit(solution)/shard_map/bias/pallas_call | solution.py:343
  62.0 0.0 collective-permute-done.5.low
  62.0 0.0 copy-start
  62.0 0.0 collective-permute-done.6.high
  62.0 0.0 copy-start.1
  62.0 1.0 %copy-done = f32[4,2,3,3,16,256]{5,4,3,2,1,0:T(8,128)} copy-done((f32[4,2,3,3,16,256]{5,4,3,2,1,0:T(8,128)}, f32[4,2,3,3,16,256]{5,4,3,2,1,0:T(8,128)S(1)}, u32[]{:S(2)}) %copy-start) | copy-done | bytes 1179672
  63.1 0.4 copy-done.1
  63.4 13.2 %ripple.1 = (f32[4,2,3,8,16,256]{5,4,3,2,1,0:T(8,128)}, f32[2,8,8,256]{3,2,1,0:T(8,128)}) custom-call(s32[8]{0:T(128)} %harmonic_numbers.1, f32[12,16,256]{2,1,0:T(8,128)} %get-tuple-element.15.nud, f32[10,16,256]{2,1,0:T(8,128)} %get-tuple-element.16.sigma, f32[4,2,3,8,16,256]{5,4,3,2,1,0:T(8,128)} %start.3, f32[4,2,3,8,16,256]{5,4,3,2,1,0:T(8,128)} %source.3, ...), custom_call_target="tpu_custom_call" | custom-call | tf_op jit(solution)/shard_map/ripple/pallas_call | solution.py:365
  76.7 0.8 %slice_bitcast_fusion = f32[8,8,256]{2,1,0:T(8,128)S(1)} fusion(f32[2,8,8,256]{3,2,1,0:T(8,128)} %get-tuple-element.18), kind=kLoop, calls=%fused_computation.3 | loop fusion | bytes 131072 | tf_op jit(solution)/shard_map/squeeze | solution.py:385
  77.5 1.5 %collective-permute-start.7 = (f32[8,8,256]{2,1,0:T(8,128)S(1)}, f32[8,8,256]{2,1,0:T(8,128)S(1)}, u32[]{:S(2)}, u32[]{:S(2)}) collective-permute-start(f32[8,8,256]{2,1,0:T(8,128)S(1)} %slice_bitcast_fusion), channel_id=1, source_target_pairs={{0,1},{1,0},{2,3},{3,2},{4,5},{5,4},{6,7},{7,6},{8,9},{9,8},{10,11... | collective-permute-start | bytes 196616 | tf_op jit(solution)/shard_map/ppermute | solution.py:385
  79.0 2.8 %collective-permute-done.7 = f32[8,8,256]{2,1,0:T(8,128)S(1)} collective-permute-done((f32[8,8,256]{2,1,0:T(8,128)S(1)}, f32[8,8,256]{2,1,0:T(8,128)S(1)}, u32[]{:S(2)}, u32[]{:S(2)}) %collective-permute-start.7) | collective-permute-done | bytes 65568 | tf_op jit(solution)/shard_map/ppermute | solution.py:385
  81.8 1.5 %bitcast_add_fusion = f32[8,8,256]{2,1,0:T(8,128)} fusion(f32[8,8,256]{2,1,0:T(8,128)S(1)} %collective-permute-done.7, f32[2,8,8,256]{3,2,1,0:T(8,128)} %get-tuple-element.18), kind=kLoop, calls=%fused_computation.2 | loop fusion | flops 16384 | bytes 196608 | tf_op jit(solution)/shard_map/add | solution.py:385
Async XLA Ops:
  3.5 58.5 %collective-permute-start.5 = (f32[4,2,3,3,16,256]{5,4,3,2,1,0:T(8,128)S(1)}, f32[4,2,3,3,16,256]{5,4,3,2,1,0:T(8,128)S(1)}, u32[]{:S(2)}, u32[]{:S(2)}) collective-permute-start(f32[4,2,3,3,16,256]{5,4,3,2,1,0:T(8,128)S(1)} %pad_maximum_fusion), channel_id=1, source_target_pairs={{0,2},{2,4},{4,6},{6,8},{8,10},{10,12},{12,14},{14,16},{16,18},{18... | collective-permute-start | bytes 3538952 | tf_op jit(solution)/shard_map/ppermute | solution.py:337
  6.6 55.5 %collective-permute-start.6 = (f32[4,2,3,3,16,256]{5,4,3,2,1,0:T(8,128)}, f32[4,2,3,3,16,256]{5,4,3,2,1,0:T(8,128)S(1)}, u32[]{:S(2)}, u32[]{:S(2)}) collective-permute-start(f32[4,2,3,3,16,256]{5,4,3,2,1,0:T(8,128)} %pad_maximum_fusion.1), channel_id=1, source_target_pairs={{2,0},{4,2},{6,4},{8,6},{10,8},{12,10},{14,12},{16,14},{18,16},{20... | collective-permute-start | bytes 3538952 | tf_op jit(solution)/shard_map/ppermute | solution.py:338
  12.2 26.4 %collective-permute-start.3 = (f32[42,8,256]{2,1,0:T(8,128)}, f32[42,8,256]{2,1,0:T(8,128)S(1)}, u32[]{:S(2)}, u32[]{:S(2)}) collective-permute-start(f32[42,8,256]{2,1,0:T(8,128)} %get-tuple-element.13), channel_id=1, source_target_pairs={{2,0},{4,2},{6,4},{8,6},{10,8},{12,10},{14,12},{16,14},{18,16},{20... | collective-permute-start | bytes 1032200 | tf_op jit(solution)/shard_map/ppermute | solution.py:331
  14.1 33.9 %collective-permute-start = (f32[56,8,256]{2,1,0:T(8,128)}, f32[56,8,256]{2,1,0:T(8,128)S(1)}, u32[]{:S(2)}, u32[]{:S(2)}) collective-permute-start(f32[56,8,256]{2,1,0:T(8,128)} %get-tuple-element.11.refs_0_), channel_id=1, source_target_pairs={{0,1},{1,0},{2,3},{3,2},{4,5},{5,4},{6,7},{7,6},{8,9},{9,8},{10,11... | collective-permute-start | bytes 1376264 | tf_op jit(solution)/shard_map/ppermute | solution.py:329
  15.7 24.4 %collective-permute-start.1 = (f32[25,8,256]{2,1,0:T(8,128)}, f32[25,8,256]{2,1,0:T(8,128)S(1)}, u32[]{:S(2)}, u32[]{:S(2)}) collective-permute-start(f32[25,8,256]{2,1,0:T(8,128)} %get-tuple-element.12), channel_id=1, source_target_pairs={{0,2},{2,4},{4,6},{6,8},{8,10},{10,12},{12,14},{14,16},{16,18},{18... | collective-permute-start | bytes 614408 | tf_op jit(solution)/shard_map/ppermute | solution.py:330
  38.6 9.5 %copy-start.3 = (f32[42,8,256]{2,1,0:T(8,128)}, f32[42,8,256]{2,1,0:T(8,128)S(1)}, u32[]{:S(2)}) copy-start(f32[42,8,256]{2,1,0:T(8,128)S(1)} %collective-permute-done.3.refs_4_) | copy-start | bytes 1032196
  38.6 9.5 %collective-permute-start.4 = (f32[42,8,256]{2,1,0:T(8,128)S(1)}, f32[42,8,256]{2,1,0:T(8,128)S(1)}, u32[]{:S(2)}, u32[]{:S(2)}) collective-permute-start(f32[42,8,256]{2,1,0:T(8,128)S(1)} %collective-permute-done.3.refs_4_), channel_id=1, source_target_pairs={{0,1},{1,0},{2,3},{3,2},{4,5},{5,4},{6,7},{7,6},{8,9},{9,8},{10,11... | collective-permute-start | bytes 1032200 | tf_op jit(solution)/shard_map/ppermute | solution.py:333
  40.1 8.0 %copy-start.5 = (f32[25,8,256]{2,1,0:T(8,128)}, f32[25,8,256]{2,1,0:T(8,128)S(1)}, u32[]{:S(2)}) copy-start(f32[25,8,256]{2,1,0:T(8,128)S(1)} %collective-permute-done.1.refs_2_) | copy-start | bytes 614404
  40.1 7.9 %collective-permute-start.2 = (f32[25,8,256]{2,1,0:T(8,128)S(1)}, f32[25,8,256]{2,1,0:T(8,128)S(1)}, u32[]{:S(2)}, u32[]{:S(2)}) collective-permute-start(f32[25,8,256]{2,1,0:T(8,128)S(1)} %collective-permute-done.1.refs_2_), channel_id=1, source_target_pairs={{0,1},{1,0},{2,3},{3,2},{4,5},{5,4},{6,7},{7,6},{8,9},{9,8},{10,11... | collective-permute-start | bytes 614408 | tf_op jit(solution)/shard_map/ppermute | solution.py:332
  48.0 0.7 copy-start.6
  48.0 0.8 %copy-start.2 = (f32[56,8,256]{2,1,0:T(8,128)}, f32[56,8,256]{2,1,0:T(8,128)S(1)}, u32[]{:S(2)}) copy-start(f32[56,8,256]{2,1,0:T(8,128)S(1)} %collective-permute-done.refs_1_) | copy-start | bytes 1376260
  48.9 0.7 copy-start.4
  62.0 1.1 %copy-start = (f32[4,2,3,3,16,256]{5,4,3,2,1,0:T(8,128)}, f32[4,2,3,3,16,256]{5,4,3,2,1,0:T(8,128)S(1)}, u32[]{:S(2)}) copy-start(f32[4,2,3,3,16,256]{5,4,3,2,1,0:T(8,128)S(1)} %collective-permute-done.5.low) | copy-start | bytes 3538948
  62.0 1.4 %copy-start.1 = (f32[4,2,3,3,16,256]{5,4,3,2,1,0:T(8,128)}, f32[4,2,3,3,16,256]{5,4,3,2,1,0:T(8,128)S(1)}, u32[]{:S(2)}) copy-start(f32[4,2,3,3,16,256]{5,4,3,2,1,0:T(8,128)S(1)} %collective-permute-done.6.high) | copy-start | bytes 3538948
  77.5 4.3 %collective-permute-start.7 = (f32[8,8,256]{2,1,0:T(8,128)S(1)}, f32[8,8,256]{2,1,0:T(8,128)S(1)}, u32[]{:S(2)}, u32[]{:S(2)}) collective-permute-start(f32[8,8,256]{2,1,0:T(8,128)S(1)} %slice_bitcast_fusion), channel_id=1, source_target_pairs={{0,1},{1,0},{2,3},{3,2},{4,5},{5,4},{6,7},{7,6},{8,9},{9,8},{10,11... | collective-permute-start | bytes 196616 | tf_op jit(solution)/shard_map/ppermute | solution.py:385

commit v2 on v1

--- a/solution.py
+++ b/solution.py
@@ -24,6 +24,12 @@
 S_LOW, S_HIGH = A_LOW[1], A_HIGH[1]
 G_LOW, G_HIGH = A_LOW[0], A_HIGH[0] - 1
 
+BIAS_WORK = 1000000000
+RP_ROOM = 58 * 2**20
+PACK_ROOM = 62 * 2**20
+RIPPLE_ROOM = 59 * 2**20 + 2**19
+RP_WORK = 0
+HOLD_WORK = 0
 VMEM = pl.BlockSpec(memory_space=pltpu.VMEM)
 SMEM = pl.BlockSpec(memory_space=pltpu.SMEM)
 ANY = pl.BlockSpec(memory_space=pl.ANY)
@@ -103,57 +109,103 @@
     return nu
 
 
-def pack_kernel(start, source, region, whole, forward, backward):
-    planes = region.shape[0]
-    marks = region[...].astype(jnp.float32)
-    for part in range(3):
-        whole[part * planes:(part + 1) * planes] = start[part]
-        whole[(3 + part) * planes:(4 + part) * planes] = source[part]
-        forward[part * A_LOW[0]:(part + 1) * A_LOW[0]] = start[part, planes - A_LOW[0]:]
-        at = 3 * A_LOW[0] + part * S_LOW
-        forward[at:at + S_LOW] = source[part, planes - S_LOW:]
-        backward[part * A_HIGH[0]:(part + 1) * A_HIGH[0]] = start[part, :A_HIGH[0]]
-        at = 3 * A_HIGH[0] + part * S_HIGH
-        backward[at:at + S_HIGH] = source[part, :S_HIGH]
-    whole[6 * planes:] = marks
-    forward[3 * (A_LOW[0] + S_LOW):] = marks[planes - G_LOW:]
-    backward[3 * (A_HIGH[0] + S_HIGH):] = marks[:G_HIGH]
-
-
 LOW_SIZE = 3 * (A_LOW[0] + S_LOW) + G_LOW
 HIGH_SIZE = 3 * (A_HIGH[0] + S_HIGH) + G_HIGH
 
 
-def bias_kernel(others, meshes, *refs):
-    wholes, lows, highs = refs[:others + 1], refs[others + 1:2 * others + 2], refs[2 * others + 2:3 * others + 3]
-    table_index, bh_base, bh_slope, conductivity = refs[3 * others + 3:3 * others + 7]
-    field_out, nud_out, sigma_out = refs[3 * others + 7:3 * others + 10]
-    a0, a1, src, marks, nu, slopes, bases = refs[3 * others + 10:]
+def edge_parts(planes, low):
+    halo_of = ((A_LOW if low else A_HIGH)[0], S_LOW if low else S_HIGH, G_LOW if low else G_HIGH)
+    at, parts = 0, []
+    for array in range(7):
+        halo = halo_of[0 if array < 3 else 1 if array < 6 else 2]
+        parts.append((array * planes + (planes - halo if low else 0), at, halo))
+        at += halo
+    return parts
+
+
+def write_edge(target, whole, low):
+    for first, at, halo in edge_parts(whole.shape[0] // 7, low):
+        target[at:at + halo] = whole[first:first + halo]
+
+
+def is_odd():
+    return lax.rem(lax.axis_index("mesh"), 2) == 1
+
+
+def pack_kernel(start, source, region, whole, apart, marks, sems):
+    planes = region.shape[0]
+    copies = [pltpu.make_async_copy(region, marks, sems.at[0])]
+    for part in range(3):
+        for at, origin in ((part, start), (3 + part, source)):
+            target = whole.at[at * planes:(at + 1) * planes]
+            copies.append(pltpu.make_async_copy(origin.at[part], target, sems.at[at + 1]))
+    for copy in copies:
+        copy.start()
+    for copy in copies:
+        copy.wait()
+    whole[6 * planes:] = marks[...].astype(jnp.float32)
+    for odd in (False, True):
+        pl.when(is_odd() == odd)(functools.partial(write_edge, apart, whole, odd))
+
+
+def pair_kernel(*refs):
+    wholes, paired = refs[:-2], refs[-1]
+    for odd in (False, True):
+
+        @pl.when(is_odd() == odd)
+        def write():
+            for turn, whole in enumerate(wholes):
+                write_edge(paired.at[turn], whole, not odd)
+
+
+def hold_kernel(apart, paired, after, apart_out, paired_out):
+    pass
+
+
+def ripple_pack_kernel(start, source, apart, paired, sems):
+    planes = start.shape[3]
+    odd = is_odd()
+    copies = []
+    for at, (target, top) in enumerate(((apart, odd), (paired, jnp.logical_not(odd)))):
+        first = jnp.where(top, planes - 2, 0)
+        copies.append(
+            pltpu.make_async_copy(start.at[:, :, :, pl.ds(first, 2)], target.at[:, :, :, 0:2], sems.at[2 * at])
+        )
+        first = jnp.where(top, planes - 1, 0)
+        copies.append(
+            pltpu.make_async_copy(source.at[:, :, :, pl.ds(first, 1)], target.at[:, :, :, 2:3], sems.at[2 * at + 1])
+        )
+    for copy in copies:
+        copy.start()
+    for copy in copies:
+        copy.wait()
+
+
+def bias_kernel(shares, meshes, *refs):
+    wholes, aparts, paired = refs[:shares], refs[shares:2 * shares], refs[2 * shares]
+    table_index, bh_base, bh_slope, conductivity, field_out, nud_out, sigma_out = refs[2 * shares + 1:2 * shares + 8]
+    a0, a1, src, marks, nu, slopes, bases = refs[2 * shares + 8:]
     planes = wholes[0].shape[0] // 7
     rows_each, lanes = wholes[0].shape[1:]
-    rows = rows_each * (others + 1)
+    rows = rows_each * shares
     mine = lax.axis_index("harm")
     here = lax.axis_index("mesh")
-    for turn in range(others + 1):
-        owner = lax.rem(mine + others + 1 - turn, others + 1)
+    arrays = [(a0.at[part], A_LOW[0]) for part in range(3)]
+    arrays += [(src.at[part], S_LOW) for part in range(3)] + [(marks, G_LOW)]
+    for turn in range(shares):
+        owner = lax.rem(mine + shares - turn, shares)
         at = pl.ds(pl.multiple_of(owner * rows_each, rows_each), rows_each)
-        whole, low, high = wholes[turn], lows[turn], highs[turn]
-
-        def place(target, part, below, own, above, first_low, first_own, first_high):
-            for count, origin, first, onto in (
-                (below, low, first_low, 0), (own, whole, first_own, below), (above, high, first_high, below + own)
-            ):
-                target[part + (slice(onto, onto + count), at, slice(None))] = origin[first:first + count]
-
-        for part in range(3):
-            place(a0, (part,), A_LOW[0], planes, A_HIGH[0], part * A_LOW[0], part * planes, part * A_HIGH[0])
-            place(
-                src, (part,), S_LOW, planes, S_HIGH,
-                3 * A_LOW[0] + part * S_LOW, (3 + part) * planes, 3 * A_HIGH[0] + part * S_HIGH,
-            )
-        place(
-            marks, (), G_LOW, planes, G_HIGH, 3 * (A_LOW[0] + S_LOW), 6 * planes, 3 * (A_HIGH[0] + S_HIGH)
-        )
+
+        def fill(low, high):
+            for (target, onto), (unused, first, halo) in zip(arrays, edge_parts(planes, True)):
+                target[0:halo, at, :] = low[first:first + halo]
+            for (target, onto), (unused, first, halo) in zip(arrays, edge_parts(planes, False)):
+                target[onto + planes:onto + planes + halo, at, :] = high[first:first + halo]
+
+        for number, (target, onto) in enumerate(arrays):
+            target[onto:onto + planes, at, :] = wholes[turn][number * planes:(number + 1) * planes]
+        pl.when(is_odd())(functools.partial(fill, paired.at[turn], aparts[turn]))
+        pl.when(jnp.logical_not(is_odd()))(functools.partial(fill, aparts[turn], paired.at[turn]))
 
     edges = Edges((rows, lanes))
     tables = [table_index[member] for member in range(MATS)]
@@ -230,25 +282,36 @@
         field_out[part] = final[part, A_LOW[ITERS_B]:A_LOW[ITERS_B] + planes, own_rows, :]
 
 
-def ripple_kernel(
-    shares, meshes, harmonic_numbers, nud, sigma, start, source, low, high, ripple_out, loss_out, r0, r1, src, loss, sems
-):
+def ripple_kernel(shares, meshes, harmonic_numbers, nud, sigma, start, source, apart, paired, ripple_out, *refs):
+    losses, (r0, r1, r2, src, loss, r_sems, s_sems, out_sems) = refs[:shares], refs[shares:]
     count, planes = start.shape[0], start.shape[3]
     rows, lanes = start.shape[4:]
     mine = lax.axis_index("harm")
     here = lax.axis_index("mesh")
-    copies = [
-        pltpu.make_async_copy(low.at[:, :, :, 0:2], r0.at[:, :, :, 0:2], sems.at[0]),
-        pltpu.make_async_copy(low.at[:, :, :, 2:3], src.at[:, :, :, 0:1], sems.at[1]),
-        pltpu.make_async_copy(start, r0.at[:, :, :, 2:planes + 2], sems.at[2]),
-        pltpu.make_async_copy(source, src.at[:, :, :, 1:planes + 1], sems.at[3]),
-        pltpu.make_async_copy(high.at[:, :, :, 0:2], r0.at[:, :, :, planes + 2:planes + 4], sems.at[4]),
-        pltpu.make_async_copy(high.at[:, :, :, 2:3], src.at[:, :, :, planes + 1:planes + 2], sems.at[5]),
-    ]
-    for copy in copies:
-        copy.start()
-    for copy in copies:
-        copy.wait()
+    top = planes + 2
+
+    def fetch(origin, first, target, onto, sems):
+        return pltpu.make_async_copy(
+            origin.at[:, :, :, pl.ds(first, 1)], target.at[:, :, :, pl.ds(onto, 1)], sems.at[onto]
+        )
+
+    odd = is_odd()
+    for origin, above in ((apart, odd), (paired, jnp.logical_not(odd))):
+        onto = jnp.where(above, top, 0)
+        for plane in range(2):
+            fetch(origin, plane, r0, onto + plane, r_sems).start()
+        fetch(origin, 2, src, jnp.where(above, planes + 1, 0), s_sems).start()
+    for plane in range(planes):
+        fetch(start, plane, r0, plane + 2, r_sems).start()
+        fetch(source, plane, src, plane + 1, s_sems).start()
+    for plane in range(2):
+        fetch(start, 0, r0, plane, r_sems).wait()
+
+    def drain(plane):
+        return pltpu.make_async_copy(
+            r2.at[:, :, :, pl.ds(plane, 1)], ripple_out.at[:, :, :, pl.ds(plane, 1)], out_sems.at[plane]
+        )
+
     edges = Edges((rows, lanes))
     omegas = [omega_step * harmonic_numbers[mine * count + harmonic].astype(jnp.float32) for harmonic in range(count)]
 
@@ -275,6 +338,8 @@
 
     def first(at, carry):
         plane = at - 1
+        fetch(start, 0, r0, at + 2, r_sems).wait()
+        fetch(start, 0, src, at, s_sems).wait()
         low_ok = jnp.logical_or(plane >= 0, here > 0)
         high_ok = jnp.logical_or(plane < planes, here < meshes - 1)
         keep = jnp.where(jnp.logical_and(low_ok, high_ok), 1.0, 0.0)
@@ -291,95 +356,125 @@
 
     def second(plane, carry):
         def store(harmonic, part, real, imag):
-            ripple_out[harmonic, 0, part, plane] = real
-            ripple_out[harmonic, 1, part, plane] = imag
+            r2[harmonic, 0, part, plane] = real
+            r2[harmonic, 1, part, plane] = imag
 
         summed = 0.0
         for harmonic, conduct, power in sweep(r1, 1, plane, store):
             summed = summed + (0.5 * omegas[harmonic] * omegas[harmonic]) * conduct * power
         loss[plane] = summed
+        drain(plane).start()
         return carry
 
     lax.fori_loop(0, planes, second, 0)
     rows_each = rows // shares
     for turn in range(shares):
         owner = lax.rem(mine + turn, shares)
-        loss_out[turn] = loss[:, pl.ds(pl.multiple_of(owner * rows_each, rows_each), rows_each), :]
+        losses[turn][...] = loss[:, pl.ds(pl.multiple_of(owner * rows_each, rows_each), rows_each), :]
+    for plane in range(planes):
+        drain(plane).wait()
+
+
+def call(kernel, operands, in_specs, out_shapes, out_specs, scratch, name, work=0, aliases={}, room=0):
+    f32 = jnp.float32
+    shapes = [o.shape for o, spec in zip(operands, in_specs) if spec is VMEM]
+    shapes += [shape for shape, spec in zip(out_shapes, out_specs) if spec is VMEM]
+    shapes += [shape for shape in scratch if isinstance(shape, tuple)]
+    held = 4 * sum(math.prod(shape) for shape in shapes)
+    return pl.pallas_call(
+        kernel,
+        out_shape=[jax.ShapeDtypeStruct(shape, f32) for shape in out_shapes],
+        in_specs=in_specs,
+        out_specs=out_specs,
+        scratch_shapes=[pltpu.VMEM(shape, f32) if isinstance(shape, tuple) else shape for shape in scratch],
+        compiler_params=pltpu.CompilerParams(vmem_limit_bytes=room or held + 6 * 2**20),
+        cost_estimate=pl.CostEstimate(flops=work * 300, bytes_accessed=work, transcendentals=0),
+        input_output_aliases=aliases,
+        name=name,
+    )(*operands)
 
 
 def body(
     meshes, shares, bias_source, bias_start, region, table_index, bh_base, bh_slope, conductivity, harmonic_numbers,
     ripple_source, ripple_start,
 ):
-    f32 = jnp.float32
     unused, planes, rows_each, lanes = bias_start.shape
     rows = rows_each * shares
     count = ripple_start.shape[0]
-    upward = [(i, i + 1) for i in range(meshes - 1)]
-    downward = [(i + 1, i) for i in range(meshes - 1)]
+    near = [(i, i + 1) for i in range(0, meshes - 1, 2)]
+    far = [(i, i + 1) for i in range(1, meshes - 1, 2)]
+    near += [(j, i) for i, j in near]
+    far += [(j, i) for i, j in far]
     turned = [[(i, (i + turn) % shares) for i in range(shares)] for turn in range(1, shares)]
 
-    whole, forward, backward = pl.pallas_call(
-        pack_kernel,
-        out_shape=[jax.ShapeDtypeStruct((size, rows_each, lanes), f32) for size in (7 * planes, LOW_SIZE, HIGH_SIZE)],
-        in_specs=[VMEM] * 3,
-        out_specs=[VMEM] * 3,
-        name="pack",
-    )(bias_start, bias_source, region)
-    wholes = [whole] + [lax.ppermute(whole, "harm", pairs) for pairs in turned]
-    low = lax.ppermute(forward, "mesh", upward)
-    high = lax.ppermute(backward, "mesh", downward)
-    lows = [low] + [lax.ppermute(low, "harm", pairs) for pairs in turned]
-    highs = [high] + [lax.ppermute(high, "harm", pairs) for pairs in turned]
-
-    ripple_up = jnp.concatenate([ripple_start[:, :, :, planes - 2:], ripple_source[:, :, :, planes - 1:]], axis=3)
-    ripple_down = jnp.concatenate([ripple_start[:, :, :, :2], ripple_source[:, :, :, :1]], axis=3)
-    ripple_low = lax.ppermute(ripple_up, "mesh", upward)
-    ripple_high = lax.ppermute(ripple_down, "mesh", downward)
-
-    def scratch(*shape):
-        return pltpu.VMEM(shape, f32)
-
-    field, nud, sigma = pl.pallas_call(
-        functools.partial(bias_kernel, shares - 1, meshes),
-        out_shape=[
-            jax.ShapeDtypeStruct(bias_start.shape, f32),
-            jax.ShapeDtypeStruct((planes + NUD_LOW + NUD_HIGH, rows, lanes), f32),
-            jax.ShapeDtypeStruct((planes + 2 * (ITERS_R - 1), rows, lanes), f32),
+    def around(block):
+        return [block] + [lax.ppermute(block, "harm", pairs) for pairs in turned]
+
+    whole, apart = call(
+        pack_kernel, (bias_start, bias_source, region), [ANY] * 3,
+        [(7 * planes, rows_each, lanes), (HIGH_SIZE, rows_each, lanes)], [VMEM] * 2,
+        [pltpu.VMEM(region.shape, region.dtype), pltpu.SemaphoreType.DMA((7,))], "pack", room=PACK_ROOM,
+    )
+    wholes = around(whole)
+    aparts = around(lax.ppermute(apart, "mesh", far))
+    edge = ripple_start.shape[:3] + (3, rows, lanes)
+    ripple_apart, ripple_paired = call(
+        ripple_pack_kernel, (ripple_start, ripple_source), [ANY] * 2, [edge, edge], [VMEM] * 2,
+        [pltpu.SemaphoreType.DMA((4,))], "ripple_pack", RP_WORK, room=RP_ROOM,
+    )
+    paired, = call(
+        pair_kernel, (*wholes, ripple_apart), [VMEM] * shares + [ANY], [(shares, HIGH_SIZE, rows_each, lanes)], [VMEM], [], "pair"
+    )
+    paired = lax.ppermute(paired, "mesh", near)
+
+    ripple_apart, ripple_paired = call(
+        hold_kernel, (ripple_apart, ripple_paired, aparts[0]), [ANY] * 3, [edge, edge], [ANY] * 2, [], "hold",
+        HOLD_WORK, {0: 0, 1: 1},
+    )
+    ripple_apart = lax.ppermute(ripple_apart, "mesh", far)
+    ripple_paired = lax.ppermute(ripple_paired, "mesh", near)
+
+    known = (planes + G_LOW + G_HIGH, rows, lanes)
+    field, nud, sigma = call(
+        functools.partial(bias_kernel, shares, meshes),
+        (*wholes, *aparts, paired, table_index, bh_base, bh_slope, conductivity),
+        [VMEM] * (2 * shares + 1) + [SMEM] * 4,
+        [
+            bias_start.shape, (planes + NUD_LOW + NUD_HIGH, rows, lanes), (planes + 2 * (ITERS_R - 1), rows, lanes)
         ],
-        in_specs=[VMEM] * (3 * shares) + [SMEM] * 4,
-        out_specs=[VMEM] * 3,
-        scratch_shapes=[
-            scratch(3, planes + A_LOW[0] + A_HIGH[0], rows, lanes),
-            scratch(3, planes + A_LOW[1] + A_HIGH[1], rows, lanes),
-            scratch(3, planes + S_LOW + S_HIGH, rows, lanes),
-            scratch(planes + G_LOW + G_HIGH, rows, lanes),
-            scratch(planes + G_LOW + G_HIGH, rows, lanes),
-            scratch(KNOTS, planes + G_LOW + G_HIGH, rows, lanes),
-            scratch(planes + G_LOW + G_HIGH, rows, lanes),
+        [VMEM] * 3,
+        [
+            (3, planes + A_LOW[0] + A_HIGH[0], rows, lanes),
+            (3, planes + A_LOW[1] + A_HIGH[1], rows, lanes),
+            (3, planes + S_LOW + S_HIGH, rows, lanes),
+            known,
+            known,
+            (KNOTS, *known),
+            known,
         ],
-        compiler_params=pltpu.CompilerParams(vmem_limit_bytes=56 * 2**20),
-        name="bias",
-    )(*wholes, *lows, *highs, table_index, bh_base, bh_slope, conductivity)
-
-    ripple, losses = pl.pallas_call(
+        "bias",
+        BIAS_WORK,
+    )
+
+    ripple, *losses = call(
         functools.partial(ripple_kernel, shares, meshes),
-        out_shape=[
-            jax.ShapeDtypeStruct(ripple_start.shape, f32),
-            jax.ShapeDtypeStruct((shares, planes, rows_each, lanes), f32),
+        (harmonic_numbers, nud, sigma, ripple_start, ripple_source, ripple_apart, ripple_paired),
+        [SMEM, VMEM, VMEM] + [ANY] * 4,
+        [ripple_start.shape] + [(planes, rows_each, lanes)] * shares,
+        [ANY] + [VMEM] * shares,
+        [
+            (count, 2, 3, planes + 4, rows, lanes),
+            (count, 2, 3, planes + 2, rows, lanes),
+            (count, 2, 3, planes, rows, lanes),
+            (count, 2, 3, planes + 2, rows, lanes),
+            (planes, rows, lanes),
+            pltpu.SemaphoreType.DMA((planes + 4,)),
+            pltpu.SemaphoreType.DMA((planes + 2,)),
+            pltpu.SemaphoreType.DMA((planes,)),
         ],
-        in_specs=[SMEM, VMEM, VMEM] + [ANY] * 4,
-        out_specs=[VMEM] * 2,
-        scratch_shapes=[
-            scratch(count, 2, 3, planes + 4, rows, lanes),
-            scratch(count, 2, 3, planes + 2, rows, lanes),
-            scratch(count, 2, 3, planes + 2, rows, lanes),
-            scratch(planes, rows, lanes),
-            pltpu.SemaphoreType.DMA((6,)),
-        ],
-        compiler_params=pltpu.CompilerParams(vmem_limit_bytes=56 * 2**20),
-        name="ripple",
-    )(harmonic_numbers, nud, sigma, ripple_start, ripple_source, ripple_low, ripple_high)
+        "ripple",
+        room=RIPPLE_ROOM,
+    )
     loss = losses[0]
     for turn, pairs in enumerate(turned):
         loss = loss + lax.ppermute(losses[turn + 1], "harm", pairs)

time: 83.7 us -> 65.7 us (0.78)
  starting transfers between devices: 15.1 us -> 8.83 us
  waiting for transfers between devices: 30.5 us -> 25.1 us
  local copies, waits for them, and re-layouts: 6.52 us -> 1.36 us
  other arithmetic: 2.72 us -> 1.48 us
    ppermute x7 -> x6, starting transfers between devices: 13.6 us -> 7.47 us  [the longest x2 2.09 us: around(): return [block] + [lax.ppermute(block, 'harm', pairs) for pairs in turned]]
    ppermute x7 -> x6, waiting for transfers between devices: 27.8 us -> 21.9 us  [the longest x2 11 us: around(): return [block] + [lax.ppermute(block, 'harm', pairs) for pairs in turned]]
    slice x2 -> x0, local copies, waits for them, and re-layouts: 2.73 us -> none  [the longest x1 1.55 us: body(): ripple_start[:, :, :, :2]]
    unnamed x14, local copies, waits for them, and re-layouts: 2.94 us -> 1.36 us
    concatenate x2 -> x0, other arithmetic: 1.25 us -> none  [the longest x1 1.13 us: body(): jnp.concatenate([ripple_start[:, :, :, :2], ripple_source[:, :, :, :1]],...]
    squeeze x1 -> x0, local copies, waits for them, and re-layouts: 0.85 us -> none  [body(): loss = loss + lax.ppermute(losses[turn + 1], 'harm', pairs)]
    pallas_call x3 -> x6, Pallas kernels: 27.7 us -> 28 us  [call(): pl.pallas_call(kernel, out_shape=[jax.ShapeDtypeStruct(shape, f32) for sh...]
  transfers between devices with their start and end apart: 8 -> 7, of which waited for: 3 -> 5; matrix products, arithmetic and copies ran while one was open for 1% -> 0% of each run, Pallas kernels for 17% -> 22%
where the time goes in v2:
time: 65.7 us; the launch traced here: 65.4 us
  Pallas kernels  28 us (43%)
  waiting for transfers between devices  25.1 us (38%)
  starting transfers between devices  8.83 us (13%)
  other arithmetic  1.48 us (2%)
  local copies, waits for them, and re-layouts  1.36 us (2%)
  between operations  0.73 us (1%)
    pallas_call x6, Pallas kernels, call(): pl.pallas_call(kernel, out_shape=[jax.ShapeDtypeStruct(shape, f32) for sh...  28 us
    ppermute x2, waiting for transfers between devices, around(): return [block] + [lax.ppermute(block, 'harm', pairs) for pairs in turned]  11 us
    ppermute x1, waiting for transfers between devices, body(): ripple_apart = lax.ppermute(ripple_apart, 'mesh', far)  9.41 us
    ppermute x1, waiting for transfers between devices, body(): loss = loss + lax.ppermute(losses[turn + 1], 'harm', pairs)  3.19 us
    ppermute x2, starting transfers between devices, around(): return [block] + [lax.ppermute(block, 'harm', pairs) for pairs in turned]  2.09 us
    ppermute x1, starting transfers between devices, body(): ripple_apart = lax.ppermute(ripple_apart, 'mesh', far)  2.05 us
    ppermute x1, starting transfers between devices, body(): aparts = around(lax.ppermute(apart, 'mesh', far))  2.04 us
    ppermute x1, waiting for transfers between devices, body(): aparts = around(lax.ppermute(apart, 'mesh', far))  1.5 us
  transfers between devices with their start and end apart: 7, of which 5 were waited for; matrix products, arithmetic and copies ran while one was open for 0% of the time, Pallas kernels for 22%

profile of v2, /device:TPU:12, one launch (start us, length us, event | category | flops | bytes accessed | tf_op | source)
XLA Modules:
  0.0 65.4 jit_solution(2638666215972116195)
XLA Ops:
  0.6 2.0 %pack.1 = (f32[56,8,256]{2,1,0:T(8,128)}, f32[42,8,256]{2,1,0:T(8,128)}) custom-call(f32[3,8,8,256]{3,2,1,0:T(8,128)} %start.3, f32[3,8,8,256]{3,2,1,0:T(8,128)} %source.3, s32[8,8,256]{2,1,0:T(8,128)} %region.1), custom_call_target="tpu_custom_call" | custom-call | tf_op jit(solution)/shard_map/pack/pallas_call | solution.py:384
  2.6 1.6 %collective-permute-start = (f32[56,8,256]{2,1,0:T(8,128)}, f32[56,8,256]{2,1,0:T(8,128)S(1)}, u32[]{:S(2)}, u32[]{:S(2)}) collective-permute-start(f32[56,8,256]{2,1,0:T(8,128)} %get-tuple-element.15.refs_0_), channel_id=1, source_target_pairs={{0,1},{1,0},{2,3},{3,2},{4,5},{5,4},{6,7},{7,6},{8,9},{9,8},{10,11... | collective-permute-start | bytes 1376264 | tf_op jit(solution)/shard_map/ppermute | solution.py:411
  4.2 0.0 copy-start
  4.2 2.0 %collective-permute-start.1 = (f32[42,8,256]{2,1,0:T(8,128)}, f32[42,8,256]{2,1,0:T(8,128)S(1)}, u32[]{:S(2)}, u32[]{:S(2)}) collective-permute-start(f32[42,8,256]{2,1,0:T(8,128)} %get-tuple-element.16), channel_id=1, source_target_pairs={{2,4},{6,8},{10,12},{14,16},{18,20},{22,24},{26,28},{4,2},{8,6},{1... | collective-permute-start | bytes 1032200 | tf_op jit(solution)/shard_map/ppermute | solution.py:419
  6.3 3.1 %ripple_pack.1 = (f32[4,2,3,3,16,256]{5,4,3,2,1,0:T(8,128)}, f32[4,2,3,3,16,256]{5,4,3,2,1,0:T(8,128)}) custom-call(f32[4,2,3,8,16,256]{5,4,3,2,1,0:T(8,128)} %start.5, f32[4,2,3,8,16,256]{5,4,3,2,1,0:T(8,128)} %source.5), custom_call_target="tpu_custom_call" | custom-call | tf_op jit(solution)/shard_map/ripple_pack/pallas_call | solution.py:384
  9.3 5.8 %collective-permute-done.refs_1_ = f32[56,8,256]{2,1,0:T(8,128)S(1)} collective-permute-done((f32[56,8,256]{2,1,0:T(8,128)}, f32[56,8,256]{2,1,0:T(8,128)S(1)}, u32[]{:S(2)}, u32[]{:S(2)}) %collective-permute-start) | collective-permute-done | bytes 458784 | tf_op jit(solution)/shard_map/ppermute | solution.py:411
  15.2 0.0 copy-done
  15.2 0.1 collective-permute-start.3
  15.3 1.5 %collective-permute-done.1.refs_2_.after = f32[42,8,256]{2,1,0:T(8,128)S(1)} collective-permute-done((f32[42,8,256]{2,1,0:T(8,128)}, f32[42,8,256]{2,1,0:T(8,128)S(1)}, u32[]{:S(2)}, u32[]{:S(2)}) %collective-permute-start.1) | collective-permute-done | bytes 344096 | tf_op jit(solution)/shard_map/ppermute | solution.py:419
  16.8 0.5 collective-permute-start.2
  17.3 0.0 copy-start.3
  17.3 0.0 copy-start.4
  17.3 0.0 copy-start.5
  17.3 0.0 copy-start.6
  17.4 2.1 %collective-permute-start.4 = (f32[4,2,3,3,16,256]{5,4,3,2,1,0:T(8,128)}, f32[4,2,3,3,16,256]{5,4,3,2,1,0:T(8,128)}, u32[]{:S(2)}, u32[]{:S(2)}) collective-permute-start(f32[4,2,3,3,16,256]{5,4,3,2,1,0:T(8,128)} %get-tuple-element.22), channel_id=1, source_target_pairs={{2,4},{6,8},{10,12},{14,16},{18,20},{22,24},{26,28},{4,2},{8,6},{1... | collective-permute-start | bytes 3538952 | tf_op jit(solution)/shard_map/ppermute | solution.py:434
  19.4 1.2 %collective-permute-start.5 = (f32[4,2,3,3,16,256]{5,4,3,2,1,0:T(8,128)}, f32[4,2,3,3,16,256]{5,4,3,2,1,0:T(8,128)}, u32[]{:S(2)}, u32[]{:S(2)}) collective-permute-start(f32[4,2,3,3,16,256]{5,4,3,2,1,0:T(8,128)} %get-tuple-element.23), channel_id=1, source_target_pairs={{0,2},{4,6},{8,10},{12,14},{16,18},{20,22},{24,26},{28,30},{2,0},{... | collective-permute-start | bytes 3538952 | tf_op jit(solution)/shard_map/ppermute | solution.py:435
  20.6 5.1 %collective-permute-done.2.refs_3_ = f32[42,8,256]{2,1,0:T(8,128)S(1)} collective-permute-done((f32[42,8,256]{2,1,0:T(8,128)S(1)}, f32[42,8,256]{2,1,0:T(8,128)S(1)}, u32[]{:S(2)}, u32[]{:S(2)}) %collective-permute-start.2) | collective-permute-done | bytes 344096 | tf_op jit(solution)/shard_map/ppermute | solution.py:411
  25.8 0.0 collective-permute-done.3.refs_4_
  25.8 0.0 copy-done.3
  25.8 0.0 copy-done.4
  25.8 0.0 copy-done.5
  25.8 0.0 copy-done.6
  25.8 11.4 %bias.1 = (f32[3,8,8,256]{3,2,1,0:T(8,128)}, f32[12,16,256]{2,1,0:T(8,128)S(1)}, f32[10,16,256]{2,1,0:T(8,128)S(1)}) custom-call(f32[56,8,256]{2,1,0:T(8,128)S(1)} %copy-done, f32[56,8,256]{2,1,0:T(8,128)S(1)} %collective-permute-done.refs_1_, f32[42,8,256]{2,1,0:T(8,128)S(1)} %collective-permute-done.1.refs_2_.after, ...), custom_call_target="tpu_custom_call" | custom-call | flops 299999985664 | bytes 1000000000 | tf_op jit(solution)/shard_map/bias/pallas_call | solution.py:384
  37.2 0.0 copy-start.1
  37.2 0.7 %copy-done.1 = f32[12,16,256]{2,1,0:T(8,128)} copy-done((f32[12,16,256]{2,1,0:T(8,128)}, f32[12,16,256]{2,1,0:T(8,128)S(1)}, u32[]{:S(2)}) %copy-start.1) | copy-done | bytes 196632
  37.9 0.0 copy-start.2
  37.9 0.7 %copy-done.2 = f32[10,16,256]{2,1,0:T(8,128)} copy-done((f32[10,16,256]{2,1,0:T(8,128)}, f32[10,16,256]{2,1,0:T(8,128)S(1)}, u32[]{:S(2)}) %copy-start.2) | copy-done | bytes 163864
  38.6 9.4 %collective-permute-done.4.apart = f32[4,2,3,3,16,256]{5,4,3,2,1,0:T(8,128)} collective-permute-done((f32[4,2,3,3,16,256]{5,4,3,2,1,0:T(8,128)}, f32[4,2,3,3,16,256]{5,4,3,2,1,0:T(8,128)}, u32[]{:S(2)}, u32[]{:S(2)}) %collective-permute-start.4) | collective-permute-done | bytes 1179680 | tf_op jit(solution)/shard_map/ppermute | solution.py:434
  48.0 0.0 collective-permute-done.5.paired
  48.0 11.4 %ripple.1 = (f32[4,2,3,8,16,256]{5,4,3,2,1,0:T(8,128)}, f32[8,8,256]{2,1,0:T(8,128)}, f32[8,8,256]{2,1,0:T(8,128)}) custom-call(s32[8]{0:T(128)} %harmonic_numbers.1, f32[12,16,256]{2,1,0:T(8,128)} %copy-done.1, f32[10,16,256]{2,1,0:T(8,128)} %copy-done.2, f32[4,2,3,8,16,256]{5,4,3,2,1,0:T(8,128)} %start.5, f32[4,2,3,8,16,256]{5,4,3,2,1,0:T(8,128)} %source.5, ...), custom_call_target="tpu_custom_call" | custom-call | tf_op jit(solution)/shard_map/ripple/pallas_call | solution.py:384
  59.4 1.4 %collective-permute-start.6 = (f32[8,8,256]{2,1,0:T(8,128)}, f32[8,8,256]{2,1,0:T(8,128)S(1)}, u32[]{:S(2)}, u32[]{:S(2)}) collective-permute-start(f32[8,8,256]{2,1,0:T(8,128)} %get-tuple-element.26), channel_id=1, source_target_pairs={{0,1},{1,0},{2,3},{3,2},{4,5},{5,4},{6,7},{7,6},{8,9},{9,8},{10,11... | collective-permute-start | bytes 196616 | tf_op jit(solution)/shard_map/ppermute | solution.py:480
  60.8 3.2 %collective-permute-done.6 = f32[8,8,256]{2,1,0:T(8,128)S(1)} collective-permute-done((f32[8,8,256]{2,1,0:T(8,128)}, f32[8,8,256]{2,1,0:T(8,128)S(1)}, u32[]{:S(2)}, u32[]{:S(2)}) %collective-permute-start.6) | collective-permute-done | bytes 65568 | tf_op jit(solution)/shard_map/ppermute | solution.py:480
  63.9 1.5 %add.3 = f32[8,8,256]{2,1,0:T(8,128)} add(f32[8,8,256]{2,1,0:T(8,128)} %get-tuple-element.25, f32[8,8,256]{2,1,0:T(8,128)S(1)} %collective-permute-done.6) | non-fusion elementwise | flops 16384 | bytes 196608 | tf_op jit(solution)/shard_map/add | solution.py:480
  (2 shorter events, 0.0 us)
Async XLA Ops:
  2.6 12.5 %collective-permute-start = (f32[56,8,256]{2,1,0:T(8,128)}, f32[56,8,256]{2,1,0:T(8,128)S(1)}, u32[]{:S(2)}, u32[]{:S(2)}) collective-permute-start(f32[56,8,256]{2,1,0:T(8,128)} %get-tuple-element.15.refs_0_), channel_id=1, source_target_pairs={{0,1},{1,0},{2,3},{3,2},{4,5},{5,4},{6,7},{7,6},{8,9},{9,8},{10,11... | collective-permute-start | bytes 1376264 | tf_op jit(solution)/shard_map/ppermute | solution.py:411
  4.2 11.0 %copy-start = (f32[56,8,256]{2,1,0:T(8,128)S(1)}, f32[56,8,256]{2,1,0:T(8,128)}, u32[]{:S(2)}) copy-start(f32[56,8,256]{2,1,0:T(8,128)} %get-tuple-element.15.refs_0_) | copy-start | bytes 1376260
  4.2 12.6 %collective-permute-start.1 = (f32[42,8,256]{2,1,0:T(8,128)}, f32[42,8,256]{2,1,0:T(8,128)S(1)}, u32[]{:S(2)}, u32[]{:S(2)}) collective-permute-start(f32[42,8,256]{2,1,0:T(8,128)} %get-tuple-element.16), channel_id=1, source_target_pairs={{2,4},{6,8},{10,12},{14,16},{18,20},{22,24},{26,28},{4,2},{8,6},{1... | collective-permute-start | bytes 1032200 | tf_op jit(solution)/shard_map/ppermute | solution.py:419
  15.2 10.5 %collective-permute-start.3 = (f32[2,42,8,256]{3,2,1,0:T(8,128)S(1)}, f32[2,42,8,256]{3,2,1,0:T(8,128)S(1)}, u32[]{:S(2)}, u32[]{:S(2)}) collective-permute-start(f32[2,42,8,256]{3,2,1,0:T(8,128)S(1)} %pair.1), channel_id=1, source_target_pairs={{0,2},{4,6},{8,10},{12,14},{16,18},{20,22},{24,26},{28,30},{2,0},{... | collective-permute-start | bytes 2064392 | tf_op jit(solution)/shard_map/ppermute | solution.py:428
  16.8 9.0 %collective-permute-start.2 = (f32[42,8,256]{2,1,0:T(8,128)S(1)}, f32[42,8,256]{2,1,0:T(8,128)S(1)}, u32[]{:S(2)}, u32[]{:S(2)}) collective-permute-start(f32[42,8,256]{2,1,0:T(8,128)S(1)} %collective-permute-done.1.refs_2_.after), channel_id=1, source_target_pairs={{0,1},{1,0},{2,3},{3,2},{4,5},{5,4},{6,7},{7,6},{8,9},{9,8},{10,11... | collective-permute-start | bytes 1032200 | tf_op jit(solution)/shard_map/ppermute | solution.py:411
  17.3 8.4 %copy-start.3 = (f32[4,8]{1,0:T(4,128)S(1)}, f32[4,8]{1,0:T(4,128)}, u32[]{:S(2)}) copy-start(f32[4,8]{1,0:T(4,128)} %refs_7_.1) | copy-start | bytes 388
  17.3 8.4 %copy-start.4 = (s32[4]{0:T(128)S(1)}, s32[4]{0:T(128)}, u32[]{:S(2)}) copy-start(s32[4]{0:T(128)} %refs_5_.1) | copy-start | bytes 52
  17.3 8.4 %copy-start.5 = (f32[4]{0:T(128)S(1)}, f32[4]{0:T(128)}, u32[]{:S(2)}) copy-start(f32[4]{0:T(128)} %refs_6_.1) | copy-start | bytes 52
  17.3 8.4 %copy-start.6 = (f32[4]{0:T(128)S(1)}, f32[4]{0:T(128)}, u32[]{:S(2)}) copy-start(f32[4]{0:T(128)} %refs_8_.1) | copy-start | bytes 52
  17.4 30.6 %collective-permute-start.4 = (f32[4,2,3,3,16,256]{5,4,3,2,1,0:T(8,128)}, f32[4,2,3,3,16,256]{5,4,3,2,1,0:T(8,128)}, u32[]{:S(2)}, u32[]{:S(2)}) collective-permute-start(f32[4,2,3,3,16,256]{5,4,3,2,1,0:T(8,128)} %get-tuple-element.22), channel_id=1, source_target_pairs={{2,4},{6,8},{10,12},{14,16},{18,20},{22,24},{26,28},{4,2},{8,6},{1... | collective-permute-start | bytes 3538952 | tf_op jit(solution)/shard_map/ppermute | solution.py:434
  19.4 28.6 %collective-permute-start.5 = (f32[4,2,3,3,16,256]{5,4,3,2,1,0:T(8,128)}, f32[4,2,3,3,16,256]{5,4,3,2,1,0:T(8,128)}, u32[]{:S(2)}, u32[]{:S(2)}) collective-permute-start(f32[4,2,3,3,16,256]{5,4,3,2,1,0:T(8,128)} %get-tuple-element.23), channel_id=1, source_target_pairs={{0,2},{4,6},{8,10},{12,14},{16,18},{20,22},{24,26},{28,30},{2,0},{... | collective-permute-start | bytes 3538952 | tf_op jit(solution)/shard_map/ppermute | solution.py:435
  37.2 0.7 %copy-start.1 = (f32[12,16,256]{2,1,0:T(8,128)}, f32[12,16,256]{2,1,0:T(8,128)S(1)}, u32[]{:S(2)}) copy-start(f32[12,16,256]{2,1,0:T(8,128)S(1)} %get-tuple-element.19.nud) | copy-start | bytes 589828
  37.9 0.7 %copy-start.2 = (f32[10,16,256]{2,1,0:T(8,128)}, f32[10,16,256]{2,1,0:T(8,128)S(1)}, u32[]{:S(2)}) copy-start(f32[10,16,256]{2,1,0:T(8,128)S(1)} %get-tuple-element.20.sigma) | copy-start | bytes 491524
  59.4 4.5 %collective-permute-start.6 = (f32[8,8,256]{2,1,0:T(8,128)}, f32[8,8,256]{2,1,0:T(8,128)S(1)}, u32[]{:S(2)}, u32[]{:S(2)}) collective-permute-start(f32[8,8,256]{2,1,0:T(8,128)} %get-tuple-element.26), channel_id=1, source_target_pairs={{0,1},{1,0},{2,3},{3,2},{4,5},{5,4},{6,7},{7,6},{8,9},{9,8},{10,11... | collective-permute-start | bytes 196616 | tf_op jit(solution)/shard_map/ppermute | solution.py:480

commit v3 on v2

--- a/solution.py
+++ b/solution.py
@@ -17,6 +17,7 @@
 knot_step = 1.5
 soft_width = 0.5
 omega_step = 0.25
+CAP = 80.0
 
 NUD_LOW, NUD_HIGH = ITERS_R, ITERS_R
 A_LOW = [NUD_LOW + ITERS_B - step for step in range(ITERS_B + 1)]
@@ -35,78 +36,124 @@
 ANY = pl.BlockSpec(memory_space=pl.ANY)
 
 
-def up(value, axis):
-    return pltpu.roll(value, value.shape[axis] - 1, axis)
-
-
-def down(value, axis):
-    return pltpu.roll(value, 1, axis)
-
-
-def index(shape, axis):
-    return lax.broadcasted_iota(jnp.int32, shape, axis)
-
-
-class Edges:
-    def __init__(self, shape):
-        rows, lanes = index(shape, 0), index(shape, 1)
-        self.last_row, self.first_row = rows == shape[0] - 1, rows == 0
-        self.last_lane, self.first_lane = lanes == shape[1] - 1, lanes == 0
-
-    def sides(self):
-        return ((up, 0, self.last_row), (down, 0, self.first_row), (up, 1, self.last_lane), (down, 1, self.first_lane))
-
-
-def couplings(center, above, below, edges):
-    weights = [0.5 * (center + above), 0.5 * (center + below)]
-    total = weights[0] + weights[1]
-    for move, axis, edge in edges.sides():
-        weight = 0.5 * (center + jnp.where(edge, 0.0, move(center, axis)))
-        total = total + weight
-        weights.append(jnp.where(edge, 0.0, weight))
-    return weights, total + kappa
-
-
-def pull(weights, center, above, below):
-    return (
-        weights[0] * above
-        + weights[1] * below
-        + weights[2] * up(center, 0)
-        + weights[3] * down(center, 0)
-        + weights[4] * up(center, 1)
-        + weights[5] * down(center, 1)
-    )
-
-
-def flux_squared(field, plane, edges):
-    ax, ay, az = (field[part, plane] for part in range(3))
-    ay_first, az_first = field[1, plane + 1], field[2, plane + 1]
-    second = [jnp.where(edges.last_row, 0.0, up(value, 0)) for value in (ax, az)]
-    third = [jnp.where(edges.last_lane, 0.0, up(value, 1)) for value in (ax, ay)]
-    flux_one = (second[1] - az) - (third[1] - ay)
-    flux_two = (third[0] - ax) - (az_first - az)
-    flux_three = (ay_first - ay) - (second[0] - ax)
-    return flux_one * flux_one + flux_two * flux_two + flux_three * flux_three
-
-
-def reluctivity(flux_sq, base, slope_of, incremental):
-    doubled = flux_sq / soft_width
-    rising, falling = jnp.exp(doubled), jnp.exp(-doubled)
-    value, slope_sum = 0.0, 0.0
+TILE = (8, 128)
+
+
+class Tiles:
+    def __init__(self, rows, lanes):
+        self.grid = (rows // TILE[0], lanes // TILE[1])
+        self.spots = [(i, j) for i in range(self.grid[0]) for j in range(self.grid[1])]
+        self.at_end, self.at_start = [], []
+        for axis in range(2):
+            place = lax.broadcasted_iota(jnp.int32, TILE, axis)
+            self.at_end.append(place == TILE[axis] - 1)
+            self.at_start.append(place == 0)
+
+    def where(self, spot):
+        return (slice(spot[0] * TILE[0], (spot[0] + 1) * TILE[0]), slice(spot[1] * TILE[1], (spot[1] + 1) * TILE[1]))
+
+    def load(self, ref, *lead):
+        return {spot: ref[lead + self.where(spot)] for spot in self.spots}
+
+    def store(self, ref, lead, values):
+        for spot in self.spots:
+            ref[lead + self.where(spot)] = values[spot]
+
+    def each(self, function, *values):
+        return {spot: function(*(value[spot] for value in values)) for spot in self.spots}
+
+    def side(self, step, axis):
+        return (self.at_end if step > 0 else self.at_start)[axis]
+
+    def is_edge(self, spot, step, axis):
+        return spot[axis] == (self.grid[axis] - 1 if step > 0 else 0)
+
+    def move(self, values, step, axis, fill):
+        rolled = self.each(lambda tile: pltpu.roll(tile, TILE[axis] - 1 if step > 0 else 1, axis), values)
+        side, moved = self.side(step, axis), {}
+        for spot in self.spots:
+            if self.is_edge(spot, step, axis):
+                moved[spot] = jnp.where(side, 0.0, rolled[spot]) if fill else rolled[spot]
+            else:
+                other = (spot[0] + step, spot[1]) if axis == 0 else (spot[0], spot[1] + step)
+                moved[spot] = jnp.where(side, rolled[other], rolled[spot])
+        return moved
+
+    def inner(self, values, step, axis):
+        side = self.side(step, axis)
+        return {
+            spot: jnp.where(side, 0.0, values[spot]) if self.is_edge(spot, step, axis) else values[spot]
+            for spot in self.spots
+        }
+
+
+SIDES = ((1, 0), (-1, 0), (1, 1), (-1, 1))
+
+
+def double_couplings(tiles, center, above, below):
+    add = lambda one, other: one + other
+    weights = [tiles.each(add, center, above), tiles.each(add, center, below)]
+    total = tiles.each(add, *weights)
+    for step, axis in SIDES:
+        weight = tiles.each(add, center, tiles.move(center, step, axis, True))
+        total = tiles.each(add, total, weight)
+        weights.append(tiles.inner(weight, step, axis))
+    return weights, tiles.each(lambda value: value + 2.0 * kappa, total)
+
+
+def pull(tiles, start, weights, center, above, below):
+    moved = [above, below] + [tiles.move(center, step, axis, False) for step, axis in SIDES]
+    total = start
+    for weight, other in zip(weights, moved):
+        total = tiles.each(lambda so_far, w, value: so_far + w * value, total, weight, other)
+    return total
+
+
+def flux_squared(tiles, field, plane):
+    ax, ay, az = (tiles.load(field, part, plane) for part in range(3))
+    ay_first, az_first = tiles.load(field, 1, plane + 1), tiles.load(field, 2, plane + 1)
+    ax_second, az_second = tiles.move(ax, 1, 0, True), tiles.move(az, 1, 0, True)
+    ax_third, ay_third = tiles.move(ax, 1, 1, True), tiles.move(ay, 1, 1, True)
+
+    def square(x, y, z, y1, z1, x2, z2, x3, y3):
+        flux_one = (z2 - z) - (y3 - y)
+        flux_two = (x3 - x) - (z1 - z)
+        flux_three = (y1 - y) - (x2 - x)
+        return flux_one * flux_one + flux_two * flux_two + flux_three * flux_three
+
+    return tiles.each(square, ax, ay, az, ay_first, az_first, ax_second, az_second, ax_third, ay_third)
+
+
+def reluctivity(tiles, flux_sq, base, slope_of, slope_total, incremental):
+    doubled = tiles.each(lambda value: value * (1.0 / soft_width), flux_sq)
+    excess = tiles.each(lambda value: jnp.maximum(value - CAP, 0.0), doubled)
+    floor = tiles.each(lambda value: jnp.exp(-value), excess)
+    rising = tiles.each(lambda value: jnp.exp(jnp.minimum(value, CAP)), doubled)
+    nu = tiles.each(lambda start, slope, value: start + slope * value, base, slope_total, excess)
+    slope_sum = None
     for knot in range(KNOTS):
+        factor = math.exp(-knot_step * knot / soft_width)
         slope = slope_of(knot)
-        offset = knot_step * knot / soft_width
-        shift = math.exp(offset)
-        small = jnp.minimum(rising * (1.0 / shift), falling * shift)
-        grown = 1.0 + small
-        value = value + slope * (jnp.maximum(doubled - offset, 0.0) + jnp.log(grown))
+        high = tiles.each(lambda value: value * factor, rising)
+        both = tiles.each(lambda one, other: one + other, high, floor)
+        nu = tiles.each(lambda so_far, weight, value: so_far + weight * jnp.log(value), nu, slope, both)
         if incremental:
-            part = 1.0 / grown
-            slope_sum = slope_sum + slope * jnp.where(doubled >= offset, part, small * part)
-    nu = base + soft_width * value
+            part = tiles.each(lambda weight, one, other: weight * (one / other), slope, high, both)
+            slope_sum = tiles.each(lambda one, other: one + other, slope_sum, part) if knot else part
     if incremental:
-        nu = nu + 2.0 * flux_sq * slope_sum
+        nu = tiles.each(lambda value, s, slope: value + (2.0 / soft_width) * (s * slope), nu, flux_sq, slope_sum)
     return nu
+
+
+def loop_in_pairs(count, body):
+    def step(at, carry):
+        body(2 * at)
+        body(2 * at + 1)
+        return carry
+
+    lax.fori_loop(0, count // 2, step, 0)
+    if count % 2:
+        body(count - 1)
 
 
 LOW_SIZE = 3 * (A_LOW[0] + S_LOW) + G_LOW
@@ -207,10 +254,10 @@
         pl.when(is_odd())(functools.partial(fill, paired.at[turn], aparts[turn]))
         pl.when(jnp.logical_not(is_odd()))(functools.partial(fill, aparts[turn], paired.at[turn]))
 
-    edges = Edges((rows, lanes))
+    tiles = Tiles(rows, lanes)
     tables = [table_index[member] for member in range(MATS)]
     base_of = [bh_base[table] for table in tables]
-    slope_of = [[bh_slope[table, knot] for table in tables] for knot in range(KNOTS)]
+    slope_of = [[soft_width * bh_slope[table, knot] for table in tables] for knot in range(KNOTS)]
     sigma_of = [conductivity[member] for member in range(MATS)]
 
     def inside(plane):
@@ -218,36 +265,51 @@
         high_ok = jnp.logical_or(plane < planes, here < meshes - 1)
         return jnp.where(jnp.logical_and(low_ok, high_ok), 1.0, 0.0)
 
-    def choose(mark, values):
-        chosen = jnp.where(mark == 1.0, values[1], values[0])
-        for member in range(2, MATS):
-            chosen = jnp.where(mark == float(member), values[member], chosen)
-        return chosen
+    def choose(marks_are, values):
+        def one(*marked):
+            chosen = jnp.where(marked[0], values[1], values[0])
+            for member in range(2, MATS):
+                chosen = jnp.where(marked[member - 1], values[member], chosen)
+            return chosen
+
+        return tiles.each(one, *marks_are)
+
+    def members(mark):
+        return [tiles.each(lambda value: value == float(member), mark) for member in range(1, MATS)]
 
     def relax_into(target, step, old):
-        def body(at, carry):
+        def body(at):
             plane = at - A_LOW[step]
-            near = plane + A_LOW[step] + 1
-            weights, total = couplings(nu[near], nu[near + 1], nu[near - 1], edges)
-            scale = inside(plane) / total
+            near = at + 1
+            weights, total = double_couplings(
+                tiles, tiles.load(nu, near), tiles.load(nu, near + 1), tiles.load(nu, near - 1)
+            )
+            keep = inside(plane)
+            scale = tiles.each(lambda value: keep / value, total)
             from_old = plane + A_LOW[step - 1]
             for part in range(3):
-                moved = pull(weights, old[part, from_old], old[part, from_old + 1], old[part, from_old - 1])
-                target[part, at] = (src[part, plane + S_LOW] + moved) * scale
-            return carry
-
-        lax.fori_loop(0, planes + A_LOW[step] + A_HIGH[step], body, 0)
-
-    def first_nu(at, carry):
-        mark = marks[at]
-        bases[at] = choose(mark, base_of)
+                twice = tiles.each(lambda value: value + value, tiles.load(src, part, plane + S_LOW))
+                near_old = [tiles.load(old, part, from_old + move) for move in (0, 1, -1)]
+                moved = pull(tiles, twice, weights, *near_old)
+                tiles.store(target, (part, at), tiles.each(lambda value, by: value * by, moved, scale))
+
+        loop_in_pairs(planes + A_LOW[step] + A_HIGH[step], body)
+
+    def first_nu(at):
+        marked = members(tiles.load(marks, at))
+        base, slope = choose(marked, base_of), [choose(marked, slope_of[knot]) for knot in range(KNOTS)]
+        whole_slope = slope[0]
+        tiles.store(bases, (at,), base)
         for knot in range(KNOTS):
-            slopes[knot, at] = choose(mark, slope_of[knot])
-        value = reluctivity(flux_squared(a0, at, edges), bases[at], lambda knot: slopes[knot, at], False)
-        nu[at] = value * inside(at - G_LOW)
-        return carry
-
-    lax.fori_loop(0, planes + G_LOW + G_HIGH, first_nu, 0)
+            tiles.store(slopes, (knot, at), slope[knot])
+            if knot:
+                whole_slope = tiles.each(lambda one, other: one + other, whole_slope, slope[knot])
+        tiles.store(slopes, (KNOTS, at), whole_slope)
+        value = reluctivity(tiles, flux_squared(tiles, a0, at), base, lambda knot: slope[knot], whole_slope, False)
+        keep = inside(at - G_LOW)
+        tiles.store(nu, (at,), tiles.each(lambda one: one * keep, value))
+
+    loop_in_pairs(planes + G_LOW + G_HIGH, first_nu)
     fields = (a0, a1)
     for step in range(1, ITERS_B + 1):
         old, new = fields[(step - 1) % 2], fields[step % 2]
@@ -256,26 +318,23 @@
         lower = NUD_LOW if last else A_LOW[step + 1] + 1
         upper = NUD_HIGH if last else A_HIGH[step + 1] + 1
 
-        def next_nu(at, carry):
+        def next_nu(at):
             plane = at - lower
             known = plane + G_LOW
             value = reluctivity(
-                flux_squared(new, plane + A_LOW[step], edges), bases[known], lambda knot: slopes[knot, known], last
+                tiles, flux_squared(tiles, new, plane + A_LOW[step]), tiles.load(bases, known),
+                lambda knot: tiles.load(slopes, knot, known), tiles.load(slopes, KNOTS, known), last,
             )
-            value = value * inside(plane)
-            if last:
-                nud_out[at] = value
-            else:
-                nu[at] = value
-            return carry
-
-        lax.fori_loop(0, planes + lower + upper, next_nu, 0)
-
-    def sigma_at(at, carry):
-        sigma_out[at] = choose(marks[at - (ITERS_R - 1) + G_LOW], sigma_of)
-        return carry
-
-    lax.fori_loop(0, planes + 2 * (ITERS_R - 1), sigma_at, 0)
+            keep = inside(plane)
+            tiles.store(nud_out if last else nu, (at,), tiles.each(lambda one: one * keep, value))
+
+        loop_in_pairs(planes + lower + upper, next_nu)
+
+    def sigma_at(at):
+        marked = members(tiles.load(marks, at - (ITERS_R - 1) + G_LOW))
+        tiles.store(sigma_out, (at,), choose(marked, sigma_of))
+
+    loop_in_pairs(planes + 2 * (ITERS_R - 1), sigma_at)
     own_rows = pl.ds(pl.multiple_of(mine * rows_each, rows_each), rows_each)
     final = fields[ITERS_B % 2]
     for part in range(3):
@@ -283,7 +342,7 @@
 
 
 def ripple_kernel(shares, meshes, harmonic_numbers, nud, sigma, start, source, apart, paired, ripple_out, *refs):
-    losses, (r0, r1, r2, src, loss, r_sems, s_sems, out_sems) = refs[:shares], refs[shares:]
+    losses, (r0, r1, r2, src, loss, faces, sides, answer, r_sems, s_sems, out_sems) = refs[:shares], refs[shares:]
     count, planes = start.shape[0], start.shape[3]
     rows, lanes = start.shape[4:]
     mine = lax.axis_index("harm")
@@ -304,51 +363,70 @@
     for plane in range(planes):
         fetch(start, plane, r0, plane + 2, r_sems).start()
         fetch(source, plane, src, plane + 1, s_sems).start()
-    for plane in range(2):
-        fetch(start, 0, r0, plane, r_sems).wait()
-
     def drain(plane):
         return pltpu.make_async_copy(
             r2.at[:, :, :, pl.ds(plane, 1)], ripple_out.at[:, :, :, pl.ds(plane, 1)], out_sems.at[plane]
         )
 
-    edges = Edges((rows, lanes))
+    tiles = Tiles(rows, lanes)
     omegas = [omega_step * harmonic_numbers[mine * count + harmonic].astype(jnp.float32) for harmonic in range(count)]
 
-    def sweep(old, offset, plane, store):
+    def prepare(at):
+        plane = at - 1
         near = plane + NUD_LOW
-        weights, total = couplings(nud[near], nud[near + 1], nud[near - 1], edges)
-        conduct = sigma[plane + 1]
-        for harmonic in range(count):
-            damp = omegas[harmonic] * conduct
-            inverse = 1.0 / (total * total + damp * damp)
-            straight, turned = total * inverse, damp * inverse
-            power = 0.0
-            for part in range(3):
-                sides = []
-                for piece in range(2):
-                    field = old.at[harmonic, piece, part]
-                    moved = pull(weights, field[plane + offset], field[plane + offset + 1], field[plane + offset - 1])
-                    sides.append(src[harmonic, piece, part, plane + 1] + moved)
-                real = sides[0] * straight + sides[1] * turned
-                imag = sides[1] * straight - sides[0] * turned
-                power = power + (real * real + imag * imag)
-                store(harmonic, part, real, imag)
-            yield harmonic, conduct, power
-
-    def first(at, carry):
-        plane = at - 1
-        fetch(start, 0, r0, at + 2, r_sems).wait()
-        fetch(start, 0, src, at, s_sems).wait()
+        weights, total = double_couplings(
+            tiles, tiles.load(nud, near), tiles.load(nud, near + 1), tiles.load(nud, near - 1)
+        )
+        half = [tiles.each(lambda value: 0.5 * value, weight) for weight in weights]
+        tiles.store(faces, (at + 1,), half[0])
+        tiles.store(faces, (at,), half[1])
+        for number in range(4):
+            tiles.store(sides, (number, at), half[2 + number])
         low_ok = jnp.logical_or(plane >= 0, here > 0)
         high_ok = jnp.logical_or(plane < planes, here < meshes - 1)
         keep = jnp.where(jnp.logical_and(low_ok, high_ok), 1.0, 0.0)
+        total = tiles.each(lambda value: 0.5 * value, total)
+        square = tiles.each(lambda value: value * value, total)
+        conduct = tiles.load(sigma, at)
+        for harmonic in range(count):
+            damp = tiles.each(lambda value: omegas[harmonic] * value, conduct)
+            inverse = tiles.each(lambda one, other: keep / (one + other * other), square, damp)
+            tiles.store(answer, (harmonic, 0, at), tiles.each(lambda one, other: one * other, total, inverse))
+            tiles.store(answer, (harmonic, 1, at), tiles.each(lambda one, other: one * other, damp, inverse))
+
+    loop_in_pairs(planes + 2, prepare)
+
+    def sweep(old, offset, plane, store):
+        at = plane + 1
+        weights = [tiles.load(faces, at + 1), tiles.load(faces, at)]
+        weights += [tiles.load(sides, number, at) for number in range(4)]
+        for harmonic in range(count):
+            straight, turned = tiles.load(answer, harmonic, 0, at), tiles.load(answer, harmonic, 1, at)
+            power = None
+            for part in range(3):
+                both = []
+                for piece in range(2):
+                    near_old = [tiles.load(old, harmonic, piece, part, plane + offset + move) for move in (0, 1, -1)]
+                    both.append(pull(tiles, tiles.load(src, harmonic, piece, part, at), weights, *near_old))
+                real = tiles.each(lambda re, im, a, b: re * a + im * b, *both, straight, turned)
+                imag = tiles.each(lambda re, im, a, b: im * a - re * b, *both, straight, turned)
+                store(harmonic, part, real, imag)
+                squared = tiles.each(lambda re, im: re * re + im * im, real, imag)
+                power = tiles.each(lambda one, other: one + other, power, squared) if part else squared
+            yield harmonic, power
+
+    for plane in range(2):
+        fetch(start, 0, r0, plane, r_sems).wait()
+
+    def first(at, carry):
+        fetch(start, 0, r0, at + 2, r_sems).wait()
+        fetch(start, 0, src, at, s_sems).wait()
 
         def store(harmonic, part, real, imag):
-            r1[harmonic, 0, part, at] = real * keep
-            r1[harmonic, 1, part, at] = imag * keep
-
-        for unused in sweep(r0, 2, plane, store):
+            tiles.store(r1, (harmonic, 0, part, at), real)
+            tiles.store(r1, (harmonic, 1, part, at), imag)
+
+        for unused in sweep(r0, 2, at - 1, store):
             pass
         return carry
 
@@ -356,13 +434,16 @@
 
     def second(plane, carry):
         def store(harmonic, part, real, imag):
-            r2[harmonic, 0, part, plane] = real
-            r2[harmonic, 1, part, plane] = imag
-
-        summed = 0.0
-        for harmonic, conduct, power in sweep(r1, 1, plane, store):
-            summed = summed + (0.5 * omegas[harmonic] * omegas[harmonic]) * conduct * power
-        loss[plane] = summed
+            tiles.store(r2, (harmonic, 0, part, plane), real)
+            tiles.store(r2, (harmonic, 1, part, plane), imag)
+
+        summed = None
+        for harmonic, power in sweep(r1, 1, plane, store):
+            factor = 0.5 * omegas[harmonic] * omegas[harmonic]
+            scaled = tiles.each(lambda value: factor * value, power)
+            summed = tiles.each(lambda one, other: one + other, summed, scaled) if harmonic else scaled
+        conduct = tiles.load(sigma, plane + 1)
+        tiles.store(loss, (plane,), tiles.each(lambda one, other: one * other, conduct, summed))
         drain(plane).start()
         return carry
 
@@ -449,7 +530,7 @@
             (3, planes + S_LOW + S_HIGH, rows, lanes),
             known,
             known,
-            (KNOTS, *known),
+            (KNOTS + 1, *known),
             known,
         ],
         "bias",
@@ -468,6 +549,9 @@
             (count, 2, 3, planes, rows, lanes),
             (count, 2, 3, planes + 2, rows, lanes),
             (planes, rows, lanes),
+            (planes + 3, rows, lanes),
+            (4, planes + 2, rows, lanes),
+            (count, 2, planes + 2, rows, lanes),
             pltpu.SemaphoreType.DMA((planes + 4,)),
             pltpu.SemaphoreType.DMA((planes + 2,)),
             pltpu.SemaphoreType.DMA((planes,)),

time: 65.7 us -> 64 us (0.974)
  Pallas kernels: 28 us -> 22.2 us
  waiting for transfers between devices: 25.1 us -> 29.1 us
    pallas_call x6, Pallas kernels: 28 us -> 22.2 us  [call(): pl.pallas_call(kernel, out_shape=[jax.ShapeDtypeStruct(shape, f32) for sh...]
    ppermute x1, waiting for transfers between devices: 9.41 us -> 13.4 us  [body(): ripple_apart = lax.ppermute(ripple_apart, 'mesh', far)]
  transfers between devices with their start and end apart: 7 -> 7, of which waited for: 5 -> 5; matrix products, arithmetic and copies ran while one was open for 0% -> 0% of each run, Pallas kernels for 22% -> 17%
where the time goes in v3:
time: 64 us; the launch traced here: 63.7 us
  waiting for transfers between devices  29.1 us (45%)
  Pallas kernels  22.2 us (35%)
  starting transfers between devices  8.83 us (14%)
  other arithmetic  1.48 us (2%)
  local copies, waits for them, and re-layouts  1.36 us (2%)
  between operations  0.73 us (1%)
    pallas_call x6, Pallas kernels, call(): pl.pallas_call(kernel, out_shape=[jax.ShapeDtypeStruct(shape, f32) for sh...  22.2 us
    ppermute x1, waiting for transfers between devices, body(): ripple_apart = lax.ppermute(ripple_apart, 'mesh', far)  13.4 us
    ppermute x2, waiting for transfers between devices, around(): return [block] + [lax.ppermute(block, 'harm', pairs) for pairs in turned]  11 us
    ppermute x1, waiting for transfers between devices, body(): loss = loss + lax.ppermute(losses[turn + 1], 'harm', pairs)  3.19 us
    ppermute x2, starting transfers between devices, around(): return [block] + [lax.ppermute(block, 'harm', pairs) for pairs in turned]  2.09 us
    ppermute x1, starting transfers between devices, body(): ripple_apart = lax.ppermute(ripple_apart, 'mesh', far)  2.05 us
    ppermute x1, starting transfers between devices, body(): aparts = around(lax.ppermute(apart, 'mesh', far))  2.04 us
    ppermute x1, waiting for transfers between devices, body(): aparts = around(lax.ppermute(apart, 'mesh', far))  1.5 us
  transfers between devices with their start and end apart: 7, of which 5 were waited for; matrix products, arithmetic and copies ran while one was open for 0% of the time, Pallas kernels for 17%

profile of v3, /device:TPU:12, one launch (start us, length us, event | category | flops | bytes accessed | tf_op | source)
XLA Modules:
  0.0 63.7 jit_solution(8158487082423485006)
XLA Ops:
  0.6 2.0 %pack.1 = (f32[56,8,256]{2,1,0:T(8,128)}, f32[42,8,256]{2,1,0:T(8,128)}) custom-call(f32[3,8,8,256]{3,2,1,0:T(8,128)} %start.3, f32[3,8,8,256]{3,2,1,0:T(8,128)} %source.3, s32[8,8,256]{2,1,0:T(8,128)} %region.1), custom_call_target="tpu_custom_call" | custom-call | tf_op jit(solution)/shard_map/pack/pallas_call | solution.py:465
  2.6 1.6 %collective-permute-start = (f32[56,8,256]{2,1,0:T(8,128)}, f32[56,8,256]{2,1,0:T(8,128)S(1)}, u32[]{:S(2)}, u32[]{:S(2)}) collective-permute-start(f32[56,8,256]{2,1,0:T(8,128)} %get-tuple-element.15.refs_0_), channel_id=1, source_target_pairs={{0,1},{1,0},{2,3},{3,2},{4,5},{5,4},{6,7},{7,6},{8,9},{9,8},{10,11... | collective-permute-start | bytes 1376264 | tf_op jit(solution)/shard_map/ppermute | solution.py:492
  4.2 0.0 copy-start
  4.2 2.0 %collective-permute-start.1 = (f32[42,8,256]{2,1,0:T(8,128)}, f32[42,8,256]{2,1,0:T(8,128)S(1)}, u32[]{:S(2)}, u32[]{:S(2)}) collective-permute-start(f32[42,8,256]{2,1,0:T(8,128)} %get-tuple-element.16), channel_id=1, source_target_pairs={{2,4},{6,8},{10,12},{14,16},{18,20},{22,24},{26,28},{4,2},{8,6},{1... | collective-permute-start | bytes 1032200 | tf_op jit(solution)/shard_map/ppermute | solution.py:500
  6.3 3.1 %ripple_pack.1 = (f32[4,2,3,3,16,256]{5,4,3,2,1,0:T(8,128)}, f32[4,2,3,3,16,256]{5,4,3,2,1,0:T(8,128)}) custom-call(f32[4,2,3,8,16,256]{5,4,3,2,1,0:T(8,128)} %start.5, f32[4,2,3,8,16,256]{5,4,3,2,1,0:T(8,128)} %source.5), custom_call_target="tpu_custom_call" | custom-call | tf_op jit(solution)/shard_map/ripple_pack/pallas_call | solution.py:465
  9.3 5.8 %collective-permute-done.refs_1_ = f32[56,8,256]{2,1,0:T(8,128)S(1)} collective-permute-done((f32[56,8,256]{2,1,0:T(8,128)}, f32[56,8,256]{2,1,0:T(8,128)S(1)}, u32[]{:S(2)}, u32[]{:S(2)}) %collective-permute-start) | collective-permute-done | bytes 458784 | tf_op jit(solution)/shard_map/ppermute | solution.py:492
  15.2 0.0 copy-done
  15.2 0.1 collective-permute-start.3
  15.3 1.5 %collective-permute-done.1.refs_2_.after = f32[42,8,256]{2,1,0:T(8,128)S(1)} collective-permute-done((f32[42,8,256]{2,1,0:T(8,128)}, f32[42,8,256]{2,1,0:T(8,128)S(1)}, u32[]{:S(2)}, u32[]{:S(2)}) %collective-permute-start.1) | collective-permute-done | bytes 344096 | tf_op jit(solution)/shard_map/ppermute | solution.py:500
  16.8 0.5 collective-permute-start.2
  17.3 0.0 copy-start.3
  17.3 0.0 copy-start.4
  17.3 0.0 copy-start.5
  17.3 0.0 copy-start.6
  17.4 2.1 %collective-permute-start.4 = (f32[4,2,3,3,16,256]{5,4,3,2,1,0:T(8,128)}, f32[4,2,3,3,16,256]{5,4,3,2,1,0:T(8,128)}, u32[]{:S(2)}, u32[]{:S(2)}) collective-permute-start(f32[4,2,3,3,16,256]{5,4,3,2,1,0:T(8,128)} %get-tuple-element.22), channel_id=1, source_target_pairs={{2,4},{6,8},{10,12},{14,16},{18,20},{22,24},{26,28},{4,2},{8,6},{1... | collective-permute-start | bytes 3538952 | tf_op jit(solution)/shard_map/ppermute | solution.py:515
  19.4 1.2 %collective-permute-start.5 = (f32[4,2,3,3,16,256]{5,4,3,2,1,0:T(8,128)}, f32[4,2,3,3,16,256]{5,4,3,2,1,0:T(8,128)}, u32[]{:S(2)}, u32[]{:S(2)}) collective-permute-start(f32[4,2,3,3,16,256]{5,4,3,2,1,0:T(8,128)} %get-tuple-element.23), channel_id=1, source_target_pairs={{0,2},{4,6},{8,10},{12,14},{16,18},{20,22},{24,26},{28,30},{2,0},{... | collective-permute-start | bytes 3538952 | tf_op jit(solution)/shard_map/ppermute | solution.py:516
  20.6 5.1 %collective-permute-done.2.refs_3_ = f32[42,8,256]{2,1,0:T(8,128)S(1)} collective-permute-done((f32[42,8,256]{2,1,0:T(8,128)S(1)}, f32[42,8,256]{2,1,0:T(8,128)S(1)}, u32[]{:S(2)}, u32[]{:S(2)}) %collective-permute-start.2) | collective-permute-done | bytes 344096 | tf_op jit(solution)/shard_map/ppermute | solution.py:492
  25.8 0.0 collective-permute-done.3.refs_4_
  25.8 0.0 copy-done.3
  25.8 0.0 copy-done.4
  25.8 0.0 copy-done.5
  25.8 0.0 copy-done.6
  25.8 7.4 %bias.1 = (f32[3,8,8,256]{3,2,1,0:T(8,128)}, f32[12,16,256]{2,1,0:T(8,128)S(1)}, f32[10,16,256]{2,1,0:T(8,128)S(1)}) custom-call(f32[56,8,256]{2,1,0:T(8,128)S(1)} %copy-done, f32[56,8,256]{2,1,0:T(8,128)S(1)} %collective-permute-done.refs_1_, f32[42,8,256]{2,1,0:T(8,128)S(1)} %collective-permute-done.1.refs_2_.after, ...), custom_call_target="tpu_custom_call" | custom-call | flops 299999985664 | bytes 1000000000 | tf_op jit(solution)/shard_map/bias/pallas_call | solution.py:465
  33.2 0.0 copy-start.1
  33.2 0.7 %copy-done.1 = f32[12,16,256]{2,1,0:T(8,128)} copy-done((f32[12,16,256]{2,1,0:T(8,128)}, f32[12,16,256]{2,1,0:T(8,128)S(1)}, u32[]{:S(2)}) %copy-start.1) | copy-done | bytes 196632
  33.9 0.0 copy-start.2
  33.9 0.7 %copy-done.2 = f32[10,16,256]{2,1,0:T(8,128)} copy-done((f32[10,16,256]{2,1,0:T(8,128)}, f32[10,16,256]{2,1,0:T(8,128)S(1)}, u32[]{:S(2)}) %copy-start.2) | copy-done | bytes 163864
  34.5 13.4 %collective-permute-done.4.apart = f32[4,2,3,3,16,256]{5,4,3,2,1,0:T(8,128)} collective-permute-done((f32[4,2,3,3,16,256]{5,4,3,2,1,0:T(8,128)}, f32[4,2,3,3,16,256]{5,4,3,2,1,0:T(8,128)}, u32[]{:S(2)}, u32[]{:S(2)}) %collective-permute-start.4) | collective-permute-done | bytes 1179680 | tf_op jit(solution)/shard_map/ppermute | solution.py:515
  48.0 0.0 collective-permute-done.5.paired
  48.0 9.7 %ripple.1 = (f32[4,2,3,8,16,256]{5,4,3,2,1,0:T(8,128)}, f32[8,8,256]{2,1,0:T(8,128)}, f32[8,8,256]{2,1,0:T(8,128)}) custom-call(s32[8]{0:T(128)} %harmonic_numbers.1, f32[12,16,256]{2,1,0:T(8,128)} %copy-done.1, f32[10,16,256]{2,1,0:T(8,128)} %copy-done.2, f32[4,2,3,8,16,256]{5,4,3,2,1,0:T(8,128)} %start.5, f32[4,2,3,8,16,256]{5,4,3,2,1,0:T(8,128)} %source.5, ...), custom_call_target="tpu_custom_call" | custom-call | tf_op jit(solution)/shard_map/ripple/pallas_call | solution.py:465
  57.7 1.4 %collective-permute-start.6 = (f32[8,8,256]{2,1,0:T(8,128)}, f32[8,8,256]{2,1,0:T(8,128)S(1)}, u32[]{:S(2)}, u32[]{:S(2)}) collective-permute-start(f32[8,8,256]{2,1,0:T(8,128)} %get-tuple-element.26), channel_id=1, source_target_pairs={{0,1},{1,0},{2,3},{3,2},{4,5},{5,4},{6,7},{7,6},{8,9},{9,8},{10,11... | collective-permute-start | bytes 196616 | tf_op jit(solution)/shard_map/ppermute | solution.py:564
  59.0 3.2 %collective-permute-done.6 = f32[8,8,256]{2,1,0:T(8,128)S(1)} collective-permute-done((f32[8,8,256]{2,1,0:T(8,128)}, f32[8,8,256]{2,1,0:T(8,128)S(1)}, u32[]{:S(2)}, u32[]{:S(2)}) %collective-permute-start.6) | collective-permute-done | bytes 65568 | tf_op jit(solution)/shard_map/ppermute | solution.py:564
  62.2 1.5 %add.3 = f32[8,8,256]{2,1,0:T(8,128)} add(f32[8,8,256]{2,1,0:T(8,128)} %get-tuple-element.25, f32[8,8,256]{2,1,0:T(8,128)S(1)} %collective-permute-done.6) | non-fusion elementwise | flops 16384 | bytes 196608 | tf_op jit(solution)/shard_map/add | solution.py:564
  (2 shorter events, 0.0 us)
Async XLA Ops:
  2.6 12.5 %collective-permute-start = (f32[56,8,256]{2,1,0:T(8,128)}, f32[56,8,256]{2,1,0:T(8,128)S(1)}, u32[]{:S(2)}, u32[]{:S(2)}) collective-permute-start(f32[56,8,256]{2,1,0:T(8,128)} %get-tuple-element.15.refs_0_), channel_id=1, source_target_pairs={{0,1},{1,0},{2,3},{3,2},{4,5},{5,4},{6,7},{7,6},{8,9},{9,8},{10,11... | collective-permute-start | bytes 1376264 | tf_op jit(solution)/shard_map/ppermute | solution.py:492
  4.2 11.0 %copy-start = (f32[56,8,256]{2,1,0:T(8,128)S(1)}, f32[56,8,256]{2,1,0:T(8,128)}, u32[]{:S(2)}) copy-start(f32[56,8,256]{2,1,0:T(8,128)} %get-tuple-element.15.refs_0_) | copy-start | bytes 1376260
  4.2 12.6 %collective-permute-start.1 = (f32[42,8,256]{2,1,0:T(8,128)}, f32[42,8,256]{2,1,0:T(8,128)S(1)}, u32[]{:S(2)}, u32[]{:S(2)}) collective-permute-start(f32[42,8,256]{2,1,0:T(8,128)} %get-tuple-element.16), channel_id=1, source_target_pairs={{2,4},{6,8},{10,12},{14,16},{18,20},{22,24},{26,28},{4,2},{8,6},{1... | collective-permute-start | bytes 1032200 | tf_op jit(solution)/shard_map/ppermute | solution.py:500
  15.2 10.5 %collective-permute-start.3 = (f32[2,42,8,256]{3,2,1,0:T(8,128)S(1)}, f32[2,42,8,256]{3,2,1,0:T(8,128)S(1)}, u32[]{:S(2)}, u32[]{:S(2)}) collective-permute-start(f32[2,42,8,256]{3,2,1,0:T(8,128)S(1)} %pair.1), channel_id=1, source_target_pairs={{0,2},{4,6},{8,10},{12,14},{16,18},{20,22},{24,26},{28,30},{2,0},{... | collective-permute-start | bytes 2064392 | tf_op jit(solution)/shard_map/ppermute | solution.py:509
  16.8 9.0 %collective-permute-start.2 = (f32[42,8,256]{2,1,0:T(8,128)S(1)}, f32[42,8,256]{2,1,0:T(8,128)S(1)}, u32[]{:S(2)}, u32[]{:S(2)}) collective-permute-start(f32[42,8,256]{2,1,0:T(8,128)S(1)} %collective-permute-done.1.refs_2_.after), channel_id=1, source_target_pairs={{0,1},{1,0},{2,3},{3,2},{4,5},{5,4},{6,7},{7,6},{8,9},{9,8},{10,11... | collective-permute-start | bytes 1032200 | tf_op jit(solution)/shard_map/ppermute | solution.py:492
  17.3 8.4 %copy-start.3 = (f32[4,8]{1,0:T(4,128)S(1)}, f32[4,8]{1,0:T(4,128)}, u32[]{:S(2)}) copy-start(f32[4,8]{1,0:T(4,128)} %refs_7_.1) | copy-start | bytes 388
  17.3 8.4 %copy-start.4 = (s32[4]{0:T(128)S(1)}, s32[4]{0:T(128)}, u32[]{:S(2)}) copy-start(s32[4]{0:T(128)} %refs_5_.1) | copy-start | bytes 52
  17.3 8.4 %copy-start.5 = (f32[4]{0:T(128)S(1)}, f32[4]{0:T(128)}, u32[]{:S(2)}) copy-start(f32[4]{0:T(128)} %refs_6_.1) | copy-start | bytes 52
  17.3 8.4 %copy-start.6 = (f32[4]{0:T(128)S(1)}, f32[4]{0:T(128)}, u32[]{:S(2)}) copy-start(f32[4]{0:T(128)} %refs_8_.1) | copy-start | bytes 52
  17.4 30.6 %collective-permute-start.4 = (f32[4,2,3,3,16,256]{5,4,3,2,1,0:T(8,128)}, f32[4,2,3,3,16,256]{5,4,3,2,1,0:T(8,128)}, u32[]{:S(2)}, u32[]{:S(2)}) collective-permute-start(f32[4,2,3,3,16,256]{5,4,3,2,1,0:T(8,128)} %get-tuple-element.22), channel_id=1, source_target_pairs={{2,4},{6,8},{10,12},{14,16},{18,20},{22,24},{26,28},{4,2},{8,6},{1... | collective-permute-start | bytes 3538952 | tf_op jit(solution)/shard_map/ppermute | solution.py:515
  19.4 28.6 %collective-permute-start.5 = (f32[4,2,3,3,16,256]{5,4,3,2,1,0:T(8,128)}, f32[4,2,3,3,16,256]{5,4,3,2,1,0:T(8,128)}, u32[]{:S(2)}, u32[]{:S(2)}) collective-permute-start(f32[4,2,3,3,16,256]{5,4,3,2,1,0:T(8,128)} %get-tuple-element.23), channel_id=1, source_target_pairs={{0,2},{4,6},{8,10},{12,14},{16,18},{20,22},{24,26},{28,30},{2,0},{... | collective-permute-start | bytes 3538952 | tf_op jit(solution)/shard_map/ppermute | solution.py:516
  33.2 0.7 %copy-start.1 = (f32[12,16,256]{2,1,0:T(8,128)}, f32[12,16,256]{2,1,0:T(8,128)S(1)}, u32[]{:S(2)}) copy-start(f32[12,16,256]{2,1,0:T(8,128)S(1)} %get-tuple-element.19.nud) | copy-start | bytes 589828
  33.9 0.7 %copy-start.2 = (f32[10,16,256]{2,1,0:T(8,128)}, f32[10,16,256]{2,1,0:T(8,128)S(1)}, u32[]{:S(2)}) copy-start(f32[10,16,256]{2,1,0:T(8,128)S(1)} %get-tuple-element.20.sigma) | copy-start | bytes 491524
  57.7 4.5 %collective-permute-start.6 = (f32[8,8,256]{2,1,0:T(8,128)}, f32[8,8,256]{2,1,0:T(8,128)S(1)}, u32[]{:S(2)}, u32[]{:S(2)}) collective-permute-start(f32[8,8,256]{2,1,0:T(8,128)} %get-tuple-element.26), channel_id=1, source_target_pairs={{0,1},{1,0},{2,3},{3,2},{4,5},{5,4},{6,7},{7,6},{8,9},{9,8},{10,11... | collective-permute-start | bytes 196616 | tf_op jit(solution)/shard_map/ppermute | solution.py:564

commit v4 on v3

--- a/solution.py
+++ b/solution.py
@@ -25,12 +25,9 @@
 S_LOW, S_HIGH = A_LOW[1], A_HIGH[1]
 G_LOW, G_HIGH = A_LOW[0], A_HIGH[0] - 1
 
-BIAS_WORK = 1000000000
+BIAS_WORK = 20000000
+PACK_ROOM = 62 * 2**20
 RP_ROOM = 58 * 2**20
-PACK_ROOM = 62 * 2**20
-RIPPLE_ROOM = 59 * 2**20 + 2**19
-RP_WORK = 0
-HOLD_WORK = 0
 VMEM = pl.BlockSpec(memory_space=pltpu.VMEM)
 SMEM = pl.BlockSpec(memory_space=pltpu.SMEM)
 ANY = pl.BlockSpec(memory_space=pl.ANY)
@@ -179,7 +176,8 @@
     return lax.rem(lax.axis_index("mesh"), 2) == 1
 
 
-def pack_kernel(start, source, region, whole, apart, marks, sems):
+def pack_kernel(start, source, region, whole, apart, paired, token, marks, sems):
+    token[...] = jnp.zeros(token.shape, token.dtype)
     planes = region.shape[0]
     copies = [pltpu.make_async_copy(region, marks, sems.at[0])]
     for part in range(3):
@@ -193,6 +191,7 @@
     whole[6 * planes:] = marks[...].astype(jnp.float32)
     for odd in (False, True):
         pl.when(is_odd() == odd)(functools.partial(write_edge, apart, whole, odd))
+        pl.when(is_odd() == odd)(functools.partial(write_edge, paired, whole, not odd))
 
 
 def pair_kernel(*refs):
@@ -205,33 +204,56 @@
                 write_edge(paired.at[turn], whole, not odd)
 
 
-def hold_kernel(apart, paired, after, apart_out, paired_out):
-    pass
-
-
-def ripple_pack_kernel(start, source, apart, paired, sems):
+def is_second():
+    return lax.rem(lax.axis_index("mesh") + 1, 4) < 2
+
+
+def edge_copies(start, source, buffer, target, top, sems):
     planes = start.shape[3]
+    ways_in = []
+    for part, (origin, count, onto) in enumerate(((start, 2, 0), (source, 1, 2))):
+        at = jnp.where(top, planes - count, 0)
+        ways_in.append(
+            pltpu.make_async_copy(planes_of(origin, at, count), planes_of(buffer, onto, count), sems.at[part])
+        )
+        ways_in[-1].start()
+    return ways_in, pltpu.make_async_copy(buffer, target, sems.at[2])
+
+
+def first_edges_kernel(start, source, after, apart, paired, token, buffers, sems):
+    token[...] = jnp.zeros(token.shape, token.dtype)
     odd = is_odd()
-    copies = []
-    for at, (target, top) in enumerate(((apart, odd), (paired, jnp.logical_not(odd)))):
-        first = jnp.where(top, planes - 2, 0)
-        copies.append(
-            pltpu.make_async_copy(start.at[:, :, :, pl.ds(first, 2)], target.at[:, :, :, 0:2], sems.at[2 * at])
-        )
-        first = jnp.where(top, planes - 1, 0)
-        copies.append(
-            pltpu.make_async_copy(source.at[:, :, :, pl.ds(first, 1)], target.at[:, :, :, 2:3], sems.at[2 * at + 1])
-        )
-    for copy in copies:
-        copy.start()
-    for copy in copies:
+    ways_in, way_out = edge_copies(start, source, buffers.at[1], paired, jnp.logical_not(odd), sems.at[1])
+
+    @pl.when(jnp.logical_not(is_second()))
+    def send_apart():
+        apart_in, apart_out = edge_copies(start, source, buffers.at[0], apart, odd, sems.at[0])
+        for copy in apart_in:
+            copy.wait()
+        apart_out.start()
+        apart_out.wait()
+
+    for copy in ways_in:
         copy.wait()
+    way_out.start()
+    way_out.wait()
+
+
+def second_edges_kernel(start, source, after, apart, buffer, sems):
+    @pl.when(is_second())
+    def send_apart():
+        apart_in, apart_out = edge_copies(start, source, buffer, apart, is_odd(), sems)
+        for copy in apart_in:
+            copy.wait()
+        apart_out.start()
+        apart_out.wait()
 
 
 def bias_kernel(shares, meshes, *refs):
-    wholes, aparts, paired = refs[:shares], refs[shares:2 * shares], refs[2 * shares]
-    table_index, bh_base, bh_slope, conductivity, field_out, nud_out, sigma_out = refs[2 * shares + 1:2 * shares + 8]
-    a0, a1, src, marks, nu, slopes, bases = refs[2 * shares + 8:]
+    wholes, aparts, (paired, others) = refs[:shares], refs[shares:2 * shares], refs[2 * shares:2 * shares + 2]
+    paireds = [paired] + [others.at[at] for at in range(shares - 1)]
+    table_index, bh_base, bh_slope, conductivity, field_out, nud_out, sigma_out = refs[2 * shares + 2:2 * shares + 9]
+    a0, a1, src, marks, nu, slopes, bases = refs[2 * shares + 9:]
     planes = wholes[0].shape[0] // 7
     rows_each, lanes = wholes[0].shape[1:]
     rows = rows_each * shares
@@ -251,8 +273,8 @@
 
         for number, (target, onto) in enumerate(arrays):
             target[onto:onto + planes, at, :] = wholes[turn][number * planes:(number + 1) * planes]
-        pl.when(is_odd())(functools.partial(fill, paired.at[turn], aparts[turn]))
-        pl.when(jnp.logical_not(is_odd()))(functools.partial(fill, aparts[turn], paired.at[turn]))
+        pl.when(is_odd())(functools.partial(fill, paireds[turn], aparts[turn]))
+        pl.when(jnp.logical_not(is_odd()))(functools.partial(fill, aparts[turn], paireds[turn]))
 
     tiles = Tiles(rows, lanes)
     tables = [table_index[member] for member in range(MATS)]
@@ -341,119 +363,192 @@
         field_out[part] = final[part, A_LOW[ITERS_B]:A_LOW[ITERS_B] + planes, own_rows, :]
 
 
-def ripple_kernel(shares, meshes, harmonic_numbers, nud, sigma, start, source, apart, paired, ripple_out, *refs):
-    losses, (r0, r1, r2, src, loss, faces, sides, answer, r_sems, s_sems, out_sems) = refs[:shares], refs[shares:]
-    count, planes = start.shape[0], start.shape[3]
-    rows, lanes = start.shape[4:]
-    mine = lax.axis_index("harm")
-    here = lax.axis_index("mesh")
-    top = planes + 2
-
-    def fetch(origin, first, target, onto, sems):
-        return pltpu.make_async_copy(
-            origin.at[:, :, :, pl.ds(first, 1)], target.at[:, :, :, pl.ds(onto, 1)], sems.at[onto]
-        )
-
-    odd = is_odd()
-    for origin, above in ((apart, odd), (paired, jnp.logical_not(odd))):
-        onto = jnp.where(above, top, 0)
-        for plane in range(2):
-            fetch(origin, plane, r0, onto + plane, r_sems).start()
-        fetch(origin, 2, src, jnp.where(above, planes + 1, 0), s_sems).start()
-    for plane in range(planes):
-        fetch(start, plane, r0, plane + 2, r_sems).start()
-        fetch(source, plane, src, plane + 1, s_sems).start()
-    def drain(plane):
-        return pltpu.make_async_copy(
-            r2.at[:, :, :, pl.ds(plane, 1)], ripple_out.at[:, :, :, pl.ds(plane, 1)], out_sems.at[plane]
-        )
-
-    tiles = Tiles(rows, lanes)
-    omegas = [omega_step * harmonic_numbers[mine * count + harmonic].astype(jnp.float32) for harmonic in range(count)]
-
-    def prepare(at):
-        plane = at - 1
-        near = plane + NUD_LOW
-        weights, total = double_couplings(
-            tiles, tiles.load(nud, near), tiles.load(nud, near + 1), tiles.load(nud, near - 1)
-        )
-        half = [tiles.each(lambda value: 0.5 * value, weight) for weight in weights]
-        tiles.store(faces, (at + 1,), half[0])
-        tiles.store(faces, (at,), half[1])
-        for number in range(4):
-            tiles.store(sides, (number, at), half[2 + number])
-        low_ok = jnp.logical_or(plane >= 0, here > 0)
-        high_ok = jnp.logical_or(plane < planes, here < meshes - 1)
-        keep = jnp.where(jnp.logical_and(low_ok, high_ok), 1.0, 0.0)
+class Ripple:
+    def __init__(self, count, rows, lanes, harmonic_numbers, nud, sigma, src, sides, answer):
+        self.count, self.nud, self.sigma, self.src, self.sides, self.answer = count, nud, sigma, src, sides, answer
+        self.tiles = Tiles(rows, lanes)
+        first = lax.axis_index("harm") * count
+        self.omegas = [omega_step * harmonic_numbers[first + at].astype(jnp.float32) for at in range(count)]
+
+    def prepare(self, slot, plane, keep):
+        tiles, near = self.tiles, plane + NUD_LOW
+        weights, total = double_couplings(tiles, *(tiles.load(self.nud, near + move) for move in (0, 1, -1)))
+        for number, weight in enumerate(weights):
+            tiles.store(self.sides, (number, slot), tiles.each(lambda value: 0.5 * value, weight))
         total = tiles.each(lambda value: 0.5 * value, total)
         square = tiles.each(lambda value: value * value, total)
-        conduct = tiles.load(sigma, at)
-        for harmonic in range(count):
-            damp = tiles.each(lambda value: omegas[harmonic] * value, conduct)
+        conduct = tiles.load(self.sigma, plane + ITERS_R - 1)
+        for harmonic in range(self.count):
+            damp = tiles.each(lambda value: self.omegas[harmonic] * value, conduct)
             inverse = tiles.each(lambda one, other: keep / (one + other * other), square, damp)
-            tiles.store(answer, (harmonic, 0, at), tiles.each(lambda one, other: one * other, total, inverse))
-            tiles.store(answer, (harmonic, 1, at), tiles.each(lambda one, other: one * other, damp, inverse))
-
-    loop_in_pairs(planes + 2, prepare)
-
-    def sweep(old, offset, plane, store):
-        at = plane + 1
-        weights = [tiles.load(faces, at + 1), tiles.load(faces, at)]
-        weights += [tiles.load(sides, number, at) for number in range(4)]
-        for harmonic in range(count):
-            straight, turned = tiles.load(answer, harmonic, 0, at), tiles.load(answer, harmonic, 1, at)
+            for part, value in enumerate((total, damp)):
+                scaled = tiles.each(lambda one, other: one * other, value, inverse)
+                tiles.store(self.answer, (harmonic, part, slot), scaled)
+
+    def sweep(self, slot, old, center, new, onto):
+        tiles = self.tiles
+        weights = [tiles.load(self.sides, number, slot) for number in range(6)]
+        for harmonic in range(self.count):
+            straight, turned = (tiles.load(self.answer, harmonic, part, slot) for part in range(2))
             power = None
             for part in range(3):
                 both = []
                 for piece in range(2):
-                    near_old = [tiles.load(old, harmonic, piece, part, plane + offset + move) for move in (0, 1, -1)]
-                    both.append(pull(tiles, tiles.load(src, harmonic, piece, part, at), weights, *near_old))
+                    near_old = [tiles.load(old, harmonic, piece, part, center + move) for move in (0, 1, -1)]
+                    both.append(pull(tiles, tiles.load(self.src, harmonic, piece, part, slot), weights, *near_old))
                 real = tiles.each(lambda re, im, a, b: re * a + im * b, *both, straight, turned)
                 imag = tiles.each(lambda re, im, a, b: im * a - re * b, *both, straight, turned)
-                store(harmonic, part, real, imag)
+                tiles.store(new, (harmonic, 0, part, onto), real)
+                tiles.store(new, (harmonic, 1, part, onto), imag)
                 squared = tiles.each(lambda re, im: re * re + im * im, real, imag)
                 power = tiles.each(lambda one, other: one + other, power, squared) if part else squared
             yield harmonic, power
 
+    def last_sweep(self, slot, old, center, new, onto, plane, loss):
+        tiles, summed = self.tiles, None
+        for harmonic, power in self.sweep(slot, old, center, new, onto):
+            factor = 0.5 * self.omegas[harmonic] * self.omegas[harmonic]
+            scaled = tiles.each(lambda value: factor * value, power)
+            summed = tiles.each(lambda one, other: one + other, summed, scaled) if harmonic else scaled
+        conduct = tiles.load(self.sigma, plane + ITERS_R - 1)
+        tiles.store(loss, (plane,), tiles.each(lambda one, other: one * other, conduct, summed))
+
+
+def planes_of(ref, first, count):
+    return ref.at[:, :, :, pl.ds(first, count)]
+
+
+def inner_kernel(
+    harmonic_numbers, nud_in, sigma_in, start, source, ripple_out, edge_out, loss_out,
+    r0, r1, r2, src, sides, answer, nud, sigma, r_sems, s_sems, out_sems, sems,
+):
+    count, planes = start.shape[0], start.shape[3]
+
+    def fetch(origin, target, plane, copy_sems):
+        return pltpu.make_async_copy(planes_of(origin, plane, 1), planes_of(target, plane, 1), copy_sems.at[plane])
+
+    def drain(plane):
+        return pltpu.make_async_copy(planes_of(r2, plane, 1), planes_of(ripple_out, plane, 1), out_sems.at[plane])
+
+    fields = [pltpu.make_async_copy(nud_in, nud, sems.at[0]), pltpu.make_async_copy(sigma_in, sigma, sems.at[1])]
+    for copy in fields:
+        copy.start()
+    for plane in range(planes):
+        fetch(start, r0, plane, r_sems).start()
+        if 0 < plane < planes - 1:
+            fetch(source, src, plane, s_sems).start()
+    ripple = Ripple(count, *start.shape[4:], harmonic_numbers, nud, sigma, src, sides, answer)
+    for copy in fields:
+        copy.wait()
+    loop_in_pairs(planes - 2, lambda at: ripple.prepare(at + 1, at + 1, 1.0))
     for plane in range(2):
-        fetch(start, 0, r0, plane, r_sems).wait()
+        fetch(start, r0, plane, r_sems).wait()
 
     def first(at, carry):
-        fetch(start, 0, r0, at + 2, r_sems).wait()
-        fetch(start, 0, src, at, s_sems).wait()
-
-        def store(harmonic, part, real, imag):
-            tiles.store(r1, (harmonic, 0, part, at), real)
-            tiles.store(r1, (harmonic, 1, part, at), imag)
-
-        for unused in sweep(r0, 2, at - 1, store):
+        fetch(start, r0, at + 1, r_sems).wait()
+        fetch(source, src, at, s_sems).wait()
+        for unused in ripple.sweep(at, r0, at, r1, at):
             pass
         return carry
 
-    lax.fori_loop(0, planes + 2, first, 0)
+    lax.fori_loop(1, planes - 1, first, 0)
+    edges = [
+        pltpu.make_async_copy(planes_of(r1, place, 2), planes_of(edge_out, onto, 2), sems.at[onto // 2])
+        for place, onto in ((1, 0), (planes - 3, 2))
+    ]
+    for copy in edges:
+        copy.start()
 
     def second(plane, carry):
-        def store(harmonic, part, real, imag):
-            tiles.store(r2, (harmonic, 0, part, plane), real)
-            tiles.store(r2, (harmonic, 1, part, plane), imag)
-
-        summed = None
-        for harmonic, power in sweep(r1, 1, plane, store):
-            factor = 0.5 * omegas[harmonic] * omegas[harmonic]
-            scaled = tiles.each(lambda value: factor * value, power)
-            summed = tiles.each(lambda one, other: one + other, summed, scaled) if harmonic else scaled
-        conduct = tiles.load(sigma, plane + 1)
-        tiles.store(loss, (plane,), tiles.each(lambda one, other: one * other, conduct, summed))
+        ripple.last_sweep(plane, r1, plane, r2, plane, plane, loss_out)
         drain(plane).start()
         return carry
 
-    lax.fori_loop(0, planes, second, 0)
+    lax.fori_loop(2, planes - 2, second, 0)
+    for copy in edges:
+        copy.wait()
+    for plane in range(2, planes - 2):
+        drain(plane).wait()
+
+
+def outer_kernel(
+    shares, meshes, harmonic_numbers, nud_in, sigma_in, start, source, first_apart, second_apart, paired, edge_in,
+    loss_in, ripple_in, ripple_out, *refs
+):
+    losses, refs = refs[:shares], refs[shares:]
+    r0, r1, r2, src, sides, answer, nud, sigma, loss, sems, halo_sems = refs
+    count, planes = start.shape[0], start.shape[3]
+    rows, lanes = start.shape[4:]
+    here = lax.axis_index("mesh")
+    copies = [
+        pltpu.make_async_copy(nud_in, nud, sems.at[0]),
+        pltpu.make_async_copy(sigma_in, sigma, sems.at[1]),
+        pltpu.make_async_copy(loss_in, loss, sems.at[2]),
+        pltpu.make_async_copy(planes_of(start, 0, 2), planes_of(r0, 2, 2), sems.at[3]),
+        pltpu.make_async_copy(planes_of(start, planes - 2, 2), planes_of(r0, 4, 2), sems.at[4]),
+        pltpu.make_async_copy(planes_of(source, 0, 2), planes_of(src, 1, 2), sems.at[5]),
+        pltpu.make_async_copy(planes_of(source, planes - 2, 2), planes_of(src, 3, 2), sems.at[6]),
+        pltpu.make_async_copy(edge_in, planes_of(r1, 2, 4), sems.at[7]),
+    ]
+    odd = is_odd()
+
+    def halo(origin, above, number):
+        onto = jnp.where(above, 6, 0), jnp.where(above, 5, 0)
+        return [
+            pltpu.make_async_copy(planes_of(origin, 0, 2), planes_of(r0, onto[0], 2), halo_sems.at[number]),
+            pltpu.make_async_copy(planes_of(origin, 2, 1), planes_of(src, onto[1], 1), halo_sems.at[number + 1]),
+        ]
+
+    for second, origin in ((False, first_apart), (True, second_apart)):
+
+        @pl.when(is_second() == second)
+        def apart():
+            for copy in halo(origin, odd, 0):
+                copy.start()
+
+    copies += halo(paired, jnp.logical_not(odd), 2)
+    for copy in copies:
+        copy.start()
+    copies += halo(first_apart, odd, 0)
+    ripple = Ripple(count, rows, lanes, harmonic_numbers, nud, sigma, src, sides, answer)
+    for copy in copies[:2]:
+        copy.wait()
+
+    def prepare(slot):
+        plane = jnp.where(slot < 3, slot - 1, planes - 5 + slot)
+        low_ok = jnp.logical_or(plane >= 0, here > 0)
+        high_ok = jnp.logical_or(plane < planes, here < meshes - 1)
+        ripple.prepare(slot, plane, jnp.where(jnp.logical_and(low_ok, high_ok), 1.0, 0.0))
+
+    loop_in_pairs(6, prepare)
+    for copy in copies[2:]:
+        copy.wait()
+
+    def first(at, carry):
+        high = at // 2
+        for unused in ripple.sweep(at + 2 * high, r0, at + 1 + 2 * high, r1, at + 4 * high):
+            pass
+        return carry
+
+    lax.fori_loop(0, 4, first, 0)
+
+    def drain(at, plane):
+        return pltpu.make_async_copy(planes_of(r2, at, 1), planes_of(ripple_out, plane, 1), sems.at[at])
+
+    def second(at, carry):
+        high = at // 2
+        plane = jnp.where(at < 2, at, planes - 4 + at)
+        ripple.last_sweep(at + 1, r1, at + 1 + 2 * high, r2, at, plane, loss)
+        drain(at, plane).start()
+        return carry
+
+    lax.fori_loop(0, 4, second, 0)
     rows_each = rows // shares
     for turn in range(shares):
-        owner = lax.rem(mine + turn, shares)
+        owner = lax.rem(lax.axis_index("harm") + turn, shares)
         losses[turn][...] = loss[:, pl.ds(pl.multiple_of(owner * rows_each, rows_each), rows_each), :]
-    for plane in range(planes):
-        drain(plane).wait()
+    for at in range(4):
+        drain(at, 0).wait()
 
 
 def call(kernel, operands, in_specs, out_shapes, out_specs, scratch, name, work=0, aliases={}, room=0):
@@ -468,7 +563,7 @@
         in_specs=in_specs,
         out_specs=out_specs,
         scratch_shapes=[pltpu.VMEM(shape, f32) if isinstance(shape, tuple) else shape for shape in scratch],
-        compiler_params=pltpu.CompilerParams(vmem_limit_bytes=room or held + 6 * 2**20),
+        compiler_params=pltpu.CompilerParams(vmem_limit_bytes=room or held + 4 * 2**20),
         cost_estimate=pl.CostEstimate(flops=work * 300, bytes_accessed=work, transcendentals=0),
         input_output_aliases=aliases,
         name=name,
@@ -491,35 +586,36 @@
     def around(block):
         return [block] + [lax.ppermute(block, "harm", pairs) for pairs in turned]
 
-    whole, apart = call(
+    whole, apart, paired, token = call(
         pack_kernel, (bias_start, bias_source, region), [ANY] * 3,
-        [(7 * planes, rows_each, lanes), (HIGH_SIZE, rows_each, lanes)], [VMEM] * 2,
+        [(7 * planes, rows_each, lanes), (HIGH_SIZE, rows_each, lanes), (HIGH_SIZE, rows_each, lanes), TILE], [VMEM] * 4,
         [pltpu.VMEM(region.shape, region.dtype), pltpu.SemaphoreType.DMA((7,))], "pack", room=PACK_ROOM,
     )
     wholes = around(whole)
     aparts = around(lax.ppermute(apart, "mesh", far))
     edge = ripple_start.shape[:3] + (3, rows, lanes)
-    ripple_apart, ripple_paired = call(
-        ripple_pack_kernel, (ripple_start, ripple_source), [ANY] * 2, [edge, edge], [VMEM] * 2,
-        [pltpu.SemaphoreType.DMA((4,))], "ripple_pack", RP_WORK, room=RP_ROOM,
-    )
-    paired, = call(
-        pair_kernel, (*wholes, ripple_apart), [VMEM] * shares + [ANY], [(shares, HIGH_SIZE, rows_each, lanes)], [VMEM], [], "pair"
-    )
-    paired = lax.ppermute(paired, "mesh", near)
-
-    ripple_apart, ripple_paired = call(
-        hold_kernel, (ripple_apart, ripple_paired, aparts[0]), [ANY] * 3, [edge, edge], [ANY] * 2, [], "hold",
-        HOLD_WORK, {0: 0, 1: 1},
-    )
-    ripple_apart = lax.ppermute(ripple_apart, "mesh", far)
+    ripple_first, ripple_paired, token = call(
+        first_edges_kernel, (ripple_start, ripple_source, token), [ANY] * 3, [edge, edge, TILE], [ANY, ANY, VMEM],
+        [(2, *edge), pltpu.SemaphoreType.DMA((2, 3))], "first_edges", room=RP_ROOM,
+    )
+    ripple_second, = call(
+        second_edges_kernel, (ripple_start, ripple_source, token), [ANY] * 3, [edge], [ANY],
+        [edge, pltpu.SemaphoreType.DMA((3,))], "second_edges", room=RP_ROOM,
+    )
+    others, = call(
+        pair_kernel, (*wholes[1:], aparts[0]), [VMEM] * (shares - 1) + [ANY],
+        [(shares - 1, HIGH_SIZE, rows_each, lanes)], [VMEM], [], "pair",
+    )
+    paireds = [lax.ppermute(paired, "mesh", near), lax.ppermute(others, "mesh", near)]
+    ripple_first = lax.ppermute(ripple_first, "mesh", [pair for pair in far if min(pair) % 4 == 1])
+    ripple_second = lax.ppermute(ripple_second, "mesh", [pair for pair in far if min(pair) % 4 == 3])
     ripple_paired = lax.ppermute(ripple_paired, "mesh", near)
 
     known = (planes + G_LOW + G_HIGH, rows, lanes)
     field, nud, sigma = call(
         functools.partial(bias_kernel, shares, meshes),
-        (*wholes, *aparts, paired, table_index, bh_base, bh_slope, conductivity),
-        [VMEM] * (2 * shares + 1) + [SMEM] * 4,
+        (*wholes, *aparts, *paireds, table_index, bh_base, bh_slope, conductivity),
+        [VMEM] * (2 * shares + 2) + [SMEM] * 4,
         [
             bias_start.shape, (planes + NUD_LOW + NUD_HIGH, rows, lanes), (planes + 2 * (ITERS_R - 1), rows, lanes)
         ],
@@ -537,27 +633,23 @@
         BIAS_WORK,
     )
 
+    lead = ripple_start.shape[:3]
+    sweeps = (harmonic_numbers, nud, sigma, ripple_start, ripple_source)
+    held = [nud.shape, sigma.shape]
+    ripple, inner_edge, inner_loss = call(
+        inner_kernel, sweeps, [SMEM] + [ANY] * 4,
+        [ripple_start.shape, lead + (4, rows, lanes), (planes, rows, lanes)], [ANY, ANY, VMEM],
+        [lead + (planes, rows, lanes)] * 4 + [(6, planes, rows, lanes), (count, 2, planes, rows, lanes)] + held
+        + [pltpu.SemaphoreType.DMA((planes,))] * 3 + [pltpu.SemaphoreType.DMA((2,))],
+        "inner_ripple",
+    )
     ripple, *losses = call(
-        functools.partial(ripple_kernel, shares, meshes),
-        (harmonic_numbers, nud, sigma, ripple_start, ripple_source, ripple_apart, ripple_paired),
-        [SMEM, VMEM, VMEM] + [ANY] * 4,
-        [ripple_start.shape] + [(planes, rows_each, lanes)] * shares,
-        [ANY] + [VMEM] * shares,
-        [
-            (count, 2, 3, planes + 4, rows, lanes),
-            (count, 2, 3, planes + 2, rows, lanes),
-            (count, 2, 3, planes, rows, lanes),
-            (count, 2, 3, planes + 2, rows, lanes),
-            (planes, rows, lanes),
-            (planes + 3, rows, lanes),
-            (4, planes + 2, rows, lanes),
-            (count, 2, planes + 2, rows, lanes),
-            pltpu.SemaphoreType.DMA((planes + 4,)),
-            pltpu.SemaphoreType.DMA((planes + 2,)),
-            pltpu.SemaphoreType.DMA((planes,)),
-        ],
-        "ripple",
-        room=RIPPLE_ROOM,
+        functools.partial(outer_kernel, shares, meshes),
+        (*sweeps, ripple_first, ripple_second, ripple_paired, inner_edge, inner_loss, ripple), [SMEM] + [ANY] * 10,
+        [ripple_start.shape] + [(planes, rows_each, lanes)] * shares, [ANY] + [VMEM] * shares,
+        [lead + (slots, rows, lanes) for slots in (8, 8, 4, 6)] + [(6, 6, rows, lanes), (count, 2, 6, rows, lanes)] + held
+        + [(planes, rows, lanes), pltpu.SemaphoreType.DMA((8,)), pltpu.SemaphoreType.DMA((4,))],
+        "outer_ripple", aliases={10: 0},
     )
     loss = losses[0]
     for turn, pairs in enumerate(turned):

time: 64 us -> 54 us (0.84)
  waiting for transfers between devices: 29.1 us -> 14.2 us
  starting transfers between devices: 8.83 us -> 12.5 us
  Pallas kernels: 22.2 us -> 25.3 us
  local copies, waits for them, and re-layouts: 1.36 us -> 0.32 us
  other arithmetic: 1.48 us -> 0.64 us
    ppermute x2 -> x4, waiting for transfers between devices: 13.4 us -> 1.43 us  [the longest x1 1.42 us: body(): lax.ppermute(ripple_first, 'mesh', [pair for pair in far if min(pair) % 4...]
    pallas_call x6 -> x7, Pallas kernels: 22.2 us -> 25.3 us  [call(): pl.pallas_call(kernel, out_shape=[jax.ShapeDtypeStruct(shape, f32) for sh...]
    ppermute x2 -> x4, starting transfers between devices: 2.12 us -> 4.73 us  [the longest x1 2.01 us: body(): lax.ppermute(ripple_first, 'mesh', [pair for pair in far if min(pair) % 4...]
    ppermute x2, waiting for transfers between devices: 11 us -> 8.97 us  [around(): return [block] + [lax.ppermute(block, 'harm', pairs) for pairs in turned]]
    ppermute x1, waiting for transfers between devices: 1.5 us -> 0.07 us  [body(): aparts = around(lax.ppermute(apart, 'mesh', far))]
    unnamed x14 -> x20, local copies, waits for them, and re-layouts: 1.36 us -> 0.32 us
    ppermute x1, starting transfers between devices: 1.22 us -> 2.2 us  [body(): ripple_paired = lax.ppermute(ripple_paired, 'mesh', near)]
    ppermute x2, starting transfers between devices: 2.09 us -> 3.05 us  [around(): return [block] + [lax.ppermute(block, 'harm', pairs) for pairs in turned]]
  transfers between devices with their start and end apart: 7 -> 9, of which waited for: 5 -> 5; matrix products, arithmetic and copies ran while one was open for 0% -> 0% of each run, Pallas kernels for 17% -> 33%
where the time goes in v4:
time: 54 us; the launch traced here: 53.7 us
  Pallas kernels  25.3 us (47%)
  waiting for transfers between devices  14.2 us (26%)
  starting transfers between devices  12.5 us (23%)
  between operations  0.84 us (2%)
  other arithmetic  0.64 us (1%)
    pallas_call x7, Pallas kernels, call(): pl.pallas_call(kernel, out_shape=[jax.ShapeDtypeStruct(shape, f32) for sh...  25.3 us
    ppermute x2, waiting for transfers between devices, around(): return [block] + [lax.ppermute(block, 'harm', pairs) for pairs in turned]  8.97 us
    ppermute x1, waiting for transfers between devices, body(): loss = loss + lax.ppermute(losses[turn + 1], 'harm', pairs)  3.73 us
    ppermute x2, starting transfers between devices, around(): return [block] + [lax.ppermute(block, 'harm', pairs) for pairs in turned]  3.05 us
    ppermute x1, starting transfers between devices, body(): ripple_paired = lax.ppermute(ripple_paired, 'mesh', near)  2.2 us
    ppermute x1, starting transfers between devices, body(): lax.ppermute(ripple_first, 'mesh', [pair for pair in far if min(pair) % 4...  2.01 us
    ppermute x1, starting transfers between devices, body(): aparts = around(lax.ppermute(apart, 'mesh', far))  1.92 us
    ppermute x1, waiting for transfers between devices, body(): lax.ppermute(ripple_first, 'mesh', [pair for pair in far if min(pair) % 4...  1.42 us
  transfers between devices with their start and end apart: 9, of which 5 were waited for; matrix products, arithmetic and copies ran while one was open for 0% of the time, Pallas kernels for 33%

profile of v4, /device:TPU:12, one launch (start us, length us, event | category | flops | bytes accessed | tf_op | source)
XLA Modules:
  0.0 53.7 jit_solution(6952809544125059560)
XLA Ops:
  0.6 2.2 %pack.1 = (f32[56,8,256]{2,1,0:T(8,128)}, f32[42,8,256]{2,1,0:T(8,128)}, f32[42,8,256]{2,1,0:T(8,128)}, f32[8,128]{1,0:T(8,128)}) custom-call(f32[3,8,8,256]{3,2,1,0:T(8,128)} %start.5, f32[3,8,8,256]{3,2,1,0:T(8,128)} %source.5, s32[8,8,256]{2,1,0:T(8,128)} %region.1), custom_call_target="tpu_custom_call" | custom-call | tf_op jit(solution)/shard_map/pack/pallas_call | solution.py:560
  2.8 1.9 %collective-permute-start.1 = (f32[42,8,256]{2,1,0:T(8,128)}, f32[42,8,256]{2,1,0:T(8,128)S(1)}, u32[]{:S(2)}, u32[]{:S(2)}) collective-permute-start(f32[42,8,256]{2,1,0:T(8,128)} %get-tuple-element.20), channel_id=1, source_target_pairs={{2,4},{6,8},{10,12},{14,16},{18,20},{22,24},{26,28},{4,2},{8,6},{1... | collective-permute-start | bytes 1032200 | tf_op jit(solution)/shard_map/ppermute | solution.py:595
  4.7 1.6 %collective-permute-start = (f32[56,8,256]{2,1,0:T(8,128)}, f32[56,8,256]{2,1,0:T(8,128)S(1)}, u32[]{:S(2)}, u32[]{:S(2)}) collective-permute-start(f32[56,8,256]{2,1,0:T(8,128)} %get-tuple-element.19.refs_0_), channel_id=1, source_target_pairs={{0,1},{1,0},{2,3},{3,2},{4,5},{5,4},{6,7},{7,6},{8,9},{9,8},{10,11... | collective-permute-start | bytes 1376264 | tf_op jit(solution)/shard_map/ppermute | solution.py:587
  6.3 1.3 %collective-permute-start.3 = (f32[42,8,256]{2,1,0:T(8,128)}, f32[42,8,256]{2,1,0:T(8,128)S(1)}, u32[]{:S(2)}, u32[]{:S(2)}) collective-permute-start(f32[42,8,256]{2,1,0:T(8,128)} %get-tuple-element.21), channel_id=1, source_target_pairs={{0,2},{4,6},{8,10},{12,14},{16,18},{20,22},{24,26},{28,30},{2,0},{... | collective-permute-start | bytes 1032200 | tf_op jit(solution)/shard_map/ppermute | solution.py:609
  7.6 4.3 %first_edges.1 = (f32[4,2,3,3,16,256]{5,4,3,2,1,0:T(8,128)}, f32[4,2,3,3,16,256]{5,4,3,2,1,0:T(8,128)}, f32[8,128]{1,0:T(8,128)}) custom-call(f32[4,2,3,8,16,256]{5,4,3,2,1,0:T(8,128)} %start.9, f32[4,2,3,8,16,256]{5,4,3,2,1,0:T(8,128)} %source.9, f32[8,128]{1,0:T(8,128)} %get-tuple-element.25.after), custom_call_target="tpu_custom_call" | custom-call | tf_op jit(solution)/shard_map/first_edges/pallas_call | solution.py:560
  11.9 0.0 copy-start.9
  11.9 0.0 copy-start.8
  11.9 0.0 copy-start.3
  12.0 0.0 copy-start.4
  12.0 0.0 copy-start.5
  12.0 0.0 copy-start.6
  12.0 0.0 copy-start.7
  12.0 0.1 second_edges.1
  12.1 0.9 %collective-permute-start.6 = (f32[4,2,3,3,16,256]{5,4,3,2,1,0:T(8,128)}, f32[4,2,3,3,16,256]{5,4,3,2,1,0:T(8,128)S(1)}, u32[]{:S(2)}, u32[]{:S(2)}) collective-permute-start(f32[4,2,3,3,16,256]{5,4,3,2,1,0:T(8,128)} %second_edges.1), channel_id=1, source_target_pairs={{6,8},{14,16},{22,24},{8,6},{16,14},{24,22},{7,9},{15,17},{23,25},... | collective-permute-start | bytes 3538952 | tf_op jit(solution)/shard_map/ppermute | solution.py:611
  12.9 0.3 copy-done.9
  13.2 2.0 %collective-permute-start.5 = (f32[4,2,3,3,16,256]{5,4,3,2,1,0:T(8,128)S(1)}, f32[4,2,3,3,16,256]{5,4,3,2,1,0:T(8,128)S(1)}, u32[]{:S(2)}, u32[]{:S(2)}) collective-permute-start(f32[4,2,3,3,16,256]{5,4,3,2,1,0:T(8,128)S(1)} %copy-done.9), channel_id=1, source_target_pairs={{2,4},{10,12},{18,20},{26,28},{4,2},{12,10},{20,18},{28,26},{3,5},... | collective-permute-start | bytes 3538952 | tf_op jit(solution)/shard_map/ppermute | solution.py:610
  15.2 0.1 collective-permute-done.1.refs_1_.refs_2_
  15.3 0.0 copy-done.8
  15.3 2.2 %collective-permute-start.7 = (f32[4,2,3,3,16,256]{5,4,3,2,1,0:T(8,128)S(1)}, f32[4,2,3,3,16,256]{5,4,3,2,1,0:T(8,128)S(1)}, u32[]{:S(2)}, u32[]{:S(2)}) collective-permute-start(f32[4,2,3,3,16,256]{5,4,3,2,1,0:T(8,128)S(1)} %copy-done.8), channel_id=1, source_target_pairs={{0,2},{4,6},{8,10},{12,14},{16,18},{20,22},{24,26},{28,30},{2,0},{... | collective-permute-start | bytes 3538952 | tf_op jit(solution)/shard_map/ppermute | solution.py:612
  17.5 0.3 collective-permute-done.refs_0_.refs_1_
  17.8 1.5 %collective-permute-start.2 = (f32[42,8,256]{2,1,0:T(8,128)S(1)}, f32[42,8,256]{2,1,0:T(8,128)S(1)}, u32[]{:S(2)}, u32[]{:S(2)}) collective-permute-start(f32[42,8,256]{2,1,0:T(8,128)S(1)} %collective-permute-done.1.refs_1_.refs_2_), channel_id=1, source_target_pairs={{0,1},{1,0},{2,3},{3,2},{4,5},{5,4},{6,7},{7,6},{8,9},{9,8},{10,11... | collective-permute-start | bytes 1032200 | tf_op jit(solution)/shard_map/ppermute | solution.py:587
  19.3 0.0 copy-start.2
  19.3 0.0 collective-permute-done.3.refs_4_
  19.4 0.5 collective-permute-start.4
  19.9 8.6 %collective-permute-done.2.refs_3_ = f32[42,8,256]{2,1,0:T(8,128)S(1)} collective-permute-done((f32[42,8,256]{2,1,0:T(8,128)S(1)}, f32[42,8,256]{2,1,0:T(8,128)S(1)}, u32[]{:S(2)}, u32[]{:S(2)}) %collective-permute-start.2) | collective-permute-done | bytes 344096 | tf_op jit(solution)/shard_map/ppermute | solution.py:587
  28.5 0.0 collective-permute-done.4.refs_5_
  28.5 0.0 copy-done.3
  28.5 0.0 copy-done.4
  28.5 0.0 copy-done.5
  28.5 0.0 copy-done.6
  28.5 0.0 copy-done.7
  28.5 0.0 copy-start
  28.6 0.0 copy-start.1
  28.6 7.4 %bias.1 = (f32[3,8,8,256]{3,2,1,0:T(8,128)}, f32[12,16,256]{2,1,0:T(8,128)S(1)}, f32[10,16,256]{2,1,0:T(8,128)S(1)}) custom-call(f32[56,8,256]{2,1,0:T(8,128)S(1)} %copy-done.3, f32[56,8,256]{2,1,0:T(8,128)S(1)} %collective-permute-done.refs_0_.refs_1_, f32[42,8,256]{2,1,0:T(8,128)S(1)} %collective-permute-done.1.refs_1_.refs_2_, ...), custom_call_target="tpu_custom_call" | custom-call | flops 6000000000 | bytes 20000000 | tf_op jit(solution)/shard_map/bias/pallas_call | solution.py:560
  36.0 0.0 copy-done.2
  36.0 0.0 copy-done
  36.0 0.0 copy-done.1
  36.0 5.9 %inner_ripple.1 = (f32[4,2,3,8,16,256]{5,4,3,2,1,0:T(8,128)}, f32[4,2,3,4,16,256]{5,4,3,2,1,0:T(8,128)S(1)}, f32[8,16,256]{2,1,0:T(8,128)S(1)}) custom-call(s32[8]{0:T(128)S(1)} %copy-done.2, f32[12,16,256]{2,1,0:T(8,128)S(1)} %get-tuple-element.23.nud_in, f32[10,16,256]{2,1,0:T(8,128)S(1)} %get-tuple-element.24.sigma_in, ...), custom_call_target="tpu_custom_call" | custom-call | tf_op jit(solution)/shard_map/inner_ripple/pallas_call | solution.py:560
  41.9 0.0 collective-permute-done.6.second_apart
  41.9 1.4 %collective-permute-done.5.first_apart = f32[4,2,3,3,16,256]{5,4,3,2,1,0:T(8,128)S(1)} collective-permute-done((f32[4,2,3,3,16,256]{5,4,3,2,1,0:T(8,128)S(1)}, f32[4,2,3,3,16,256]{5,4,3,2,1,0:T(8,128)S(1)}, u32[]{:S(2)}, u32[]{:S(2)}) %collective-permute-start.5) | collective-permute-done | bytes 1179680 | tf_op jit(solution)/shard_map/ppermute | solution.py:610
  43.3 0.0 collective-permute-done.7.paired
  43.3 5.4 %outer_ripple.1 = (f32[4,2,3,8,16,256]{5,4,3,2,1,0:T(8,128)}, f32[8,8,256]{2,1,0:T(8,128)S(1)}, f32[8,8,256]{2,1,0:T(8,128)S(1)}) custom-call(s32[8]{0:T(128)S(1)} %copy-done.2, f32[12,16,256]{2,1,0:T(8,128)S(1)} %get-tuple-element.23.nud_in, f32[10,16,256]{2,1,0:T(8,128)S(1)} %get-tuple-element.24.sigma_in, ...), custom_call_target="tpu_custom_call", output_to_operand_aliasing={{0}: (10, {})} | custom-call | tf_op jit(solution)/shard_map/outer_ripple/pallas_call | solution.py:560
  48.8 0.6 %collective-permute-start.8 = (f32[8,8,256]{2,1,0:T(8,128)S(1)}, f32[8,8,256]{2,1,0:T(8,128)S(1)}, u32[]{:S(2)}, u32[]{:S(2)}) collective-permute-start(f32[8,8,256]{2,1,0:T(8,128)S(1)} %get-tuple-element.34), channel_id=1, source_target_pairs={{0,1},{1,0},{2,3},{3,2},{4,5},{5,4},{6,7},{7,6},{8,9},{9,8},{10,11... | collective-permute-start | bytes 196616 | tf_op jit(solution)/shard_map/ppermute | solution.py:656
  49.4 3.7 %collective-permute-done.8 = f32[8,8,256]{2,1,0:T(8,128)S(1)} collective-permute-done((f32[8,8,256]{2,1,0:T(8,128)S(1)}, f32[8,8,256]{2,1,0:T(8,128)S(1)}, u32[]{:S(2)}, u32[]{:S(2)}) %collective-permute-start.8) | collective-permute-done | bytes 65568 | tf_op jit(solution)/shard_map/ppermute | solution.py:656
  53.1 0.6 %add.3 = f32[8,8,256]{2,1,0:T(8,128)} add(f32[8,8,256]{2,1,0:T(8,128)S(1)} %get-tuple-element.33, f32[8,8,256]{2,1,0:T(8,128)S(1)} %collective-permute-done.8) | non-fusion elementwise | flops 16384 | bytes 196608 | tf_op jit(solution)/shard_map/add | solution.py:656
  (1 shorter events, 0.0 us)
Async XLA Ops:
  2.8 12.5 %collective-permute-start.1 = (f32[42,8,256]{2,1,0:T(8,128)}, f32[42,8,256]{2,1,0:T(8,128)S(1)}, u32[]{:S(2)}, u32[]{:S(2)}) collective-permute-start(f32[42,8,256]{2,1,0:T(8,128)} %get-tuple-element.20), channel_id=1, source_target_pairs={{2,4},{6,8},{10,12},{14,16},{18,20},{22,24},{26,28},{4,2},{8,6},{1... | collective-permute-start | bytes 1032200 | tf_op jit(solution)/shard_map/ppermute | solution.py:595
  4.7 13.1 %collective-permute-start = (f32[56,8,256]{2,1,0:T(8,128)}, f32[56,8,256]{2,1,0:T(8,128)S(1)}, u32[]{:S(2)}, u32[]{:S(2)}) collective-permute-start(f32[56,8,256]{2,1,0:T(8,128)} %get-tuple-element.19.refs_0_), channel_id=1, source_target_pairs={{0,1},{1,0},{2,3},{3,2},{4,5},{5,4},{6,7},{7,6},{8,9},{9,8},{10,11... | collective-permute-start | bytes 1376264 | tf_op jit(solution)/shard_map/ppermute | solution.py:587
  6.3 13.0 %collective-permute-start.3 = (f32[42,8,256]{2,1,0:T(8,128)}, f32[42,8,256]{2,1,0:T(8,128)S(1)}, u32[]{:S(2)}, u32[]{:S(2)}) collective-permute-start(f32[42,8,256]{2,1,0:T(8,128)} %get-tuple-element.21), channel_id=1, source_target_pairs={{0,2},{4,6},{8,10},{12,14},{16,18},{20,22},{24,26},{28,30},{2,0},{... | collective-permute-start | bytes 1032200 | tf_op jit(solution)/shard_map/ppermute | solution.py:609
  11.9 1.3 %copy-start.9 = (f32[4,2,3,3,16,256]{5,4,3,2,1,0:T(8,128)S(1)}, f32[4,2,3,3,16,256]{5,4,3,2,1,0:T(8,128)}, u32[]{:S(2)}) copy-start(f32[4,2,3,3,16,256]{5,4,3,2,1,0:T(8,128)} %get-tuple-element.26) | copy-start | bytes 3538948
  11.9 3.4 %copy-start.8 = (f32[4,2,3,3,16,256]{5,4,3,2,1,0:T(8,128)S(1)}, f32[4,2,3,3,16,256]{5,4,3,2,1,0:T(8,128)}, u32[]{:S(2)}) copy-start(f32[4,2,3,3,16,256]{5,4,3,2,1,0:T(8,128)} %get-tuple-element.28) | copy-start | bytes 3538948
  11.9 16.6 %copy-start.3 = (f32[56,8,256]{2,1,0:T(8,128)S(1)}, f32[56,8,256]{2,1,0:T(8,128)}, u32[]{:S(2)}) copy-start(f32[56,8,256]{2,1,0:T(8,128)} %get-tuple-element.19.refs_0_) | copy-start | bytes 1376260
  12.0 16.6 %copy-start.4 = (f32[4,8]{1,0:T(4,128)S(1)}, f32[4,8]{1,0:T(4,128)}, u32[]{:S(2)}) copy-start(f32[4,8]{1,0:T(4,128)} %refs_8_.1) | copy-start | bytes 388
  12.0 16.5 %copy-start.5 = (s32[4]{0:T(128)S(1)}, s32[4]{0:T(128)}, u32[]{:S(2)}) copy-start(s32[4]{0:T(128)} %refs_6_.1) | copy-start | bytes 52
  12.0 16.5 %copy-start.6 = (f32[4]{0:T(128)S(1)}, f32[4]{0:T(128)}, u32[]{:S(2)}) copy-start(f32[4]{0:T(128)} %refs_7_.1) | copy-start | bytes 52
  12.0 16.5 %copy-start.7 = (f32[4]{0:T(128)S(1)}, f32[4]{0:T(128)}, u32[]{:S(2)}) copy-start(f32[4]{0:T(128)} %refs_9_.1) | copy-start | bytes 52
  12.1 29.9 %collective-permute-start.6 = (f32[4,2,3,3,16,256]{5,4,3,2,1,0:T(8,128)}, f32[4,2,3,3,16,256]{5,4,3,2,1,0:T(8,128)S(1)}, u32[]{:S(2)}, u32[]{:S(2)}) collective-permute-start(f32[4,2,3,3,16,256]{5,4,3,2,1,0:T(8,128)} %second_edges.1), channel_id=1, source_target_pairs={{6,8},{14,16},{22,24},{8,6},{16,14},{24,22},{7,9},{15,17},{23,25},... | collective-permute-start | bytes 3538952 | tf_op jit(solution)/shard_map/ppermute | solution.py:611
  13.2 30.1 %collective-permute-start.5 = (f32[4,2,3,3,16,256]{5,4,3,2,1,0:T(8,128)S(1)}, f32[4,2,3,3,16,256]{5,4,3,2,1,0:T(8,128)S(1)}, u32[]{:S(2)}, u32[]{:S(2)}) collective-permute-start(f32[4,2,3,3,16,256]{5,4,3,2,1,0:T(8,128)S(1)} %copy-done.9), channel_id=1, source_target_pairs={{2,4},{10,12},{18,20},{26,28},{4,2},{12,10},{20,18},{28,26},{3,5},... | collective-permute-start | bytes 3538952 | tf_op jit(solution)/shard_map/ppermute | solution.py:610
  15.3 28.1 %collective-permute-start.7 = (f32[4,2,3,3,16,256]{5,4,3,2,1,0:T(8,128)S(1)}, f32[4,2,3,3,16,256]{5,4,3,2,1,0:T(8,128)S(1)}, u32[]{:S(2)}, u32[]{:S(2)}) collective-permute-start(f32[4,2,3,3,16,256]{5,4,3,2,1,0:T(8,128)S(1)} %copy-done.8), channel_id=1, source_target_pairs={{0,2},{4,6},{8,10},{12,14},{16,18},{20,22},{24,26},{28,30},{2,0},{... | collective-permute-start | bytes 3538952 | tf_op jit(solution)/shard_map/ppermute | solution.py:612
  17.8 10.7 %collective-permute-start.2 = (f32[42,8,256]{2,1,0:T(8,128)S(1)}, f32[42,8,256]{2,1,0:T(8,128)S(1)}, u32[]{:S(2)}, u32[]{:S(2)}) collective-permute-start(f32[42,8,256]{2,1,0:T(8,128)S(1)} %collective-permute-done.1.refs_1_.refs_2_), channel_id=1, source_target_pairs={{0,1},{1,0},{2,3},{3,2},{4,5},{5,4},{6,7},{7,6},{8,9},{9,8},{10,11... | collective-permute-start | bytes 1032200 | tf_op jit(solution)/shard_map/ppermute | solution.py:587
  19.3 16.6 %copy-start.2 = (s32[8]{0:T(128)S(1)}, s32[8]{0:T(128)}, u32[]{:S(2)}) copy-start(s32[8]{0:T(128)} %harmonic_numbers.3) | copy-start | bytes 100
  19.4 9.2 %collective-permute-start.4 = (f32[1,42,8,256]{3,2,1,0:T(8,128)S(1)}, f32[1,42,8,256]{3,2,1,0:T(8,128)S(1)}, u32[]{:S(2)}, u32[]{:S(2)}) collective-permute-start(f32[1,42,8,256]{3,2,1,0:T(8,128)S(1)} %pair.1), channel_id=1, source_target_pairs={{0,2},{4,6},{8,10},{12,14},{16,18},{20,22},{24,26},{28,30},{2,0},{... | collective-permute-start | bytes 1032200 | tf_op jit(solution)/shard_map/ppermute | solution.py:609
  28.5 7.4 %copy-start = (f32[4,2,3,8,16,256]{5,4,3,2,1,0:T(8,128)S(1)}, f32[4,2,3,8,16,256]{5,4,3,2,1,0:T(8,128)}, u32[]{:S(2)}) copy-start(f32[4,2,3,8,16,256]{5,4,3,2,1,0:T(8,128)} %start.9) | copy-start | bytes 9437188
  28.6 7.4 %copy-start.1 = (f32[4,2,3,8,16,256]{5,4,3,2,1,0:T(8,128)S(1)}, f32[4,2,3,8,16,256]{5,4,3,2,1,0:T(8,128)}, u32[]{:S(2)}) copy-start(f32[4,2,3,8,16,256]{5,4,3,2,1,0:T(8,128)} %source.9) | copy-start | bytes 9437188
  48.8 4.3 %collective-permute-start.8 = (f32[8,8,256]{2,1,0:T(8,128)S(1)}, f32[8,8,256]{2,1,0:T(8,128)S(1)}, u32[]{:S(2)}, u32[]{:S(2)}) collective-permute-start(f32[8,8,256]{2,1,0:T(8,128)S(1)} %get-tuple-element.34), channel_id=1, source_target_pairs={{0,1},{1,0},{2,3},{3,2},{4,5},{5,4},{6,7},{7,6},{8,9},{9,8},{10,11... | collective-permute-start | bytes 196616 | tf_op jit(solution)/shard_map/ppermute | solution.py:656

commit v5 on v4

--- a/solution.py
+++ b/solution.py
@@ -28,6 +28,7 @@
 BIAS_WORK = 20000000
 PACK_ROOM = 62 * 2**20
 RP_ROOM = 58 * 2**20
+NEAR_ROOM = 58 * 2**20
 VMEM = pl.BlockSpec(memory_space=pltpu.VMEM)
 SMEM = pl.BlockSpec(memory_space=pltpu.SMEM)
 ANY = pl.BlockSpec(memory_space=pl.ANY)
@@ -195,7 +196,8 @@
 
 
 def pair_kernel(*refs):
-    wholes, paired = refs[:-2], refs[-1]
+    wholes, (paired, token) = refs[:-3], refs[-2:]
+    token[...] = jnp.zeros(token.shape, token.dtype)
     for odd in (False, True):
 
         @pl.when(is_odd() == odd)
@@ -208,45 +210,80 @@
     return lax.rem(lax.axis_index("mesh") + 1, 4) < 2
 
 
-def edge_copies(start, source, buffer, target, top, sems):
+def edge_copies(start, source, buffer, target, top, sems, harmonics):
     planes = start.shape[3]
     ways_in = []
     for part, (origin, count, onto) in enumerate(((start, 2, 0), (source, 1, 2))):
         at = jnp.where(top, planes - count, 0)
         ways_in.append(
-            pltpu.make_async_copy(planes_of(origin, at, count), planes_of(buffer, onto, count), sems.at[part])
+            pltpu.make_async_copy(
+                planes_of(origin.at[harmonics], at, count), planes_of(buffer.at[harmonics], onto, count), sems.at[part]
+            )
         )
         ways_in[-1].start()
-    return ways_in, pltpu.make_async_copy(buffer, target, sems.at[2])
-
-
-def first_edges_kernel(start, source, after, apart, paired, token, buffers, sems):
+    return ways_in, pltpu.make_async_copy(buffer.at[harmonics], target, sems.at[2])
+
+
+def send_edges(start, source, buffer, targets, top, sems, parts):
+    ways = [
+        edge_copies(start, source, buffer, target, top, sems.at[at], harmonics)
+        for at, (target, harmonics) in enumerate(zip(targets, parts))
+    ]
+    for ways_in, way_out in ways:
+        for copy in ways_in:
+            copy.wait()
+        way_out.start()
+    for unused, way_out in ways:
+        way_out.wait()
+
+
+def send_near_edges(start, source, targets, buffers, sems):
+    planes = start.shape[3]
+    ways = []
+    for number, (origin, buffer, target) in enumerate(zip((start, source), buffers, targets)):
+        count = target.shape[3]
+        first = jnp.where(is_odd(), 0, planes - count)
+        held = planes_of(buffer, 0, count)
+        ways.append(
+            (
+                pltpu.make_async_copy(planes_of(origin, first, count), held, sems.at[2 * number]),
+                pltpu.make_async_copy(held, target, sems.at[2 * number + 1]),
+            )
+        )
+    for way_in, unused in ways:
+        way_in.start()
+    for way_in, way_out in ways:
+        way_in.wait()
+        way_out.start()
+    for unused, way_out in ways:
+        way_out.wait()
+
+
+def first_edges_kernel(parts, start, source, after, *refs):
+    aparts, (paired_start, paired_source, token, buffer, other_buffer, sems, near_sems) = refs[:len(parts)], refs[len(parts):]
     token[...] = jnp.zeros(token.shape, token.dtype)
-    odd = is_odd()
-    ways_in, way_out = edge_copies(start, source, buffers.at[1], paired, jnp.logical_not(odd), sems.at[1])
 
     @pl.when(jnp.logical_not(is_second()))
     def send_apart():
-        apart_in, apart_out = edge_copies(start, source, buffers.at[0], apart, odd, sems.at[0])
-        for copy in apart_in:
-            copy.wait()
-        apart_out.start()
-        apart_out.wait()
-
-    for copy in ways_in:
-        copy.wait()
-    way_out.start()
-    way_out.wait()
-
-
-def second_edges_kernel(start, source, after, apart, buffer, sems):
+        send_edges(start, source, buffer, aparts, is_odd(), sems, parts)
+
+    @pl.when(is_second())
+    def send_near():
+        send_near_edges(start, source, (paired_start, paired_source), (buffer, other_buffer), near_sems)
+
+
+def near_edges_kernel(start, source, after, start_in, source_in, paired_start, paired_source, buffer, other_buffer, sems):
+    @pl.when(jnp.logical_not(is_second()))
+    def send_near():
+        send_near_edges(start, source, (paired_start, paired_source), (buffer, other_buffer), sems)
+
+
+def second_edges_kernel(parts, start, source, after, *refs):
+    aparts, (buffer, sems) = refs[:len(parts)], refs[len(parts):]
+
     @pl.when(is_second())
     def send_apart():
-        apart_in, apart_out = edge_copies(start, source, buffer, apart, is_odd(), sems)
-        for copy in apart_in:
-            copy.wait()
-        apart_out.start()
-        apart_out.wait()
+        send_edges(start, source, buffer, aparts, is_odd(), sems, parts)
 
 
 def bias_kernel(shares, meshes, *refs):
@@ -363,192 +400,177 @@
         field_out[part] = final[part, A_LOW[ITERS_B]:A_LOW[ITERS_B] + planes, own_rows, :]
 
 
+def planes_of(ref, first, count):
+    return ref.at[:, :, :, pl.ds(first, count)]
+
+
 class Ripple:
-    def __init__(self, count, rows, lanes, harmonic_numbers, nud, sigma, src, sides, answer):
-        self.count, self.nud, self.sigma, self.src, self.sides, self.answer = count, nud, sigma, src, sides, answer
-        self.tiles = Tiles(rows, lanes)
+    def __init__(self, rows, lanes, harmonic_numbers, count, sides, answer):
+        self.sides, self.answer, self.tiles = sides, answer, Tiles(rows, lanes)
         first = lax.axis_index("harm") * count
         self.omegas = [omega_step * harmonic_numbers[first + at].astype(jnp.float32) for at in range(count)]
 
-    def prepare(self, slot, plane, keep):
-        tiles, near = self.tiles, plane + NUD_LOW
-        weights, total = double_couplings(tiles, *(tiles.load(self.nud, near + move) for move in (0, 1, -1)))
+    def prepare(self, nud, sigma, slot, keep):
+        tiles, near = self.tiles, slot + NUD_LOW - 1
+        weights, total = double_couplings(tiles, *(tiles.load(nud, near + move) for move in (0, 1, -1)))
         for number, weight in enumerate(weights):
             tiles.store(self.sides, (number, slot), tiles.each(lambda value: 0.5 * value, weight))
         total = tiles.each(lambda value: 0.5 * value, total)
         square = tiles.each(lambda value: value * value, total)
-        conduct = tiles.load(self.sigma, plane + ITERS_R - 1)
-        for harmonic in range(self.count):
-            damp = tiles.each(lambda value: self.omegas[harmonic] * value, conduct)
+        conduct = tiles.load(sigma, slot)
+        for harmonic, omega in enumerate(self.omegas):
+            damp = tiles.each(lambda value: omega * value, conduct)
             inverse = tiles.each(lambda one, other: keep / (one + other * other), square, damp)
             for part, value in enumerate((total, damp)):
                 scaled = tiles.each(lambda one, other: one * other, value, inverse)
                 tiles.store(self.answer, (harmonic, part, slot), scaled)
 
-    def sweep(self, slot, old, center, new, onto):
-        tiles = self.tiles
+    def sweep(self, slot, harmonics, old, source, put):
+        tiles, loss = self.tiles, None
         weights = [tiles.load(self.sides, number, slot) for number in range(6)]
-        for harmonic in range(self.count):
+        for harmonic in harmonics:
             straight, turned = (tiles.load(self.answer, harmonic, part, slot) for part in range(2))
             power = None
             for part in range(3):
                 both = []
                 for piece in range(2):
-                    near_old = [tiles.load(old, harmonic, piece, part, center + move) for move in (0, 1, -1)]
-                    both.append(pull(tiles, tiles.load(self.src, harmonic, piece, part, slot), weights, *near_old))
+                    near_old = [tiles.load(*old(move, harmonic, piece, part)) for move in (0, 1, -1)]
+                    both.append(pull(tiles, tiles.load(*source(harmonic, piece, part)), weights, *near_old))
                 real = tiles.each(lambda re, im, a, b: re * a + im * b, *both, straight, turned)
                 imag = tiles.each(lambda re, im, a, b: im * a - re * b, *both, straight, turned)
-                tiles.store(new, (harmonic, 0, part, onto), real)
-                tiles.store(new, (harmonic, 1, part, onto), imag)
+                for piece, value in enumerate((real, imag)):
+                    where = put(harmonic, piece, part)
+                    tiles.store(where[0], where[1:], value)
                 squared = tiles.each(lambda re, im: re * re + im * im, real, imag)
                 power = tiles.each(lambda one, other: one + other, power, squared) if part else squared
-            yield harmonic, power
-
-    def last_sweep(self, slot, old, center, new, onto, plane, loss):
-        tiles, summed = self.tiles, None
-        for harmonic, power in self.sweep(slot, old, center, new, onto):
             factor = 0.5 * self.omegas[harmonic] * self.omegas[harmonic]
             scaled = tiles.each(lambda value: factor * value, power)
-            summed = tiles.each(lambda one, other: one + other, summed, scaled) if harmonic else scaled
-        conduct = tiles.load(self.sigma, plane + ITERS_R - 1)
-        tiles.store(loss, (plane,), tiles.each(lambda one, other: one * other, conduct, summed))
-
-
-def planes_of(ref, first, count):
-    return ref.at[:, :, :, pl.ds(first, count)]
+            loss = tiles.each(lambda one, other: one + other, loss, scaled) if loss else scaled
+        return loss
 
 
 def inner_kernel(
-    harmonic_numbers, nud_in, sigma_in, start, source, ripple_out, edge_out, loss_out,
-    r0, r1, r2, src, sides, answer, nud, sigma, r_sems, s_sems, out_sems, sems,
+    meshes, harmonic_numbers, nud, sigma, start, source, ripple_out, edge_out, loss_out, sides, answer, r1, r2, sems
 ):
     count, planes = start.shape[0], start.shape[3]
-
-    def fetch(origin, target, plane, copy_sems):
-        return pltpu.make_async_copy(planes_of(origin, plane, 1), planes_of(target, plane, 1), copy_sems.at[plane])
+    here = lax.axis_index("mesh")
+    ripple = Ripple(*start.shape[4:], harmonic_numbers, count, sides, answer)
+    tiles = ripple.tiles
+
+    def prepare(slot):
+        low_ok = jnp.logical_or(slot > 0, here > 0)
+        high_ok = jnp.logical_or(slot < planes + 1, here < meshes - 1)
+        ripple.prepare(nud, sigma, slot, jnp.where(jnp.logical_and(low_ok, high_ok), 1.0, 0.0))
 
     def drain(plane):
-        return pltpu.make_async_copy(planes_of(r2, plane, 1), planes_of(ripple_out, plane, 1), out_sems.at[plane])
-
-    fields = [pltpu.make_async_copy(nud_in, nud, sems.at[0]), pltpu.make_async_copy(sigma_in, sigma, sems.at[1])]
-    for copy in fields:
-        copy.start()
-    for plane in range(planes):
-        fetch(start, r0, plane, r_sems).start()
-        if 0 < plane < planes - 1:
-            fetch(source, src, plane, s_sems).start()
-    ripple = Ripple(count, *start.shape[4:], harmonic_numbers, nud, sigma, src, sides, answer)
-    for copy in fields:
-        copy.wait()
-    loop_in_pairs(planes - 2, lambda at: ripple.prepare(at + 1, at + 1, 1.0))
-    for plane in range(2):
-        fetch(start, r0, plane, r_sems).wait()
-
-    def first(at, carry):
-        fetch(start, r0, at + 1, r_sems).wait()
-        fetch(source, src, at, s_sems).wait()
-        for unused in ripple.sweep(at, r0, at, r1, at):
-            pass
+        return pltpu.make_async_copy(planes_of(r2, plane, 1), planes_of(ripple_out, plane, 1), sems.at[plane])
+
+    def sweep(plane, old, new):
+        return ripple.sweep(
+            plane + 1, range(count), lambda move, *lead: (old, *lead, plane + move), lambda *lead: (source, *lead, plane),
+            lambda *lead: (new, *lead, plane),
+        )
+
+    def first(plane, carry):
+        sweep(plane, start, r1)
         return carry
 
-    lax.fori_loop(1, planes - 1, first, 0)
-    edges = [
-        pltpu.make_async_copy(planes_of(r1, place, 2), planes_of(edge_out, onto, 2), sems.at[onto // 2])
-        for place, onto in ((1, 0), (planes - 3, 2))
-    ]
-    for copy in edges:
-        copy.start()
-
     def second(plane, carry):
-        ripple.last_sweep(plane, r1, plane, r2, plane, plane, loss_out)
+        loss = sweep(plane, r1, r2)
+        tiles.store(loss_out, (plane,), tiles.each(lambda one, other: one * other, tiles.load(sigma, plane + 1), loss))
         drain(plane).start()
         return carry
 
+    loop_in_pairs(planes + 2, prepare)
+    lax.fori_loop(1, planes - 1, first, 0)
     lax.fori_loop(2, planes - 2, second, 0)
-    for copy in edges:
-        copy.wait()
+    for place, onto in ((1, 0), (planes - 3, 2)):
+        edge_out[:, :, :, onto:onto + 2] = r1[:, :, :, place:place + 2]
     for plane in range(2, planes - 2):
         drain(plane).wait()
 
 
 def outer_kernel(
-    shares, meshes, harmonic_numbers, nud_in, sigma_in, start, source, first_apart, second_apart, paired, edge_in,
-    loss_in, ripple_in, ripple_out, *refs
+    harmonics, shares, harmonic_numbers, sigma, start, source, first_apart, second_apart, paired_start, paired_source, edge, sides, answer,
+    loss_in, so_far, ripple_in, ripple_out, *refs
 ):
-    losses, refs = refs[:shares], refs[shares:]
-    r0, r1, r2, src, sides, answer, nud, sigma, loss, sems, halo_sems = refs
+    losses, (r0, r1, r2, src, loss, sems, halo_sems) = refs[:-7], refs[-7:]
     count, planes = start.shape[0], start.shape[3]
     rows, lanes = start.shape[4:]
-    here = lax.axis_index("mesh")
-    copies = [
-        pltpu.make_async_copy(nud_in, nud, sems.at[0]),
-        pltpu.make_async_copy(sigma_in, sigma, sems.at[1]),
-        pltpu.make_async_copy(loss_in, loss, sems.at[2]),
-        pltpu.make_async_copy(planes_of(start, 0, 2), planes_of(r0, 2, 2), sems.at[3]),
-        pltpu.make_async_copy(planes_of(start, planes - 2, 2), planes_of(r0, 4, 2), sems.at[4]),
-        pltpu.make_async_copy(planes_of(source, 0, 2), planes_of(src, 1, 2), sems.at[5]),
-        pltpu.make_async_copy(planes_of(source, planes - 2, 2), planes_of(src, 3, 2), sems.at[6]),
-        pltpu.make_async_copy(edge_in, planes_of(r1, 2, 4), sems.at[7]),
-    ]
+    begin, chosen = harmonics.start, slice(harmonics.start, harmonics.stop)
     odd = is_odd()
 
-    def halo(origin, above, number):
-        onto = jnp.where(above, 6, 0), jnp.where(above, 5, 0)
+    def halo(start_part, source_part, above, number):
         return [
-            pltpu.make_async_copy(planes_of(origin, 0, 2), planes_of(r0, onto[0], 2), halo_sems.at[number]),
-            pltpu.make_async_copy(planes_of(origin, 2, 1), planes_of(src, onto[1], 1), halo_sems.at[number + 1]),
+            pltpu.make_async_copy(start_part, planes_of(r0, jnp.where(above, 2, 0), 2), halo_sems.at[number]),
+            pltpu.make_async_copy(source_part, planes_of(src, jnp.where(above, 1, 0), 1), halo_sems.at[number + 1]),
         ]
 
-    for second, origin in ((False, first_apart), (True, second_apart)):
+    def apart_halo(origin):
+        return halo(planes_of(origin, 0, 2), planes_of(origin, 2, 1), odd, 0)
+
+    for second, origin in ((False, first_apart), (True, second_apart.at[chosen])):
 
         @pl.when(is_second() == second)
-        def apart():
-            for copy in halo(origin, odd, 0):
+        def start_apart():
+            for copy in apart_halo(origin):
                 copy.start()
 
-    copies += halo(paired, jnp.logical_not(odd), 2)
-    for copy in copies:
+    near = halo(paired_start.at[chosen], paired_source.at[chosen], jnp.logical_not(odd), 2)
+    for copy in near:
         copy.start()
-    copies += halo(first_apart, odd, 0)
-    ripple = Ripple(count, rows, lanes, harmonic_numbers, nud, sigma, src, sides, answer)
-    for copy in copies[:2]:
+    for copy in apart_halo(first_apart) + near:
         copy.wait()
-
-    def prepare(slot):
-        plane = jnp.where(slot < 3, slot - 1, planes - 5 + slot)
-        low_ok = jnp.logical_or(plane >= 0, here > 0)
-        high_ok = jnp.logical_or(plane < planes, here < meshes - 1)
-        ripple.prepare(slot, plane, jnp.where(jnp.logical_and(low_ok, high_ok), 1.0, 0.0))
-
-    loop_in_pairs(6, prepare)
-    for copy in copies[2:]:
-        copy.wait()
-
-    def first(at, carry):
-        high = at // 2
-        for unused in ripple.sweep(at + 2 * high, r0, at + 1 + 2 * high, r1, at + 4 * high):
-            pass
-        return carry
-
-    lax.fori_loop(0, 4, first, 0)
-
-    def drain(at, plane):
-        return pltpu.make_async_copy(planes_of(r2, at, 1), planes_of(ripple_out, plane, 1), sems.at[at])
-
-    def second(at, carry):
-        high = at // 2
-        plane = jnp.where(at < 2, at, planes - 4 + at)
-        ripple.last_sweep(at + 1, r1, at + 1 + 2 * high, r2, at, plane, loss)
-        drain(at, plane).start()
-        return carry
-
-    lax.fori_loop(0, 4, second, 0)
-    rows_each = rows // shares
-    for turn in range(shares):
-        owner = lax.rem(lax.axis_index("harm") + turn, shares)
-        losses[turn][...] = loss[:, pl.ds(pl.multiple_of(owner * rows_each, rows_each), rows_each), :]
-    for at in range(4):
-        drain(at, 0).wait()
+    ripple = Ripple(rows, lanes, harmonic_numbers, count, sides, answer)
+    tiles = ripple.tiles
+    old = {-2: (r0, 0), -1: (r0, 1), planes: (r0, 2), planes + 1: (r0, 3)}
+    old.update({plane: (start, plane) for plane in (0, 1, planes - 2, planes - 1)})
+    new = {-1: (r1, 0), 0: (r1, 1), planes - 1: (r1, 2), planes: (r1, 3)}
+    new.update({1: (edge, 0), 2: (edge, 1), planes - 3: (edge, 2), planes - 2: (edge, 3)})
+    given = {-1: (src, 0), planes: (src, 1)}
+    given.update({plane: (source, plane) for plane in (0, 1, planes - 2, planes - 1)})
+
+    def at(place, harmonic, *lead):
+        ref, slot = place
+        shift = 0 if ref.shape[0] == count else begin
+        return (ref, harmonic - shift, *lead, slot)
+
+    for plane in (-1, 0, planes - 1, planes):
+        ripple.sweep(
+            plane + 1, harmonics, lambda move, *lead: at(old[plane + move], *lead), lambda *lead: at(given[plane], *lead),
+            lambda *lead: at(new[plane], *lead),
+        )
+
+    def drain(slot, plane):
+        return pltpu.make_async_copy(
+            planes_of(r2, slot, 1), planes_of(ripple_out.at[chosen], plane, 1), sems.at[slot]
+        )
+
+    edges = list(enumerate((0, 1, planes - 2, planes - 1)))
+    last = harmonics.stop == count
+    for slot, plane in edges:
+        added = ripple.sweep(
+            plane + 1, harmonics, lambda move, *lead: at(new[plane + move], *lead), lambda *lead: at(given[plane], *lead),
+            lambda *lead: at((r2, slot), *lead),
+        )
+        drain(slot, plane).start()
+        if begin:
+            added = tiles.each(lambda one, other: one + other, added, tiles.load(so_far, slot))
+        if last:
+            added = tiles.each(lambda one, other: one * other, tiles.load(sigma, plane + 1), added)
+            tiles.store(loss, (slot,), added)
+        else:
+            tiles.store(losses[0], (slot,), added)
+    if last:
+        rows_each = rows // shares
+        for turn in range(shares):
+            owner = lax.rem(lax.axis_index("harm") + turn, shares)
+            part = pl.ds(pl.multiple_of(owner * rows_each, rows_each), rows_each)
+            losses[turn][2:planes - 2] = loss_in[2:planes - 2, part, :]
+            for slot, plane in edges:
+                losses[turn][plane] = loss[slot, part, :]
+    for slot, plane in edges:
+        drain(slot, plane).wait()
 
 
 def call(kernel, operands, in_specs, out_shapes, out_specs, scratch, name, work=0, aliases={}, room=0):
@@ -594,22 +616,33 @@
     wholes = around(whole)
     aparts = around(lax.ppermute(apart, "mesh", far))
     edge = ripple_start.shape[:3] + (3, rows, lanes)
-    ripple_first, ripple_paired, token = call(
-        first_edges_kernel, (ripple_start, ripple_source, token), [ANY] * 3, [edge, edge, TILE], [ANY, ANY, VMEM],
-        [(2, *edge), pltpu.SemaphoreType.DMA((2, 3))], "first_edges", room=RP_ROOM,
+    parts = [range(0, count)]
+    spans = [slice(part.start, part.stop) for part in parts]
+    near_edges = [edge[:3] + (size, rows, lanes) for size in (2, 1)]
+    part_edges = [(len(part), *edge[1:]) for part in parts]
+    *ripple_firsts, paired_start, paired_source, token = call(
+        functools.partial(first_edges_kernel, spans), (ripple_start, ripple_source, token), [ANY] * 3,
+        part_edges + near_edges + [TILE], [ANY] * (len(parts) + 2) + [VMEM],
+        [edge, edge, pltpu.SemaphoreType.DMA((len(parts), 3)), pltpu.SemaphoreType.DMA((4,))], "first_edges", room=RP_ROOM,
     )
-    ripple_second, = call(
-        second_edges_kernel, (ripple_start, ripple_source, token), [ANY] * 3, [edge], [ANY],
-        [edge, pltpu.SemaphoreType.DMA((3,))], "second_edges", room=RP_ROOM,
+    ripple_seconds = call(
+        functools.partial(second_edges_kernel, spans), (ripple_start, ripple_source, token), [ANY] * 3,
+        part_edges, [ANY] * len(parts), [edge, pltpu.SemaphoreType.DMA((len(parts), 3))], "second_edges", room=RP_ROOM,
     )
-    others, = call(
+    others, token = call(
         pair_kernel, (*wholes[1:], aparts[0]), [VMEM] * (shares - 1) + [ANY],
-        [(shares - 1, HIGH_SIZE, rows_each, lanes)], [VMEM], [], "pair",
+        [(shares - 1, HIGH_SIZE, rows_each, lanes), TILE], [VMEM] * 2, [], "pair",
+    )
+    ripple_paireds = call(
+        near_edges_kernel, (ripple_start, ripple_source, token, paired_start, paired_source), [ANY] * 5,
+        near_edges, [ANY] * 2, [edge, edge, pltpu.SemaphoreType.DMA((4,))], "near_edges", aliases={3: 0, 4: 1},
+        room=NEAR_ROOM,
     )
     paireds = [lax.ppermute(paired, "mesh", near), lax.ppermute(others, "mesh", near)]
-    ripple_first = lax.ppermute(ripple_first, "mesh", [pair for pair in far if min(pair) % 4 == 1])
-    ripple_second = lax.ppermute(ripple_second, "mesh", [pair for pair in far if min(pair) % 4 == 3])
-    ripple_paired = lax.ppermute(ripple_paired, "mesh", near)
+    first_pairs, second_pairs = ([pair for pair in far if min(pair) % 4 == kind] for kind in (1, 3))
+    ripple_firsts = [lax.ppermute(part, "mesh", first_pairs) for part in ripple_firsts]
+    ripple_seconds = [lax.ppermute(part, "mesh", second_pairs) for part in ripple_seconds]
+    ripple_paireds = [lax.ppermute(part, "mesh", near) for part in ripple_paireds]
 
     known = (planes + G_LOW + G_HIGH, rows, lanes)
     field, nud, sigma = call(
@@ -634,23 +667,31 @@
     )
 
     lead = ripple_start.shape[:3]
-    sweeps = (harmonic_numbers, nud, sigma, ripple_start, ripple_source)
-    held = [nud.shape, sigma.shape]
-    ripple, inner_edge, inner_loss = call(
-        inner_kernel, sweeps, [SMEM] + [ANY] * 4,
-        [ripple_start.shape, lead + (4, rows, lanes), (planes, rows, lanes)], [ANY, ANY, VMEM],
-        [lead + (planes, rows, lanes)] * 4 + [(6, planes, rows, lanes), (count, 2, planes, rows, lanes)] + held
-        + [pltpu.SemaphoreType.DMA((planes,))] * 3 + [pltpu.SemaphoreType.DMA((2,))],
-        "inner_ripple",
+    slots = (planes + 2, rows, lanes)
+    ripple, inner_edge, inner_loss, sides, answer = call(
+        functools.partial(inner_kernel, meshes), (harmonic_numbers, nud, sigma, ripple_start, ripple_source),
+        [SMEM] + [VMEM] * 4,
+        [ripple_start.shape, lead + (4, rows, lanes), (planes, rows, lanes), (6, *slots), (count, 2, *slots)],
+        [ANY] + [VMEM] * 4, [lead + (planes, rows, lanes)] * 2 + [pltpu.SemaphoreType.DMA((planes,))], "inner_ripple",
     )
-    ripple, *losses = call(
-        functools.partial(outer_kernel, shares, meshes),
-        (*sweeps, ripple_first, ripple_second, ripple_paired, inner_edge, inner_loss, ripple), [SMEM] + [ANY] * 10,
-        [ripple_start.shape] + [(planes, rows_each, lanes)] * shares, [ANY] + [VMEM] * shares,
-        [lead + (slots, rows, lanes) for slots in (8, 8, 4, 6)] + [(6, 6, rows, lanes), (count, 2, 6, rows, lanes)] + held
-        + [(planes, rows, lanes), pltpu.SemaphoreType.DMA((8,)), pltpu.SemaphoreType.DMA((4,))],
-        "outer_ripple", aliases={10: 0},
-    )
+    so_far = inner_loss
+    for part, ripple_first, ripple_second in zip(parts, ripple_firsts, ripple_seconds):
+        last = part.stop == count
+        here = (len(part), *lead[1:])
+        ripple, *losses = call(
+            functools.partial(outer_kernel, part, shares),
+            (
+                harmonic_numbers, sigma, ripple_start, ripple_source, ripple_first, ripple_second, *ripple_paireds,
+                inner_edge, sides, answer, inner_loss, so_far, ripple,
+            ),
+            [SMEM] + [VMEM] * 3 + [ANY] * 4 + [VMEM] * 5 + [ANY],
+            [ripple_start.shape] + ([(planes, rows_each, lanes)] * shares if last else [(4, rows, lanes)]),
+            [ANY] + [VMEM] * (shares if last else 1),
+            [here + (4, rows, lanes)] * 3 + [here + (2, rows, lanes), (4, rows, lanes)]
+            + [pltpu.SemaphoreType.DMA((4,))] * 2,
+            "outer_ripple", aliases={13: 0},
+        )
+        so_far = losses[0]
     loss = losses[0]
     for turn, pairs in enumerate(turned):
         loss = loss + lax.ppermute(losses[turn + 1], "harm", pairs)

time: 54 us -> 51.4 us (0.952)
  Pallas kernels: 25.3 us -> 24.1 us
  waiting for transfers between devices: 14.2 us -> 13.1 us
  starting transfers between devices: 12.5 us -> 11.5 us
  local copies, waits for them, and re-layouts: 0.32 us -> 0.96 us
    ppermute x2, waiting for transfers between devices: 8.97 us -> 6.17 us  [around(): return [block] + [lax.ppermute(block, 'harm', pairs) for pairs in turned]]
    ppermute x3 -> x4, waiting for transfers between devices: 1.43 us -> 2.85 us  [the longest x1 2.84 us: body(): lax.ppermute(part, 'mesh', first_pairs)]
    pallas_call x7 -> x8, Pallas kernels: 25.3 us -> 24.1 us  [call(): pl.pallas_call(kernel, out_shape=[jax.ShapeDtypeStruct(shape, f32) for sh...]
    ppermute x1, starting transfers between devices: 1.34 us -> 2.36 us  [body(): lax.ppermute(paired, 'mesh', near)]
    ppermute x2, starting transfers between devices: 3.05 us -> 2.09 us  [around(): return [block] + [lax.ppermute(block, 'harm', pairs) for pairs in turned]]
    unnamed x20, local copies, waits for them, and re-layouts: 0.32 us -> 0.96 us
    ppermute x3 -> x4, starting transfers between devices: 5.07 us -> 4.57 us  [the longest x1 3.63 us: body(): lax.ppermute(part, 'mesh', first_pairs)]
  transfers between devices with their start and end apart: 9 -> 10, of which waited for: 5 -> 4; matrix products, arithmetic and copies ran while one was open for 0% -> 0% of each run, Pallas kernels for 33% -> 35%
where the time goes in v5:
time: 51.4 us; the launch traced here: 51.2 us
  Pallas kernels  24.1 us (47%)
  waiting for transfers between devices  13.1 us (25%)
  starting transfers between devices  11.5 us (22%)
  local copies, waits for them, and re-layouts  0.96 us (2%)
  between operations  0.85 us (2%)
  other arithmetic  0.64 us (1%)
    pallas_call x8, Pallas kernels, call(): pl.pallas_call(kernel, out_shape=[jax.ShapeDtypeStruct(shape, f32) for sh...  24.1 us
    ppermute x2, waiting for transfers between devices, around(): return [block] + [lax.ppermute(block, 'harm', pairs) for pairs in turned]  6.17 us
    ppermute x1, waiting for transfers between devices, body(): loss = loss + lax.ppermute(losses[turn + 1], 'harm', pairs)  3.73 us
    ppermute x1, starting transfers between devices, body(): lax.ppermute(part, 'mesh', first_pairs)  3.63 us
    ppermute x1, waiting for transfers between devices, body(): lax.ppermute(part, 'mesh', first_pairs)  2.84 us
    ppermute x1, starting transfers between devices, body(): lax.ppermute(paired, 'mesh', near)  2.36 us
    ppermute x2, starting transfers between devices, around(): return [block] + [lax.ppermute(block, 'harm', pairs) for pairs in turned]  2.09 us
    ppermute x1, starting transfers between devices, body(): aparts = around(lax.ppermute(apart, 'mesh', far))  1.91 us
  transfers between devices with their start and end apart: 10, of which 4 were waited for; matrix products, arithmetic and copies ran while one was open for 0% of the time, Pallas kernels for 35%

profile of v5, /device:TPU:12, one launch (start us, length us, event | category | flops | bytes accessed | tf_op | source)
XLA Modules:
  0.0 51.2 jit_solution(12275326296158172635)
XLA Ops:
  0.6 2.2 %pack.1 = (f32[56,8,256]{2,1,0:T(8,128)}, f32[42,8,256]{2,1,0:T(8,128)}, f32[42,8,256]{2,1,0:T(8,128)}, f32[8,128]{1,0:T(8,128)}) custom-call(f32[3,8,8,256]{3,2,1,0:T(8,128)} %start.6, f32[3,8,8,256]{3,2,1,0:T(8,128)} %source.6, s32[8,8,256]{2,1,0:T(8,128)} %region.1), custom_call_target="tpu_custom_call" | custom-call | tf_op jit(solution)/shard_map/pack/pallas_call | solution.py:582
  2.8 1.6 %collective-permute-start = (f32[56,8,256]{2,1,0:T(8,128)}, f32[56,8,256]{2,1,0:T(8,128)S(1)}, u32[]{:S(2)}, u32[]{:S(2)}) collective-permute-start(f32[56,8,256]{2,1,0:T(8,128)} %get-tuple-element.26.refs_0_), channel_id=1, source_target_pairs={{0,1},{1,0},{2,3},{3,2},{4,5},{5,4},{6,7},{7,6},{8,9},{9,8},{10,11... | collective-permute-start | bytes 1376264 | tf_op jit(solution)/shard_map/ppermute | solution.py:609
  4.3 1.9 %collective-permute-start.1 = (f32[42,8,256]{2,1,0:T(8,128)}, f32[42,8,256]{2,1,0:T(8,128)S(1)}, u32[]{:S(2)}, u32[]{:S(2)}) collective-permute-start(f32[42,8,256]{2,1,0:T(8,128)} %get-tuple-element.27), channel_id=1, source_target_pairs={{2,4},{6,8},{10,12},{14,16},{18,20},{22,24},{26,28},{4,2},{8,6},{1... | collective-permute-start | bytes 1032200 | tf_op jit(solution)/shard_map/ppermute | solution.py:617
  6.3 2.9 %first_edges.1 = (f32[4,2,3,3,16,256]{5,4,3,2,1,0:T(8,128)}, f32[4,2,3,2,16,256]{5,4,3,2,1,0:T(8,128)}, f32[4,2,3,1,16,256]{5,4,3,2,1,0:T(8,128)}, f32[8,128]{1,0:T(8,128)}) custom-call(f32[4,2,3,8,16,256]{5,4,3,2,1,0:T(8,128)} %start.11, f32[4,2,3,8,16,256]{5,4,3,2,1,0:T(8,128)} %source.11, f32[8,128]{1,0:T(8,128)} %get-tuple-element.32.after), custom_call_target="tpu_custom_call" | custom-call | tf_op jit(solution)/shard_map/first_edges/pallas_call | solution.py:582
  9.2 0.0 copy-start.9
  9.2 0.1 second_edges.1
  9.3 0.9 %collective-permute-start.6 = (f32[4,2,3,3,16,256]{5,4,3,2,1,0:T(8,128)}, f32[4,2,3,3,16,256]{5,4,3,2,1,0:T(8,128)S(1)}, u32[]{:S(2)}, u32[]{:S(2)}) collective-permute-start(f32[4,2,3,3,16,256]{5,4,3,2,1,0:T(8,128)} %second_edges.1), channel_id=1, source_target_pairs={{6,8},{14,16},{22,24},{8,6},{16,14},{24,22},{7,9},{15,17},{23,25},... | collective-permute-start | bytes 3538952 | tf_op jit(solution)/shard_map/ppermute | solution.py:644
  10.1 0.3 copy-done.9
  10.5 3.6 %collective-permute-start.5 = (f32[4,2,3,3,16,256]{5,4,3,2,1,0:T(8,128)S(1)}, f32[4,2,3,3,16,256]{5,4,3,2,1,0:T(8,128)S(1)}, u32[]{:S(2)}, u32[]{:S(2)}) collective-permute-start(f32[4,2,3,3,16,256]{5,4,3,2,1,0:T(8,128)S(1)} %copy-done.9), channel_id=1, source_target_pairs={{2,4},{10,12},{18,20},{26,28},{4,2},{12,10},{20,18},{28,26},{3,5},... | collective-permute-start | bytes 3538952 | tf_op jit(solution)/shard_map/ppermute | solution.py:643
  14.1 2.4 %collective-permute-start.3 = (f32[42,8,256]{2,1,0:T(8,128)}, f32[42,8,256]{2,1,0:T(8,128)S(1)}, u32[]{:S(2)}, u32[]{:S(2)}) collective-permute-start(f32[42,8,256]{2,1,0:T(8,128)} %get-tuple-element.28), channel_id=1, source_target_pairs={{0,2},{4,6},{8,10},{12,14},{16,18},{20,22},{24,26},{28,30},{2,0},{... | collective-permute-start | bytes 1032200 | tf_op jit(solution)/shard_map/ppermute | solution.py:641
  16.5 0.3 collective-permute-done.1.refs_1_.refs_2_
  16.8 0.5 %collective-permute-start.2 = (f32[42,8,256]{2,1,0:T(8,128)S(1)}, f32[42,8,256]{2,1,0:T(8,128)S(1)}, u32[]{:S(2)}, u32[]{:S(2)}) collective-permute-start(f32[42,8,256]{2,1,0:T(8,128)S(1)} %collective-permute-done.1.refs_1_.refs_2_), channel_id=1, source_target_pairs={{0,1},{1,0},{2,3},{3,2},{4,5},{5,4},{6,7},{7,6},{8,9},{9,8},{10,11... | collective-permute-start | bytes 1032200 | tf_op jit(solution)/shard_map/ppermute | solution.py:609
  17.3 0.0 collective-permute-done.refs_0_.refs_1_
  17.4 0.0 copy-start.2
  17.4 0.6 %copy-done.2 = f32[8,128]{1,0:T(8,128)} copy-done((f32[8,128]{1,0:T(8,128)}, f32[8,128]{1,0:T(8,128)S(1)}, u32[]{:S(2)}) %copy-start.2) | copy-done | bytes 4120
  18.0 0.0 collective-permute-start.4
  18.0 0.0 copy-start.4
  18.0 0.0 copy-start.5
  18.0 0.0 copy-start.6
  18.0 0.0 copy-start.7
  18.0 0.0 copy-start.8
  18.0 2.3 %near_edges.1 = (f32[4,2,3,2,16,256]{5,4,3,2,1,0:T(8,128)}, f32[4,2,3,1,16,256]{5,4,3,2,1,0:T(8,128)}) custom-call(f32[4,2,3,8,16,256]{5,4,3,2,1,0:T(8,128)} %start.11, f32[4,2,3,8,16,256]{5,4,3,2,1,0:T(8,128)} %source.11, f32[8,128]{1,0:T(8,128)} %copy-done.2, ...), custom_call_target="tpu_custom_call", output_to_operand_aliasing={{0}: (3, {}), {1}: (4, {})} | custom-call | tf_op jit(solution)/shard_map/near_edges/pallas_call | solution.py:582
  20.3 0.0 collective-permute-done.3.refs_4_
  20.3 0.1 collective-permute-start.7
  20.3 6.2 %collective-permute-done.2.refs_3_ = f32[42,8,256]{2,1,0:T(8,128)S(1)} collective-permute-done((f32[42,8,256]{2,1,0:T(8,128)S(1)}, f32[42,8,256]{2,1,0:T(8,128)S(1)}, u32[]{:S(2)}, u32[]{:S(2)}) %collective-permute-start.2) | collective-permute-done | bytes 344096 | tf_op jit(solution)/shard_map/ppermute | solution.py:609
  26.5 0.0 copy-start.3
  26.5 0.0 collective-permute-start.8
  26.5 0.0 collective-permute-done.4.refs_5_
  26.5 0.0 copy-done.4
  26.5 0.0 copy-done.5
  26.6 0.0 copy-done.6
  26.6 0.0 copy-done.7
  26.6 0.0 copy-done.8
  26.6 0.0 copy-start
  26.6 0.0 copy-start.1
  26.6 7.4 %bias.1 = (f32[3,8,8,256]{3,2,1,0:T(8,128)}, f32[12,16,256]{2,1,0:T(8,128)S(1)}, f32[10,16,256]{2,1,0:T(8,128)S(1)}) custom-call(f32[56,8,256]{2,1,0:T(8,128)S(1)} %copy-done.4, f32[56,8,256]{2,1,0:T(8,128)S(1)} %collective-permute-done.refs_0_.refs_1_, f32[42,8,256]{2,1,0:T(8,128)S(1)} %collective-permute-done.1.refs_1_.refs_2_, ...), custom_call_target="tpu_custom_call" | custom-call | flops 6000000000 | bytes 20000000 | tf_op jit(solution)/shard_map/bias/pallas_call | solution.py:582
  34.0 0.0 copy-done.3
  34.0 0.0 copy-done
  34.0 0.0 copy-done.1
  34.0 5.2 %inner_ripple.1 = (f32[4,2,3,8,16,256]{5,4,3,2,1,0:T(8,128)}, f32[4,2,3,4,16,256]{5,4,3,2,1,0:T(8,128)S(1)}, f32[8,16,256]{2,1,0:T(8,128)S(1)}, f32[6,10,16,256]{3,2,1,0:T(8,128)S(1)}, f32[4,2,10,16,256]{4,3,2,1,0:T(8,128)S(1)}) custom-call(s32[8]{0:T(128)S(1)} %copy-done.3, f32[12,16,256]{2,1,0:T(8,128)S(1)} %get-tuple-element.40.nud, ...), custom_call_target="tpu_custom_call" | custom-call | tf_op jit(solution)/shard_map/inner_ripple/pallas_call | solution.py:582
  39.2 0.0 collective-permute-done.8.paired_source
  39.2 0.0 collective-permute-done.6.second_apart
  39.2 2.8 %collective-permute-done.5.first_apart = f32[4,2,3,3,16,256]{5,4,3,2,1,0:T(8,128)S(1)} collective-permute-done((f32[4,2,3,3,16,256]{5,4,3,2,1,0:T(8,128)S(1)}, f32[4,2,3,3,16,256]{5,4,3,2,1,0:T(8,128)S(1)}, u32[]{:S(2)}, u32[]{:S(2)}) %collective-permute-start.5) | collective-permute-done | bytes 1179680 | tf_op jit(solution)/shard_map/ppermute | solution.py:643
  42.1 0.0 collective-permute-done.7.paired_start
  42.1 4.1 %outer_ripple.1 = (f32[4,2,3,8,16,256]{5,4,3,2,1,0:T(8,128)}, f32[8,8,256]{2,1,0:T(8,128)S(1)}, f32[8,8,256]{2,1,0:T(8,128)S(1)}) custom-call(s32[8]{0:T(128)S(1)} %copy-done.3, f32[10,16,256]{2,1,0:T(8,128)S(1)} %get-tuple-element.31.sigma, f32[4,2,3,8,16,256]{5,4,3,2,1,0:T(8,128)S(1)} %copy-done, ...), custom_call_target="tpu_custom_call", output_to_operand_aliasing={{0}: (13, {})} | custom-call | tf_op jit(solution)/shard_map/outer_ripple/pallas_call | solution.py:582
  46.2 0.6 %collective-permute-start.9 = (f32[8,8,256]{2,1,0:T(8,128)S(1)}, f32[8,8,256]{2,1,0:T(8,128)S(1)}, u32[]{:S(2)}, u32[]{:S(2)}) collective-permute-start(f32[8,8,256]{2,1,0:T(8,128)S(1)} %get-tuple-element.48), channel_id=1, source_target_pairs={{0,1},{1,0},{2,3},{3,2},{4,5},{5,4},{6,7},{7,6},{8,9},{9,8},{10,11... | collective-permute-start | bytes 196616 | tf_op jit(solution)/shard_map/ppermute | solution.py:697
  46.8 3.7 %collective-permute-done.9 = f32[8,8,256]{2,1,0:T(8,128)S(1)} collective-permute-done((f32[8,8,256]{2,1,0:T(8,128)S(1)}, f32[8,8,256]{2,1,0:T(8,128)S(1)}, u32[]{:S(2)}, u32[]{:S(2)}) %collective-permute-start.9) | collective-permute-done | bytes 65568 | tf_op jit(solution)/shard_map/ppermute | solution.py:697
  50.5 0.6 %add.3 = f32[8,8,256]{2,1,0:T(8,128)} add(f32[8,8,256]{2,1,0:T(8,128)S(1)} %get-tuple-element.47, f32[8,8,256]{2,1,0:T(8,128)S(1)} %collective-permute-done.9) | non-fusion elementwise | flops 16384 | bytes 196608 | tf_op jit(solution)/shard_map/add | solution.py:697
  (1 shorter events, 0.0 us)
Async XLA Ops:
  2.8 14.5 %collective-permute-start = (f32[56,8,256]{2,1,0:T(8,128)}, f32[56,8,256]{2,1,0:T(8,128)S(1)}, u32[]{:S(2)}, u32[]{:S(2)}) collective-permute-start(f32[56,8,256]{2,1,0:T(8,128)} %get-tuple-element.26.refs_0_), channel_id=1, source_target_pairs={{0,1},{1,0},{2,3},{3,2},{4,5},{5,4},{6,7},{7,6},{8,9},{9,8},{10,11... | collective-permute-start | bytes 1376264 | tf_op jit(solution)/shard_map/ppermute | solution.py:609
  4.3 12.5 %collective-permute-start.1 = (f32[42,8,256]{2,1,0:T(8,128)}, f32[42,8,256]{2,1,0:T(8,128)S(1)}, u32[]{:S(2)}, u32[]{:S(2)}) collective-permute-start(f32[42,8,256]{2,1,0:T(8,128)} %get-tuple-element.27), channel_id=1, source_target_pairs={{2,4},{6,8},{10,12},{14,16},{18,20},{22,24},{26,28},{4,2},{8,6},{1... | collective-permute-start | bytes 1032200 | tf_op jit(solution)/shard_map/ppermute | solution.py:617
  9.2 1.3 %copy-start.9 = (f32[4,2,3,3,16,256]{5,4,3,2,1,0:T(8,128)S(1)}, f32[4,2,3,3,16,256]{5,4,3,2,1,0:T(8,128)}, u32[]{:S(2)}) copy-start(f32[4,2,3,3,16,256]{5,4,3,2,1,0:T(8,128)} %get-tuple-element.33) | copy-start | bytes 3538948
  9.3 30.0 %collective-permute-start.6 = (f32[4,2,3,3,16,256]{5,4,3,2,1,0:T(8,128)}, f32[4,2,3,3,16,256]{5,4,3,2,1,0:T(8,128)S(1)}, u32[]{:S(2)}, u32[]{:S(2)}) collective-permute-start(f32[4,2,3,3,16,256]{5,4,3,2,1,0:T(8,128)} %second_edges.1), channel_id=1, source_target_pairs={{6,8},{14,16},{22,24},{8,6},{16,14},{24,22},{7,9},{15,17},{23,25},... | collective-permute-start | bytes 3538952 | tf_op jit(solution)/shard_map/ppermute | solution.py:644
  10.5 31.6 %collective-permute-start.5 = (f32[4,2,3,3,16,256]{5,4,3,2,1,0:T(8,128)S(1)}, f32[4,2,3,3,16,256]{5,4,3,2,1,0:T(8,128)S(1)}, u32[]{:S(2)}, u32[]{:S(2)}) collective-permute-start(f32[4,2,3,3,16,256]{5,4,3,2,1,0:T(8,128)S(1)} %copy-done.9), channel_id=1, source_target_pairs={{2,4},{10,12},{18,20},{26,28},{4,2},{12,10},{20,18},{28,26},{3,5},... | collective-permute-start | bytes 3538952 | tf_op jit(solution)/shard_map/ppermute | solution.py:643
  14.1 6.2 %collective-permute-start.3 = (f32[42,8,256]{2,1,0:T(8,128)}, f32[42,8,256]{2,1,0:T(8,128)S(1)}, u32[]{:S(2)}, u32[]{:S(2)}) collective-permute-start(f32[42,8,256]{2,1,0:T(8,128)} %get-tuple-element.28), channel_id=1, source_target_pairs={{0,2},{4,6},{8,10},{12,14},{16,18},{20,22},{24,26},{28,30},{2,0},{... | collective-permute-start | bytes 1032200 | tf_op jit(solution)/shard_map/ppermute | solution.py:641
  16.8 9.7 %collective-permute-start.2 = (f32[42,8,256]{2,1,0:T(8,128)S(1)}, f32[42,8,256]{2,1,0:T(8,128)S(1)}, u32[]{:S(2)}, u32[]{:S(2)}) collective-permute-start(f32[42,8,256]{2,1,0:T(8,128)S(1)} %collective-permute-done.1.refs_1_.refs_2_), channel_id=1, source_target_pairs={{0,1},{1,0},{2,3},{3,2},{4,5},{5,4},{6,7},{7,6},{8,9},{9,8},{10,11... | collective-permute-start | bytes 1032200 | tf_op jit(solution)/shard_map/ppermute | solution.py:609
  17.4 0.6 %copy-start.2 = (f32[8,128]{1,0:T(8,128)}, f32[8,128]{1,0:T(8,128)S(1)}, u32[]{:S(2)}) copy-start(f32[8,128]{1,0:T(8,128)S(1)} %get-tuple-element.35.after) | copy-start | bytes 12292
  18.0 8.6 %collective-permute-start.4 = (f32[1,42,8,256]{3,2,1,0:T(8,128)S(1)}, f32[1,42,8,256]{3,2,1,0:T(8,128)S(1)}, u32[]{:S(2)}, u32[]{:S(2)}) collective-permute-start(f32[1,42,8,256]{3,2,1,0:T(8,128)S(1)} %get-tuple-element.29), channel_id=1, source_target_pairs={{0,2},{4,6},{8,10},{12,14},{16,18},{20,22},{24,26},{28,30},{2,0},{... | collective-permute-start | bytes 1032200 | tf_op jit(solution)/shard_map/ppermute | solution.py:641
  18.0 8.6 %copy-start.4 = (f32[56,8,256]{2,1,0:T(8,128)S(1)}, f32[56,8,256]{2,1,0:T(8,128)}, u32[]{:S(2)}) copy-start(f32[56,8,256]{2,1,0:T(8,128)} %get-tuple-element.26.refs_0_) | copy-start | bytes 1376260
  18.0 8.6 %copy-start.5 = (f32[4,8]{1,0:T(4,128)S(1)}, f32[4,8]{1,0:T(4,128)}, u32[]{:S(2)}) copy-start(f32[4,8]{1,0:T(4,128)} %refs_8_.1) | copy-start | bytes 388
  18.0 8.6 %copy-start.6 = (s32[4]{0:T(128)S(1)}, s32[4]{0:T(128)}, u32[]{:S(2)}) copy-start(s32[4]{0:T(128)} %refs_6_.1) | copy-start | bytes 52
  18.0 8.6 %copy-start.7 = (f32[4]{0:T(128)S(1)}, f32[4]{0:T(128)}, u32[]{:S(2)}) copy-start(f32[4]{0:T(128)} %refs_7_.1) | copy-start | bytes 52
  18.0 8.6 %copy-start.8 = (f32[4]{0:T(128)S(1)}, f32[4]{0:T(128)}, u32[]{:S(2)}) copy-start(f32[4]{0:T(128)} %refs_9_.1) | copy-start | bytes 52
  20.3 21.8 %collective-permute-start.7 = (f32[4,2,3,2,16,256]{5,4,3,2,1,0:T(8,128)}, f32[4,2,3,2,16,256]{5,4,3,2,1,0:T(8,128)S(1)}, u32[]{:S(2)}, u32[]{:S(2)}) collective-permute-start(f32[4,2,3,2,16,256]{5,4,3,2,1,0:T(8,128)} %get-tuple-element.38), channel_id=1, source_target_pairs={{0,2},{4,6},{8,10},{12,14},{16,18},{20,22},{24,26},{28,30},{2,0},{... | collective-permute-start | bytes 2359304 | tf_op jit(solution)/shard_map/ppermute | solution.py:645
  26.5 7.5 %copy-start.3 = (s32[8]{0:T(128)S(1)}, s32[8]{0:T(128)}, u32[]{:S(2)}) copy-start(s32[8]{0:T(128)} %harmonic_numbers.3) | copy-start | bytes 100
  26.5 12.7 %collective-permute-start.8 = (f32[4,2,3,1,16,256]{5,4,3,2,1,0:T(8,128)}, f32[4,2,3,1,16,256]{5,4,3,2,1,0:T(8,128)S(1)}, u32[]{:S(2)}, u32[]{:S(2)}) collective-permute-start(f32[4,2,3,1,16,256]{5,4,3,2,1,0:T(8,128)} %get-tuple-element.39), channel_id=1, source_target_pairs={{0,2},{4,6},{8,10},{12,14},{16,18},{20,22},{24,26},{28,30},{2,0},{... | collective-permute-start | bytes 1179656 | tf_op jit(solution)/shard_map/ppermute | solution.py:645
  26.6 7.4 %copy-start = (f32[4,2,3,8,16,256]{5,4,3,2,1,0:T(8,128)S(1)}, f32[4,2,3,8,16,256]{5,4,3,2,1,0:T(8,128)}, u32[]{:S(2)}) copy-start(f32[4,2,3,8,16,256]{5,4,3,2,1,0:T(8,128)} %start.11) | copy-start | bytes 9437188
  26.6 7.4 %copy-start.1 = (f32[4,2,3,8,16,256]{5,4,3,2,1,0:T(8,128)S(1)}, f32[4,2,3,8,16,256]{5,4,3,2,1,0:T(8,128)}, u32[]{:S(2)}) copy-start(f32[4,2,3,8,16,256]{5,4,3,2,1,0:T(8,128)} %source.11) | copy-start | bytes 9437188
  46.2 4.3 %collective-permute-start.9 = (f32[8,8,256]{2,1,0:T(8,128)S(1)}, f32[8,8,256]{2,1,0:T(8,128)S(1)}, u32[]{:S(2)}, u32[]{:S(2)}) collective-permute-start(f32[8,8,256]{2,1,0:T(8,128)S(1)} %get-tuple-element.48), channel_id=1, source_target_pairs={{0,1},{1,0},{2,3},{3,2},{4,5},{5,4},{6,7},{7,6},{8,9},{9,8},{10,11... | collective-permute-start | bytes 196616 | tf_op jit(solution)/shard_map/ppermute | solution.py:697

commit v6 on v5

--- a/solution.py
+++ b/solution.py
@@ -210,31 +210,20 @@
     return lax.rem(lax.axis_index("mesh") + 1, 4) < 2
 
 
-def edge_copies(start, source, buffer, target, top, sems, harmonics):
+def send_edges(start, source, buffer, target, top, sems):
     planes = start.shape[3]
     ways_in = []
     for part, (origin, count, onto) in enumerate(((start, 2, 0), (source, 1, 2))):
         at = jnp.where(top, planes - count, 0)
         ways_in.append(
-            pltpu.make_async_copy(
-                planes_of(origin.at[harmonics], at, count), planes_of(buffer.at[harmonics], onto, count), sems.at[part]
-            )
+            pltpu.make_async_copy(planes_of(origin, at, count), planes_of(buffer, onto, count), sems.at[part])
         )
         ways_in[-1].start()
-    return ways_in, pltpu.make_async_copy(buffer.at[harmonics], target, sems.at[2])
-
-
-def send_edges(start, source, buffer, targets, top, sems, parts):
-    ways = [
-        edge_copies(start, source, buffer, target, top, sems.at[at], harmonics)
-        for at, (target, harmonics) in enumerate(zip(targets, parts))
-    ]
-    for ways_in, way_out in ways:
-        for copy in ways_in:
-            copy.wait()
-        way_out.start()
-    for unused, way_out in ways:
-        way_out.wait()
+    for copy in ways_in:
+        copy.wait()
+    way_out = pltpu.make_async_copy(buffer, target, sems.at[2])
+    way_out.start()
+    way_out.wait()
 
 
 def send_near_edges(start, source, targets, buffers, sems):
@@ -259,13 +248,14 @@
         way_out.wait()
 
 
-def first_edges_kernel(parts, start, source, after, *refs):
-    aparts, (paired_start, paired_source, token, buffer, other_buffer, sems, near_sems) = refs[:len(parts)], refs[len(parts):]
+def first_edges_kernel(
+    start, source, after, apart, paired_start, paired_source, token, buffer, other_buffer, sems, near_sems
+):
     token[...] = jnp.zeros(token.shape, token.dtype)
 
     @pl.when(jnp.logical_not(is_second()))
     def send_apart():
-        send_edges(start, source, buffer, aparts, is_odd(), sems, parts)
+        send_edges(start, source, buffer, apart, is_odd(), sems)
 
     @pl.when(is_second())
     def send_near():
@@ -278,12 +268,10 @@
         send_near_edges(start, source, (paired_start, paired_source), (buffer, other_buffer), sems)
 
 
-def second_edges_kernel(parts, start, source, after, *refs):
-    aparts, (buffer, sems) = refs[:len(parts)], refs[len(parts):]
-
+def second_edges_kernel(start, source, after, apart, buffer, sems):
     @pl.when(is_second())
     def send_apart():
-        send_edges(start, source, buffer, aparts, is_odd(), sems, parts)
+        send_edges(start, source, buffer, apart, is_odd(), sems)
 
 
 def bias_kernel(shares, meshes, *refs):
@@ -425,22 +413,22 @@
                 scaled = tiles.each(lambda one, other: one * other, value, inverse)
                 tiles.store(self.answer, (harmonic, part, slot), scaled)
 
-    def sweep(self, slot, harmonics, old, source, put):
+    def sweep(self, slot, old, source, put, turned_round=0):
         tiles, loss = self.tiles, None
-        weights = [tiles.load(self.sides, number, slot) for number in range(6)]
-        for harmonic in harmonics:
+        weights = [tiles.load(self.sides, number, slot) for number in (turned_round, 1 - turned_round, 2, 3, 4, 5)]
+        for harmonic in range(len(self.omegas)):
             straight, turned = (tiles.load(self.answer, harmonic, part, slot) for part in range(2))
             power = None
             for part in range(3):
                 both = []
                 for piece in range(2):
-                    near_old = [tiles.load(*old(move, harmonic, piece, part)) for move in (0, 1, -1)]
-                    both.append(pull(tiles, tiles.load(*source(harmonic, piece, part)), weights, *near_old))
+                    lead = (harmonic, piece, part)
+                    near_old = [tiles.load(ref, *lead, at) for ref, at in old]
+                    both.append(pull(tiles, tiles.load(source[0], *lead, source[1]), weights, *near_old))
                 real = tiles.each(lambda re, im, a, b: re * a + im * b, *both, straight, turned)
                 imag = tiles.each(lambda re, im, a, b: im * a - re * b, *both, straight, turned)
                 for piece, value in enumerate((real, imag)):
-                    where = put(harmonic, piece, part)
-                    tiles.store(where[0], where[1:], value)
+                    tiles.store(put[0], (harmonic, piece, part, put[1]), value)
                 squared = tiles.each(lambda re, im: re * re + im * im, real, imag)
                 power = tiles.each(lambda one, other: one + other, power, squared) if part else squared
             factor = 0.5 * self.omegas[harmonic] * self.omegas[harmonic]
@@ -449,11 +437,34 @@
         return loss
 
 
+class Side:
+    def __init__(self, planes, high):
+        pick = lambda above, below: jnp.where(high, above, below)
+        self.turned_round = pick(1, 0)
+        self.own, self.second = pick(planes - 1, 0), pick(planes - 2, 1)
+        self.beyond_slot, self.own_slot, self.second_slot = pick(planes + 1, 0), pick(planes, 1), pick(planes - 1, 2)
+        self.halo, self.far_halo = pick(0, 1), pick(1, 0)
+        self.third = pick(planes - 3, 2)
+
+
+def first_on_side(ripple, side, start, source, halo_start, halo_source, put_beyond, put_own):
+    ripple.sweep(
+        side.beyond_slot, [(halo_start, side.halo), (start, side.own), (halo_start, side.far_halo)], (halo_source, 0),
+        put_beyond, side.turned_round,
+    )
+    ripple.sweep(
+        side.own_slot, [(start, side.own), (start, side.second), (halo_start, side.halo)], (source, side.own),
+        put_own, side.turned_round,
+    )
+
+
 def inner_kernel(
-    meshes, harmonic_numbers, nud, sigma, start, source, ripple_out, edge_out, loss_out, sides, answer, r1, r2, sems
+    meshes, harmonic_numbers, nud, sigma, start, source, paired_start, paired_source, ripple_out, edge_out, loss_out,
+    sides, answer, r1, r2, sems
 ):
     count, planes = start.shape[0], start.shape[3]
     here = lax.axis_index("mesh")
+    odd = is_odd()
     ripple = Ripple(*start.shape[4:], harmonic_numbers, count, sides, answer)
     tiles = ripple.tiles
 
@@ -465,112 +476,85 @@
     def drain(plane):
         return pltpu.make_async_copy(planes_of(r2, plane, 1), planes_of(ripple_out, plane, 1), sems.at[plane])
 
-    def sweep(plane, old, new):
-        return ripple.sweep(
-            plane + 1, range(count), lambda move, *lead: (old, *lead, plane + move), lambda *lead: (source, *lead, plane),
-            lambda *lead: (new, *lead, plane),
+    def first(plane, carry):
+        ripple.sweep(
+            plane + 1, [(start, plane), (start, plane + 1), (start, plane - 1)], (source, plane), (r1, plane + 1)
         )
-
-    def first(plane, carry):
-        sweep(plane, start, r1)
         return carry
 
     def second(plane, carry):
-        loss = sweep(plane, r1, r2)
+        loss = ripple.sweep(
+            plane + 1, [(r1, plane + 1), (r1, plane + 2), (r1, plane)], (source, plane), (r2, plane)
+        )
         tiles.store(loss_out, (plane,), tiles.each(lambda one, other: one * other, tiles.load(sigma, plane + 1), loss))
         drain(plane).start()
         return carry
 
+    def finish(plane, carry):
+        drain(plane).wait()
+        return carry
+
+    near, far = Side(planes, jnp.logical_not(odd)), Side(planes, odd)
     loop_in_pairs(planes + 2, prepare)
     lax.fori_loop(1, planes - 1, first, 0)
-    lax.fori_loop(2, planes - 2, second, 0)
-    for place, onto in ((1, 0), (planes - 3, 2)):
-        edge_out[:, :, :, onto:onto + 2] = r1[:, :, :, place:place + 2]
-    for plane in range(2, planes - 2):
-        drain(plane).wait()
+    first_on_side(
+        ripple, near, start, source, paired_start, paired_source, (r1, near.beyond_slot), (r1, near.own_slot)
+    )
+    begin, end = jnp.where(odd, 0, 2), jnp.where(odd, planes - 2, planes)
+    lax.fori_loop(begin, end, second, 0)
+    for onto, plane in enumerate((far.second, far.third)):
+        edge_out[:, :, :, onto] = r1[:, :, :, plane + 1]
+    lax.fori_loop(begin, end, finish, 0)
 
 
 def outer_kernel(
-    harmonics, shares, harmonic_numbers, sigma, start, source, first_apart, second_apart, paired_start, paired_source, edge, sides, answer,
-    loss_in, so_far, ripple_in, ripple_out, *refs
+    shares, harmonic_numbers, sigma, start, source, first_apart, second_apart, edge, sides, answer, loss_in, ripple_in,
+    ripple_out, *refs
 ):
-    losses, (r0, r1, r2, src, loss, sems, halo_sems) = refs[:-7], refs[-7:]
+    losses, (halo_start, halo_source, r1, r2, loss, sems, halo_sems) = refs[:shares], refs[shares:]
     count, planes = start.shape[0], start.shape[3]
     rows, lanes = start.shape[4:]
-    begin, chosen = harmonics.start, slice(harmonics.start, harmonics.stop)
-    odd = is_odd()
-
-    def halo(start_part, source_part, above, number):
+
+    def halo(origin):
         return [
-            pltpu.make_async_copy(start_part, planes_of(r0, jnp.where(above, 2, 0), 2), halo_sems.at[number]),
-            pltpu.make_async_copy(source_part, planes_of(src, jnp.where(above, 1, 0), 1), halo_sems.at[number + 1]),
+            pltpu.make_async_copy(planes_of(origin, 0, 2), halo_start, halo_sems.at[0]),
+            pltpu.make_async_copy(planes_of(origin, 2, 1), halo_source, halo_sems.at[1]),
         ]
 
-    def apart_halo(origin):
-        return halo(planes_of(origin, 0, 2), planes_of(origin, 2, 1), odd, 0)
-
-    for second, origin in ((False, first_apart), (True, second_apart.at[chosen])):
+    for second, origin in ((False, first_apart), (True, second_apart)):
 
         @pl.when(is_second() == second)
-        def start_apart():
-            for copy in apart_halo(origin):
+        def bring_halo():
+            for copy in halo(origin):
                 copy.start()
-
-    near = halo(paired_start.at[chosen], paired_source.at[chosen], jnp.logical_not(odd), 2)
-    for copy in near:
-        copy.start()
-    for copy in apart_halo(first_apart) + near:
-        copy.wait()
+            for copy in halo(origin):
+                copy.wait()
+
+    far = Side(planes, is_odd())
     ripple = Ripple(rows, lanes, harmonic_numbers, count, sides, answer)
     tiles = ripple.tiles
-    old = {-2: (r0, 0), -1: (r0, 1), planes: (r0, 2), planes + 1: (r0, 3)}
-    old.update({plane: (start, plane) for plane in (0, 1, planes - 2, planes - 1)})
-    new = {-1: (r1, 0), 0: (r1, 1), planes - 1: (r1, 2), planes: (r1, 3)}
-    new.update({1: (edge, 0), 2: (edge, 1), planes - 3: (edge, 2), planes - 2: (edge, 3)})
-    given = {-1: (src, 0), planes: (src, 1)}
-    given.update({plane: (source, plane) for plane in (0, 1, planes - 2, planes - 1)})
-
-    def at(place, harmonic, *lead):
-        ref, slot = place
-        shift = 0 if ref.shape[0] == count else begin
-        return (ref, harmonic - shift, *lead, slot)
-
-    for plane in (-1, 0, planes - 1, planes):
-        ripple.sweep(
-            plane + 1, harmonics, lambda move, *lead: at(old[plane + move], *lead), lambda *lead: at(given[plane], *lead),
-            lambda *lead: at(new[plane], *lead),
-        )
+    first_on_side(ripple, far, start, source, halo_start, halo_source, (r1, 0), (r1, 1))
 
     def drain(slot, plane):
-        return pltpu.make_async_copy(
-            planes_of(r2, slot, 1), planes_of(ripple_out.at[chosen], plane, 1), sems.at[slot]
-        )
-
-    edges = list(enumerate((0, 1, planes - 2, planes - 1)))
-    last = harmonics.stop == count
-    for slot, plane in edges:
-        added = ripple.sweep(
-            plane + 1, harmonics, lambda move, *lead: at(new[plane + move], *lead), lambda *lead: at(given[plane], *lead),
-            lambda *lead: at((r2, slot), *lead),
-        )
-        drain(slot, plane).start()
-        if begin:
-            added = tiles.each(lambda one, other: one + other, added, tiles.load(so_far, slot))
-        if last:
-            added = tiles.each(lambda one, other: one * other, tiles.load(sigma, plane + 1), added)
-            tiles.store(loss, (slot,), added)
-        else:
-            tiles.store(losses[0], (slot,), added)
-    if last:
-        rows_each = rows // shares
-        for turn in range(shares):
-            owner = lax.rem(lax.axis_index("harm") + turn, shares)
-            part = pl.ds(pl.multiple_of(owner * rows_each, rows_each), rows_each)
-            losses[turn][2:planes - 2] = loss_in[2:planes - 2, part, :]
-            for slot, plane in edges:
-                losses[turn][plane] = loss[slot, part, :]
-    for slot, plane in edges:
-        drain(slot, plane).wait()
+        return pltpu.make_async_copy(planes_of(r2, slot, 1), planes_of(ripple_out, plane, 1), sems.at[slot])
+
+    steps = (
+        (far.own, far.own_slot, [(r1, 1), (edge, 0), (r1, 0)]),
+        (far.second, far.second_slot, [(edge, 0), (edge, 1), (r1, 1)]),
+    )
+    for at, (plane, slot, old) in enumerate(steps):
+        added = ripple.sweep(slot, old, (source, plane), (r2, at), far.turned_round)
+        drain(at, plane).start()
+        tiles.store(loss, (at,), tiles.each(lambda one, other: one * other, tiles.load(sigma, slot), added))
+    rows_each = rows // shares
+    for turn in range(shares):
+        owner = lax.rem(lax.axis_index("harm") + turn, shares)
+        part = pl.ds(pl.multiple_of(owner * rows_each, rows_each), rows_each)
+        losses[turn][...] = loss_in[:, part, :]
+        for at, (plane, unused, unused_too) in enumerate(steps):
+            losses[turn][plane] = loss[at, part, :]
+    for at, (plane, unused, unused_too) in enumerate(steps):
+        drain(at, plane).wait()
 
 
 def call(kernel, operands, in_specs, out_shapes, out_specs, scratch, name, work=0, aliases={}, room=0):
@@ -616,18 +600,15 @@
     wholes = around(whole)
     aparts = around(lax.ppermute(apart, "mesh", far))
     edge = ripple_start.shape[:3] + (3, rows, lanes)
-    parts = [range(0, count)]
-    spans = [slice(part.start, part.stop) for part in parts]
     near_edges = [edge[:3] + (size, rows, lanes) for size in (2, 1)]
-    part_edges = [(len(part), *edge[1:]) for part in parts]
-    *ripple_firsts, paired_start, paired_source, token = call(
-        functools.partial(first_edges_kernel, spans), (ripple_start, ripple_source, token), [ANY] * 3,
-        part_edges + near_edges + [TILE], [ANY] * (len(parts) + 2) + [VMEM],
-        [edge, edge, pltpu.SemaphoreType.DMA((len(parts), 3)), pltpu.SemaphoreType.DMA((4,))], "first_edges", room=RP_ROOM,
-    )
-    ripple_seconds = call(
-        functools.partial(second_edges_kernel, spans), (ripple_start, ripple_source, token), [ANY] * 3,
-        part_edges, [ANY] * len(parts), [edge, pltpu.SemaphoreType.DMA((len(parts), 3))], "second_edges", room=RP_ROOM,
+    ripple_first, paired_start, paired_source, token = call(
+        first_edges_kernel, (ripple_start, ripple_source, token), [ANY] * 3,
+        [edge] + near_edges + [TILE], [ANY] * 3 + [VMEM],
+        [edge, edge, pltpu.SemaphoreType.DMA((3,)), pltpu.SemaphoreType.DMA((4,))], "first_edges", room=RP_ROOM,
+    )
+    ripple_second, = call(
+        second_edges_kernel, (ripple_start, ripple_source, token), [ANY] * 3, [edge], [ANY],
+        [edge, pltpu.SemaphoreType.DMA((3,))], "second_edges", room=RP_ROOM,
     )
     others, token = call(
         pair_kernel, (*wholes[1:], aparts[0]), [VMEM] * (shares - 1) + [ANY],
@@ -640,8 +621,8 @@
     )
     paireds = [lax.ppermute(paired, "mesh", near), lax.ppermute(others, "mesh", near)]
     first_pairs, second_pairs = ([pair for pair in far if min(pair) % 4 == kind] for kind in (1, 3))
-    ripple_firsts = [lax.ppermute(part, "mesh", first_pairs) for part in ripple_firsts]
-    ripple_seconds = [lax.ppermute(part, "mesh", second_pairs) for part in ripple_seconds]
+    ripple_first = lax.ppermute(ripple_first, "mesh", first_pairs)
+    ripple_second = lax.ppermute(ripple_second, "mesh", second_pairs)
     ripple_paireds = [lax.ppermute(part, "mesh", near) for part in ripple_paireds]
 
     known = (planes + G_LOW + G_HIGH, rows, lanes)
@@ -668,30 +649,25 @@
 
     lead = ripple_start.shape[:3]
     slots = (planes + 2, rows, lanes)
-    ripple, inner_edge, inner_loss, sides, answer = call(
-        functools.partial(inner_kernel, meshes), (harmonic_numbers, nud, sigma, ripple_start, ripple_source),
-        [SMEM] + [VMEM] * 4,
-        [ripple_start.shape, lead + (4, rows, lanes), (planes, rows, lanes), (6, *slots), (count, 2, *slots)],
-        [ANY] + [VMEM] * 4, [lead + (planes, rows, lanes)] * 2 + [pltpu.SemaphoreType.DMA((planes,))], "inner_ripple",
-    )
-    so_far = inner_loss
-    for part, ripple_first, ripple_second in zip(parts, ripple_firsts, ripple_seconds):
-        last = part.stop == count
-        here = (len(part), *lead[1:])
-        ripple, *losses = call(
-            functools.partial(outer_kernel, part, shares),
-            (
-                harmonic_numbers, sigma, ripple_start, ripple_source, ripple_first, ripple_second, *ripple_paireds,
-                inner_edge, sides, answer, inner_loss, so_far, ripple,
-            ),
-            [SMEM] + [VMEM] * 3 + [ANY] * 4 + [VMEM] * 5 + [ANY],
-            [ripple_start.shape] + ([(planes, rows_each, lanes)] * shares if last else [(4, rows, lanes)]),
-            [ANY] + [VMEM] * (shares if last else 1),
-            [here + (4, rows, lanes)] * 3 + [here + (2, rows, lanes), (4, rows, lanes)]
-            + [pltpu.SemaphoreType.DMA((4,))] * 2,
-            "outer_ripple", aliases={13: 0},
-        )
-        so_far = losses[0]
+    ripple, edge, inner_loss, sides, answer = call(
+        functools.partial(inner_kernel, meshes),
+        (harmonic_numbers, nud, sigma, ripple_start, ripple_source, *ripple_paireds), [SMEM] + [VMEM] * 6,
+        [ripple_start.shape, lead + (2, rows, lanes), (planes, rows, lanes), (6, *slots), (count, 2, *slots)],
+        [ANY] + [VMEM] * 4, [lead + slots, lead + (planes, rows, lanes), pltpu.SemaphoreType.DMA((planes,))],
+        "inner_ripple",
+    )
+    ripple, *losses = call(
+        functools.partial(outer_kernel, shares),
+        (
+            harmonic_numbers, sigma, ripple_start, ripple_source, ripple_first, ripple_second, edge, sides, answer,
+            inner_loss, ripple,
+        ),
+        [SMEM] + [VMEM] * 3 + [ANY] * 2 + [VMEM] * 4 + [ANY],
+        [ripple_start.shape] + [(planes, rows_each, lanes)] * shares, [ANY] + [VMEM] * shares,
+        [lead + (size, rows, lanes) for size in (2, 1, 2, 2)] + [(2, rows, lanes)]
+        + [pltpu.SemaphoreType.DMA((2,))] * 2,
+        "outer_ripple", aliases={10: 0},
+    )
     loss = losses[0]
     for turn, pairs in enumerate(turned):
         loss = loss + lax.ppermute(losses[turn + 1], "harm", pairs)

time: 51.4 us -> 50.1 us (0.975)
  waiting for transfers between devices: 13.1 us -> 11.8 us
    ppermute x2, waiting for transfers between devices: 2.84 us -> 1.52 us  [the longest x1 1.52 us: body(): ripple_first = lax.ppermute(ripple_first, 'mesh', first_pairs)]
  transfers between devices with their start and end apart: 10 -> 10, of which waited for: 4 -> 4; matrix products, arithmetic and copies ran while one was open for 0% -> 0% of each run, Pallas kernels for 35% -> 38%
where the time goes in v6:
time: 50.1 us; the launch traced here: 49.8 us
  Pallas kernels  24.1 us (48%)
  waiting for transfers between devices  11.8 us (24%)
  starting transfers between devices  11.5 us (23%)
  local copies, waits for them, and re-layouts  0.96 us (2%)
  between operations  0.86 us (2%)
  other arithmetic  0.64 us (1%)
    pallas_call x8, Pallas kernels, call(): pl.pallas_call(kernel, out_shape=[jax.ShapeDtypeStruct(shape, f32) for sh...  24.1 us
    ppermute x2, waiting for transfers between devices, around(): return [block] + [lax.ppermute(block, 'harm', pairs) for pairs in turned]  6.17 us
    ppermute x1, waiting for transfers between devices, body(): loss = loss + lax.ppermute(losses[turn + 1], 'harm', pairs)  3.73 us
    ppermute x1, starting transfers between devices, body(): ripple_first = lax.ppermute(ripple_first, 'mesh', first_pairs)  3.63 us
    ppermute x1, starting transfers between devices, body(): lax.ppermute(paired, 'mesh', near)  2.36 us
    ppermute x2, starting transfers between devices, around(): return [block] + [lax.ppermute(block, 'harm', pairs) for pairs in turned]  2.09 us
    ppermute x1, starting transfers between devices, body(): aparts = around(lax.ppermute(apart, 'mesh', far))  1.91 us
    ppermute x1, waiting for transfers between devices, body(): ripple_first = lax.ppermute(ripple_first, 'mesh', first_pairs)  1.52 us
  transfers between devices with their start and end apart: 10, of which 4 were waited for; matrix products, arithmetic and copies ran while one was open for 0% of the time, Pallas kernels for 38%

profile of v6, /device:TPU:12, one launch (start us, length us, event | category | flops | bytes accessed | tf_op | source)
XLA Modules:
  0.0 49.8 jit_solution(5892902080871411229)
XLA Ops:
  0.6 2.2 %pack.1 = (f32[56,8,256]{2,1,0:T(8,128)}, f32[42,8,256]{2,1,0:T(8,128)}, f32[42,8,256]{2,1,0:T(8,128)}, f32[8,128]{1,0:T(8,128)}) custom-call(f32[3,8,8,256]{3,2,1,0:T(8,128)} %start.6, f32[3,8,8,256]{3,2,1,0:T(8,128)} %source.6, s32[8,8,256]{2,1,0:T(8,128)} %region.1), custom_call_target="tpu_custom_call" | custom-call | tf_op jit(solution)/shard_map/pack/pallas_call | solution.py:566
  2.8 1.6 %collective-permute-start = (f32[56,8,256]{2,1,0:T(8,128)}, f32[56,8,256]{2,1,0:T(8,128)S(1)}, u32[]{:S(2)}, u32[]{:S(2)}) collective-permute-start(f32[56,8,256]{2,1,0:T(8,128)} %get-tuple-element.26.refs_0_), channel_id=1, source_target_pairs={{0,1},{1,0},{2,3},{3,2},{4,5},{5,4},{6,7},{7,6},{8,9},{9,8},{10,11... | collective-permute-start | bytes 1376264 | tf_op jit(solution)/shard_map/ppermute | solution.py:593
  4.3 1.9 %collective-permute-start.1 = (f32[42,8,256]{2,1,0:T(8,128)}, f32[42,8,256]{2,1,0:T(8,128)S(1)}, u32[]{:S(2)}, u32[]{:S(2)}) collective-permute-start(f32[42,8,256]{2,1,0:T(8,128)} %get-tuple-element.27), channel_id=1, source_target_pairs={{2,4},{6,8},{10,12},{14,16},{18,20},{22,24},{26,28},{4,2},{8,6},{1... | collective-permute-start | bytes 1032200 | tf_op jit(solution)/shard_map/ppermute | solution.py:601
  6.3 2.9 %first_edges.1 = (f32[4,2,3,3,16,256]{5,4,3,2,1,0:T(8,128)}, f32[4,2,3,2,16,256]{5,4,3,2,1,0:T(8,128)}, f32[4,2,3,1,16,256]{5,4,3,2,1,0:T(8,128)}, f32[8,128]{1,0:T(8,128)}) custom-call(f32[4,2,3,8,16,256]{5,4,3,2,1,0:T(8,128)} %start.11, f32[4,2,3,8,16,256]{5,4,3,2,1,0:T(8,128)} %source.11, f32[8,128]{1,0:T(8,128)} %get-tuple-element.32.after), custom_call_target="tpu_custom_call" | custom-call | tf_op jit(solution)/shard_map/first_edges/pallas_call | solution.py:566
  9.2 0.0 copy-start.9
  9.2 0.1 second_edges.1
  9.3 0.9 %collective-permute-start.6 = (f32[4,2,3,3,16,256]{5,4,3,2,1,0:T(8,128)}, f32[4,2,3,3,16,256]{5,4,3,2,1,0:T(8,128)S(1)}, u32[]{:S(2)}, u32[]{:S(2)}) collective-permute-start(f32[4,2,3,3,16,256]{5,4,3,2,1,0:T(8,128)} %second_edges.1), channel_id=1, source_target_pairs={{6,8},{14,16},{22,24},{8,6},{16,14},{24,22},{7,9},{15,17},{23,25},... | collective-permute-start | bytes 3538952 | tf_op jit(solution)/shard_map/ppermute | solution.py:625
  10.1 0.3 copy-done.9
  10.5 3.6 %collective-permute-start.5 = (f32[4,2,3,3,16,256]{5,4,3,2,1,0:T(8,128)S(1)}, f32[4,2,3,3,16,256]{5,4,3,2,1,0:T(8,128)S(1)}, u32[]{:S(2)}, u32[]{:S(2)}) collective-permute-start(f32[4,2,3,3,16,256]{5,4,3,2,1,0:T(8,128)S(1)} %copy-done.9), channel_id=1, source_target_pairs={{2,4},{10,12},{18,20},{26,28},{4,2},{12,10},{20,18},{28,26},{3,5},... | collective-permute-start | bytes 3538952 | tf_op jit(solution)/shard_map/ppermute | solution.py:624
  14.1 2.4 %collective-permute-start.3 = (f32[42,8,256]{2,1,0:T(8,128)}, f32[42,8,256]{2,1,0:T(8,128)S(1)}, u32[]{:S(2)}, u32[]{:S(2)}) collective-permute-start(f32[42,8,256]{2,1,0:T(8,128)} %get-tuple-element.28), channel_id=1, source_target_pairs={{0,2},{4,6},{8,10},{12,14},{16,18},{20,22},{24,26},{28,30},{2,0},{... | collective-permute-start | bytes 1032200 | tf_op jit(solution)/shard_map/ppermute | solution.py:622
  16.5 0.3 collective-permute-done.1.refs_1_.refs_2_
  16.8 0.5 %collective-permute-start.2 = (f32[42,8,256]{2,1,0:T(8,128)S(1)}, f32[42,8,256]{2,1,0:T(8,128)S(1)}, u32[]{:S(2)}, u32[]{:S(2)}) collective-permute-start(f32[42,8,256]{2,1,0:T(8,128)S(1)} %collective-permute-done.1.refs_1_.refs_2_), channel_id=1, source_target_pairs={{0,1},{1,0},{2,3},{3,2},{4,5},{5,4},{6,7},{7,6},{8,9},{9,8},{10,11... | collective-permute-start | bytes 1032200 | tf_op jit(solution)/shard_map/ppermute | solution.py:593
  17.3 0.0 collective-permute-done.refs_0_.refs_1_
  17.4 0.0 copy-start.2
  17.4 0.6 %copy-done.2 = f32[8,128]{1,0:T(8,128)} copy-done((f32[8,128]{1,0:T(8,128)}, f32[8,128]{1,0:T(8,128)S(1)}, u32[]{:S(2)}) %copy-start.2) | copy-done | bytes 4120
  18.0 0.0 collective-permute-start.4
  18.0 0.0 copy-start.4
  18.0 0.0 copy-start.5
  18.0 0.0 copy-start.6
  18.0 0.0 copy-start.7
  18.0 0.0 copy-start.8
  18.0 2.3 %near_edges.1 = (f32[4,2,3,2,16,256]{5,4,3,2,1,0:T(8,128)}, f32[4,2,3,1,16,256]{5,4,3,2,1,0:T(8,128)}) custom-call(f32[4,2,3,8,16,256]{5,4,3,2,1,0:T(8,128)} %start.11, f32[4,2,3,8,16,256]{5,4,3,2,1,0:T(8,128)} %source.11, f32[8,128]{1,0:T(8,128)} %copy-done.2, ...), custom_call_target="tpu_custom_call", output_to_operand_aliasing={{0}: (3, {}), {1}: (4, {})} | custom-call | tf_op jit(solution)/shard_map/near_edges/pallas_call | solution.py:566
  20.3 0.0 collective-permute-done.3.refs_4_
  20.3 0.1 collective-permute-start.7
  20.3 6.2 %collective-permute-done.2.refs_3_ = f32[42,8,256]{2,1,0:T(8,128)S(1)} collective-permute-done((f32[42,8,256]{2,1,0:T(8,128)S(1)}, f32[42,8,256]{2,1,0:T(8,128)S(1)}, u32[]{:S(2)}, u32[]{:S(2)}) %collective-permute-start.2) | collective-permute-done | bytes 344096 | tf_op jit(solution)/shard_map/ppermute | solution.py:593
  26.5 0.0 copy-start.3
  26.5 0.0 collective-permute-start.8
  26.5 0.0 collective-permute-done.4.refs_5_
  26.5 0.0 copy-done.4
  26.5 0.0 copy-done.5
  26.6 0.0 copy-done.6
  26.6 0.0 copy-done.7
  26.6 0.0 copy-done.8
  26.6 0.0 copy-start
  26.6 0.0 copy-start.1
  26.6 7.4 %bias.1 = (f32[3,8,8,256]{3,2,1,0:T(8,128)}, f32[12,16,256]{2,1,0:T(8,128)S(1)}, f32[10,16,256]{2,1,0:T(8,128)S(1)}) custom-call(f32[56,8,256]{2,1,0:T(8,128)S(1)} %copy-done.4, f32[56,8,256]{2,1,0:T(8,128)S(1)} %collective-permute-done.refs_0_.refs_1_, f32[42,8,256]{2,1,0:T(8,128)S(1)} %collective-permute-done.1.refs_1_.refs_2_, ...), custom_call_target="tpu_custom_call" | custom-call | flops 6000000000 | bytes 20000000 | tf_op jit(solution)/shard_map/bias/pallas_call | solution.py:566
  34.0 0.0 collective-permute-done.8.paired_source
  34.0 0.0 collective-permute-done.7.paired_start
  34.0 0.0 copy-done.3
  34.0 0.0 copy-done
  34.0 0.0 copy-done.1
  34.0 6.5 %inner_ripple.1 = (f32[4,2,3,8,16,256]{5,4,3,2,1,0:T(8,128)}, f32[4,2,3,2,16,256]{5,4,3,2,1,0:T(8,128)S(1)}, f32[8,16,256]{2,1,0:T(8,128)S(1)}, f32[6,10,16,256]{3,2,1,0:T(8,128)S(1)}, f32[4,2,10,16,256]{4,3,2,1,0:T(8,128)S(1)}) custom-call(s32[8]{0:T(128)S(1)} %copy-done.3, f32[12,16,256]{2,1,0:T(8,128)S(1)} %get-tuple-element.35.nud, ...), custom_call_target="tpu_custom_call" | custom-call | tf_op jit(solution)/shard_map/inner_ripple/pallas_call | solution.py:566
  40.5 0.0 collective-permute-done.6.second_apart
  40.6 1.5 %collective-permute-done.5.first_apart = f32[4,2,3,3,16,256]{5,4,3,2,1,0:T(8,128)S(1)} collective-permute-done((f32[4,2,3,3,16,256]{5,4,3,2,1,0:T(8,128)S(1)}, f32[4,2,3,3,16,256]{5,4,3,2,1,0:T(8,128)S(1)}, u32[]{:S(2)}, u32[]{:S(2)}) %collective-permute-start.5) | collective-permute-done | bytes 1179680 | tf_op jit(solution)/shard_map/ppermute | solution.py:624
  42.1 2.8 %outer_ripple.1 = (f32[4,2,3,8,16,256]{5,4,3,2,1,0:T(8,128)}, f32[8,8,256]{2,1,0:T(8,128)S(1)}, f32[8,8,256]{2,1,0:T(8,128)S(1)}) custom-call(s32[8]{0:T(128)S(1)} %copy-done.3, f32[10,16,256]{2,1,0:T(8,128)S(1)} %get-tuple-element.31.sigma, f32[4,2,3,8,16,256]{5,4,3,2,1,0:T(8,128)S(1)} %copy-done, ...), custom_call_target="tpu_custom_call", output_to_operand_aliasing={{0}: (10, {})} | custom-call | tf_op jit(solution)/shard_map/outer_ripple/pallas_call | solution.py:566
  44.9 0.6 %collective-permute-start.9 = (f32[8,8,256]{2,1,0:T(8,128)S(1)}, f32[8,8,256]{2,1,0:T(8,128)S(1)}, u32[]{:S(2)}, u32[]{:S(2)}) collective-permute-start(f32[8,8,256]{2,1,0:T(8,128)S(1)} %get-tuple-element.48), channel_id=1, source_target_pairs={{0,1},{1,0},{2,3},{3,2},{4,5},{5,4},{6,7},{7,6},{8,9},{9,8},{10,11... | collective-permute-start | bytes 196616 | tf_op jit(solution)/shard_map/ppermute | solution.py:673
  45.5 3.7 %collective-permute-done.9 = f32[8,8,256]{2,1,0:T(8,128)S(1)} collective-permute-done((f32[8,8,256]{2,1,0:T(8,128)S(1)}, f32[8,8,256]{2,1,0:T(8,128)S(1)}, u32[]{:S(2)}, u32[]{:S(2)}) %collective-permute-start.9) | collective-permute-done | bytes 65568 | tf_op jit(solution)/shard_map/ppermute | solution.py:673
  49.2 0.6 %add.3 = f32[8,8,256]{2,1,0:T(8,128)} add(f32[8,8,256]{2,1,0:T(8,128)S(1)} %get-tuple-element.47, f32[8,8,256]{2,1,0:T(8,128)S(1)} %collective-permute-done.9) | non-fusion elementwise | flops 16384 | bytes 196608 | tf_op jit(solution)/shard_map/add | solution.py:673
  (1 shorter events, 0.0 us)
Async XLA Ops:
  2.8 14.5 %collective-permute-start = (f32[56,8,256]{2,1,0:T(8,128)}, f32[56,8,256]{2,1,0:T(8,128)S(1)}, u32[]{:S(2)}, u32[]{:S(2)}) collective-permute-start(f32[56,8,256]{2,1,0:T(8,128)} %get-tuple-element.26.refs_0_), channel_id=1, source_target_pairs={{0,1},{1,0},{2,3},{3,2},{4,5},{5,4},{6,7},{7,6},{8,9},{9,8},{10,11... | collective-permute-start | bytes 1376264 | tf_op jit(solution)/shard_map/ppermute | solution.py:593
  4.3 12.5 %collective-permute-start.1 = (f32[42,8,256]{2,1,0:T(8,128)}, f32[42,8,256]{2,1,0:T(8,128)S(1)}, u32[]{:S(2)}, u32[]{:S(2)}) collective-permute-start(f32[42,8,256]{2,1,0:T(8,128)} %get-tuple-element.27), channel_id=1, source_target_pairs={{2,4},{6,8},{10,12},{14,16},{18,20},{22,24},{26,28},{4,2},{8,6},{1... | collective-permute-start | bytes 1032200 | tf_op jit(solution)/shard_map/ppermute | solution.py:601
  9.2 1.3 %copy-start.9 = (f32[4,2,3,3,16,256]{5,4,3,2,1,0:T(8,128)S(1)}, f32[4,2,3,3,16,256]{5,4,3,2,1,0:T(8,128)}, u32[]{:S(2)}) copy-start(f32[4,2,3,3,16,256]{5,4,3,2,1,0:T(8,128)} %get-tuple-element.33) | copy-start | bytes 3538948
  9.3 31.3 %collective-permute-start.6 = (f32[4,2,3,3,16,256]{5,4,3,2,1,0:T(8,128)}, f32[4,2,3,3,16,256]{5,4,3,2,1,0:T(8,128)S(1)}, u32[]{:S(2)}, u32[]{:S(2)}) collective-permute-start(f32[4,2,3,3,16,256]{5,4,3,2,1,0:T(8,128)} %second_edges.1), channel_id=1, source_target_pairs={{6,8},{14,16},{22,24},{8,6},{16,14},{24,22},{7,9},{15,17},{23,25},... | collective-permute-start | bytes 3538952 | tf_op jit(solution)/shard_map/ppermute | solution.py:625
  10.5 31.6 %collective-permute-start.5 = (f32[4,2,3,3,16,256]{5,4,3,2,1,0:T(8,128)S(1)}, f32[4,2,3,3,16,256]{5,4,3,2,1,0:T(8,128)S(1)}, u32[]{:S(2)}, u32[]{:S(2)}) collective-permute-start(f32[4,2,3,3,16,256]{5,4,3,2,1,0:T(8,128)S(1)} %copy-done.9), channel_id=1, source_target_pairs={{2,4},{10,12},{18,20},{26,28},{4,2},{12,10},{20,18},{28,26},{3,5},... | collective-permute-start | bytes 3538952 | tf_op jit(solution)/shard_map/ppermute | solution.py:624
  14.1 6.2 %collective-permute-start.3 = (f32[42,8,256]{2,1,0:T(8,128)}, f32[42,8,256]{2,1,0:T(8,128)S(1)}, u32[]{:S(2)}, u32[]{:S(2)}) collective-permute-start(f32[42,8,256]{2,1,0:T(8,128)} %get-tuple-element.28), channel_id=1, source_target_pairs={{0,2},{4,6},{8,10},{12,14},{16,18},{20,22},{24,26},{28,30},{2,0},{... | collective-permute-start | bytes 1032200 | tf_op jit(solution)/shard_map/ppermute | solution.py:622
  16.8 9.7 %collective-permute-start.2 = (f32[42,8,256]{2,1,0:T(8,128)S(1)}, f32[42,8,256]{2,1,0:T(8,128)S(1)}, u32[]{:S(2)}, u32[]{:S(2)}) collective-permute-start(f32[42,8,256]{2,1,0:T(8,128)S(1)} %collective-permute-done.1.refs_1_.refs_2_), channel_id=1, source_target_pairs={{0,1},{1,0},{2,3},{3,2},{4,5},{5,4},{6,7},{7,6},{8,9},{9,8},{10,11... | collective-permute-start | bytes 1032200 | tf_op jit(solution)/shard_map/ppermute | solution.py:593
  17.4 0.6 %copy-start.2 = (f32[8,128]{1,0:T(8,128)}, f32[8,128]{1,0:T(8,128)S(1)}, u32[]{:S(2)}) copy-start(f32[8,128]{1,0:T(8,128)S(1)} %get-tuple-element.36.after) | copy-start | bytes 12292
  18.0 8.6 %collective-permute-start.4 = (f32[1,42,8,256]{3,2,1,0:T(8,128)S(1)}, f32[1,42,8,256]{3,2,1,0:T(8,128)S(1)}, u32[]{:S(2)}, u32[]{:S(2)}) collective-permute-start(f32[1,42,8,256]{3,2,1,0:T(8,128)S(1)} %get-tuple-element.29), channel_id=1, source_target_pairs={{0,2},{4,6},{8,10},{12,14},{16,18},{20,22},{24,26},{28,30},{2,0},{... | collective-permute-start | bytes 1032200 | tf_op jit(solution)/shard_map/ppermute | solution.py:622
  18.0 8.6 %copy-start.4 = (f32[56,8,256]{2,1,0:T(8,128)S(1)}, f32[56,8,256]{2,1,0:T(8,128)}, u32[]{:S(2)}) copy-start(f32[56,8,256]{2,1,0:T(8,128)} %get-tuple-element.26.refs_0_) | copy-start | bytes 1376260
  18.0 8.6 %copy-start.5 = (f32[4,8]{1,0:T(4,128)S(1)}, f32[4,8]{1,0:T(4,128)}, u32[]{:S(2)}) copy-start(f32[4,8]{1,0:T(4,128)} %refs_8_.1) | copy-start | bytes 388
  18.0 8.6 %copy-start.6 = (s32[4]{0:T(128)S(1)}, s32[4]{0:T(128)}, u32[]{:S(2)}) copy-start(s32[4]{0:T(128)} %refs_6_.1) | copy-start | bytes 52
  18.0 8.6 %copy-start.7 = (f32[4]{0:T(128)S(1)}, f32[4]{0:T(128)}, u32[]{:S(2)}) copy-start(f32[4]{0:T(128)} %refs_7_.1) | copy-start | bytes 52
  18.0 8.6 %copy-start.8 = (f32[4]{0:T(128)S(1)}, f32[4]{0:T(128)}, u32[]{:S(2)}) copy-start(f32[4]{0:T(128)} %refs_9_.1) | copy-start | bytes 52
  20.3 13.7 %collective-permute-start.7 = (f32[4,2,3,2,16,256]{5,4,3,2,1,0:T(8,128)}, f32[4,2,3,2,16,256]{5,4,3,2,1,0:T(8,128)S(1)}, u32[]{:S(2)}, u32[]{:S(2)}) collective-permute-start(f32[4,2,3,2,16,256]{5,4,3,2,1,0:T(8,128)} %get-tuple-element.39), channel_id=1, source_target_pairs={{0,2},{4,6},{8,10},{12,14},{16,18},{20,22},{24,26},{28,30},{2,0},{... | collective-permute-start | bytes 2359304 | tf_op jit(solution)/shard_map/ppermute | solution.py:626
  26.5 7.5 %copy-start.3 = (s32[8]{0:T(128)S(1)}, s32[8]{0:T(128)}, u32[]{:S(2)}) copy-start(s32[8]{0:T(128)} %harmonic_numbers.3) | copy-start | bytes 100
  26.5 7.5 %collective-permute-start.8 = (f32[4,2,3,1,16,256]{5,4,3,2,1,0:T(8,128)}, f32[4,2,3,1,16,256]{5,4,3,2,1,0:T(8,128)S(1)}, u32[]{:S(2)}, u32[]{:S(2)}) collective-permute-start(f32[4,2,3,1,16,256]{5,4,3,2,1,0:T(8,128)} %get-tuple-element.40), channel_id=1, source_target_pairs={{0,2},{4,6},{8,10},{12,14},{16,18},{20,22},{24,26},{28,30},{2,0},{... | collective-permute-start | bytes 1179656 | tf_op jit(solution)/shard_map/ppermute | solution.py:626
  26.6 7.4 %copy-start = (f32[4,2,3,8,16,256]{5,4,3,2,1,0:T(8,128)S(1)}, f32[4,2,3,8,16,256]{5,4,3,2,1,0:T(8,128)}, u32[]{:S(2)}) copy-start(f32[4,2,3,8,16,256]{5,4,3,2,1,0:T(8,128)} %start.11) | copy-start | bytes 9437188
  26.6 7.4 %copy-start.1 = (f32[4,2,3,8,16,256]{5,4,3,2,1,0:T(8,128)S(1)}, f32[4,2,3,8,16,256]{5,4,3,2,1,0:T(8,128)}, u32[]{:S(2)}) copy-start(f32[4,2,3,8,16,256]{5,4,3,2,1,0:T(8,128)} %source.11) | copy-start | bytes 9437188
  44.9 4.3 %collective-permute-start.9 = (f32[8,8,256]{2,1,0:T(8,128)S(1)}, f32[8,8,256]{2,1,0:T(8,128)S(1)}, u32[]{:S(2)}, u32[]{:S(2)}) collective-permute-start(f32[8,8,256]{2,1,0:T(8,128)S(1)} %get-tuple-element.48), channel_id=1, source_target_pairs={{0,1},{1,0},{2,3},{3,2},{4,5},{5,4},{6,7},{7,6},{8,9},{9,8},{10,11... | collective-permute-start | bytes 196616 | tf_op jit(solution)/shard_map/ppermute | solution.py:673

commit v7 on v6

--- a/solution.py
+++ b/solution.py
@@ -155,7 +155,7 @@
 
 
 LOW_SIZE = 3 * (A_LOW[0] + S_LOW) + G_LOW
-HIGH_SIZE = 3 * (A_HIGH[0] + S_HIGH) + G_HIGH
+HIGH_SIZE = 3 * (A_HIGH[0] + S_HIGH) + G_HIGH - 2
 
 
 def edge_parts(planes, low):
@@ -163,6 +163,8 @@
     at, parts = 0, []
     for array in range(7):
         halo = halo_of[0 if array < 3 else 1 if array < 6 else 2]
+        if not low and array in (0, 3):
+            halo -= 1
         parts.append((array * planes + (planes - halo if low else 0), at, halo))
         at += halo
     return parts
@@ -268,7 +270,7 @@
         send_near_edges(start, source, (paired_start, paired_source), (buffer, other_buffer), sems)
 
 
-def second_edges_kernel(start, source, after, apart, buffer, sems):
+def second_edges_kernel(start, source, after, apart_in, apart, buffer, sems):
     @pl.when(is_second())
     def send_apart():
         send_edges(start, source, buffer, apart, is_odd(), sems)
@@ -447,9 +449,10 @@
         self.third = pick(planes - 3, 2)
 
 
-def first_on_side(ripple, side, start, source, halo_start, halo_source, put_beyond, put_own):
+def first_on_side(ripple, side, start, source, halo_start, halo_source, put_beyond, put_own, source_at=0):
     ripple.sweep(
-        side.beyond_slot, [(halo_start, side.halo), (start, side.own), (halo_start, side.far_halo)], (halo_source, 0),
+        side.beyond_slot, [(halo_start, side.halo), (start, side.own), (halo_start, side.far_halo)],
+        (halo_source, source_at),
         put_beyond, side.turned_round,
     )
     ripple.sweep(
@@ -508,32 +511,17 @@
 
 
 def outer_kernel(
-    shares, harmonic_numbers, sigma, start, source, first_apart, second_apart, edge, sides, answer, loss_in, ripple_in,
+    shares, harmonic_numbers, sigma, start, source, apart, edge, sides, answer, loss_in, ripple_in,
     ripple_out, *refs
 ):
-    losses, (halo_start, halo_source, r1, r2, loss, sems, halo_sems) = refs[:shares], refs[shares:]
+    losses, (r1, r2, loss, sems) = refs[:shares], refs[shares:]
     count, planes = start.shape[0], start.shape[3]
     rows, lanes = start.shape[4:]
-
-    def halo(origin):
-        return [
-            pltpu.make_async_copy(planes_of(origin, 0, 2), halo_start, halo_sems.at[0]),
-            pltpu.make_async_copy(planes_of(origin, 2, 1), halo_source, halo_sems.at[1]),
-        ]
-
-    for second, origin in ((False, first_apart), (True, second_apart)):
-
-        @pl.when(is_second() == second)
-        def bring_halo():
-            for copy in halo(origin):
-                copy.start()
-            for copy in halo(origin):
-                copy.wait()
 
     far = Side(planes, is_odd())
     ripple = Ripple(rows, lanes, harmonic_numbers, count, sides, answer)
     tiles = ripple.tiles
-    first_on_side(ripple, far, start, source, halo_start, halo_source, (r1, 0), (r1, 1))
+    first_on_side(ripple, far, start, source, apart, apart, (r1, 0), (r1, 1), 2)
 
     def drain(slot, plane):
         return pltpu.make_async_copy(planes_of(r2, slot, 1), planes_of(ripple_out, plane, 1), sems.at[slot])
@@ -601,14 +589,14 @@
     aparts = around(lax.ppermute(apart, "mesh", far))
     edge = ripple_start.shape[:3] + (3, rows, lanes)
     near_edges = [edge[:3] + (size, rows, lanes) for size in (2, 1)]
-    ripple_first, paired_start, paired_source, token = call(
+    ripple_apart, paired_start, paired_source, token = call(
         first_edges_kernel, (ripple_start, ripple_source, token), [ANY] * 3,
         [edge] + near_edges + [TILE], [ANY] * 3 + [VMEM],
         [edge, edge, pltpu.SemaphoreType.DMA((3,)), pltpu.SemaphoreType.DMA((4,))], "first_edges", room=RP_ROOM,
     )
-    ripple_second, = call(
-        second_edges_kernel, (ripple_start, ripple_source, token), [ANY] * 3, [edge], [ANY],
-        [edge, pltpu.SemaphoreType.DMA((3,))], "second_edges", room=RP_ROOM,
+    ripple_apart, = call(
+        second_edges_kernel, (ripple_start, ripple_source, token, ripple_apart), [ANY] * 4, [edge], [ANY],
+        [edge, pltpu.SemaphoreType.DMA((3,))], "second_edges", aliases={3: 0}, room=RP_ROOM,
     )
     others, token = call(
         pair_kernel, (*wholes[1:], aparts[0]), [VMEM] * (shares - 1) + [ANY],
@@ -620,9 +608,7 @@
         room=NEAR_ROOM,
     )
     paireds = [lax.ppermute(paired, "mesh", near), lax.ppermute(others, "mesh", near)]
-    first_pairs, second_pairs = ([pair for pair in far if min(pair) % 4 == kind] for kind in (1, 3))
-    ripple_first = lax.ppermute(ripple_first, "mesh", first_pairs)
-    ripple_second = lax.ppermute(ripple_second, "mesh", second_pairs)
+    ripple_apart = lax.ppermute(ripple_apart, "mesh", far)
     ripple_paireds = [lax.ppermute(part, "mesh", near) for part in ripple_paireds]
 
     known = (planes + G_LOW + G_HIGH, rows, lanes)
@@ -659,14 +645,12 @@
     ripple, *losses = call(
         functools.partial(outer_kernel, shares),
         (
-            harmonic_numbers, sigma, ripple_start, ripple_source, ripple_first, ripple_second, edge, sides, answer,
-            inner_loss, ripple,
+            harmonic_numbers, sigma, ripple_start, ripple_source, ripple_apart, edge, sides, answer, inner_loss, ripple,
         ),
-        [SMEM] + [VMEM] * 3 + [ANY] * 2 + [VMEM] * 4 + [ANY],
+        [SMEM] + [VMEM] * 8 + [ANY],
         [ripple_start.shape] + [(planes, rows_each, lanes)] * shares, [ANY] + [VMEM] * shares,
-        [lead + (size, rows, lanes) for size in (2, 1, 2, 2)] + [(2, rows, lanes)]
-        + [pltpu.SemaphoreType.DMA((2,))] * 2,
-        "outer_ripple", aliases={10: 0},
+        [lead + (2, rows, lanes)] * 2 + [(2, rows, lanes), pltpu.SemaphoreType.DMA((2,))],
+        "outer_ripple", aliases={9: 0},
     )
     loss = losses[0]
     for turn, pairs in enumerate(turned):

time: 50.1 us -> 49.6 us (0.990)
    ppermute x2, waiting for transfers between devices: 6.17 us -> 4.8 us  [around(): return [block] + [lax.ppermute(block, 'harm', pairs) for pairs in turned]]
    ppermute x2 -> x1, waiting for transfers between devices: 1.52 us -> 2.39 us  [body(): ripple_apart = lax.ppermute(ripple_apart, 'mesh', far)]
    ppermute x2 -> x1, starting transfers between devices: 4.5 us -> 3.77 us  [body(): ripple_apart = lax.ppermute(ripple_apart, 'mesh', far)]
    ppermute x2, starting transfers between devices: 0.07 us -> 0.6 us  [body(): lax.ppermute(part, 'mesh', near)]
  transfers between devices with their start and end apart: 10 -> 9, of which waited for: 4 -> 4; matrix products, arithmetic and copies ran while one was open for 0% -> 0% of each run, Pallas kernels for 38% -> 39%
where the time goes in v7:
time: 49.6 us; the launch traced here: 49.4 us
  Pallas kernels  24 us (48%)
  waiting for transfers between devices  11.7 us (24%)
  starting transfers between devices  11.6 us (23%)
  between operations  0.84 us (2%)
  other arithmetic  0.64 us (1%)
  local copies, waits for them, and re-layouts  0.63 us (1%)
    pallas_call x8, Pallas kernels, call(): pl.pallas_call(kernel, out_shape=[jax.ShapeDtypeStruct(shape, f32) for sh...  24 us
    ppermute x2, waiting for transfers between devices, around(): return [block] + [lax.ppermute(block, 'harm', pairs) for pairs in turned]  4.8 us
    ppermute x1, starting transfers between devices, body(): ripple_apart = lax.ppermute(ripple_apart, 'mesh', far)  3.77 us
    ppermute x1, waiting for transfers between devices, body(): loss = loss + lax.ppermute(losses[turn + 1], 'harm', pairs)  3.73 us
    ppermute x1, starting transfers between devices, body(): lax.ppermute(paired, 'mesh', near)  2.6 us
    ppermute x1, waiting for transfers between devices, body(): ripple_apart = lax.ppermute(ripple_apart, 'mesh', far)  2.39 us
    ppermute x2, starting transfers between devices, around(): return [block] + [lax.ppermute(block, 'harm', pairs) for pairs in turned]  2.09 us
    ppermute x1, starting transfers between devices, body(): aparts = around(lax.ppermute(apart, 'mesh', far))  1.91 us
  transfers between devices with their start and end apart: 9, of which 4 were waited for; matrix products, arithmetic and copies ran while one was open for 0% of the time, Pallas kernels for 39%

profile of v7, /device:TPU:12, one launch (start us, length us, event | category | flops | bytes accessed | tf_op | source)
XLA Modules:
  0.0 49.4 jit_solution(1706228869510642454)
XLA Ops:
  0.6 2.2 %pack.1 = (f32[56,8,256]{2,1,0:T(8,128)}, f32[40,8,256]{2,1,0:T(8,128)}, f32[40,8,256]{2,1,0:T(8,128)}, f32[8,128]{1,0:T(8,128)}) custom-call(f32[3,8,8,256]{3,2,1,0:T(8,128)} %start.6, f32[3,8,8,256]{3,2,1,0:T(8,128)} %source.6, s32[8,8,256]{2,1,0:T(8,128)} %region.1), custom_call_target="tpu_custom_call" | custom-call | tf_op jit(solution)/shard_map/pack/pallas_call | solution.py:554
  2.8 1.6 %collective-permute-start = (f32[56,8,256]{2,1,0:T(8,128)}, f32[56,8,256]{2,1,0:T(8,128)S(1)}, u32[]{:S(2)}, u32[]{:S(2)}) collective-permute-start(f32[56,8,256]{2,1,0:T(8,128)} %get-tuple-element.26.refs_0_), channel_id=1, source_target_pairs={{0,1},{1,0},{2,3},{3,2},{4,5},{5,4},{6,7},{7,6},{8,9},{9,8},{10,11... | collective-permute-start | bytes 1376264 | tf_op jit(solution)/shard_map/ppermute | solution.py:581
  4.4 1.9 %collective-permute-start.1 = (f32[40,8,256]{2,1,0:T(8,128)}, f32[40,8,256]{2,1,0:T(8,128)S(1)}, u32[]{:S(2)}, u32[]{:S(2)}) collective-permute-start(f32[40,8,256]{2,1,0:T(8,128)} %get-tuple-element.27), channel_id=1, source_target_pairs={{2,4},{6,8},{10,12},{14,16},{18,20},{22,24},{26,28},{4,2},{8,6},{1... | collective-permute-start | bytes 983048 | tf_op jit(solution)/shard_map/ppermute | solution.py:589
  6.3 2.9 %first_edges.1 = (f32[4,2,3,3,16,256]{5,4,3,2,1,0:T(8,128)}, f32[4,2,3,2,16,256]{5,4,3,2,1,0:T(8,128)}, f32[4,2,3,1,16,256]{5,4,3,2,1,0:T(8,128)}, f32[8,128]{1,0:T(8,128)}) custom-call(f32[4,2,3,8,16,256]{5,4,3,2,1,0:T(8,128)} %start.11, f32[4,2,3,8,16,256]{5,4,3,2,1,0:T(8,128)} %source.11, f32[8,128]{1,0:T(8,128)} %get-tuple-element.32.after), custom_call_target="tpu_custom_call" | custom-call | tf_op jit(solution)/shard_map/first_edges/pallas_call | solution.py:554
  9.2 0.0 copy-start.9
  9.3 0.1 second_edges.1
  9.3 3.8 %collective-permute-start.5 = (f32[4,2,3,3,16,256]{5,4,3,2,1,0:T(8,128)}, f32[4,2,3,3,16,256]{5,4,3,2,1,0:T(8,128)S(1)}, u32[]{:S(2)}, u32[]{:S(2)}) collective-permute-start(f32[4,2,3,3,16,256]{5,4,3,2,1,0:T(8,128)} %second_edges.1), channel_id=1, source_target_pairs={{2,4},{6,8},{10,12},{14,16},{18,20},{22,24},{26,28},{4,2},{8,6},{1... | collective-permute-start | bytes 3538952 | tf_op jit(solution)/shard_map/ppermute | solution.py:611
  13.1 0.0 copy-done.9
  13.1 2.6 %collective-permute-start.3 = (f32[40,8,256]{2,1,0:T(8,128)S(1)}, f32[40,8,256]{2,1,0:T(8,128)S(1)}, u32[]{:S(2)}, u32[]{:S(2)}) collective-permute-start(f32[40,8,256]{2,1,0:T(8,128)S(1)} %copy-done.9), channel_id=1, source_target_pairs={{0,2},{4,6},{8,10},{12,14},{16,18},{20,22},{24,26},{28,30},{2,0},{... | collective-permute-start | bytes 983048 | tf_op jit(solution)/shard_map/ppermute | solution.py:610
  15.7 0.8 %collective-permute-done.1.refs_1_.refs_2_ = f32[40,8,256]{2,1,0:T(8,128)S(1)} collective-permute-done((f32[40,8,256]{2,1,0:T(8,128)}, f32[40,8,256]{2,1,0:T(8,128)S(1)}, u32[]{:S(2)}, u32[]{:S(2)}) %collective-permute-start.1) | collective-permute-done | bytes 327712 | tf_op jit(solution)/shard_map/ppermute | solution.py:589
  16.5 0.5 %collective-permute-start.2 = (f32[40,8,256]{2,1,0:T(8,128)S(1)}, f32[40,8,256]{2,1,0:T(8,128)S(1)}, u32[]{:S(2)}, u32[]{:S(2)}) collective-permute-start(f32[40,8,256]{2,1,0:T(8,128)S(1)} %collective-permute-done.1.refs_1_.refs_2_), channel_id=1, source_target_pairs={{0,1},{1,0},{2,3},{3,2},{4,5},{5,4},{6,7},{7,6},{8,9},{9,8},{10,11... | collective-permute-start | bytes 983048 | tf_op jit(solution)/shard_map/ppermute | solution.py:581
  17.0 0.0 collective-permute-done.refs_0_.refs_1_
  17.0 0.0 copy-start.2
  17.1 0.6 %copy-done.2 = f32[8,128]{1,0:T(8,128)} copy-done((f32[8,128]{1,0:T(8,128)}, f32[8,128]{1,0:T(8,128)S(1)}, u32[]{:S(2)}) %copy-start.2) | copy-done | bytes 4120
  17.6 0.0 collective-permute-start.4
  17.6 0.0 copy-start.4
  17.6 0.0 copy-start.5
  17.6 0.0 copy-start.6
  17.7 0.0 copy-start.7
  17.7 0.0 copy-start.8
  17.7 2.3 %near_edges.1 = (f32[4,2,3,2,16,256]{5,4,3,2,1,0:T(8,128)}, f32[4,2,3,1,16,256]{5,4,3,2,1,0:T(8,128)}) custom-call(f32[4,2,3,8,16,256]{5,4,3,2,1,0:T(8,128)} %start.11, f32[4,2,3,8,16,256]{5,4,3,2,1,0:T(8,128)} %source.11, f32[8,128]{1,0:T(8,128)} %copy-done.2, ...), custom_call_target="tpu_custom_call", output_to_operand_aliasing={{0}: (3, {}), {1}: (4, {})} | custom-call | tf_op jit(solution)/shard_map/near_edges/pallas_call | solution.py:554
  20.0 0.1 collective-permute-start.6
  20.0 0.0 collective-permute-done.3.refs_4_
  20.0 0.0 copy-start
  20.1 0.0 copy-start.1
  20.1 0.0 copy-start.3
  20.1 0.5 %collective-permute-start.7 = (f32[4,2,3,1,16,256]{5,4,3,2,1,0:T(8,128)}, f32[4,2,3,1,16,256]{5,4,3,2,1,0:T(8,128)S(1)}, u32[]{:S(2)}, u32[]{:S(2)}) collective-permute-start(f32[4,2,3,1,16,256]{5,4,3,2,1,0:T(8,128)} %get-tuple-element.40), channel_id=1, source_target_pairs={{0,2},{4,6},{8,10},{12,14},{16,18},{20,22},{24,26},{28,30},{2,0},{... | collective-permute-start | bytes 1179656 | tf_op jit(solution)/shard_map/ppermute | solution.py:612
  20.6 4.8 %collective-permute-done.2.refs_3_ = f32[40,8,256]{2,1,0:T(8,128)S(1)} collective-permute-done((f32[40,8,256]{2,1,0:T(8,128)S(1)}, f32[40,8,256]{2,1,0:T(8,128)S(1)}, u32[]{:S(2)}, u32[]{:S(2)}) %collective-permute-start.2) | collective-permute-done | bytes 327712 | tf_op jit(solution)/shard_map/ppermute | solution.py:581
  25.4 0.0 collective-permute-done.4.refs_5_
  25.4 0.0 copy-done.4
  25.4 0.0 copy-done.5
  25.4 0.0 copy-done.6
  25.4 0.0 copy-done.7
  25.4 0.0 copy-done.8
  25.4 7.4 %bias.1 = (f32[3,8,8,256]{3,2,1,0:T(8,128)}, f32[12,16,256]{2,1,0:T(8,128)S(1)}, f32[10,16,256]{2,1,0:T(8,128)S(1)}) custom-call(f32[56,8,256]{2,1,0:T(8,128)S(1)} %copy-done.4, f32[56,8,256]{2,1,0:T(8,128)S(1)} %collective-permute-done.refs_0_.refs_1_, f32[40,8,256]{2,1,0:T(8,128)S(1)} %collective-permute-done.1.refs_1_.refs_2_, ...), custom_call_target="tpu_custom_call" | custom-call | flops 6000000000 | bytes 20000000 | tf_op jit(solution)/shard_map/bias/pallas_call | solution.py:554
  32.8 0.0 collective-permute-done.7.paired_source
  32.8 0.0 collective-permute-done.6.paired_start
  32.8 0.0 copy-done
  32.9 0.0 copy-done.1
  32.9 0.0 copy-done.3
  32.9 6.5 %inner_ripple.1 = (f32[4,2,3,8,16,256]{5,4,3,2,1,0:T(8,128)}, f32[4,2,3,2,16,256]{5,4,3,2,1,0:T(8,128)S(1)}, f32[8,16,256]{2,1,0:T(8,128)S(1)}, f32[6,10,16,256]{3,2,1,0:T(8,128)S(1)}, f32[4,2,10,16,256]{4,3,2,1,0:T(8,128)S(1)}) custom-call(s32[8]{0:T(128)S(1)} %copy-done.3, f32[12,16,256]{2,1,0:T(8,128)S(1)} %get-tuple-element.35.nud, ...), custom_call_target="tpu_custom_call" | custom-call | tf_op jit(solution)/shard_map/inner_ripple/pallas_call | solution.py:554
  39.4 2.4 %collective-permute-done.5.apart = f32[4,2,3,3,16,256]{5,4,3,2,1,0:T(8,128)S(1)} collective-permute-done((f32[4,2,3,3,16,256]{5,4,3,2,1,0:T(8,128)}, f32[4,2,3,3,16,256]{5,4,3,2,1,0:T(8,128)S(1)}, u32[]{:S(2)}, u32[]{:S(2)}) %collective-permute-start.5) | collective-permute-done | bytes 1179680 | tf_op jit(solution)/shard_map/ppermute | solution.py:611
  41.8 2.6 %outer_ripple.1 = (f32[4,2,3,8,16,256]{5,4,3,2,1,0:T(8,128)}, f32[8,8,256]{2,1,0:T(8,128)S(1)}, f32[8,8,256]{2,1,0:T(8,128)S(1)}) custom-call(s32[8]{0:T(128)S(1)} %copy-done.3, f32[10,16,256]{2,1,0:T(8,128)S(1)} %get-tuple-element.31.sigma, f32[4,2,3,8,16,256]{5,4,3,2,1,0:T(8,128)S(1)} %copy-done, ...), custom_call_target="tpu_custom_call", output_to_operand_aliasing={{0}: (9, {})} | custom-call | tf_op jit(solution)/shard_map/outer_ripple/pallas_call | solution.py:554
  44.4 0.6 %collective-permute-start.8 = (f32[8,8,256]{2,1,0:T(8,128)S(1)}, f32[8,8,256]{2,1,0:T(8,128)S(1)}, u32[]{:S(2)}, u32[]{:S(2)}) collective-permute-start(f32[8,8,256]{2,1,0:T(8,128)S(1)} %get-tuple-element.48), channel_id=1, source_target_pairs={{0,1},{1,0},{2,3},{3,2},{4,5},{5,4},{6,7},{7,6},{8,9},{9,8},{10,11... | collective-permute-start | bytes 196616 | tf_op jit(solution)/shard_map/ppermute | solution.py:657
  45.0 3.7 %collective-permute-done.8 = f32[8,8,256]{2,1,0:T(8,128)S(1)} collective-permute-done((f32[8,8,256]{2,1,0:T(8,128)S(1)}, f32[8,8,256]{2,1,0:T(8,128)S(1)}, u32[]{:S(2)}, u32[]{:S(2)}) %collective-permute-start.8) | collective-permute-done | bytes 65568 | tf_op jit(solution)/shard_map/ppermute | solution.py:657
  48.7 0.6 %add.3 = f32[8,8,256]{2,1,0:T(8,128)} add(f32[8,8,256]{2,1,0:T(8,128)S(1)} %get-tuple-element.47, f32[8,8,256]{2,1,0:T(8,128)S(1)} %collective-permute-done.8) | non-fusion elementwise | flops 16384 | bytes 196608 | tf_op jit(solution)/shard_map/add | solution.py:657
  (1 shorter events, 0.0 us)
Async XLA Ops:
  2.8 14.2 %collective-permute-start = (f32[56,8,256]{2,1,0:T(8,128)}, f32[56,8,256]{2,1,0:T(8,128)S(1)}, u32[]{:S(2)}, u32[]{:S(2)}) collective-permute-start(f32[56,8,256]{2,1,0:T(8,128)} %get-tuple-element.26.refs_0_), channel_id=1, source_target_pairs={{0,1},{1,0},{2,3},{3,2},{4,5},{5,4},{6,7},{7,6},{8,9},{9,8},{10,11... | collective-permute-start | bytes 1376264 | tf_op jit(solution)/shard_map/ppermute | solution.py:581
  4.4 12.1 %collective-permute-start.1 = (f32[40,8,256]{2,1,0:T(8,128)}, f32[40,8,256]{2,1,0:T(8,128)S(1)}, u32[]{:S(2)}, u32[]{:S(2)}) collective-permute-start(f32[40,8,256]{2,1,0:T(8,128)} %get-tuple-element.27), channel_id=1, source_target_pairs={{2,4},{6,8},{10,12},{14,16},{18,20},{22,24},{26,28},{4,2},{8,6},{1... | collective-permute-start | bytes 983048 | tf_op jit(solution)/shard_map/ppermute | solution.py:589
  9.2 3.9 %copy-start.9 = (f32[40,8,256]{2,1,0:T(8,128)S(1)}, f32[40,8,256]{2,1,0:T(8,128)}, u32[]{:S(2)}) copy-start(f32[40,8,256]{2,1,0:T(8,128)} %get-tuple-element.28) | copy-start | bytes 983044
  9.3 32.4 %collective-permute-start.5 = (f32[4,2,3,3,16,256]{5,4,3,2,1,0:T(8,128)}, f32[4,2,3,3,16,256]{5,4,3,2,1,0:T(8,128)S(1)}, u32[]{:S(2)}, u32[]{:S(2)}) collective-permute-start(f32[4,2,3,3,16,256]{5,4,3,2,1,0:T(8,128)} %second_edges.1), channel_id=1, source_target_pairs={{2,4},{6,8},{10,12},{14,16},{18,20},{22,24},{26,28},{4,2},{8,6},{1... | collective-permute-start | bytes 3538952 | tf_op jit(solution)/shard_map/ppermute | solution.py:611
  13.1 6.9 %collective-permute-start.3 = (f32[40,8,256]{2,1,0:T(8,128)S(1)}, f32[40,8,256]{2,1,0:T(8,128)S(1)}, u32[]{:S(2)}, u32[]{:S(2)}) collective-permute-start(f32[40,8,256]{2,1,0:T(8,128)S(1)} %copy-done.9), channel_id=1, source_target_pairs={{0,2},{4,6},{8,10},{12,14},{16,18},{20,22},{24,26},{28,30},{2,0},{... | collective-permute-start | bytes 983048 | tf_op jit(solution)/shard_map/ppermute | solution.py:610
  16.5 8.9 %collective-permute-start.2 = (f32[40,8,256]{2,1,0:T(8,128)S(1)}, f32[40,8,256]{2,1,0:T(8,128)S(1)}, u32[]{:S(2)}, u32[]{:S(2)}) collective-permute-start(f32[40,8,256]{2,1,0:T(8,128)S(1)} %collective-permute-done.1.refs_1_.refs_2_), channel_id=1, source_target_pairs={{0,1},{1,0},{2,3},{3,2},{4,5},{5,4},{6,7},{7,6},{8,9},{9,8},{10,11... | collective-permute-start | bytes 983048 | tf_op jit(solution)/shard_map/ppermute | solution.py:581
  17.0 0.6 %copy-start.2 = (f32[8,128]{1,0:T(8,128)}, f32[8,128]{1,0:T(8,128)S(1)}, u32[]{:S(2)}) copy-start(f32[8,128]{1,0:T(8,128)S(1)} %get-tuple-element.36.after) | copy-start | bytes 12292
  17.6 7.8 %collective-permute-start.4 = (f32[1,40,8,256]{3,2,1,0:T(8,128)S(1)}, f32[1,40,8,256]{3,2,1,0:T(8,128)S(1)}, u32[]{:S(2)}, u32[]{:S(2)}) collective-permute-start(f32[1,40,8,256]{3,2,1,0:T(8,128)S(1)} %get-tuple-element.29), channel_id=1, source_target_pairs={{0,2},{4,6},{8,10},{12,14},{16,18},{20,22},{24,26},{28,30},{2,0},{... | collective-permute-start | bytes 983048 | tf_op jit(solution)/shard_map/ppermute | solution.py:610
  17.6 7.8 %copy-start.4 = (f32[56,8,256]{2,1,0:T(8,128)S(1)}, f32[56,8,256]{2,1,0:T(8,128)}, u32[]{:S(2)}) copy-start(f32[56,8,256]{2,1,0:T(8,128)} %get-tuple-element.26.refs_0_) | copy-start | bytes 1376260
  17.6 7.8 %copy-start.5 = (f32[4,8]{1,0:T(4,128)S(1)}, f32[4,8]{1,0:T(4,128)}, u32[]{:S(2)}) copy-start(f32[4,8]{1,0:T(4,128)} %refs_8_.1) | copy-start | bytes 388
  17.6 7.8 %copy-start.6 = (s32[4]{0:T(128)S(1)}, s32[4]{0:T(128)}, u32[]{:S(2)}) copy-start(s32[4]{0:T(128)} %refs_6_.1) | copy-start | bytes 52
  17.7 7.8 %copy-start.7 = (f32[4]{0:T(128)S(1)}, f32[4]{0:T(128)}, u32[]{:S(2)}) copy-start(f32[4]{0:T(128)} %refs_7_.1) | copy-start | bytes 52
  17.7 7.8 %copy-start.8 = (f32[4]{0:T(128)S(1)}, f32[4]{0:T(128)}, u32[]{:S(2)}) copy-start(f32[4]{0:T(128)} %refs_9_.1) | copy-start | bytes 52
  20.0 12.9 %collective-permute-start.6 = (f32[4,2,3,2,16,256]{5,4,3,2,1,0:T(8,128)}, f32[4,2,3,2,16,256]{5,4,3,2,1,0:T(8,128)S(1)}, u32[]{:S(2)}, u32[]{:S(2)}) collective-permute-start(f32[4,2,3,2,16,256]{5,4,3,2,1,0:T(8,128)} %get-tuple-element.39), channel_id=1, source_target_pairs={{0,2},{4,6},{8,10},{12,14},{16,18},{20,22},{24,26},{28,30},{2,0},{... | collective-permute-start | bytes 2359304 | tf_op jit(solution)/shard_map/ppermute | solution.py:612
  20.0 12.8 %copy-start = (f32[4,2,3,8,16,256]{5,4,3,2,1,0:T(8,128)S(1)}, f32[4,2,3,8,16,256]{5,4,3,2,1,0:T(8,128)}, u32[]{:S(2)}) copy-start(f32[4,2,3,8,16,256]{5,4,3,2,1,0:T(8,128)} %start.11) | copy-start | bytes 9437188
  20.1 12.8 %copy-start.1 = (f32[4,2,3,8,16,256]{5,4,3,2,1,0:T(8,128)S(1)}, f32[4,2,3,8,16,256]{5,4,3,2,1,0:T(8,128)}, u32[]{:S(2)}) copy-start(f32[4,2,3,8,16,256]{5,4,3,2,1,0:T(8,128)} %source.11) | copy-start | bytes 9437188
  20.1 12.8 %copy-start.3 = (s32[8]{0:T(128)S(1)}, s32[8]{0:T(128)}, u32[]{:S(2)}) copy-start(s32[8]{0:T(128)} %harmonic_numbers.3) | copy-start | bytes 100
  20.1 12.8 %collective-permute-start.7 = (f32[4,2,3,1,16,256]{5,4,3,2,1,0:T(8,128)}, f32[4,2,3,1,16,256]{5,4,3,2,1,0:T(8,128)S(1)}, u32[]{:S(2)}, u32[]{:S(2)}) collective-permute-start(f32[4,2,3,1,16,256]{5,4,3,2,1,0:T(8,128)} %get-tuple-element.40), channel_id=1, source_target_pairs={{0,2},{4,6},{8,10},{12,14},{16,18},{20,22},{24,26},{28,30},{2,0},{... | collective-permute-start | bytes 1179656 | tf_op jit(solution)/shard_map/ppermute | solution.py:612
  44.4 4.3 %collective-permute-start.8 = (f32[8,8,256]{2,1,0:T(8,128)S(1)}, f32[8,8,256]{2,1,0:T(8,128)S(1)}, u32[]{:S(2)}, u32[]{:S(2)}) collective-permute-start(f32[8,8,256]{2,1,0:T(8,128)S(1)} %get-tuple-element.48), channel_id=1, source_target_pairs={{0,1},{1,0},{2,3},{3,2},{4,5},{5,4},{6,7},{7,6},{8,9},{9,8},{10,11... | collective-permute-start | bytes 196616 | tf_op jit(solution)/shard_map/ppermute | solution.py:657

commit v8 on v7

--- a/solution.py
+++ b/solution.py
@@ -99,8 +99,8 @@
     return weights, tiles.each(lambda value: value + 2.0 * kappa, total)
 
 
-def pull(tiles, start, weights, center, above, below):
-    moved = [above, below] + [tiles.move(center, step, axis, False) for step, axis in SIDES]
+def pull(tiles, start, weights, center, beside):
+    moved = list(beside) + [tiles.move(center, step, axis, False) for step, axis in SIDES]
     total = start
     for weight, other in zip(weights, moved):
         total = tiles.each(lambda so_far, w, value: so_far + w * value, total, weight, other)
@@ -228,11 +228,10 @@
     way_out.wait()
 
 
-def send_near_edges(start, source, targets, buffers, sems):
-    planes = start.shape[3]
+def send_near_edges(origins, targets, buffers, sems):
     ways = []
-    for number, (origin, buffer, target) in enumerate(zip((start, source), buffers, targets)):
-        count = target.shape[3]
+    for number, (origin, buffer, target) in enumerate(zip(origins, buffers, targets)):
+        planes, count = origin.shape[3], target.shape[3]
         first = jnp.where(is_odd(), 0, planes - count)
         held = planes_of(buffer, 0, count)
         ways.append(
@@ -251,7 +250,7 @@
 
 
 def first_edges_kernel(
-    start, source, after, apart, paired_start, paired_source, token, buffer, other_buffer, sems, near_sems
+    start, source, after, apart, paired_start, paired_source, token, buffer, sems, near_sems
 ):
     token[...] = jnp.zeros(token.shape, token.dtype)
 
@@ -261,13 +260,17 @@
 
     @pl.when(is_second())
     def send_near():
-        send_near_edges(start, source, (paired_start, paired_source), (buffer, other_buffer), near_sems)
+        send_near_edges([source], [paired_source], [buffer], near_sems)
 
 
 def near_edges_kernel(start, source, after, start_in, source_in, paired_start, paired_source, buffer, other_buffer, sems):
     @pl.when(jnp.logical_not(is_second()))
-    def send_near():
-        send_near_edges(start, source, (paired_start, paired_source), (buffer, other_buffer), sems)
+    def send_both():
+        send_near_edges([start, source], [paired_start, paired_source], [buffer, other_buffer], sems)
+
+    @pl.when(is_second())
+    def send_start():
+        send_near_edges([start], [paired_start], [buffer], sems)
 
 
 def second_edges_kernel(start, source, after, apart_in, apart, buffer, sems):
@@ -339,7 +342,7 @@
             for part in range(3):
                 twice = tiles.each(lambda value: value + value, tiles.load(src, part, plane + S_LOW))
                 near_old = [tiles.load(old, part, from_old + move) for move in (0, 1, -1)]
-                moved = pull(tiles, twice, weights, *near_old)
+                moved = pull(tiles, twice, weights, near_old[0], near_old[1:])
                 tiles.store(target, (part, at), tiles.each(lambda value, by: value * by, moved, scale))
 
         loop_in_pairs(planes + A_LOW[step] + A_HIGH[step], body)
@@ -415,7 +418,7 @@
                 scaled = tiles.each(lambda one, other: one * other, value, inverse)
                 tiles.store(self.answer, (harmonic, part, slot), scaled)
 
-    def sweep(self, slot, old, source, put, turned_round=0):
+    def sweep(self, slot, old, source, put, turned_round=0, begin=False, begun=False):
         tiles, loss = self.tiles, None
         weights = [tiles.load(self.sides, number, slot) for number in (turned_round, 1 - turned_round, 2, 3, 4, 5)]
         for harmonic in range(len(self.omegas)):
@@ -426,13 +429,25 @@
                 for piece in range(2):
                     lead = (harmonic, piece, part)
                     near_old = [tiles.load(ref, *lead, at) for ref, at in old]
-                    both.append(pull(tiles, tiles.load(source[0], *lead, source[1]), weights, *near_old))
+                    given = tiles.load(source[0], *lead, source[1])
+                    if begun:
+                        add_last = lambda so_far, weight, value: so_far + weight * value
+                        both.append(tiles.each(add_last, given, weights[1], near_old[0]))
+                        continue
+                    used = weights[:1] + weights[2:] if begin else weights
+                    both.append(pull(tiles, given, used, near_old[0], near_old[1:]))
+                if begin:
+                    for piece, value in enumerate(both):
+                        tiles.store(put[0], (harmonic, piece, part, put[1]), value)
+                    continue
                 real = tiles.each(lambda re, im, a, b: re * a + im * b, *both, straight, turned)
                 imag = tiles.each(lambda re, im, a, b: im * a - re * b, *both, straight, turned)
                 for piece, value in enumerate((real, imag)):
                     tiles.store(put[0], (harmonic, piece, part, put[1]), value)
                 squared = tiles.each(lambda re, im: re * re + im * im, real, imag)
                 power = tiles.each(lambda one, other: one + other, power, squared) if part else squared
+            if begin:
+                continue
             factor = 0.5 * self.omegas[harmonic] * self.omegas[harmonic]
             scaled = tiles.each(lambda value: factor * value, power)
             loss = tiles.each(lambda one, other: one + other, loss, scaled) if loss else scaled
@@ -449,10 +464,10 @@
         self.third = pick(planes - 3, 2)
 
 
-def first_on_side(ripple, side, start, source, halo_start, halo_source, put_beyond, put_own, source_at=0):
+def first_on_side(ripple, side, start, source, halo_start, halo_source, put_beyond, put_own):
     ripple.sweep(
         side.beyond_slot, [(halo_start, side.halo), (start, side.own), (halo_start, side.far_halo)],
-        (halo_source, source_at),
+        (halo_source, 0),
         put_beyond, side.turned_round,
     )
     ripple.sweep(
@@ -462,8 +477,8 @@
 
 
 def inner_kernel(
-    meshes, harmonic_numbers, nud, sigma, start, source, paired_start, paired_source, ripple_out, edge_out, loss_out,
-    sides, answer, r1, r2, sems
+    meshes, harmonic_numbers, nud, sigma, start, source, paired_start, paired_source, ripple_out, edge_out, begun_out,
+    loss_out, sides, answer, r1, r2, sems
 ):
     count, planes = start.shape[0], start.shape[3]
     here = lax.axis_index("mesh")
@@ -505,13 +520,19 @@
     )
     begin, end = jnp.where(odd, 0, 2), jnp.where(odd, planes - 2, planes)
     lax.fori_loop(begin, end, second, 0)
-    for onto, plane in enumerate((far.second, far.third)):
-        edge_out[:, :, :, onto] = r1[:, :, :, plane + 1]
+    edge_out[:, :, :, 0] = r1[:, :, :, far.second_slot]
+    ripple.sweep(
+        far.own_slot, [(start, far.own), (start, far.second)], (source, far.own), (begun_out, 0), far.turned_round, begin=True
+    )
+    ripple.sweep(
+        far.second_slot, [(r1, far.second_slot), (r1, far.third + 1)], (source, far.second), (begun_out, 1),
+        far.turned_round, begin=True,
+    )
     lax.fori_loop(begin, end, finish, 0)
 
 
 def outer_kernel(
-    shares, harmonic_numbers, sigma, start, source, apart, edge, sides, answer, loss_in, ripple_in,
+    shares, harmonic_numbers, sigma, start, source, apart, edge, begun, sides, answer, loss_in, ripple_in,
     ripple_out, *refs
 ):
     losses, (r1, r2, loss, sems) = refs[:shares], refs[shares:]
@@ -521,17 +542,20 @@
     far = Side(planes, is_odd())
     ripple = Ripple(rows, lanes, harmonic_numbers, count, sides, answer)
     tiles = ripple.tiles
-    first_on_side(ripple, far, start, source, apart, apart, (r1, 0), (r1, 1), 2)
+    ripple.sweep(
+        far.beyond_slot, [(apart, far.halo), (start, far.own), (apart, far.far_halo)], (apart, 2), (r1, 0), far.turned_round
+    )
+    ripple.sweep(far.own_slot, [(apart, far.halo)], (begun, 0), (r1, 1), far.turned_round, begun=True)
 
     def drain(slot, plane):
         return pltpu.make_async_copy(planes_of(r2, slot, 1), planes_of(ripple_out, plane, 1), sems.at[slot])
 
     steps = (
-        (far.own, far.own_slot, [(r1, 1), (edge, 0), (r1, 0)]),
-        (far.second, far.second_slot, [(edge, 0), (edge, 1), (r1, 1)]),
-    )
-    for at, (plane, slot, old) in enumerate(steps):
-        added = ripple.sweep(slot, old, (source, plane), (r2, at), far.turned_round)
+        (far.own, far.own_slot, [(r1, 1), (edge, 0), (r1, 0)], (source, far.own), False),
+        (far.second, far.second_slot, [(r1, 1)], (begun, 1), True),
+    )
+    for at, (plane, slot, old, given, is_begun) in enumerate(steps):
+        added = ripple.sweep(slot, old, given, (r2, at), far.turned_round, begun=is_begun)
         drain(at, plane).start()
         tiles.store(loss, (at,), tiles.each(lambda one, other: one * other, tiles.load(sigma, slot), added))
     rows_each = rows // shares
@@ -539,9 +563,9 @@
         owner = lax.rem(lax.axis_index("harm") + turn, shares)
         part = pl.ds(pl.multiple_of(owner * rows_each, rows_each), rows_each)
         losses[turn][...] = loss_in[:, part, :]
-        for at, (plane, unused, unused_too) in enumerate(steps):
+        for at, (plane, *unused) in enumerate(steps):
             losses[turn][plane] = loss[at, part, :]
-    for at, (plane, unused, unused_too) in enumerate(steps):
+    for at, (plane, *unused) in enumerate(steps):
         drain(at, plane).wait()
 
 
@@ -592,7 +616,7 @@
     ripple_apart, paired_start, paired_source, token = call(
         first_edges_kernel, (ripple_start, ripple_source, token), [ANY] * 3,
         [edge] + near_edges + [TILE], [ANY] * 3 + [VMEM],
-        [edge, edge, pltpu.SemaphoreType.DMA((3,)), pltpu.SemaphoreType.DMA((4,))], "first_edges", room=RP_ROOM,
+        [edge, pltpu.SemaphoreType.DMA((3,)), pltpu.SemaphoreType.DMA((2,))], "first_edges", room=RP_ROOM,
     )
     ripple_apart, = call(
         second_edges_kernel, (ripple_start, ripple_source, token, ripple_apart), [ANY] * 4, [edge], [ANY],
@@ -635,22 +659,26 @@
 
     lead = ripple_start.shape[:3]
     slots = (planes + 2, rows, lanes)
-    ripple, edge, inner_loss, sides, answer = call(
+    ripple, edge, begun, inner_loss, sides, answer = call(
         functools.partial(inner_kernel, meshes),
         (harmonic_numbers, nud, sigma, ripple_start, ripple_source, *ripple_paireds), [SMEM] + [VMEM] * 6,
-        [ripple_start.shape, lead + (2, rows, lanes), (planes, rows, lanes), (6, *slots), (count, 2, *slots)],
-        [ANY] + [VMEM] * 4, [lead + slots, lead + (planes, rows, lanes), pltpu.SemaphoreType.DMA((planes,))],
+        [
+            ripple_start.shape, lead + (1, rows, lanes), lead + (2, rows, lanes), (planes, rows, lanes), (6, *slots),
+            (count, 2, *slots),
+        ],
+        [ANY] + [VMEM] * 5, [lead + slots, lead + (planes, rows, lanes), pltpu.SemaphoreType.DMA((planes,))],
         "inner_ripple",
     )
     ripple, *losses = call(
         functools.partial(outer_kernel, shares),
         (
-            harmonic_numbers, sigma, ripple_start, ripple_source, ripple_apart, edge, sides, answer, inner_loss, ripple,
+            harmonic_numbers, sigma, ripple_start, ripple_source, ripple_apart, edge, begun, sides, answer, inner_loss,
+            ripple,
         ),
-        [SMEM] + [VMEM] * 8 + [ANY],
+        [SMEM] + [VMEM] * 9 + [ANY],
         [ripple_start.shape] + [(planes, rows_each, lanes)] * shares, [ANY] + [VMEM] * shares,
         [lead + (2, rows, lanes)] * 2 + [(2, rows, lanes), pltpu.SemaphoreType.DMA((2,))],
-        "outer_ripple", aliases={9: 0},
+        "outer_ripple", aliases={10: 0},
     )
     loss = losses[0]
     for turn, pairs in enumerate(turned):

time: 49.6 us -> 49.3 us (level)
  Pallas kernels: 24 us -> 23.5 us
  waiting for transfers between devices: 11.7 us -> 12.2 us
    ppermute x1, waiting for transfers between devices: 2.39 us -> 2.92 us  [body(): ripple_apart = lax.ppermute(ripple_apart, 'mesh', far)]
where the time goes in v8:
time: 49.3 us; the launch traced here: 49 us
  Pallas kernels  23.5 us (48%)
  waiting for transfers between devices  12.2 us (25%)
  starting transfers between devices  11.2 us (23%)
  between operations  0.81 us (2%)
  other arithmetic  0.64 us (1%)
  local copies, waits for them, and re-layouts  0.63 us (1%)
    pallas_call x8, Pallas kernels, call(): pl.pallas_call(kernel, out_shape=[jax.ShapeDtypeStruct(shape, f32) for sh...  23.5 us
    ppermute x2, waiting for transfers between devices, around(): return [block] + [lax.ppermute(block, 'harm', pairs) for pairs in turned]  4.38 us
    ppermute x1, starting transfers between devices, body(): ripple_apart = lax.ppermute(ripple_apart, 'mesh', far)  3.77 us
    ppermute x1, waiting for transfers between devices, body(): loss = loss + lax.ppermute(losses[turn + 1], 'harm', pairs)  3.73 us
    ppermute x1, waiting for transfers between devices, body(): ripple_apart = lax.ppermute(ripple_apart, 'mesh', far)  2.92 us
    ppermute x1, starting transfers between devices, body(): lax.ppermute(paired, 'mesh', near)  2.2 us
    ppermute x2, starting transfers between devices, around(): return [block] + [lax.ppermute(block, 'harm', pairs) for pairs in turned]  2.09 us
    ppermute x1, starting transfers between devices, body(): aparts = around(lax.ppermute(apart, 'mesh', far))  1.91 us
  transfers between devices with their start and end apart: 9, of which 4 were waited for; matrix products, arithmetic and copies ran while one was open for 0% of the time, Pallas kernels for 39%

profile of v8, /device:TPU:12, one launch (start us, length us, event | category | flops | bytes accessed | tf_op | source)
XLA Modules:
  0.0 49.0 jit_solution(10799394181590576627)
XLA Ops:
  0.6 2.2 %pack.1 = (f32[56,8,256]{2,1,0:T(8,128)}, f32[40,8,256]{2,1,0:T(8,128)}, f32[40,8,256]{2,1,0:T(8,128)}, f32[8,128]{1,0:T(8,128)}) custom-call(f32[3,8,8,256]{3,2,1,0:T(8,128)} %start.6, f32[3,8,8,256]{3,2,1,0:T(8,128)} %source.6, s32[8,8,256]{2,1,0:T(8,128)} %region.1), custom_call_target="tpu_custom_call" | custom-call | tf_op jit(solution)/shard_map/pack/pallas_call | solution.py:578
  2.8 1.6 %collective-permute-start = (f32[56,8,256]{2,1,0:T(8,128)}, f32[56,8,256]{2,1,0:T(8,128)S(1)}, u32[]{:S(2)}, u32[]{:S(2)}) collective-permute-start(f32[56,8,256]{2,1,0:T(8,128)} %get-tuple-element.27.refs_0_), channel_id=1, source_target_pairs={{0,1},{1,0},{2,3},{3,2},{4,5},{5,4},{6,7},{7,6},{8,9},{9,8},{10,11... | collective-permute-start | bytes 1376264 | tf_op jit(solution)/shard_map/ppermute | solution.py:605
  4.4 1.9 %collective-permute-start.1 = (f32[40,8,256]{2,1,0:T(8,128)}, f32[40,8,256]{2,1,0:T(8,128)S(1)}, u32[]{:S(2)}, u32[]{:S(2)}) collective-permute-start(f32[40,8,256]{2,1,0:T(8,128)} %get-tuple-element.28), channel_id=1, source_target_pairs={{2,4},{6,8},{10,12},{14,16},{18,20},{22,24},{26,28},{4,2},{8,6},{1... | collective-permute-start | bytes 983048 | tf_op jit(solution)/shard_map/ppermute | solution.py:613
  6.3 2.9 %first_edges.1 = (f32[4,2,3,3,16,256]{5,4,3,2,1,0:T(8,128)}, f32[4,2,3,2,16,256]{5,4,3,2,1,0:T(8,128)}, f32[4,2,3,1,16,256]{5,4,3,2,1,0:T(8,128)}, f32[8,128]{1,0:T(8,128)}) custom-call(f32[4,2,3,8,16,256]{5,4,3,2,1,0:T(8,128)} %start.11, f32[4,2,3,8,16,256]{5,4,3,2,1,0:T(8,128)} %source.11, f32[8,128]{1,0:T(8,128)} %get-tuple-element.33.after), custom_call_target="tpu_custom_call" | custom-call | tf_op jit(solution)/shard_map/first_edges/pallas_call | solution.py:578
  9.2 0.0 copy-start.9
  9.2 0.1 second_edges.1
  9.3 3.8 %collective-permute-start.5 = (f32[4,2,3,3,16,256]{5,4,3,2,1,0:T(8,128)}, f32[4,2,3,3,16,256]{5,4,3,2,1,0:T(8,128)S(1)}, u32[]{:S(2)}, u32[]{:S(2)}) collective-permute-start(f32[4,2,3,3,16,256]{5,4,3,2,1,0:T(8,128)} %second_edges.1), channel_id=1, source_target_pairs={{2,4},{6,8},{10,12},{14,16},{18,20},{22,24},{26,28},{4,2},{8,6},{1... | collective-permute-start | bytes 3538952 | tf_op jit(solution)/shard_map/ppermute | solution.py:635
  13.1 0.0 copy-done.9
  13.1 2.2 %collective-permute-start.3 = (f32[40,8,256]{2,1,0:T(8,128)S(1)}, f32[40,8,256]{2,1,0:T(8,128)S(1)}, u32[]{:S(2)}, u32[]{:S(2)}) collective-permute-start(f32[40,8,256]{2,1,0:T(8,128)S(1)} %copy-done.9), channel_id=1, source_target_pairs={{0,2},{4,6},{8,10},{12,14},{16,18},{20,22},{24,26},{28,30},{2,0},{... | collective-permute-start | bytes 983048 | tf_op jit(solution)/shard_map/ppermute | solution.py:634
  15.3 1.2 %collective-permute-done.1.refs_1_.refs_2_ = f32[40,8,256]{2,1,0:T(8,128)S(1)} collective-permute-done((f32[40,8,256]{2,1,0:T(8,128)}, f32[40,8,256]{2,1,0:T(8,128)S(1)}, u32[]{:S(2)}, u32[]{:S(2)}) %collective-permute-start.1) | collective-permute-done | bytes 327712 | tf_op jit(solution)/shard_map/ppermute | solution.py:613
  16.5 0.5 %collective-permute-start.2 = (f32[40,8,256]{2,1,0:T(8,128)S(1)}, f32[40,8,256]{2,1,0:T(8,128)S(1)}, u32[]{:S(2)}, u32[]{:S(2)}) collective-permute-start(f32[40,8,256]{2,1,0:T(8,128)S(1)} %collective-permute-done.1.refs_1_.refs_2_), channel_id=1, source_target_pairs={{0,1},{1,0},{2,3},{3,2},{4,5},{5,4},{6,7},{7,6},{8,9},{9,8},{10,11... | collective-permute-start | bytes 983048 | tf_op jit(solution)/shard_map/ppermute | solution.py:605
  17.0 0.0 collective-permute-done.refs_0_.refs_1_
  17.0 0.0 copy-start.2
  17.1 0.6 %copy-done.2 = f32[8,128]{1,0:T(8,128)} copy-done((f32[8,128]{1,0:T(8,128)}, f32[8,128]{1,0:T(8,128)S(1)}, u32[]{:S(2)}) %copy-start.2) | copy-done | bytes 4120
  17.6 0.0 collective-permute-start.4
  17.6 0.0 copy-start.4
  17.6 0.0 copy-start.5
  17.6 0.0 copy-start.6
  17.7 0.0 copy-start.7
  17.7 0.0 copy-start.8
  17.7 2.3 %near_edges.1 = (f32[4,2,3,2,16,256]{5,4,3,2,1,0:T(8,128)}, f32[4,2,3,1,16,256]{5,4,3,2,1,0:T(8,128)}) custom-call(f32[4,2,3,8,16,256]{5,4,3,2,1,0:T(8,128)} %start.11, f32[4,2,3,8,16,256]{5,4,3,2,1,0:T(8,128)} %source.11, f32[8,128]{1,0:T(8,128)} %copy-done.2, ...), custom_call_target="tpu_custom_call", output_to_operand_aliasing={{0}: (3, {}), {1}: (4, {})} | custom-call | tf_op jit(solution)/shard_map/near_edges/pallas_call | solution.py:578
  20.0 0.4 collective-permute-start.6
  20.4 0.0 collective-permute-done.3.refs_4_
  20.4 0.0 copy-start
  20.4 0.0 copy-start.1
  20.4 0.0 copy-start.3
  20.4 0.2 collective-permute-start.7
  20.6 4.4 %collective-permute-done.2.refs_3_ = f32[40,8,256]{2,1,0:T(8,128)S(1)} collective-permute-done((f32[40,8,256]{2,1,0:T(8,128)S(1)}, f32[40,8,256]{2,1,0:T(8,128)S(1)}, u32[]{:S(2)}, u32[]{:S(2)}) %collective-permute-start.2) | collective-permute-done | bytes 327712 | tf_op jit(solution)/shard_map/ppermute | solution.py:605
  25.0 0.0 collective-permute-done.4.refs_5_
  25.0 0.0 copy-done.4
  25.0 0.0 copy-done.5
  25.0 0.0 copy-done.6
  25.0 0.0 copy-done.7
  25.0 0.0 copy-done.8
  25.0 7.4 %bias.1 = (f32[3,8,8,256]{3,2,1,0:T(8,128)}, f32[12,16,256]{2,1,0:T(8,128)S(1)}, f32[10,16,256]{2,1,0:T(8,128)S(1)}) custom-call(f32[56,8,256]{2,1,0:T(8,128)S(1)} %copy-done.4, f32[56,8,256]{2,1,0:T(8,128)S(1)} %collective-permute-done.refs_0_.refs_1_, f32[40,8,256]{2,1,0:T(8,128)S(1)} %collective-permute-done.1.refs_1_.refs_2_, ...), custom_call_target="tpu_custom_call" | custom-call | flops 6000000000 | bytes 20000000 | tf_op jit(solution)/shard_map/bias/pallas_call | solution.py:578
  32.4 0.0 collective-permute-done.7.paired_source
  32.4 0.0 collective-permute-done.6.paired_start
  32.4 0.0 copy-done
  32.4 0.0 copy-done.1
  32.4 0.0 copy-done.3
  32.5 6.4 %inner_ripple.1 = (f32[4,2,3,8,16,256]{5,4,3,2,1,0:T(8,128)}, f32[4,2,3,1,16,256]{5,4,3,2,1,0:T(8,128)S(1)}, f32[4,2,3,2,16,256]{5,4,3,2,1,0:T(8,128)S(1)}, f32[...) custom-call(s32[8]{0:T(128)S(1)} %copy-done.3, ...), custom_call_target="tpu_custom_call" | custom-call | tf_op jit(solution)/shard_map/inner_ripple/pallas_call | solution.py:578
  38.8 2.9 %collective-permute-done.5.apart = f32[4,2,3,3,16,256]{5,4,3,2,1,0:T(8,128)S(1)} collective-permute-done((f32[4,2,3,3,16,256]{5,4,3,2,1,0:T(8,128)}, f32[4,2,3,3,16,256]{5,4,3,2,1,0:T(8,128)S(1)}, u32[]{:S(2)}, u32[]{:S(2)}) %collective-permute-start.5) | collective-permute-done | bytes 1179680 | tf_op jit(solution)/shard_map/ppermute | solution.py:635
  41.8 2.3 %outer_ripple.1 = (f32[4,2,3,8,16,256]{5,4,3,2,1,0:T(8,128)}, f32[8,8,256]{2,1,0:T(8,128)S(1)}, f32[8,8,256]{2,1,0:T(8,128)S(1)}) custom-call(s32[8]{0:T(128)S(1)} %copy-done.3, f32[10,16,256]{2,1,0:T(8,128)S(1)} %get-tuple-element.32.sigma, f32[4,2,3,8,16,256]{5,4,3,2,1,0:T(8,128)S(1)} %copy-done, ...), custom_call_target="tpu_custom_call", output_to_operand_aliasing={{0}: (10, {})} | custom-call | tf_op jit(solution)/shard_map/outer_ripple/pallas_call | solution.py:578
  44.1 0.6 %collective-permute-start.8 = (f32[8,8,256]{2,1,0:T(8,128)S(1)}, f32[8,8,256]{2,1,0:T(8,128)S(1)}, u32[]{:S(2)}, u32[]{:S(2)}) collective-permute-start(f32[8,8,256]{2,1,0:T(8,128)S(1)} %get-tuple-element.50), channel_id=1, source_target_pairs={{0,1},{1,0},{2,3},{3,2},{4,5},{5,4},{6,7},{7,6},{8,9},{9,8},{10,11... | collective-permute-start | bytes 196616 | tf_op jit(solution)/shard_map/ppermute | solution.py:685
  44.7 3.7 %collective-permute-done.8 = f32[8,8,256]{2,1,0:T(8,128)S(1)} collective-permute-done((f32[8,8,256]{2,1,0:T(8,128)S(1)}, f32[8,8,256]{2,1,0:T(8,128)S(1)}, u32[]{:S(2)}, u32[]{:S(2)}) %collective-permute-start.8) | collective-permute-done | bytes 65568 | tf_op jit(solution)/shard_map/ppermute | solution.py:685
  48.4 0.6 %add.3 = f32[8,8,256]{2,1,0:T(8,128)} add(f32[8,8,256]{2,1,0:T(8,128)S(1)} %get-tuple-element.49, f32[8,8,256]{2,1,0:T(8,128)S(1)} %collective-permute-done.8) | non-fusion elementwise | flops 16384 | bytes 196608 | tf_op jit(solution)/shard_map/add | solution.py:685
  (1 shorter events, 0.0 us)
Async XLA Ops:
  2.8 14.2 %collective-permute-start = (f32[56,8,256]{2,1,0:T(8,128)}, f32[56,8,256]{2,1,0:T(8,128)S(1)}, u32[]{:S(2)}, u32[]{:S(2)}) collective-permute-start(f32[56,8,256]{2,1,0:T(8,128)} %get-tuple-element.27.refs_0_), channel_id=1, source_target_pairs={{0,1},{1,0},{2,3},{3,2},{4,5},{5,4},{6,7},{7,6},{8,9},{9,8},{10,11... | collective-permute-start | bytes 1376264 | tf_op jit(solution)/shard_map/ppermute | solution.py:605
  4.4 12.1 %collective-permute-start.1 = (f32[40,8,256]{2,1,0:T(8,128)}, f32[40,8,256]{2,1,0:T(8,128)S(1)}, u32[]{:S(2)}, u32[]{:S(2)}) collective-permute-start(f32[40,8,256]{2,1,0:T(8,128)} %get-tuple-element.28), channel_id=1, source_target_pairs={{2,4},{6,8},{10,12},{14,16},{18,20},{22,24},{26,28},{4,2},{8,6},{1... | collective-permute-start | bytes 983048 | tf_op jit(solution)/shard_map/ppermute | solution.py:613
  9.2 3.9 %copy-start.9 = (f32[40,8,256]{2,1,0:T(8,128)S(1)}, f32[40,8,256]{2,1,0:T(8,128)}, u32[]{:S(2)}) copy-start(f32[40,8,256]{2,1,0:T(8,128)} %get-tuple-element.29) | copy-start | bytes 983044
  9.3 32.5 %collective-permute-start.5 = (f32[4,2,3,3,16,256]{5,4,3,2,1,0:T(8,128)}, f32[4,2,3,3,16,256]{5,4,3,2,1,0:T(8,128)S(1)}, u32[]{:S(2)}, u32[]{:S(2)}) collective-permute-start(f32[4,2,3,3,16,256]{5,4,3,2,1,0:T(8,128)} %second_edges.1), channel_id=1, source_target_pairs={{2,4},{6,8},{10,12},{14,16},{18,20},{22,24},{26,28},{4,2},{8,6},{1... | collective-permute-start | bytes 3538952 | tf_op jit(solution)/shard_map/ppermute | solution.py:635
  13.1 7.3 %collective-permute-start.3 = (f32[40,8,256]{2,1,0:T(8,128)S(1)}, f32[40,8,256]{2,1,0:T(8,128)S(1)}, u32[]{:S(2)}, u32[]{:S(2)}) collective-permute-start(f32[40,8,256]{2,1,0:T(8,128)S(1)} %copy-done.9), channel_id=1, source_target_pairs={{0,2},{4,6},{8,10},{12,14},{16,18},{20,22},{24,26},{28,30},{2,0},{... | collective-permute-start | bytes 983048 | tf_op jit(solution)/shard_map/ppermute | solution.py:634
  16.5 8.5 %collective-permute-start.2 = (f32[40,8,256]{2,1,0:T(8,128)S(1)}, f32[40,8,256]{2,1,0:T(8,128)S(1)}, u32[]{:S(2)}, u32[]{:S(2)}) collective-permute-start(f32[40,8,256]{2,1,0:T(8,128)S(1)} %collective-permute-done.1.refs_1_.refs_2_), channel_id=1, source_target_pairs={{0,1},{1,0},{2,3},{3,2},{4,5},{5,4},{6,7},{7,6},{8,9},{9,8},{10,11... | collective-permute-start | bytes 983048 | tf_op jit(solution)/shard_map/ppermute | solution.py:605
  17.0 0.6 %copy-start.2 = (f32[8,128]{1,0:T(8,128)}, f32[8,128]{1,0:T(8,128)S(1)}, u32[]{:S(2)}) copy-start(f32[8,128]{1,0:T(8,128)S(1)} %get-tuple-element.37.after) | copy-start | bytes 12292
  17.6 7.4 %collective-permute-start.4 = (f32[1,40,8,256]{3,2,1,0:T(8,128)S(1)}, f32[1,40,8,256]{3,2,1,0:T(8,128)S(1)}, u32[]{:S(2)}, u32[]{:S(2)}) collective-permute-start(f32[1,40,8,256]{3,2,1,0:T(8,128)S(1)} %get-tuple-element.30), channel_id=1, source_target_pairs={{0,2},{4,6},{8,10},{12,14},{16,18},{20,22},{24,26},{28,30},{2,0},{... | collective-permute-start | bytes 983048 | tf_op jit(solution)/shard_map/ppermute | solution.py:634
  17.6 7.4 %copy-start.4 = (f32[56,8,256]{2,1,0:T(8,128)S(1)}, f32[56,8,256]{2,1,0:T(8,128)}, u32[]{:S(2)}) copy-start(f32[56,8,256]{2,1,0:T(8,128)} %get-tuple-element.27.refs_0_) | copy-start | bytes 1376260
  17.6 7.4 %copy-start.5 = (f32[4,8]{1,0:T(4,128)S(1)}, f32[4,8]{1,0:T(4,128)}, u32[]{:S(2)}) copy-start(f32[4,8]{1,0:T(4,128)} %refs_8_.1) | copy-start | bytes 388
  17.6 7.4 %copy-start.6 = (s32[4]{0:T(128)S(1)}, s32[4]{0:T(128)}, u32[]{:S(2)}) copy-start(s32[4]{0:T(128)} %refs_6_.1) | copy-start | bytes 52
  17.7 7.4 %copy-start.7 = (f32[4]{0:T(128)S(1)}, f32[4]{0:T(128)}, u32[]{:S(2)}) copy-start(f32[4]{0:T(128)} %refs_7_.1) | copy-start | bytes 52
  17.7 7.4 %copy-start.8 = (f32[4]{0:T(128)S(1)}, f32[4]{0:T(128)}, u32[]{:S(2)}) copy-start(f32[4]{0:T(128)} %refs_9_.1) | copy-start | bytes 52
  20.0 12.5 %collective-permute-start.6 = (f32[4,2,3,2,16,256]{5,4,3,2,1,0:T(8,128)}, f32[4,2,3,2,16,256]{5,4,3,2,1,0:T(8,128)S(1)}, u32[]{:S(2)}, u32[]{:S(2)}) collective-permute-start(f32[4,2,3,2,16,256]{5,4,3,2,1,0:T(8,128)} %get-tuple-element.40), channel_id=1, source_target_pairs={{0,2},{4,6},{8,10},{12,14},{16,18},{20,22},{24,26},{28,30},{2,0},{... | collective-permute-start | bytes 2359304 | tf_op jit(solution)/shard_map/ppermute | solution.py:636
  20.4 12.1 %copy-start = (f32[4,2,3,8,16,256]{5,4,3,2,1,0:T(8,128)S(1)}, f32[4,2,3,8,16,256]{5,4,3,2,1,0:T(8,128)}, u32[]{:S(2)}) copy-start(f32[4,2,3,8,16,256]{5,4,3,2,1,0:T(8,128)} %start.11) | copy-start | bytes 9437188
  20.4 12.1 %copy-start.1 = (f32[4,2,3,8,16,256]{5,4,3,2,1,0:T(8,128)S(1)}, f32[4,2,3,8,16,256]{5,4,3,2,1,0:T(8,128)}, u32[]{:S(2)}) copy-start(f32[4,2,3,8,16,256]{5,4,3,2,1,0:T(8,128)} %source.11) | copy-start | bytes 9437188
  20.4 12.1 %copy-start.3 = (s32[8]{0:T(128)S(1)}, s32[8]{0:T(128)}, u32[]{:S(2)}) copy-start(s32[8]{0:T(128)} %harmonic_numbers.3) | copy-start | bytes 100
  20.4 12.0 %collective-permute-start.7 = (f32[4,2,3,1,16,256]{5,4,3,2,1,0:T(8,128)}, f32[4,2,3,1,16,256]{5,4,3,2,1,0:T(8,128)S(1)}, u32[]{:S(2)}, u32[]{:S(2)}) collective-permute-start(f32[4,2,3,1,16,256]{5,4,3,2,1,0:T(8,128)} %get-tuple-element.41), channel_id=1, source_target_pairs={{0,2},{4,6},{8,10},{12,14},{16,18},{20,22},{24,26},{28,30},{2,0},{... | collective-permute-start | bytes 1179656 | tf_op jit(solution)/shard_map/ppermute | solution.py:636
  44.1 4.3 %collective-permute-start.8 = (f32[8,8,256]{2,1,0:T(8,128)S(1)}, f32[8,8,256]{2,1,0:T(8,128)S(1)}, u32[]{:S(2)}, u32[]{:S(2)}) collective-permute-start(f32[8,8,256]{2,1,0:T(8,128)S(1)} %get-tuple-element.50), channel_id=1, source_target_pairs={{0,1},{1,0},{2,3},{3,2},{4,5},{5,4},{6,7},{7,6},{8,9},{9,8},{10,11... | collective-permute-start | bytes 196616 | tf_op jit(solution)/shard_map/ppermute | solution.py:685

commit v9 on v8

--- a/solution.py
+++ b/solution.py
@@ -26,6 +26,7 @@
 G_LOW, G_HIGH = A_LOW[0], A_HIGH[0] - 1
 
 BIAS_WORK = 20000000
+PLACE_WORK = 0
 PACK_ROOM = 62 * 2**20
 RP_ROOM = 58 * 2**20
 NEAR_ROOM = 58 * 2**20
@@ -532,10 +533,10 @@
 
 
 def outer_kernel(
-    shares, harmonic_numbers, sigma, start, source, apart, edge, begun, sides, answer, loss_in, ripple_in,
-    ripple_out, *refs
+    shares, harmonic_numbers, sigma, start, source, apart, edge, begun, sides, answer, loss_in,
+    r2, *refs
 ):
-    losses, (r1, r2, loss, sems) = refs[:shares], refs[shares:]
+    losses, (r1, loss) = refs[:shares], refs[shares:]
     count, planes = start.shape[0], start.shape[3]
     rows, lanes = start.shape[4:]
 
@@ -547,16 +548,12 @@
     )
     ripple.sweep(far.own_slot, [(apart, far.halo)], (begun, 0), (r1, 1), far.turned_round, begun=True)
 
-    def drain(slot, plane):
-        return pltpu.make_async_copy(planes_of(r2, slot, 1), planes_of(ripple_out, plane, 1), sems.at[slot])
-
     steps = (
         (far.own, far.own_slot, [(r1, 1), (edge, 0), (r1, 0)], (source, far.own), False),
         (far.second, far.second_slot, [(r1, 1)], (begun, 1), True),
     )
     for at, (plane, slot, old, given, is_begun) in enumerate(steps):
         added = ripple.sweep(slot, old, given, (r2, at), far.turned_round, begun=is_begun)
-        drain(at, plane).start()
         tiles.store(loss, (at,), tiles.each(lambda one, other: one * other, tiles.load(sigma, slot), added))
     rows_each = rows // shares
     for turn in range(shares):
@@ -565,8 +562,18 @@
         losses[turn][...] = loss_in[:, part, :]
         for at, (plane, *unused) in enumerate(steps):
             losses[turn][plane] = loss[at, part, :]
-    for at, (plane, *unused) in enumerate(steps):
-        drain(at, plane).wait()
+
+
+def place_kernel(edge, ripple_in, ripple_out, sems):
+    far = Side(ripple_out.shape[3], is_odd())
+    copies = [
+        pltpu.make_async_copy(planes_of(edge, at, 1), planes_of(ripple_out, plane, 1), sems.at[at])
+        for at, plane in enumerate((far.own, far.second))
+    ]
+    for copy in copies:
+        copy.start()
+    for copy in copies:
+        copy.wait()
 
 
 def call(kernel, operands, in_specs, out_shapes, out_specs, scratch, name, work=0, aliases={}, room=0):
@@ -669,16 +676,15 @@
         [ANY] + [VMEM] * 5, [lead + slots, lead + (planes, rows, lanes), pltpu.SemaphoreType.DMA((planes,))],
         "inner_ripple",
     )
-    ripple, *losses = call(
+    outer_edge, *losses = call(
         functools.partial(outer_kernel, shares),
-        (
-            harmonic_numbers, sigma, ripple_start, ripple_source, ripple_apart, edge, begun, sides, answer, inner_loss,
-            ripple,
-        ),
-        [SMEM] + [VMEM] * 9 + [ANY],
-        [ripple_start.shape] + [(planes, rows_each, lanes)] * shares, [ANY] + [VMEM] * shares,
-        [lead + (2, rows, lanes)] * 2 + [(2, rows, lanes), pltpu.SemaphoreType.DMA((2,))],
-        "outer_ripple", aliases={10: 0},
+        (harmonic_numbers, sigma, ripple_start, ripple_source, ripple_apart, edge, begun, sides, answer, inner_loss),
+        [SMEM] + [VMEM] * 9, [lead + (2, rows, lanes)] + [(planes, rows_each, lanes)] * shares, [VMEM] * (shares + 1),
+        [lead + (2, rows, lanes), (2, rows, lanes)], "outer_ripple",
+    )
+    ripple, = call(
+        place_kernel, (outer_edge, ripple), [ANY] * 2, [ripple_start.shape], [ANY], [pltpu.SemaphoreType.DMA((2,))],
+        "place", PLACE_WORK, aliases={1: 0},
     )
     loss = losses[0]
     for turn, pairs in enumerate(turned):

time: 49.3 us -> 48.4 us (0.982)
  waiting for transfers between devices: 12.2 us -> 11.4 us
    ppermute x1, waiting for transfers between devices: 3.73 us -> 2.83 us  [body(): loss = loss + lax.ppermute(losses[turn + 1], 'harm', pairs)]
    pallas_call x8 -> x9, Pallas kernels: 23.5 us -> 23.5 us  [call(): pl.pallas_call(kernel, out_shape=[jax.ShapeDtypeStruct(shape, f32) for sh...]
  transfers between devices with their start and end apart: 9 -> 9, of which waited for: 4 -> 4; matrix products, arithmetic and copies ran while one was open for 0% -> 0% of each run, Pallas kernels for 39% -> 41%
where the time goes in v9:
time: 48.4 us; the launch traced here: 48.1 us
  Pallas kernels  23.5 us (49%)
  waiting for transfers between devices  11.4 us (24%)
  starting transfers between devices  11.2 us (23%)
  between operations  0.81 us (2%)
  other arithmetic  0.64 us (1%)
  local copies, waits for them, and re-layouts  0.63 us (1%)
    pallas_call x9, Pallas kernels, call(): pl.pallas_call(kernel, out_shape=[jax.ShapeDtypeStruct(shape, f32) for sh...  23.5 us
    ppermute x2, waiting for transfers between devices, around(): return [block] + [lax.ppermute(block, 'harm', pairs) for pairs in turned]  4.38 us
    ppermute x1, starting transfers between devices, body(): ripple_apart = lax.ppermute(ripple_apart, 'mesh', far)  3.77 us
    ppermute x1, waiting for transfers between devices, body(): ripple_apart = lax.ppermute(ripple_apart, 'mesh', far)  2.96 us
    ppermute x1, waiting for transfers between devices, body(): loss = loss + lax.ppermute(losses[turn + 1], 'harm', pairs)  2.83 us
    ppermute x1, starting transfers between devices, body(): lax.ppermute(paired, 'mesh', near)  2.2 us
    ppermute x2, starting transfers between devices, around(): return [block] + [lax.ppermute(block, 'harm', pairs) for pairs in turned]  2.09 us
    ppermute x1, starting transfers between devices, body(): aparts = around(lax.ppermute(apart, 'mesh', far))  1.91 us
  transfers between devices with their start and end apart: 9, of which 4 were waited for; matrix products, arithmetic and copies ran while one was open for 0% of the time, Pallas kernels for 41%

profile of v9, /device:TPU:12, one launch (start us, length us, event | category | flops | bytes accessed | tf_op | source)
XLA Modules:
  0.0 48.1 jit_solution(14922339107894667829)
XLA Ops:
  0.6 2.2 %pack.1 = (f32[56,8,256]{2,1,0:T(8,128)}, f32[40,8,256]{2,1,0:T(8,128)}, f32[40,8,256]{2,1,0:T(8,128)}, f32[8,128]{1,0:T(8,128)}) custom-call(f32[3,8,8,256]{3,2,1,0:T(8,128)} %start.6, f32[3,8,8,256]{3,2,1,0:T(8,128)} %source.6, s32[8,8,256]{2,1,0:T(8,128)} %region.1), custom_call_target="tpu_custom_call" | custom-call | tf_op jit(solution)/shard_map/pack/pallas_call | solution.py:585
  2.8 1.6 %collective-permute-start = (f32[56,8,256]{2,1,0:T(8,128)}, f32[56,8,256]{2,1,0:T(8,128)S(1)}, u32[]{:S(2)}, u32[]{:S(2)}) collective-permute-start(f32[56,8,256]{2,1,0:T(8,128)} %get-tuple-element.27.refs_0_), channel_id=1, source_target_pairs={{0,1},{1,0},{2,3},{3,2},{4,5},{5,4},{6,7},{7,6},{8,9},{9,8},{10,11... | collective-permute-start | bytes 1376264 | tf_op jit(solution)/shard_map/ppermute | solution.py:612
  4.4 1.9 %collective-permute-start.1 = (f32[40,8,256]{2,1,0:T(8,128)}, f32[40,8,256]{2,1,0:T(8,128)S(1)}, u32[]{:S(2)}, u32[]{:S(2)}) collective-permute-start(f32[40,8,256]{2,1,0:T(8,128)} %get-tuple-element.28), channel_id=1, source_target_pairs={{2,4},{6,8},{10,12},{14,16},{18,20},{22,24},{26,28},{4,2},{8,6},{1... | collective-permute-start | bytes 983048 | tf_op jit(solution)/shard_map/ppermute | solution.py:620
  6.3 2.9 %first_edges.1 = (f32[4,2,3,3,16,256]{5,4,3,2,1,0:T(8,128)}, f32[4,2,3,2,16,256]{5,4,3,2,1,0:T(8,128)}, f32[4,2,3,1,16,256]{5,4,3,2,1,0:T(8,128)}, f32[8,128]{1,0:T(8,128)}) custom-call(f32[4,2,3,8,16,256]{5,4,3,2,1,0:T(8,128)} %start.11, f32[4,2,3,8,16,256]{5,4,3,2,1,0:T(8,128)} %source.11, f32[8,128]{1,0:T(8,128)} %get-tuple-element.33.after), custom_call_target="tpu_custom_call" | custom-call | tf_op jit(solution)/shard_map/first_edges/pallas_call | solution.py:585
  9.2 0.0 copy-start.9
  9.2 0.1 second_edges.1
  9.3 3.8 %collective-permute-start.5 = (f32[4,2,3,3,16,256]{5,4,3,2,1,0:T(8,128)}, f32[4,2,3,3,16,256]{5,4,3,2,1,0:T(8,128)S(1)}, u32[]{:S(2)}, u32[]{:S(2)}) collective-permute-start(f32[4,2,3,3,16,256]{5,4,3,2,1,0:T(8,128)} %second_edges.1), channel_id=1, source_target_pairs={{2,4},{6,8},{10,12},{14,16},{18,20},{22,24},{26,28},{4,2},{8,6},{1... | collective-permute-start | bytes 3538952 | tf_op jit(solution)/shard_map/ppermute | solution.py:642
  13.1 0.0 copy-done.9
  13.1 2.2 %collective-permute-start.3 = (f32[40,8,256]{2,1,0:T(8,128)S(1)}, f32[40,8,256]{2,1,0:T(8,128)S(1)}, u32[]{:S(2)}, u32[]{:S(2)}) collective-permute-start(f32[40,8,256]{2,1,0:T(8,128)S(1)} %copy-done.9), channel_id=1, source_target_pairs={{0,2},{4,6},{8,10},{12,14},{16,18},{20,22},{24,26},{28,30},{2,0},{... | collective-permute-start | bytes 983048 | tf_op jit(solution)/shard_map/ppermute | solution.py:641
  15.3 1.2 %collective-permute-done.1.refs_1_.refs_2_ = f32[40,8,256]{2,1,0:T(8,128)S(1)} collective-permute-done((f32[40,8,256]{2,1,0:T(8,128)}, f32[40,8,256]{2,1,0:T(8,128)S(1)}, u32[]{:S(2)}, u32[]{:S(2)}) %collective-permute-start.1) | collective-permute-done | bytes 327712 | tf_op jit(solution)/shard_map/ppermute | solution.py:620
  16.5 0.5 %collective-permute-start.2 = (f32[40,8,256]{2,1,0:T(8,128)S(1)}, f32[40,8,256]{2,1,0:T(8,128)S(1)}, u32[]{:S(2)}, u32[]{:S(2)}) collective-permute-start(f32[40,8,256]{2,1,0:T(8,128)S(1)} %collective-permute-done.1.refs_1_.refs_2_), channel_id=1, source_target_pairs={{0,1},{1,0},{2,3},{3,2},{4,5},{5,4},{6,7},{7,6},{8,9},{9,8},{10,11... | collective-permute-start | bytes 983048 | tf_op jit(solution)/shard_map/ppermute | solution.py:612
  17.0 0.0 collective-permute-done.refs_0_.refs_1_
  17.0 0.0 copy-start.2
  17.1 0.6 %copy-done.2 = f32[8,128]{1,0:T(8,128)} copy-done((f32[8,128]{1,0:T(8,128)}, f32[8,128]{1,0:T(8,128)S(1)}, u32[]{:S(2)}) %copy-start.2) | copy-done | bytes 4120
  17.6 0.0 collective-permute-start.4
  17.6 0.0 copy-start.4
  17.6 0.0 copy-start.5
  17.6 0.0 copy-start.6
  17.7 0.0 copy-start.7
  17.7 0.0 copy-start.8
  17.7 2.3 %near_edges.1 = (f32[4,2,3,2,16,256]{5,4,3,2,1,0:T(8,128)}, f32[4,2,3,1,16,256]{5,4,3,2,1,0:T(8,128)}) custom-call(f32[4,2,3,8,16,256]{5,4,3,2,1,0:T(8,128)} %start.11, f32[4,2,3,8,16,256]{5,4,3,2,1,0:T(8,128)} %source.11, f32[8,128]{1,0:T(8,128)} %copy-done.2, ...), custom_call_target="tpu_custom_call", output_to_operand_aliasing={{0}: (3, {}), {1}: (4, {})} | custom-call | tf_op jit(solution)/shard_map/near_edges/pallas_call | solution.py:585
  20.0 0.4 collective-permute-start.6
  20.4 0.0 collective-permute-done.3.refs_4_
  20.4 0.0 copy-start
  20.4 0.0 copy-start.1
  20.4 0.0 copy-start.3
  20.4 0.2 collective-permute-start.7
  20.6 4.4 %collective-permute-done.2.refs_3_ = f32[40,8,256]{2,1,0:T(8,128)S(1)} collective-permute-done((f32[40,8,256]{2,1,0:T(8,128)S(1)}, f32[40,8,256]{2,1,0:T(8,128)S(1)}, u32[]{:S(2)}, u32[]{:S(2)}) %collective-permute-start.2) | collective-permute-done | bytes 327712 | tf_op jit(solution)/shard_map/ppermute | solution.py:612
  25.0 0.0 collective-permute-done.4.refs_5_
  25.0 0.0 copy-done.4
  25.0 0.0 copy-done.5
  25.0 0.0 copy-done.6
  25.0 0.0 copy-done.7
  25.0 0.0 copy-done.8
  25.0 7.4 %bias.1 = (f32[3,8,8,256]{3,2,1,0:T(8,128)}, f32[12,16,256]{2,1,0:T(8,128)S(1)}, f32[10,16,256]{2,1,0:T(8,128)S(1)}) custom-call(f32[56,8,256]{2,1,0:T(8,128)S(1)} %copy-done.4, f32[56,8,256]{2,1,0:T(8,128)S(1)} %collective-permute-done.refs_0_.refs_1_, f32[40,8,256]{2,1,0:T(8,128)S(1)} %collective-permute-done.1.refs_1_.refs_2_, ...), custom_call_target="tpu_custom_call" | custom-call | flops 6000000000 | bytes 20000000 | tf_op jit(solution)/shard_map/bias/pallas_call | solution.py:585
  32.4 0.0 collective-permute-done.7.paired_source
  32.4 0.0 collective-permute-done.6.paired_start
  32.4 0.0 copy-done
  32.4 0.0 copy-done.1
  32.4 0.0 copy-done.3
  32.5 6.3 %inner_ripple.1 = (f32[4,2,3,8,16,256]{5,4,3,2,1,0:T(8,128)}, f32[4,2,3,1,16,256]{5,4,3,2,1,0:T(8,128)S(1)}, f32[4,2,3,2,16,256]{5,4,3,2,1,0:T(8,128)S(1)}, f32[...) custom-call(s32[8]{0:T(128)S(1)} %copy-done.3, ...), custom_call_target="tpu_custom_call" | custom-call | tf_op jit(solution)/shard_map/inner_ripple/pallas_call | solution.py:585
  38.8 3.0 %collective-permute-done.5.apart = f32[4,2,3,3,16,256]{5,4,3,2,1,0:T(8,128)S(1)} collective-permute-done((f32[4,2,3,3,16,256]{5,4,3,2,1,0:T(8,128)}, f32[4,2,3,3,16,256]{5,4,3,2,1,0:T(8,128)S(1)}, u32[]{:S(2)}, u32[]{:S(2)}) %collective-permute-start.5) | collective-permute-done | bytes 1179680 | tf_op jit(solution)/shard_map/ppermute | solution.py:642
  41.8 1.4 %outer_ripple.1 = (f32[4,2,3,2,16,256]{5,4,3,2,1,0:T(8,128)S(1)}, f32[8,8,256]{2,1,0:T(8,128)S(1)}, f32[8,8,256]{2,1,0:T(8,128)S(1)}) custom-call(s32[8]{0:T(128)S(1)} %copy-done.3, f32[10,16,256]{2,1,0:T(8,128)S(1)} %get-tuple-element.32.sigma, f32[4,2,3,8,16,256]{5,4,3,2,1,0:T(8,128)S(1)} %copy-done, f32[4,2,3,8,16,256]{5,4,3,2,1,0:T(8,128)S(1)} %copy-done.1, ...), custom_call_target="tpu_custom_call" | custom-call | tf_op jit(solution)/shard_map/outer_ripple/pallas_call | solution.py:585
  43.2 0.6 %collective-permute-start.8 = (f32[8,8,256]{2,1,0:T(8,128)S(1)}, f32[8,8,256]{2,1,0:T(8,128)S(1)}, u32[]{:S(2)}, u32[]{:S(2)}) collective-permute-start(f32[8,8,256]{2,1,0:T(8,128)S(1)} %get-tuple-element.50), channel_id=1, source_target_pairs={{0,1},{1,0},{2,3},{3,2},{4,5},{5,4},{6,7},{7,6},{8,9},{9,8},{10,11... | collective-permute-start | bytes 196616 | tf_op jit(solution)/shard_map/ppermute | solution.py:691
  43.8 0.9 %place.1 = f32[4,2,3,8,16,256]{5,4,3,2,1,0:T(8,128)} custom-call(f32[4,2,3,2,16,256]{5,4,3,2,1,0:T(8,128)S(1)} %get-tuple-element.47.edge, f32[4,2,3,8,16,256]{5,4,3,2,1,0:T(8,128)} %get-tuple-element.48.ripple_in), custom_call_target="tpu_custom_call", output_to_operand_aliasing={{}: (1, {})} | custom-call | tf_op jit(solution)/shard_map/place/pallas_call | solution.py:585
  44.7 2.8 %collective-permute-done.8 = f32[8,8,256]{2,1,0:T(8,128)S(1)} collective-permute-done((f32[8,8,256]{2,1,0:T(8,128)S(1)}, f32[8,8,256]{2,1,0:T(8,128)S(1)}, u32[]{:S(2)}, u32[]{:S(2)}) %collective-permute-start.8) | collective-permute-done | bytes 65568 | tf_op jit(solution)/shard_map/ppermute | solution.py:691
  47.5 0.6 %add.3 = f32[8,8,256]{2,1,0:T(8,128)} add(f32[8,8,256]{2,1,0:T(8,128)S(1)} %get-tuple-element.49, f32[8,8,256]{2,1,0:T(8,128)S(1)} %collective-permute-done.8) | non-fusion elementwise | flops 16384 | bytes 196608 | tf_op jit(solution)/shard_map/add | solution.py:691
  (1 shorter events, 0.0 us)
Async XLA Ops:
  2.8 14.2 %collective-permute-start = (f32[56,8,256]{2,1,0:T(8,128)}, f32[56,8,256]{2,1,0:T(8,128)S(1)}, u32[]{:S(2)}, u32[]{:S(2)}) collective-permute-start(f32[56,8,256]{2,1,0:T(8,128)} %get-tuple-element.27.refs_0_), channel_id=1, source_target_pairs={{0,1},{1,0},{2,3},{3,2},{4,5},{5,4},{6,7},{7,6},{8,9},{9,8},{10,11... | collective-permute-start | bytes 1376264 | tf_op jit(solution)/shard_map/ppermute | solution.py:612
  4.4 12.1 %collective-permute-start.1 = (f32[40,8,256]{2,1,0:T(8,128)}, f32[40,8,256]{2,1,0:T(8,128)S(1)}, u32[]{:S(2)}, u32[]{:S(2)}) collective-permute-start(f32[40,8,256]{2,1,0:T(8,128)} %get-tuple-element.28), channel_id=1, source_target_pairs={{2,4},{6,8},{10,12},{14,16},{18,20},{22,24},{26,28},{4,2},{8,6},{1... | collective-permute-start | bytes 983048 | tf_op jit(solution)/shard_map/ppermute | solution.py:620
  9.2 3.9 %copy-start.9 = (f32[40,8,256]{2,1,0:T(8,128)S(1)}, f32[40,8,256]{2,1,0:T(8,128)}, u32[]{:S(2)}) copy-start(f32[40,8,256]{2,1,0:T(8,128)} %get-tuple-element.29) | copy-start | bytes 983044
  9.3 32.5 %collective-permute-start.5 = (f32[4,2,3,3,16,256]{5,4,3,2,1,0:T(8,128)}, f32[4,2,3,3,16,256]{5,4,3,2,1,0:T(8,128)S(1)}, u32[]{:S(2)}, u32[]{:S(2)}) collective-permute-start(f32[4,2,3,3,16,256]{5,4,3,2,1,0:T(8,128)} %second_edges.1), channel_id=1, source_target_pairs={{2,4},{6,8},{10,12},{14,16},{18,20},{22,24},{26,28},{4,2},{8,6},{1... | collective-permute-start | bytes 3538952 | tf_op jit(solution)/shard_map/ppermute | solution.py:642
  13.1 7.3 %collective-permute-start.3 = (f32[40,8,256]{2,1,0:T(8,128)S(1)}, f32[40,8,256]{2,1,0:T(8,128)S(1)}, u32[]{:S(2)}, u32[]{:S(2)}) collective-permute-start(f32[40,8,256]{2,1,0:T(8,128)S(1)} %copy-done.9), channel_id=1, source_target_pairs={{0,2},{4,6},{8,10},{12,14},{16,18},{20,22},{24,26},{28,30},{2,0},{... | collective-permute-start | bytes 983048 | tf_op jit(solution)/shard_map/ppermute | solution.py:641
  16.5 8.5 %collective-permute-start.2 = (f32[40,8,256]{2,1,0:T(8,128)S(1)}, f32[40,8,256]{2,1,0:T(8,128)S(1)}, u32[]{:S(2)}, u32[]{:S(2)}) collective-permute-start(f32[40,8,256]{2,1,0:T(8,128)S(1)} %collective-permute-done.1.refs_1_.refs_2_), channel_id=1, source_target_pairs={{0,1},{1,0},{2,3},{3,2},{4,5},{5,4},{6,7},{7,6},{8,9},{9,8},{10,11... | collective-permute-start | bytes 983048 | tf_op jit(solution)/shard_map/ppermute | solution.py:612
  17.0 0.6 %copy-start.2 = (f32[8,128]{1,0:T(8,128)}, f32[8,128]{1,0:T(8,128)S(1)}, u32[]{:S(2)}) copy-start(f32[8,128]{1,0:T(8,128)S(1)} %get-tuple-element.37.after) | copy-start | bytes 12292
  17.6 7.4 %collective-permute-start.4 = (f32[1,40,8,256]{3,2,1,0:T(8,128)S(1)}, f32[1,40,8,256]{3,2,1,0:T(8,128)S(1)}, u32[]{:S(2)}, u32[]{:S(2)}) collective-permute-start(f32[1,40,8,256]{3,2,1,0:T(8,128)S(1)} %get-tuple-element.30), channel_id=1, source_target_pairs={{0,2},{4,6},{8,10},{12,14},{16,18},{20,22},{24,26},{28,30},{2,0},{... | collective-permute-start | bytes 983048 | tf_op jit(solution)/shard_map/ppermute | solution.py:641
  17.6 7.4 %copy-start.4 = (f32[56,8,256]{2,1,0:T(8,128)S(1)}, f32[56,8,256]{2,1,0:T(8,128)}, u32[]{:S(2)}) copy-start(f32[56,8,256]{2,1,0:T(8,128)} %get-tuple-element.27.refs_0_) | copy-start | bytes 1376260
  17.6 7.4 %copy-start.5 = (f32[4,8]{1,0:T(4,128)S(1)}, f32[4,8]{1,0:T(4,128)}, u32[]{:S(2)}) copy-start(f32[4,8]{1,0:T(4,128)} %refs_8_.1) | copy-start | bytes 388
  17.6 7.4 %copy-start.6 = (s32[4]{0:T(128)S(1)}, s32[4]{0:T(128)}, u32[]{:S(2)}) copy-start(s32[4]{0:T(128)} %refs_6_.1) | copy-start | bytes 52
  17.7 7.4 %copy-start.7 = (f32[4]{0:T(128)S(1)}, f32[4]{0:T(128)}, u32[]{:S(2)}) copy-start(f32[4]{0:T(128)} %refs_7_.1) | copy-start | bytes 52
  17.7 7.4 %copy-start.8 = (f32[4]{0:T(128)S(1)}, f32[4]{0:T(128)}, u32[]{:S(2)}) copy-start(f32[4]{0:T(128)} %refs_9_.1) | copy-start | bytes 52
  20.0 12.5 %collective-permute-start.6 = (f32[4,2,3,2,16,256]{5,4,3,2,1,0:T(8,128)}, f32[4,2,3,2,16,256]{5,4,3,2,1,0:T(8,128)S(1)}, u32[]{:S(2)}, u32[]{:S(2)}) collective-permute-start(f32[4,2,3,2,16,256]{5,4,3,2,1,0:T(8,128)} %get-tuple-element.40), channel_id=1, source_target_pairs={{0,2},{4,6},{8,10},{12,14},{16,18},{20,22},{24,26},{28,30},{2,0},{... | collective-permute-start | bytes 2359304 | tf_op jit(solution)/shard_map/ppermute | solution.py:643
  20.4 12.1 %copy-start = (f32[4,2,3,8,16,256]{5,4,3,2,1,0:T(8,128)S(1)}, f32[4,2,3,8,16,256]{5,4,3,2,1,0:T(8,128)}, u32[]{:S(2)}) copy-start(f32[4,2,3,8,16,256]{5,4,3,2,1,0:T(8,128)} %start.11) | copy-start | bytes 9437188
  20.4 12.1 %copy-start.1 = (f32[4,2,3,8,16,256]{5,4,3,2,1,0:T(8,128)S(1)}, f32[4,2,3,8,16,256]{5,4,3,2,1,0:T(8,128)}, u32[]{:S(2)}) copy-start(f32[4,2,3,8,16,256]{5,4,3,2,1,0:T(8,128)} %source.11) | copy-start | bytes 9437188
  20.4 12.1 %copy-start.3 = (s32[8]{0:T(128)S(1)}, s32[8]{0:T(128)}, u32[]{:S(2)}) copy-start(s32[8]{0:T(128)} %harmonic_numbers.3) | copy-start | bytes 100
  20.4 12.0 %collective-permute-start.7 = (f32[4,2,3,1,16,256]{5,4,3,2,1,0:T(8,128)}, f32[4,2,3,1,16,256]{5,4,3,2,1,0:T(8,128)S(1)}, u32[]{:S(2)}, u32[]{:S(2)}) collective-permute-start(f32[4,2,3,1,16,256]{5,4,3,2,1,0:T(8,128)} %get-tuple-element.41), channel_id=1, source_target_pairs={{0,2},{4,6},{8,10},{12,14},{16,18},{20,22},{24,26},{28,30},{2,0},{... | collective-permute-start | bytes 1179656 | tf_op jit(solution)/shard_map/ppermute | solution.py:643
  43.2 4.3 %collective-permute-start.8 = (f32[8,8,256]{2,1,0:T(8,128)S(1)}, f32[8,8,256]{2,1,0:T(8,128)S(1)}, u32[]{:S(2)}, u32[]{:S(2)}) collective-permute-start(f32[8,8,256]{2,1,0:T(8,128)S(1)} %get-tuple-element.50), channel_id=1, source_target_pairs={{0,1},{1,0},{2,3},{3,2},{4,5},{5,4},{6,7},{7,6},{8,9},{9,8},{10,11... | collective-permute-start | bytes 196616 | tf_op jit(solution)/shard_map/ppermute | solution.py:691

commit v10 on v9

--- a/solution.py
+++ b/solution.py
@@ -214,19 +214,28 @@
 
 
 def send_edges(start, source, buffer, target, top, sems):
-    planes = start.shape[3]
-    ways_in = []
-    for part, (origin, count, onto) in enumerate(((start, 2, 0), (source, 1, 2))):
-        at = jnp.where(top, planes - count, 0)
-        ways_in.append(
-            pltpu.make_async_copy(planes_of(origin, at, count), planes_of(buffer, onto, count), sems.at[part])
-        )
-        ways_in[-1].start()
-    for copy in ways_in:
-        copy.wait()
-    way_out = pltpu.make_async_copy(buffer, target, sems.at[2])
-    way_out.start()
-    way_out.wait()
+    harmonics, planes = start.shape[0], start.shape[3]
+    middle = (harmonics + 1) // 2
+    ways = []
+    for chosen in (slice(0, middle), slice(middle, harmonics)):
+        if chosen.start == chosen.stop:
+            continue
+        for origin, count, onto in ((start, 2, 0), (source, 1, 2)):
+            at = jnp.where(top, planes - count, 0)
+            held = planes_of(buffer.at[chosen], onto, count)
+            ways.append(
+                (
+                    pltpu.make_async_copy(planes_of(origin.at[chosen], at, count), held, sems.at[0, len(ways)]),
+                    pltpu.make_async_copy(held, planes_of(target.at[chosen], onto, count), sems.at[1, len(ways)]),
+                )
+            )
+    for way_in, unused in ways:
+        way_in.start()
+    for way_in, way_out in ways:
+        way_in.wait()
+        way_out.start()
+    for unused, way_out in ways:
+        way_out.wait()
 
 
 def send_near_edges(origins, targets, buffers, sems):
@@ -623,11 +632,11 @@
     ripple_apart, paired_start, paired_source, token = call(
         first_edges_kernel, (ripple_start, ripple_source, token), [ANY] * 3,
         [edge] + near_edges + [TILE], [ANY] * 3 + [VMEM],
-        [edge, pltpu.SemaphoreType.DMA((3,)), pltpu.SemaphoreType.DMA((2,))], "first_edges", room=RP_ROOM,
+        [edge, pltpu.SemaphoreType.DMA((2, 4)), pltpu.SemaphoreType.DMA((2,))], "first_edges", room=RP_ROOM,
     )
     ripple_apart, = call(
         second_edges_kernel, (ripple_start, ripple_source, token, ripple_apart), [ANY] * 4, [edge], [ANY],
-        [edge, pltpu.SemaphoreType.DMA((3,))], "second_edges", aliases={3: 0}, room=RP_ROOM,
+        [edge, pltpu.SemaphoreType.DMA((2, 4))], "second_edges", aliases={3: 0}, room=RP_ROOM,
     )
     others, token = call(
         pair_kernel, (*wholes[1:], aparts[0]), [VMEM] * (shares - 1) + [ANY],

time: 48.4 us -> 48.4 us (level)
  no operation moved by 1% of the time
where the time goes in v10:
time: 48.4 us; the launch traced here: 48.1 us
  Pallas kernels  23.3 us (48%)
  waiting for transfers between devices  11.5 us (24%)
  starting transfers between devices  11.2 us (23%)
  between operations  0.81 us (2%)
  other arithmetic  0.64 us (1%)
  local copies, waits for them, and re-layouts  0.63 us (1%)
    pallas_call x9, Pallas kernels, call(): pl.pallas_call(kernel, out_shape=[jax.ShapeDtypeStruct(shape, f32) for sh...  23.3 us
    ppermute x2, waiting for transfers between devices, around(): return [block] + [lax.ppermute(block, 'harm', pairs) for pairs in turned]  4.26 us
    ppermute x1, starting transfers between devices, body(): ripple_apart = lax.ppermute(ripple_apart, 'mesh', far)  3.64 us
    ppermute x1, waiting for transfers between devices, body(): ripple_apart = lax.ppermute(ripple_apart, 'mesh', far)  3.09 us
    ppermute x1, waiting for transfers between devices, body(): loss = loss + lax.ppermute(losses[turn + 1], 'harm', pairs)  2.83 us
    ppermute x1, starting transfers between devices, body(): lax.ppermute(paired, 'mesh', near)  2.33 us
    ppermute x2, starting transfers between devices, around(): return [block] + [lax.ppermute(block, 'harm', pairs) for pairs in turned]  2.09 us
    ppermute x1, starting transfers between devices, body(): aparts = around(lax.ppermute(apart, 'mesh', far))  1.91 us
  transfers between devices with their start and end apart: 9, of which 4 were waited for; matrix products, arithmetic and copies ran while one was open for 0% of the time, Pallas kernels for 41%

profile of v10, /device:TPU:12, one launch (start us, length us, event | category | flops | bytes accessed | tf_op | source)
XLA Modules:
  0.0 48.1 jit_solution(11242867309905054678)
XLA Ops:
  0.6 2.2 %pack.1 = (f32[56,8,256]{2,1,0:T(8,128)}, f32[40,8,256]{2,1,0:T(8,128)}, f32[40,8,256]{2,1,0:T(8,128)}, f32[8,128]{1,0:T(8,128)}) custom-call(f32[3,8,8,256]{3,2,1,0:T(8,128)} %start.6, f32[3,8,8,256]{3,2,1,0:T(8,128)} %source.6, s32[8,8,256]{2,1,0:T(8,128)} %region.1), custom_call_target="tpu_custom_call" | custom-call | tf_op jit(solution)/shard_map/pack/pallas_call | solution.py:594
  2.8 1.6 %collective-permute-start = (f32[56,8,256]{2,1,0:T(8,128)}, f32[56,8,256]{2,1,0:T(8,128)S(1)}, u32[]{:S(2)}, u32[]{:S(2)}) collective-permute-start(f32[56,8,256]{2,1,0:T(8,128)} %get-tuple-element.27.refs_0_), channel_id=1, source_target_pairs={{0,1},{1,0},{2,3},{3,2},{4,5},{5,4},{6,7},{7,6},{8,9},{9,8},{10,11... | collective-permute-start | bytes 1376264 | tf_op jit(solution)/shard_map/ppermute | solution.py:621
  4.4 1.9 %collective-permute-start.1 = (f32[40,8,256]{2,1,0:T(8,128)}, f32[40,8,256]{2,1,0:T(8,128)S(1)}, u32[]{:S(2)}, u32[]{:S(2)}) collective-permute-start(f32[40,8,256]{2,1,0:T(8,128)} %get-tuple-element.28), channel_id=1, source_target_pairs={{2,4},{6,8},{10,12},{14,16},{18,20},{22,24},{26,28},{4,2},{8,6},{1... | collective-permute-start | bytes 983048 | tf_op jit(solution)/shard_map/ppermute | solution.py:629
  6.3 2.7 %first_edges.1 = (f32[4,2,3,3,16,256]{5,4,3,2,1,0:T(8,128)}, f32[4,2,3,2,16,256]{5,4,3,2,1,0:T(8,128)}, f32[4,2,3,1,16,256]{5,4,3,2,1,0:T(8,128)}, f32[8,128]{1,0:T(8,128)}) custom-call(f32[4,2,3,8,16,256]{5,4,3,2,1,0:T(8,128)} %start.11, f32[4,2,3,8,16,256]{5,4,3,2,1,0:T(8,128)} %source.11, f32[8,128]{1,0:T(8,128)} %get-tuple-element.33.after), custom_call_target="tpu_custom_call" | custom-call | tf_op jit(solution)/shard_map/first_edges/pallas_call | solution.py:594
  9.0 0.0 copy-start.9
  9.1 0.1 second_edges.1
  9.2 3.6 %collective-permute-start.5 = (f32[4,2,3,3,16,256]{5,4,3,2,1,0:T(8,128)}, f32[4,2,3,3,16,256]{5,4,3,2,1,0:T(8,128)S(1)}, u32[]{:S(2)}, u32[]{:S(2)}) collective-permute-start(f32[4,2,3,3,16,256]{5,4,3,2,1,0:T(8,128)} %second_edges.1), channel_id=1, source_target_pairs={{2,4},{6,8},{10,12},{14,16},{18,20},{22,24},{26,28},{4,2},{8,6},{1... | collective-permute-start | bytes 3538952 | tf_op jit(solution)/shard_map/ppermute | solution.py:651
  12.8 0.0 copy-done.9
  12.8 2.3 %collective-permute-start.3 = (f32[40,8,256]{2,1,0:T(8,128)S(1)}, f32[40,8,256]{2,1,0:T(8,128)S(1)}, u32[]{:S(2)}, u32[]{:S(2)}) collective-permute-start(f32[40,8,256]{2,1,0:T(8,128)S(1)} %copy-done.9), channel_id=1, source_target_pairs={{0,2},{4,6},{8,10},{12,14},{16,18},{20,22},{24,26},{28,30},{2,0},{... | collective-permute-start | bytes 983048 | tf_op jit(solution)/shard_map/ppermute | solution.py:650
  15.2 1.3 %collective-permute-done.1.refs_1_.refs_2_ = f32[40,8,256]{2,1,0:T(8,128)S(1)} collective-permute-done((f32[40,8,256]{2,1,0:T(8,128)}, f32[40,8,256]{2,1,0:T(8,128)S(1)}, u32[]{:S(2)}, u32[]{:S(2)}) %collective-permute-start.1) | collective-permute-done | bytes 327712 | tf_op jit(solution)/shard_map/ppermute | solution.py:629
  16.5 0.5 %collective-permute-start.2 = (f32[40,8,256]{2,1,0:T(8,128)S(1)}, f32[40,8,256]{2,1,0:T(8,128)S(1)}, u32[]{:S(2)}, u32[]{:S(2)}) collective-permute-start(f32[40,8,256]{2,1,0:T(8,128)S(1)} %collective-permute-done.1.refs_1_.refs_2_), channel_id=1, source_target_pairs={{0,1},{1,0},{2,3},{3,2},{4,5},{5,4},{6,7},{7,6},{8,9},{9,8},{10,11... | collective-permute-start | bytes 983048 | tf_op jit(solution)/shard_map/ppermute | solution.py:621
  17.0 0.0 collective-permute-done.refs_0_.refs_1_
  17.0 0.0 copy-start.2
  17.1 0.6 %copy-done.2 = f32[8,128]{1,0:T(8,128)} copy-done((f32[8,128]{1,0:T(8,128)}, f32[8,128]{1,0:T(8,128)S(1)}, u32[]{:S(2)}) %copy-start.2) | copy-done | bytes 4120
  17.6 0.0 collective-permute-start.4
  17.6 0.0 copy-start.4
  17.6 0.0 copy-start.5
  17.6 0.0 copy-start.6
  17.7 0.0 copy-start.7
  17.7 0.0 copy-start.8
  17.7 2.3 %near_edges.1 = (f32[4,2,3,2,16,256]{5,4,3,2,1,0:T(8,128)}, f32[4,2,3,1,16,256]{5,4,3,2,1,0:T(8,128)}) custom-call(f32[4,2,3,8,16,256]{5,4,3,2,1,0:T(8,128)} %start.11, f32[4,2,3,8,16,256]{5,4,3,2,1,0:T(8,128)} %source.11, f32[8,128]{1,0:T(8,128)} %copy-done.2, ...), custom_call_target="tpu_custom_call", output_to_operand_aliasing={{0}: (3, {}), {1}: (4, {})} | custom-call | tf_op jit(solution)/shard_map/near_edges/pallas_call | solution.py:594
  20.0 0.4 collective-permute-start.6
  20.4 0.0 collective-permute-done.3.refs_4_
  20.4 0.0 copy-start
  20.4 0.0 copy-start.1
  20.4 0.0 copy-start.3
  20.4 0.2 collective-permute-start.7
  20.6 4.3 %collective-permute-done.2.refs_3_ = f32[40,8,256]{2,1,0:T(8,128)S(1)} collective-permute-done((f32[40,8,256]{2,1,0:T(8,128)S(1)}, f32[40,8,256]{2,1,0:T(8,128)S(1)}, u32[]{:S(2)}, u32[]{:S(2)}) %collective-permute-start.2) | collective-permute-done | bytes 327712 | tf_op jit(solution)/shard_map/ppermute | solution.py:621
  24.9 0.0 collective-permute-done.4.refs_5_
  24.9 0.0 copy-done.4
  24.9 0.0 copy-done.5
  24.9 0.0 copy-done.6
  24.9 0.0 copy-done.7
  24.9 0.0 copy-done.8
  24.9 7.4 %bias.1 = (f32[3,8,8,256]{3,2,1,0:T(8,128)}, f32[12,16,256]{2,1,0:T(8,128)S(1)}, f32[10,16,256]{2,1,0:T(8,128)S(1)}) custom-call(f32[56,8,256]{2,1,0:T(8,128)S(1)} %copy-done.4, f32[56,8,256]{2,1,0:T(8,128)S(1)} %collective-permute-done.refs_0_.refs_1_, f32[40,8,256]{2,1,0:T(8,128)S(1)} %collective-permute-done.1.refs_1_.refs_2_, ...), custom_call_target="tpu_custom_call" | custom-call | flops 6000000000 | bytes 20000000 | tf_op jit(solution)/shard_map/bias/pallas_call | solution.py:594
  32.3 0.0 collective-permute-done.7.paired_source
  32.3 0.0 collective-permute-done.6.paired_start
  32.3 0.0 copy-done
  32.3 0.0 copy-done.1
  32.3 0.0 copy-done.3
  32.3 6.3 %inner_ripple.1 = (f32[4,2,3,8,16,256]{5,4,3,2,1,0:T(8,128)}, f32[4,2,3,1,16,256]{5,4,3,2,1,0:T(8,128)S(1)}, f32[4,2,3,2,16,256]{5,4,3,2,1,0:T(8,128)S(1)}, f32[...) custom-call(s32[8]{0:T(128)S(1)} %copy-done.3, ...), custom_call_target="tpu_custom_call" | custom-call | tf_op jit(solution)/shard_map/inner_ripple/pallas_call | solution.py:594
  38.7 3.1 %collective-permute-done.5.apart = f32[4,2,3,3,16,256]{5,4,3,2,1,0:T(8,128)S(1)} collective-permute-done((f32[4,2,3,3,16,256]{5,4,3,2,1,0:T(8,128)}, f32[4,2,3,3,16,256]{5,4,3,2,1,0:T(8,128)S(1)}, u32[]{:S(2)}, u32[]{:S(2)}) %collective-permute-start.5) | collective-permute-done | bytes 1179680 | tf_op jit(solution)/shard_map/ppermute | solution.py:651
  41.8 1.4 %outer_ripple.1 = (f32[4,2,3,2,16,256]{5,4,3,2,1,0:T(8,128)S(1)}, f32[8,8,256]{2,1,0:T(8,128)S(1)}, f32[8,8,256]{2,1,0:T(8,128)S(1)}) custom-call(s32[8]{0:T(128)S(1)} %copy-done.3, f32[10,16,256]{2,1,0:T(8,128)S(1)} %get-tuple-element.32.sigma, f32[4,2,3,8,16,256]{5,4,3,2,1,0:T(8,128)S(1)} %copy-done, f32[4,2,3,8,16,256]{5,4,3,2,1,0:T(8,128)S(1)} %copy-done.1, ...), custom_call_target="tpu_custom_call" | custom-call | tf_op jit(solution)/shard_map/outer_ripple/pallas_call | solution.py:594
  43.2 0.6 %collective-permute-start.8 = (f32[8,8,256]{2,1,0:T(8,128)S(1)}, f32[8,8,256]{2,1,0:T(8,128)S(1)}, u32[]{:S(2)}, u32[]{:S(2)}) collective-permute-start(f32[8,8,256]{2,1,0:T(8,128)S(1)} %get-tuple-element.50), channel_id=1, source_target_pairs={{0,1},{1,0},{2,3},{3,2},{4,5},{5,4},{6,7},{7,6},{8,9},{9,8},{10,11... | collective-permute-start | bytes 196616 | tf_op jit(solution)/shard_map/ppermute | solution.py:700
  43.8 0.9 %place.1 = f32[4,2,3,8,16,256]{5,4,3,2,1,0:T(8,128)} custom-call(f32[4,2,3,2,16,256]{5,4,3,2,1,0:T(8,128)S(1)} %get-tuple-element.47.edge, f32[4,2,3,8,16,256]{5,4,3,2,1,0:T(8,128)} %get-tuple-element.48.ripple_in), custom_call_target="tpu_custom_call", output_to_operand_aliasing={{}: (1, {})} | custom-call | tf_op jit(solution)/shard_map/place/pallas_call | solution.py:594
  44.7 2.8 %collective-permute-done.8 = f32[8,8,256]{2,1,0:T(8,128)S(1)} collective-permute-done((f32[8,8,256]{2,1,0:T(8,128)S(1)}, f32[8,8,256]{2,1,0:T(8,128)S(1)}, u32[]{:S(2)}, u32[]{:S(2)}) %collective-permute-start.8) | collective-permute-done | bytes 65568 | tf_op jit(solution)/shard_map/ppermute | solution.py:700
  47.5 0.6 %add.3 = f32[8,8,256]{2,1,0:T(8,128)} add(f32[8,8,256]{2,1,0:T(8,128)S(1)} %get-tuple-element.49, f32[8,8,256]{2,1,0:T(8,128)S(1)} %collective-permute-done.8) | non-fusion elementwise | flops 16384 | bytes 196608 | tf_op jit(solution)/shard_map/add | solution.py:700
  (1 shorter events, 0.0 us)
Async XLA Ops:
  2.8 14.2 %collective-permute-start = (f32[56,8,256]{2,1,0:T(8,128)}, f32[56,8,256]{2,1,0:T(8,128)S(1)}, u32[]{:S(2)}, u32[]{:S(2)}) collective-permute-start(f32[56,8,256]{2,1,0:T(8,128)} %get-tuple-element.27.refs_0_), channel_id=1, source_target_pairs={{0,1},{1,0},{2,3},{3,2},{4,5},{5,4},{6,7},{7,6},{8,9},{9,8},{10,11... | collective-permute-start | bytes 1376264 | tf_op jit(solution)/shard_map/ppermute | solution.py:621
  4.4 12.1 %collective-permute-start.1 = (f32[40,8,256]{2,1,0:T(8,128)}, f32[40,8,256]{2,1,0:T(8,128)S(1)}, u32[]{:S(2)}, u32[]{:S(2)}) collective-permute-start(f32[40,8,256]{2,1,0:T(8,128)} %get-tuple-element.28), channel_id=1, source_target_pairs={{2,4},{6,8},{10,12},{14,16},{18,20},{22,24},{26,28},{4,2},{8,6},{1... | collective-permute-start | bytes 983048 | tf_op jit(solution)/shard_map/ppermute | solution.py:629
  9.0 3.8 %copy-start.9 = (f32[40,8,256]{2,1,0:T(8,128)S(1)}, f32[40,8,256]{2,1,0:T(8,128)}, u32[]{:S(2)}) copy-start(f32[40,8,256]{2,1,0:T(8,128)} %get-tuple-element.29) | copy-start | bytes 983044
  9.2 32.6 %collective-permute-start.5 = (f32[4,2,3,3,16,256]{5,4,3,2,1,0:T(8,128)}, f32[4,2,3,3,16,256]{5,4,3,2,1,0:T(8,128)S(1)}, u32[]{:S(2)}, u32[]{:S(2)}) collective-permute-start(f32[4,2,3,3,16,256]{5,4,3,2,1,0:T(8,128)} %second_edges.1), channel_id=1, source_target_pairs={{2,4},{6,8},{10,12},{14,16},{18,20},{22,24},{26,28},{4,2},{8,6},{1... | collective-permute-start | bytes 3538952 | tf_op jit(solution)/shard_map/ppermute | solution.py:651
  12.8 7.5 %collective-permute-start.3 = (f32[40,8,256]{2,1,0:T(8,128)S(1)}, f32[40,8,256]{2,1,0:T(8,128)S(1)}, u32[]{:S(2)}, u32[]{:S(2)}) collective-permute-start(f32[40,8,256]{2,1,0:T(8,128)S(1)} %copy-done.9), channel_id=1, source_target_pairs={{0,2},{4,6},{8,10},{12,14},{16,18},{20,22},{24,26},{28,30},{2,0},{... | collective-permute-start | bytes 983048 | tf_op jit(solution)/shard_map/ppermute | solution.py:650
  16.5 8.4 %collective-permute-start.2 = (f32[40,8,256]{2,1,0:T(8,128)S(1)}, f32[40,8,256]{2,1,0:T(8,128)S(1)}, u32[]{:S(2)}, u32[]{:S(2)}) collective-permute-start(f32[40,8,256]{2,1,0:T(8,128)S(1)} %collective-permute-done.1.refs_1_.refs_2_), channel_id=1, source_target_pairs={{0,1},{1,0},{2,3},{3,2},{4,5},{5,4},{6,7},{7,6},{8,9},{9,8},{10,11... | collective-permute-start | bytes 983048 | tf_op jit(solution)/shard_map/ppermute | solution.py:621
  17.0 0.6 %copy-start.2 = (f32[8,128]{1,0:T(8,128)}, f32[8,128]{1,0:T(8,128)S(1)}, u32[]{:S(2)}) copy-start(f32[8,128]{1,0:T(8,128)S(1)} %get-tuple-element.37.after) | copy-start | bytes 12292
  17.6 7.2 %collective-permute-start.4 = (f32[1,40,8,256]{3,2,1,0:T(8,128)S(1)}, f32[1,40,8,256]{3,2,1,0:T(8,128)S(1)}, u32[]{:S(2)}, u32[]{:S(2)}) collective-permute-start(f32[1,40,8,256]{3,2,1,0:T(8,128)S(1)} %get-tuple-element.30), channel_id=1, source_target_pairs={{0,2},{4,6},{8,10},{12,14},{16,18},{20,22},{24,26},{28,30},{2,0},{... | collective-permute-start | bytes 983048 | tf_op jit(solution)/shard_map/ppermute | solution.py:650
  17.6 7.2 %copy-start.4 = (f32[56,8,256]{2,1,0:T(8,128)S(1)}, f32[56,8,256]{2,1,0:T(8,128)}, u32[]{:S(2)}) copy-start(f32[56,8,256]{2,1,0:T(8,128)} %get-tuple-element.27.refs_0_) | copy-start | bytes 1376260
  17.6 7.2 %copy-start.5 = (f32[4,8]{1,0:T(4,128)S(1)}, f32[4,8]{1,0:T(4,128)}, u32[]{:S(2)}) copy-start(f32[4,8]{1,0:T(4,128)} %refs_8_.1) | copy-start | bytes 388
  17.6 7.2 %copy-start.6 = (s32[4]{0:T(128)S(1)}, s32[4]{0:T(128)}, u32[]{:S(2)}) copy-start(s32[4]{0:T(128)} %refs_6_.1) | copy-start | bytes 52
  17.7 7.2 %copy-start.7 = (f32[4]{0:T(128)S(1)}, f32[4]{0:T(128)}, u32[]{:S(2)}) copy-start(f32[4]{0:T(128)} %refs_7_.1) | copy-start | bytes 52
  17.7 7.2 %copy-start.8 = (f32[4]{0:T(128)S(1)}, f32[4]{0:T(128)}, u32[]{:S(2)}) copy-start(f32[4]{0:T(128)} %refs_9_.1) | copy-start | bytes 52
  20.0 12.4 %collective-permute-start.6 = (f32[4,2,3,2,16,256]{5,4,3,2,1,0:T(8,128)}, f32[4,2,3,2,16,256]{5,4,3,2,1,0:T(8,128)S(1)}, u32[]{:S(2)}, u32[]{:S(2)}) collective-permute-start(f32[4,2,3,2,16,256]{5,4,3,2,1,0:T(8,128)} %get-tuple-element.40), channel_id=1, source_target_pairs={{0,2},{4,6},{8,10},{12,14},{16,18},{20,22},{24,26},{28,30},{2,0},{... | collective-permute-start | bytes 2359304 | tf_op jit(solution)/shard_map/ppermute | solution.py:652
  20.4 11.9 %copy-start = (f32[4,2,3,8,16,256]{5,4,3,2,1,0:T(8,128)S(1)}, f32[4,2,3,8,16,256]{5,4,3,2,1,0:T(8,128)}, u32[]{:S(2)}) copy-start(f32[4,2,3,8,16,256]{5,4,3,2,1,0:T(8,128)} %start.11) | copy-start | bytes 9437188
  20.4 11.9 %copy-start.1 = (f32[4,2,3,8,16,256]{5,4,3,2,1,0:T(8,128)S(1)}, f32[4,2,3,8,16,256]{5,4,3,2,1,0:T(8,128)}, u32[]{:S(2)}) copy-start(f32[4,2,3,8,16,256]{5,4,3,2,1,0:T(8,128)} %source.11) | copy-start | bytes 9437188
  20.4 12.0 %copy-start.3 = (s32[8]{0:T(128)S(1)}, s32[8]{0:T(128)}, u32[]{:S(2)}) copy-start(s32[8]{0:T(128)} %harmonic_numbers.3) | copy-start | bytes 100
  20.4 11.9 %collective-permute-start.7 = (f32[4,2,3,1,16,256]{5,4,3,2,1,0:T(8,128)}, f32[4,2,3,1,16,256]{5,4,3,2,1,0:T(8,128)S(1)}, u32[]{:S(2)}, u32[]{:S(2)}) collective-permute-start(f32[4,2,3,1,16,256]{5,4,3,2,1,0:T(8,128)} %get-tuple-element.41), channel_id=1, source_target_pairs={{0,2},{4,6},{8,10},{12,14},{16,18},{20,22},{24,26},{28,30},{2,0},{... | collective-permute-start | bytes 1179656 | tf_op jit(solution)/shard_map/ppermute | solution.py:652
  43.2 4.3 %collective-permute-start.8 = (f32[8,8,256]{2,1,0:T(8,128)S(1)}, f32[8,8,256]{2,1,0:T(8,128)S(1)}, u32[]{:S(2)}, u32[]{:S(2)}) collective-permute-start(f32[8,8,256]{2,1,0:T(8,128)S(1)} %get-tuple-element.50), channel_id=1, source_target_pairs={{0,1},{1,0},{2,3},{3,2},{4,5},{5,4},{6,7},{7,6},{8,9},{9,8},{10,11... | collective-permute-start | bytes 196616 | tf_op jit(solution)/shard_map/ppermute | solution.py:700
